TPU v7x, 32 devices: a whole 2x2x4 slice. The times are simulated.
32 devices in a mesh: lat: 8 (over z, y), lon: 4 (over x, core).
Axes of the slice: x: 2, y: 2, z: 4, core: 2. Of those that a mesh axis runs over, the one named last changes fastest.
Arguments:
- inputs: bfloat16 [320, 720, 256], P('lat', 'lon'), may hold values from -6 to 6
- w_enc: bfloat16 [3, 3, 256, 256], replicated, may hold values from -0.125 to 0.125
- w_proj: bfloat16 [256, 128], replicated, may hold values from -0.375 to 0.375
- film_scale: float32 [720, 128], replicated, may hold values from -3 to 3
- film_shift: float32 [720, 128], replicated, may hold values from -3 to 3
- lead_ids: int32 [8], replicated, may hold values from 0 to 719
- w_head: bfloat16 [3, 3, 128, 128], replicated, may hold values from -0.1875 to 0.1875
- zonal_mix: bfloat16 [360, 360], replicated, may hold values from -0.3125 to 0.3125
Outputs:
- forecast: bfloat16 [8, 160, 360, 128], P('lon', 'lat')
Inputs may be any that keep to these rules, and one draw needn't show every extreme that they name: `lead_ids`: rows of the tables; repeats may occur.
All inputs are finite; a program needn't handle non-finite values.
Results may differ from a plain program's by a relative error of at most 0.015.
Values may be sent and summed in bfloat16 or wider, within the bound.
No kernel may reach another device: no remote copies, remote signals or barrier semaphores. Data moves between devices by JAX's collectives and lax.ppermute only.
A program may use at most 128 MiB of HBM per device.

v0:
```python
import jax
import jax.numpy as jnp
from jax import lax
from jax.sharding import PartitionSpec as P

LEAD_DEV = 2


def extended(x, sides, width, wrap):
    for axis, dim in sides:
        devices, length = (lax.axis_size(axis), x.shape[dim])
        up = [(i, (i + 1) % devices) for i in range(devices if wrap else devices - 1)]
        down = [(j, i) for i, j in up]
        last = lax.slice_in_dim(x, length - width, length, axis=dim)
        initial = lax.slice_in_dim(x, 0, width, axis=dim)
        before = lax.ppermute(last, axis, up)
        after = lax.ppermute(initial, axis, down)
        x = jnp.concatenate([before, x, after], axis=dim)
    return x


def conv_three(padded, weight):
    batched = padded if padded.ndim == 4 else padded[None]
    result = lax.conv_general_dilated(
        batched,
        weight,
        (1, 1),
        "VALID",
        dimension_numbers=("NHWC", "HWIO", "NHWC"),
        preferred_element_type=jnp.float32,
    )
    return result if padded.ndim == 4 else result[0]


def pool_pairs(field):
    summed = lax.reduce_window(
        field, jnp.array(0, field.dtype), lax.add, (2, 2, 1), (2, 2, 1), "VALID"
    )
    return summed * 0.25


def wrap_columns(field):
    return jnp.concatenate([field[..., -1:, :], field, field[..., :1, :]], axis=-2)


def modulate(projected, scales, shifts):
    widened = projected.astype(jnp.float32)[None]
    return (widened * (1.0 + scales[:, None, None, :]) + shifts[:, None, None, :]).astype(
        jnp.bfloat16
    )


def shards(inputs, w_enc, w_proj, film_scale, film_shift, lead_ids, w_head, zonal_mix):
    lat_rows, lon_cols, channels = inputs.shape
    with_rows = extended(inputs, (("lat", 0),), 1, False)
    padded = extended(with_rows, (("lon", 1),), 1, True)
    encoded = jax.nn.gelu(conv_three(padded, w_enc))
    pooled = pool_pairs(encoded).astype(jnp.bfloat16)
    head_width = w_proj.shape[1]
    lon_group = lax.axis_index("lon")
    my_rows = lax.dynamic_slice_in_dim(lead_ids, lon_group * LEAD_DEV, LEAD_DEV)
    flat = jnp.dot(pooled.reshape(-1, channels), w_proj, preferred_element_type=jnp.float32)
    band_proj = lax.all_gather(
        flat.astype(jnp.bfloat16).reshape(pooled.shape[0], pooled.shape[1], head_width),
        "lon",
        axis=1,
        tiled=True,
    )
    onehot = (my_rows[:, None] == jnp.arange(film_scale.shape[0], dtype=jnp.int32)[None, :]).astype(
        jnp.float32
    )
    scales = jnp.dot(onehot, film_scale, precision=lax.Precision.HIGHEST)
    shifts = jnp.dot(onehot, film_shift, precision=lax.Precision.HIGHEST)
    scales, shifts = (scales, shifts)
    with_band = None
    modulated = modulate(band_proj, scales, shifts)
    with_band = extended(modulated, (("lat", 1),), 1, False)
    padded_head = wrap_columns(with_band)
    hidden = jax.nn.gelu(conv_three(padded_head, w_head)).astype(jnp.bfloat16)
    mixed = jnp.einsum("ij,bajc->baic", zonal_mix, hidden, preferred_element_type=jnp.float32)
    return (modulated.astype(jnp.float32) + mixed).astype(jnp.bfloat16)


def solution(mesh):
    in_specs = (P("lat", "lon", None), P(), P(), P(), P(), P(), P(), P())
    out_specs = P("lon", "lat", None, None)
    return jax.shard_map(shards, mesh=mesh, in_specs=in_specs, out_specs=out_specs, check_vma=False)
```

profile of v0, /device:TPU:25, one launch (start us, length us, event | category | flops | bytes accessed | tf_op | source)
XLA Modules:
  0.0 148.7 jit_solution(1572415162376120875)
XLA Ops:
  6.5 1.8 %fusion.46 = (bf16[1,180,256]{2,0,1:T(2,128)(2,1)S(1)}, bf16[1,180,256]{2,0,1:T(2,128)(2,1)S(1)}) fusion(bf16[40,180,256]{2,0,1:T(8,128)(2,1)} %param.8), kind=kLoop, calls=%fused_computation.63 | loop fusion | bytes 368640 | tf_op jit(solution)/shard_map/slice | solution.py:14
  8.4 3.3 %collective-permute-start = (bf16[1,180,256]{2,1,0:T(8,128)(2,1)S(1)}, bf16[1,180,256]{2,1,0:T(8,128)(2,1)S(1)}, u32[]{:S(2)}, u32[]{:S(2)}) collective-permute-start(bf16[1,180,256]{2,1,0:T(8,128)(2,1)S(1)} %copy.63), channel_id=1, source_target_pairs={{0,4},{4,8},{8,12},{12,16},{16,20},{20,24},{24,28},{1,5},{5,9},{9,... | collective-permute-start | bytes 276488 | tf_op jit(solution)/shard_map/ppermute | solution.py:16
  11.7 3.0 %collective-permute-start.1 = (bf16[1,180,256]{2,1,0:T(8,128)(2,1)S(1)}, bf16[1,180,256]{2,1,0:T(8,128)(2,1)S(1)}, u32[]{:S(2)}, u32[]{:S(2)}) collective-permute-start(bf16[1,180,256]{2,1,0:T(8,128)(2,1)S(1)} %copy.64), channel_id=1, source_target_pairs={{4,0},{8,4},{12,8},{16,12},{20,16},{24,20},{28,24},{5,1},{9,5},{13... | collective-permute-start | bytes 276488 | tf_op jit(solution)/shard_map/ppermute | solution.py:17
  14.9 2.1 %collective-permute-done.1 = bf16[1,180,256]{2,1,0:T(8,128)(2,1)S(1)} collective-permute-done((bf16[1,180,256]{2,1,0:T(8,128)(2,1)S(1)}, bf16[1,180,256]{2,1,0:T(8,128)(2,1)S(1)}, u32[]{:S(2)}, u32[]{:S(2)}) %collective-permute-start.1) | collective-permute-done | bytes 92192 | tf_op jit(solution)/shard_map/ppermute | solution.py:17
  17.1 0.8 pad_maximum_fusion.6
  17.9 3.3 %collective-permute-start.2 = (bf16[42,1,256]{2,0,1:T(8,128)(2,1)S(1)}, bf16[42,1,256]{2,0,1:T(8,128)(2,1)S(1)}, u32[]{:S(2)}, u32[]{:S(2)}) collective-permute-start(bf16[42,1,256]{2,0,1:T(8,128)(2,1)S(1)} %get-tuple-element.5), channel_id=1, source_target_pairs={{0,1},{1,2},{2,3},{3,0},{4,5},{5,6},{6,7},{7,4},{8,9},{9,10},{10,1... | collective-permute-start | bytes 64520 | tf_op jit(solution)/shard_map/ppermute | solution.py:16
  21.2 0.9 collective-permute-done.2
  22.1 2.3 %collective-permute-done.3 = bf16[42,1,256]{2,0,1:T(8,128)(2,1)S(1)} collective-permute-done((bf16[42,1,256]{2,0,1:T(8,128)(2,1)S(1)}, bf16[42,1,256]{2,0,1:T(8,128)(2,1)S(1)}, u32[]{:S(2)}, u32[]{:S(2)}) %collective-permute-start.3) | collective-permute-done | bytes 21536 | tf_op jit(solution)/shard_map/ppermute | solution.py:17
  24.4 2.8 %maximum_bitcast_fusion = bf16[42,1,182,256]{3,0,2,1:T(8,128)(2,1)S(1)} fusion(bf16[42,1,256]{2,0,1:T(8,128)(2,1)S(1)} %collective-permute-done.3, bf16[1,180,256]{2,0,1:T(2,128)(2,1)S(1)} %copy.46, bf16[40,180,256]{2,0,1:T(8,128)(2,1)S(1)} %copy-done.2, bf16[1,180,256]{2,0,1:T(2,128)(2,1)S(1)} %copy.45, bf16[42,1,256]{2,0,1:T(8,128)(2,1)S(1)} %collective-permute-done.2), kind=kLoop, calls=%fused_computation.25 | loop fusion | flops 19568640 | bytes 7827456 | tf_op jit(solution)/shard_map/broadcast_in_dim | solution.py:23
  27.6 1.5 %copy.49 = bf16[42,1,8,23,256]{4,2,3,0,1:T(8,128)(2,1)S(1)} copy(bf16[42,1,8,23,256]{4,0,3,2,1:T(8,128)(2,1)S(1)} %bitcast.45) | data formatting | bytes 7913472 | tf_op jit(solution)/shard_map/conv_general_dilated | solution.py:24
  29.3 9.5 %broadcast_select_fusion = f32[40,8,23,256]{3,1,2,0:T(8,128)S(1)} fusion(pred[8,23]{0,1:T(8,128)(4,1)S(1)} %copy-done.11, bf16[3,3,256,256]{3,2,1,0:T(8,128)(2,1)S(1)} %copy-done, bf16[42,1,7,2,256]{4,2,3,0,1:T(8,128)(2,1)S(1)} %slice.36, bf16[42,1,8,23,256]{4,2,3,0,1:T(8,128)(2,1)S(1)} %copy.49), kind=kOutput, calls=%fused_computation.43 | convolution fusion | flops 8696995840 | bytes 12974264 | tf_op jit(solution)/shard_map/conv_general_dilated | solution.py:24
  38.8 2.6 %copy.50 = f32[40,8,23,256]{3,0,2,1:T(8,128)S(1)} copy(f32[40,8,23,256]{3,1,2,0:T(8,128)S(1)} %broadcast_select_fusion) | data formatting | bytes 15073280 | tf_op jit(solution)/shard_map/conv_general_dilated | solution.py:24
  41.4 4.1 %fusion.16 = f32[40,180,256]{2,0,1:T(8,128)} fusion(f32[40,1,184,256]{3,0,2,1:T(8,128)S(1)} %bitcast.44), kind=kLoop, calls=%fused_computation.20 | loop fusion | flops 14745600 | bytes 14745600 | tf_op jit(solution)/shard_map/mul | solution.py:57
  45.5 8.4 %reduce_window.7 = f32[20,90,256]{2,0,1:T(8,128)S(1)} reduce-window(f32[40,180,256]{2,0,1:T(8,128)} %fusion.16, f32[]{:T(128)} %constant.14.clone.1), window={size=2x2x1 stride=2x2x1}, to_apply=%region_0.0 | reduce-window | flops 1382400 | bytes 9216004 | tf_op jit(solution)/shard_map/reduce_window | solution.py:36
  54.7 0.4 convolution_convert_fusion
  55.2 1.0 copy.52
  56.9 22.6 %all-gather.2.cloned.1.call-done = bf16[20,360,128]{2,0,1:T(8,128)(2,1)} async-done(((bf16[20,90,128]{2,0,1:T(8,128)(2,1)}), bf16[20,360,128]{2,0,1:T(8,128)(2,1)}) %all-gather.2.cloned.1.call-update) | async-done | bytes 1843216 | tf_op jit(solution)/shard_map/all_gather | solution.py:63
  79.5 1.9 %copy_convert_fusion = f32[20,360,128]{2,1,0:T(8,128)S(1)} fusion(bf16[20,360,128]{2,0,1:T(8,128)(2,1)} %all-gather.2.cloned.1.call-done), kind=kLoop, calls=%fused_computation.49 | loop fusion | flops 921600 | bytes 5529600 | tf_op jit(solution)/shard_map/convert_element_type | solution.py:47
  81.3 0.8 add_convert_fusion
  82.2 3.1 %collective-permute-start.4 = (bf16[2,1,360,128]{3,2,1,0:T(8,128)(2,1)S(1)}, bf16[2,1,360,128]{3,2,1,0:T(8,128)(2,1)S(1)}, u32[]{:S(2)}, u32[]{:S(2)}) collective-permute-start(bf16[2,1,360,128]{3,2,1,0:T(8,128)(2,1)S(1)} %get-tuple-element.7), channel_id=1, source_target_pairs={{0,4},{4,8},{8,12},{12,16},{16,20},{20,24},{24,28},{1,5},{5,9},{9,... | collective-permute-start | bytes 552968 | tf_op jit(solution)/shard_map/ppermute | solution.py:16
  85.3 3.1 %collective-permute-start.5 = (bf16[2,1,360,128]{3,2,1,0:T(8,128)(2,1)S(1)}, bf16[2,1,360,128]{3,2,1,0:T(8,128)(2,1)S(1)}, u32[]{:S(2)}, u32[]{:S(2)}) collective-permute-start(bf16[2,1,360,128]{3,2,1,0:T(8,128)(2,1)S(1)} %get-tuple-element.8), channel_id=1, source_target_pairs={{4,0},{8,4},{12,8},{16,12},{20,16},{24,20},{28,24},{5,1},{9,5},{13... | collective-permute-start | bytes 552968 | tf_op jit(solution)/shard_map/ppermute | solution.py:17
  88.4 2.6 %collective-permute-done.4 = bf16[2,1,360,128]{3,2,1,0:T(8,128)(2,1)S(1)} collective-permute-done((bf16[2,1,360,128]{3,2,1,0:T(8,128)(2,1)S(1)}, bf16[2,1,360,128]{3,2,1,0:T(8,128)(2,1)S(1)}, u32[]{:S(2)}, u32[]{:S(2)}) %collective-permute-start.4) | collective-permute-done | bytes 184352 | tf_op jit(solution)/shard_map/ppermute | solution.py:16
  90.9 4.5 %collective-permute-done.5 = bf16[2,1,360,128]{3,2,1,0:T(8,128)(2,1)S(1)} collective-permute-done((bf16[2,1,360,128]{3,2,1,0:T(8,128)(2,1)S(1)}, bf16[2,1,360,128]{3,2,1,0:T(8,128)(2,1)S(1)}, u32[]{:S(2)}, u32[]{:S(2)}) %collective-permute-start.5) | collective-permute-done | bytes 184352 | tf_op jit(solution)/shard_map/ppermute | solution.py:17
  95.5 5.3 %fusion.30 = bf16[22,2,362,128]{3,2,0,1:T(8,128)(2,1)S(1)} fusion(bf16[2,1,360,128]{3,2,1,0:T(8,128)(2,1)S(1)} %collective-permute-done.5, bf16[2,20,360,128]{3,2,1,0:T(8,128)(2,1)S(1)} %add_convert_fusion, bf16[2,1,360,128]{3,2,1,0:T(8,128)(2,1)S(1)} %collective-permute-done.4), kind=kLoop, calls=%fused_computation.38 | loop fusion | flops 36698112 | bytes 8132608 | tf_op jit(solution)/shard_map/concatenate | solution.py:43
  100.8 2.3 %pad.2 = bf16[22,2,368,128]{3,2,0,1:T(8,128)(2,1)} pad(bf16[22,2,362,128]{3,2,0,1:T(8,128)(2,1)S(1)} %fusion.30, bf16[]{:T(256)} %constant.5), padding=0_0x0_0x0_6x0_0 | pad | bytes 8222722 | tf_op jit(solution)/shard_map/concatenate | solution.py:43
  103.1 6.9 %reshape.39 = bf16[22,2,8,46,128]{4,3,2,0,1:T(8,128)(2,1)} reshape(bf16[22,2,368,128]{3,2,0,1:T(8,128)(2,1)} %pad.2) | data formatting | bytes 8290304 | tf_op jit(solution)/shard_map/conv_general_dilated | solution.py:24
  110.0 1.2 slice.40
  111.3 2.9 %fusion.18 = bf16[22,2,8,48,128]{4,3,2,1,0:T(8,128)(2,1)S(1)} fusion(bf16[22,2,7,2,128]{4,3,2,1,0:T(2,128)(2,1)S(1)} %copy.79, bf16[22,2,8,46,128]{4,3,2,0,1:T(8,128)(2,1)} %reshape.39), kind=kLoop, calls=%fused_computation.26 | loop fusion | flops 12976128 | bytes 8628224 | tf_op jit(solution)/shard_map/conv_general_dilated | solution.py:24
  114.3 10.7 %fusion.9 = bf16[20,16,46,128]{3,1,2,0:T(8,128)(2,1)S(1)} fusion(pred[16,46]{0,1:T(8,128)(4,1)S(1)} %copy-done.10, bf16[3,3,128,128]{3,2,1,0:T(8,128)(2,1)S(1)} %copy-done.7, bf16[22,2,8,48,128]{4,3,2,1,0:T(8,128)(2,1)S(1)} %fusion.18), kind=kOutput, calls=%fused_computation.13 | convolution fusion | flops 4359946240 | bytes 8389344 | tf_op jit(solution)/shard_map/conv_general_dilated | solution.py:24
  125.0 2.9 %copy.56 = bf16[20,16,46,128]{3,2,1,0:T(8,128)(2,1)} copy(bf16[20,16,46,128]{3,1,2,0:T(8,128)(2,1)S(1)} %fusion.9) | data formatting | bytes 7536640 | tf_op jit(solution)/shard_map/convert_element_type | solution.py:79
  127.9 6.8 %reshape.27 = bf16[20,2,368,128]{3,2,1,0:T(8,128)(2,1)} reshape(bf16[20,16,46,128]{3,2,1,0:T(8,128)(2,1)} %copy.56) | data formatting | bytes 7536640 | tf_op jit(solution)/shard_map/convert_element_type | solution.py:79
  134.6 7.2 %fusion.17 = bf16[2,20,360,128]{3,2,1,0:T(8,128)(2,1)} fusion(bf16[2,20,360,128]{3,2,1,0:T(8,128)(2,1)} %copy-done.3, bf16[360,360]{1,0:T(8,128)(2,1)S(1)} %copy-done.8, bf16[20,2,368,128]{3,2,1,0:T(8,128)(2,1)} %reshape.27), kind=kOutput, calls=%fused_computation.23 | convolution fusion | flops 1332633600 | bytes 11318400 | tf_op jit(solution)/shard_map/ij,bajc->baic/dot_general | solution.py:80
  (43 shorter events, 2.5 us)
Async XLA Ops:
  6.5 22.7 %copy-start = (bf16[3,3,256,256]{3,2,1,0:T(8,128)(2,1)S(1)}, bf16[3,3,256,256]{3,2,1,0:T(8,128)(2,1)}, u32[]{:S(2)}) copy-start(bf16[3,3,256,256]{3,2,1,0:T(8,128)(2,1)} %param.9) | copy-start | bytes 3538948
  6.5 72.9 %all-gather.2.cloned.1.call-start = ((), (), s32[]{:S(2)}) async-start(), calls=%async_computation | async-start | bytes 2764800 | tf_op jit(solution)/shard_map/all_gather | solution.py:63
  6.5 17.9 %copy-start.2 = (bf16[40,180,256]{2,0,1:T(8,128)(2,1)S(1)}, bf16[40,180,256]{2,0,1:T(8,128)(2,1)}, u32[]{:S(2)}) copy-start(bf16[40,180,256]{2,0,1:T(8,128)(2,1)} %param.8) | copy-start | bytes 11059204
  8.4 6.4 %collective-permute-start = (bf16[1,180,256]{2,1,0:T(8,128)(2,1)S(1)}, bf16[1,180,256]{2,1,0:T(8,128)(2,1)S(1)}, u32[]{:S(2)}, u32[]{:S(2)}) collective-permute-start(bf16[1,180,256]{2,1,0:T(8,128)(2,1)S(1)} %copy.63), channel_id=1, source_target_pairs={{0,4},{4,8},{8,12},{12,16},{16,20},{20,24},{24,28},{1,5},{5,9},{9,... | collective-permute-start | bytes 276488 | tf_op jit(solution)/shard_map/ppermute | solution.py:16
  11.7 5.3 %collective-permute-start.1 = (bf16[1,180,256]{2,1,0:T(8,128)(2,1)S(1)}, bf16[1,180,256]{2,1,0:T(8,128)(2,1)S(1)}, u32[]{:S(2)}, u32[]{:S(2)}) collective-permute-start(bf16[1,180,256]{2,1,0:T(8,128)(2,1)S(1)} %copy.64), channel_id=1, source_target_pairs={{4,0},{8,4},{12,8},{16,12},{20,16},{24,20},{28,24},{5,1},{9,5},{13... | collective-permute-start | bytes 276488 | tf_op jit(solution)/shard_map/ppermute | solution.py:17
  17.9 4.2 %collective-permute-start.2 = (bf16[42,1,256]{2,0,1:T(8,128)(2,1)S(1)}, bf16[42,1,256]{2,0,1:T(8,128)(2,1)S(1)}, u32[]{:S(2)}, u32[]{:S(2)}) collective-permute-start(bf16[42,1,256]{2,0,1:T(8,128)(2,1)S(1)} %get-tuple-element.5), channel_id=1, source_target_pairs={{0,1},{1,2},{2,3},{3,0},{4,5},{5,6},{6,7},{7,4},{8,9},{9,10},{10,1... | collective-permute-start | bytes 64520 | tf_op jit(solution)/shard_map/ppermute | solution.py:16
  21.2 3.3 %collective-permute-start.3 = (bf16[42,1,256]{2,0,1:T(8,128)(2,1)S(1)}, bf16[42,1,256]{2,0,1:T(8,128)(2,1)S(1)}, u32[]{:S(2)}, u32[]{:S(2)}) collective-permute-start(bf16[42,1,256]{2,0,1:T(8,128)(2,1)S(1)} %get-tuple-element.6), channel_id=1, source_target_pairs={{1,0},{2,1},{3,2},{0,3},{5,4},{6,5},{7,6},{4,7},{9,8},{10,9},{11,1... | collective-permute-start | bytes 64520 | tf_op jit(solution)/shard_map/ppermute | solution.py:17
  27.6 1.6 %copy-start.11 = (pred[8,23]{0,1:T(8,128)(4,1)S(1)}, pred[8,23]{0,1:T(8,128)(4,1)}, u32[]{:S(2)}) copy-start(pred[8,23]{0,1:T(8,128)(4,1)} %constant.35) | copy-start | bytes 556
  53.9 0.8 copy-start.6
  54.1 2.2 %copy-start.9 = (s32[8]{0:T(128)S(1)}, s32[8]{0:T(128)}, u32[]{:S(2)}) copy-start(s32[8]{0:T(128)} %param.13) | copy-start | bytes 100
  54.1 2.3 %copy-start.4 = (f32[720,128]{1,0:T(8,128)S(1)}, f32[720,128]{1,0:T(8,128)}, u32[]{:S(2)}) copy-start(f32[720,128]{1,0:T(8,128)} %param.11) | copy-start | bytes 1105924
  54.1 2.5 %copy-start.5 = (f32[720,128]{1,0:T(8,128)S(1)}, f32[720,128]{1,0:T(8,128)}, u32[]{:S(2)}) copy-start(f32[720,128]{1,0:T(8,128)} %param.12) | copy-start | bytes 1105924
  82.1 13.4 %copy-start.3 = (bf16[2,20,360,128]{3,2,1,0:T(8,128)(2,1)}, bf16[2,20,360,128]{3,2,1,0:T(8,128)(2,1)S(1)}, u32[]{:S(2)}) copy-start(bf16[2,20,360,128]{3,2,1,0:T(8,128)(2,1)S(1)} %add_convert_fusion) | copy-start | bytes 11059204
  82.2 8.8 %collective-permute-start.4 = (bf16[2,1,360,128]{3,2,1,0:T(8,128)(2,1)S(1)}, bf16[2,1,360,128]{3,2,1,0:T(8,128)(2,1)S(1)}, u32[]{:S(2)}, u32[]{:S(2)}) collective-permute-start(bf16[2,1,360,128]{3,2,1,0:T(8,128)(2,1)S(1)} %get-tuple-element.7), channel_id=1, source_target_pairs={{0,4},{4,8},{8,12},{12,16},{16,20},{20,24},{24,28},{1,5},{5,9},{9,... | collective-permute-start | bytes 552968 | tf_op jit(solution)/shard_map/ppermute | solution.py:16
  85.3 10.2 %collective-permute-start.5 = (bf16[2,1,360,128]{3,2,1,0:T(8,128)(2,1)S(1)}, bf16[2,1,360,128]{3,2,1,0:T(8,128)(2,1)S(1)}, u32[]{:S(2)}, u32[]{:S(2)}) collective-permute-start(bf16[2,1,360,128]{3,2,1,0:T(8,128)(2,1)S(1)} %get-tuple-element.8), channel_id=1, source_target_pairs={{4,0},{8,4},{12,8},{16,12},{20,16},{24,20},{28,24},{5,1},{9,5},{13... | collective-permute-start | bytes 552968 | tf_op jit(solution)/shard_map/ppermute | solution.py:17
  111.3 2.9 %copy-start.7 = (bf16[3,3,128,128]{3,2,1,0:T(8,128)(2,1)S(1)}, bf16[3,3,128,128]{3,2,1,0:T(8,128)(2,1)}, u32[]{:S(2)}) copy-start(bf16[3,3,128,128]{3,2,1,0:T(8,128)(2,1)} %param.14) | copy-start | bytes 884740
  111.3 2.9 %copy-start.10 = (pred[16,46]{0,1:T(8,128)(4,1)S(1)}, pred[16,46]{0,1:T(8,128)(4,1)}, u32[]{:S(2)}) copy-start(pred[16,46]{0,1:T(8,128)(4,1)} %constant.36) | copy-start | bytes 2212
  127.8 6.8 %copy-start.8 = (bf16[360,360]{1,0:T(8,128)(2,1)S(1)}, bf16[360,360]{1,0:T(8,128)(2,1)}, u32[]{:S(2)}) copy-start(bf16[360,360]{1,0:T(8,128)(2,1)} %param.15) | copy-start | bytes 777604
  127.9 14.0 %copy-start.1 = (bf16[3,3,256,256]{3,2,1,0:T(8,128)(2,1)S(1)}, bf16[3,3,256,256]{3,2,1,0:T(8,128)(2,1)}, u32[]{:S(2)}) copy-start(bf16[3,3,256,256]{3,2,1,0:T(8,128)(2,1)} %param.9) | copy-start | bytes 3538948
Sparse Core Ops, SparseCore 0:
  56.4 23.0 all-gather.1
where the time goes:
time: 150 us; the launch traced here: 149 us
  waiting for transfers between devices  35.1 us (23%)
  local copies, waits for them, and re-layouts  28.8 us (19%)
  matrix products  28.3 us (19%)
  other arithmetic  27 us (18%)
  starting transfers between devices  15.8 us (11%)
  between operations  13.7 us (9%)
    all_gather x1, waiting for transfers between devices, shards(): lax.all_gather(flat.astype(jnp.bfloat16).reshape(pooled.shape[0], pooled....  22.6 us
    conv_general_dilated x2, matrix products, conv_three(): lax.conv_general_dilated(batched, weight, (1, 1), 'VALID', dimension_numb...  20.2 us
    conv_general_dilated x5, local copies, waits for them, and re-layouts, conv_three(): lax.conv_general_dilated(batched, weight, (1, 1), 'VALID', dimension_numb...  12.4 us
    convert_element_type x2, local copies, waits for them, and re-layouts, shards(): hidden = jax.nn.gelu(conv_three(padded_head, w_head)).astype(jnp.bfloat16)  9.65 us
    ppermute x3, starting transfers between devices, extended(): before = lax.ppermute(last, axis, up)  9.64 us
    ppermute x3, waiting for transfers between devices, extended(): after = lax.ppermute(initial, axis, down)  8.97 us
    another operation x1, other arithmetic, pool_pairs(): lax.reduce_window(field, jnp.array(0, field.dtype), lax.add, (2, 2, 1), (...  8.37 us
    dot_general x1, matrix products, shards(): jnp.einsum('ij,bajc->baic', zonal_mix, hidden, preferred_element_type=jnp...  7.18 us
  transfers between devices with their start and end apart: 7, of which 6 were waited for; matrix products, arithmetic and copies ran while one was open for 1% of the time, Pallas kernels for 0%

commit v1 on v0

v1 whole, which is shorter than its diff:
```python
import functools

import jax
import jax.numpy as jnp
from jax import lax
from jax.experimental import pallas as pl
from jax.experimental.pallas import tpu as pltpu
from jax.sharding import PartitionSpec as P

BF = jnp.bfloat16
F32 = jnp.float32
VMEM_LIMIT = 56 * 1024 * 1024


def up16(n):
    return -(-n // 16) * 16


def gelu_twice(x):
    inner = x * (0.7978845608028654 + 0.035677408136300125 * (x * x))
    return x + x * jnp.tanh(inner)


def encoder_kernel(x_ref, up_ref, dn_ref, west_ref, east_ref, g_ref, wp_ref, out_ref, xs, ts, mt, *, pairs):
    rows, cols, ch = x_ref.shape
    wide = xs.shape[1]
    halfw = wide // 2

    def stage(slot, row, r):
        west = west_ref[r : r + 1, :]
        east = east_ref[r : r + 1, :]
        xs[slot, :cols, ch : 2 * ch] = row
        xs[slot, :cols, :ch] = jnp.concatenate([west, row[:-1]], axis=0)
        xs[slot, :cols, 2 * ch :] = jnp.concatenate([row[1:], east], axis=0)

    at = lax.broadcasted_iota(jnp.int32, (halfw, wide), 0)
    of = lax.broadcasted_iota(jnp.int32, (halfw, wide), 1)
    pool = jnp.where((of == 2 * at) | (of == 2 * at + 1), 0.125, 0.0).astype(BF)
    if wide > cols:
        xs[:, cols:, :] = jnp.zeros((rows + 2, wide - cols, 3 * ch), BF)
    stage(0, up_ref[0], 0)
    stage(rows + 1, dn_ref[0], rows + 1)
    for r in range(rows):
        stage(r + 1, x_ref[r], r + 1)
    @pl.loop(0, rows // (2 * pairs))
    def _(c):
        for k in range(4):
            for q in range(pairs):
                d = [xs.at[2 * (c * pairs + q) + i] for i in range(4)]
                pick = ((0, 2), (1, 2), (2, 1), (1, 3))[k]
                one, two = d[pick[0]][...], d[pick[1]][...]
                ts[q * wide : (q + 1) * wide] = one + two if k == 1 else one - two
            mt[k] = jnp.dot(ts[...], g_ref[k], preferred_element_type=F32)
        for q in range(pairs):
            part = pl.ds(q * wide, wide)
            y0 = mt[0, part] + mt[1, part] + mt[2, part]
            y1 = mt[1, part] - mt[2, part] - mt[3, part]
            both = (gelu_twice(y0) + gelu_twice(y1)).astype(BF)
            pooled = jnp.dot(pool, both, preferred_element_type=F32).astype(BF)
            proj = jnp.dot(pooled, wp_ref[...], preferred_element_type=F32).astype(BF)
            out_ref[c * pairs + q] = proj[: cols // 2]


def encode(x, up, dn, west, east, g, wp, pairs):
    rows, cols, ch = x.shape
    head = wp.shape[1]
    wide = -(-cols // 32) * 32
    return pl.pallas_call(
        functools.partial(encoder_kernel, pairs=pairs),
        out_shape=jax.ShapeDtypeStruct((rows // 2, cols // 2, head), BF),
        scratch_shapes=[
            pltpu.VMEM((rows + 2, wide, 3 * ch), BF),
            pltpu.VMEM((pairs * wide, 3 * ch), BF),
            pltpu.VMEM((4, pairs * wide, ch), F32),
        ],
        compiler_params=pltpu.CompilerParams(vmem_limit_bytes=VMEM_LIMIT),
        name="encode",
    )(x, up, dn, west, east, g, wp)


def head_kernel(meta_ref, p_ref, halo_ref, scale_ref, shift_ref, w_ref, z_ref, out_ref, ps, ws, bs, zs, ms, *, rows_step):
    shards, rows, piece, ch = p_ref.shape
    cols = shards * piece
    wide = ps.shape[1]
    leads = out_ref.shape[0]
    step = pl.program_id(0)

    def stage(slot, parts):
        row = jnp.concatenate(parts, axis=0)
        ps[slot, :cols, ch : 2 * ch] = row
        ps[slot, :cols, :ch] = jnp.concatenate([row[-1:], row[:-1]], axis=0)
        ps[slot, :cols, 2 * ch :] = jnp.concatenate([row[1:], row[:1]], axis=0)

    @pl.when(step == 0)
    def _():
        if wide > cols:
            ps[:, cols:, :] = jnp.zeros((rows + 2, wide - cols, 3 * ch), BF)
        zs[...] = jnp.zeros(zs.shape, BF)
        zs[:cols, :cols] = z_ref[...]
        stage(0, [halo_ref[s, 0] for s in range(shards)])
        stage(rows + 1, [halo_ref[s, 1] for s in range(shards)])
        for r in range(rows):
            stage(r + 1, [p_ref[s, r] for s in range(shards)])
        for lead in range(leads):
            row_at = meta_ref[2 + lead]
            gain = 1.0 + scale_ref[pl.ds(row_at, 1), :]
            shift = shift_ref[pl.ds(row_at, 1), :]
            ms[2 * lead : 2 * lead + 1, :] = gain
            ms[2 * lead + 1 : 2 * lead + 2, :] = shift
            gain_t = jnp.transpose(jnp.broadcast_to(gain, (ch, ch)))
            shift_t = jnp.transpose(jnp.broadcast_to(shift, (ch, ch)))
            for dr in range(3):
                total = jnp.zeros((ch, ch), F32)
                for dc in range(3):
                    at = (dr * 3 + dc) * ch
                    w = w_ref[at : at + ch, :].astype(F32)
                    ws[at : at + ch, lead * ch : (lead + 1) * ch] = (w * gain_t).astype(BF)
                    total = total + w * shift_t
                bs[dr : dr + 1, lead * ch : (lead + 1) * ch] = jnp.sum(total, axis=0, keepdims=True)

    first = jnp.where(step == 0, meta_ref[0], 0).astype(F32)
    last = jnp.where(step == pl.num_programs(0) - 1, meta_ref[1], 0).astype(F32)
    bias = bs[0:1, :] + bs[1:2, :] + bs[2:3, :]
    bias_first = bias - first * bs[0:1, :]
    bias_last = bias - last * bs[2:3, :]
    base = step * rows_step
    lhs = jnp.concatenate(
        [jnp.concatenate([ps[base + i + dr] for dr in range(3)], axis=1) for i in range(rows_step)],
        axis=0,
    )
    conv = jnp.dot(lhs, ws[...], preferred_element_type=F32)
    for i in range(rows_step):
        row_bias = bias_first if i == 0 else (bias_last if i == rows_step - 1 else bias)
        y = conv[i * wide : (i + 1) * wide] + row_bias
        hidden = (0.5 * gelu_twice(y)).astype(BF)
        mixed = jnp.dot(zs[...], hidden, preferred_element_type=F32)
        center = ps[base + i + 1, :, ch : 2 * ch].astype(F32)
        for lead in range(leads):
            mod = center * ms[2 * lead : 2 * lead + 1, :] + ms[2 * lead + 1 : 2 * lead + 2, :]
            res = (mod + mixed[:, lead * ch : (lead + 1) * ch]).astype(BF)
            out_ref[lead, i] = res[:cols]


def forecast_heads(meta, band, halo, scale, shift, w, z, leads, rows_step):
    shards, rows, piece, ch = band.shape
    cols = shards * piece
    wide = up16(cols)
    full = lambda a: pl.BlockSpec(a.shape, lambda i, m: (0,) * a.ndim)
    return pl.pallas_call(
        functools.partial(head_kernel, rows_step=rows_step),
        grid_spec=pltpu.PrefetchScalarGridSpec(
            num_scalar_prefetch=1,
            grid=(rows // rows_step,),
            in_specs=[full(a) for a in (band, halo, scale, shift, w, z)],
            out_specs=pl.BlockSpec((leads, rows_step, cols, ch), lambda i, m: (0, i, 0, 0)),
            scratch_shapes=[
                pltpu.VMEM((rows + 2, wide, 3 * ch), BF),
                pltpu.VMEM((9 * ch, leads * ch), BF),
                pltpu.VMEM((8, leads * ch), F32),
                pltpu.VMEM((wide, wide), BF),
                pltpu.VMEM((8, ch), F32),
            ],
        ),
        out_shape=jax.ShapeDtypeStruct((leads, rows, cols, ch), BF),
        compiler_params=pltpu.CompilerParams(vmem_limit_bytes=VMEM_LIMIT),
        name="heads",
    )(meta, band, halo, scale, shift, w, z)


def neighbours(axis, size, wrap):
    count = size if wrap else size - 1
    up = [(i, (i + 1) % size) for i in range(count)]
    return up, [(j, i) for i, j in up]


def shards(inputs, w_enc, w_proj, film_scale, film_shift, lead_ids, w_head, zonal_mix):
    rows, cols, ch = inputs.shape
    lat = lax.axis_size("lat")
    lon = lax.axis_size("lon")
    lat_up, lat_dn = neighbours("lat", lat, False)
    lon_up, lon_dn = neighbours("lon", lon, True)
    above = lax.ppermute(inputs[-1:], "lat", lat_up)
    below = lax.ppermute(inputs[:1], "lat", lat_dn)
    west_out = jnp.concatenate([above[:, -1], inputs[:, -1], below[:, -1]], axis=0)
    east_out = jnp.concatenate([above[:, 0], inputs[:, 0], below[:, 0]], axis=0)
    west = lax.ppermute(west_out, "lon", lon_up)
    east = lax.ppermute(east_out, "lon", lon_dn)
    w = w_enc.astype(F32)
    half = 0.5 * (w[0] + w[2])
    g = jnp.stack([w[0], half + 0.5 * w[1], half - 0.5 * w[1], w[2]]).astype(BF)
    g = g.reshape(4, 3 * ch, w_enc.shape[-1])
    proj = encode(inputs, above, below, west, east, g, w_proj, 4)
    band = lax.all_gather(proj, "lon", axis=0, tiled=False)
    p_above = lax.ppermute(proj[-1:], "lat", lat_up)
    p_below = lax.ppermute(proj[:1], "lat", lat_dn)
    halo = lax.all_gather(jnp.concatenate([p_above, p_below], axis=0), "lon", axis=0, tiled=False)
    leads = lead_ids.shape[0] // lon
    mine = lax.dynamic_slice_in_dim(lead_ids, lax.axis_index("lon") * leads, leads)
    lat_at = lax.axis_index("lat")
    flags = jnp.stack([lat_at == 0, lat_at == lat - 1]).astype(jnp.int32)
    meta = jnp.concatenate([flags, mine])
    wh = w_head.reshape(-1, w_head.shape[-1])
    return forecast_heads(meta, band, halo, film_scale, film_shift, wh, zonal_mix, leads, 4)


def solution(mesh):
    in_specs = (P("lat", "lon", None), P(), P(), P(), P(), P(), P(), P())
    out_specs = P("lon", "lat", None, None)
    return jax.shard_map(shards, mesh=mesh, in_specs=in_specs, out_specs=out_specs, check_vma=False)
```

time: 150 us -> 88.1 us (0.59)
  Pallas kernels: 0 us -> 31.3 us
  matrix products: 28.3 us -> 0 us
  other arithmetic: 27 us -> 2.5 us
  waiting for transfers between devices: 35.1 us -> 11.3 us
  local copies, waits for them, and re-layouts: 28.8 us -> 5.18 us
  blocking collectives: 0 us -> 7.77 us
    pallas_call x0 -> x2, Pallas kernels: none -> 31.3 us  [the longest x1 16.3 us: forecast_heads(): pl.pallas_call(functools.partial(head_kernel, rows_step=rows_step), grid_...]
    conv_general_dilated x2 -> x0, matrix products: 20.2 us -> none  [conv_three(): lax.conv_general_dilated(batched, weight, (1, 1), 'VALID', dimension_numb...]
    all_gather x1, waiting for transfers between devices: 22.6 us -> 6.45 us  [shards(): band = lax.all_gather(proj, 'lon', axis=0, tiled=False)]
    conv_general_dilated x5 -> x0, local copies, waits for them, and re-layouts: 12.4 us -> none  [conv_three(): lax.conv_general_dilated(batched, weight, (1, 1), 'VALID', dimension_numb...]
    convert_element_type x4 -> x0, local copies, waits for them, and re-layouts: 10.1 us -> none  [the longest x2 9.65 us: shards(): hidden = jax.nn.gelu(conv_three(padded_head, w_head)).astype(jnp.bfloat16)]
    dot_general x4 -> x0, matrix products: 8.1 us -> none  [the longest x1 7.18 us: shards(): jnp.einsum('ij,bajc->baic', zonal_mix, hidden, preferred_element_type=jnp...]
    all_gather x0 -> x1, blocking collectives: none -> 7.77 us  [shards(): lax.all_gather(jnp.concatenate([p_above, p_below], axis=0), 'lon', axis=0...]
    ppermute x6, waiting for transfers between devices: 12.5 us -> 4.85 us  [the longest x1 2.66 us: shards(): above = lax.ppermute(inputs[-1:], 'lat', lat_up)]
  transfers between devices with their start and end apart: 7 -> 7, of which waited for: 6 -> 4; matrix products, arithmetic and copies ran while one was open for 1% -> 5% of each run, Pallas kernels for 0% -> 0%
where the time goes in v1:
time: 88.1 us; the launch traced here: 86.4 us
  Pallas kernels  31.3 us (36%)
  starting transfers between devices  14.8 us (17%)
  between operations  13.5 us (15%)
  waiting for transfers between devices  11.3 us (13%)
  blocking collectives  7.77 us (9%)
  local copies, waits for them, and re-layouts  5.18 us (6%)
  other arithmetic  2.5 us (3%)
    pallas_call x1, Pallas kernels, forecast_heads(): pl.pallas_call(functools.partial(head_kernel, rows_step=rows_step), grid_...  16.3 us
    pallas_call x1, Pallas kernels, encode(): pl.pallas_call(functools.partial(encoder_kernel, pairs=pairs), out_shape=...  15.1 us
    all_gather x1, blocking collectives, shards(): lax.all_gather(jnp.concatenate([p_above, p_below], axis=0), 'lon', axis=0...  7.77 us
    all_gather x1, waiting for transfers between devices, shards(): band = lax.all_gather(proj, 'lon', axis=0, tiled=False)  6.45 us
    ppermute x1, starting transfers between devices, shards(): p_below = lax.ppermute(proj[:1], 'lat', lat_dn)  4.26 us
    unnamed x15, local copies, waits for them, and re-layouts  3.51 us
    ppermute x1, starting transfers between devices, shards(): west = lax.ppermute(west_out, 'lon', lon_up)  3.25 us
    ppermute x1, starting transfers between devices, shards(): below = lax.ppermute(inputs[:1], 'lat', lat_dn)  3.03 us
  transfers between devices with their start and end apart: 7, of which 4 were waited for; matrix products, arithmetic and copies ran while one was open for 5% of the time, Pallas kernels for 0%

profile of v1, /device:TPU:25, one launch (start us, length us, event | category | flops | bytes accessed | tf_op | source)
XLA Modules:
  0.0 86.4 jit_solution(15946949218775061392)
XLA Ops:
  6.5 2.9 %copy.14.x_ref = bf16[40,180,256]{2,1,0:T(8,128)(2,1)S(1)} copy(bf16[40,180,256]{2,0,1:T(8,128)(2,1)} %param.8) | data formatting | bytes 7372800 | tf_op args[0]
  9.4 0.0 copy-start
  9.5 3.0 %collective-permute-start.1 = (bf16[1,180,256]{2,1,0:T(8,128)(2,1)S(1)}, bf16[1,180,256]{2,1,0:T(8,128)(2,1)S(1)}, u32[]{:S(2)}, u32[]{:S(2)}) collective-permute-start(bf16[1,180,256]{2,1,0:T(8,128)(2,1)S(1)} %get-tuple-element.5), channel_id=1, source_target_pairs={{4,0},{8,4},{12,8},{16,12},{20,16},{24,20},{28,24},{5,1},{9,5},{13... | collective-permute-start | bytes 276488 | tf_op jit(solution)/shard_map/ppermute | solution.py:183
  12.5 2.2 %collective-permute-start = (bf16[1,180,256]{2,1,0:T(8,128)(2,1)S(1)}, bf16[1,180,256]{2,1,0:T(8,128)(2,1)S(1)}, u32[]{:S(2)}, u32[]{:S(2)}) collective-permute-start(bf16[1,180,256]{2,1,0:T(8,128)(2,1)S(1)} %get-tuple-element.6), channel_id=1, source_target_pairs={{0,4},{4,8},{8,12},{12,16},{16,20},{20,24},{24,28},{1,5},{5,9},{9,... | collective-permute-start | bytes 276488 | tf_op jit(solution)/shard_map/ppermute | solution.py:182
  14.8 0.1 fusion.1
  14.8 0.2 convert_element_type.9
  15.1 0.2 add_convert_fusion
  15.3 0.8 slice_bitcast_fusion
  16.0 0.0 collective-permute-done.1.dn_ref
  16.1 2.7 %collective-permute-done.up_ref = bf16[1,180,256]{2,1,0:T(8,128)(2,1)S(1)} collective-permute-done((bf16[1,180,256]{2,1,0:T(8,128)(2,1)S(1)}, bf16[1,180,256]{2,1,0:T(8,128)(2,1)S(1)}, u32[]{:S(2)}, u32[]{:S(2)}) %collective-permute-start) | collective-permute-done | bytes 92192 | tf_op jit(solution)/shard_map/ppermute | solution.py:182
  18.7 3.3 %collective-permute-start.2 = (bf16[42,256]{1,0:T(8,128)(2,1)S(1)}, bf16[42,256]{1,0:T(8,128)(2,1)S(1)}, u32[]{:S(2)}, u32[]{:S(2)}) collective-permute-start(bf16[42,256]{1,0:T(8,128)(2,1)S(1)} %pad_maximum_fusion.2), channel_id=1, source_target_pairs={{0,1},{1,2},{2,3},{3,0},{4,5},{5,6},{6,7},{7,4},{8,9},{9,10},{10,1... | collective-permute-start | bytes 64520 | tf_op jit(solution)/shard_map/ppermute | solution.py:186
  22.0 0.1 collective-permute-start.3
  22.1 1.3 %pad_maximum_fusion.g_ref = bf16[4,768,256]{2,1,0:T(8,128)(2,1)} fusion(bf16[1,768,256]{2,1,0:T(8,128)(2,1)S(1)} %bitcast.25, bf16[1,768,256]{2,1,0:T(8,128)(2,1)S(1)} %bitcast.23, bf16[1,768,256]{2,1,0:T(8,128)(2,1)S(1)} %bitcast.22, bf16[1,768,256]{2,1,0:T(8,128)(2,1)S(1)} %bitcast.24), kind=kLoop, calls=%fused_computation | loop fusion | flops 2359296 | bytes 3145728 | tf_op jit(solution)/shard_map/stack | solution.py:190
  23.4 0.0 copy-done.2
  23.4 0.0 collective-permute-done.2.west_ref
  23.4 0.0 copy-start.4
  23.4 1.9 %collective-permute-done.3.east_ref = bf16[42,256]{1,0:T(8,128)(2,1)S(1)} collective-permute-done((bf16[42,256]{1,0:T(8,128)(2,1)S(1)}, bf16[42,256]{1,0:T(8,128)(2,1)S(1)}, u32[]{:S(2)}, u32[]{:S(2)}) %collective-permute-start.3) | collective-permute-done | bytes 21536 | tf_op jit(solution)/shard_map/ppermute | solution.py:187
  25.3 0.6 copy-done.5
  25.9 15.1 %encode.1 = bf16[20,90,128]{2,1,0:T(8,128)(2,1)} custom-call(bf16[40,180,256]{2,1,0:T(8,128)(2,1)} %copy-done, bf16[1,180,256]{2,1,0:T(8,128)(2,1)} %copy-done.3, bf16[1,180,256]{2,1,0:T(8,128)(2,1)} %copy-done.2, bf16[42,256]{1,0:T(8,128)(2,1)} %copy-done.4, bf16[42,256]{1,0:T(8,128)(2,1)} %copy-done.5, bf16[4,768,256]{2,1,0:T(8,128)(2,1)} %pad_maximum_fusion.g_ref, ...), custom_call_target="tpu_custom_call" | custom-call | tf_op jit(solution)/shard_map/encode/pallas_call | solution.py:68
  41.0 0.0 all-gather.4.cloned.1.call-update
  41.0 0.0 copy-done.6
  41.0 0.1 dynamic_slice.3
  41.1 0.1 add_convert_fusion.1
  41.2 0.8 fusion.2
  41.9 1.9 %collective-permute-start.4 = (bf16[1,90,128]{2,1,0:T(8,128)(2,1)S(1)}, bf16[1,90,128]{2,1,0:T(8,128)(2,1)S(1)}, u32[]{:S(2)}, u32[]{:S(2)}) collective-permute-start(bf16[1,90,128]{2,1,0:T(8,128)(2,1)S(1)} %get-tuple-element.13), channel_id=1, source_target_pairs={{0,4},{4,8},{8,12},{12,16},{16,20},{20,24},{24,28},{1,5},{5,9},{9,... | collective-permute-start | bytes 69128 | tf_op jit(solution)/shard_map/ppermute | solution.py:194
  43.9 4.3 %collective-permute-start.5 = (bf16[1,90,128]{2,1,0:T(8,128)(2,1)S(1)}, bf16[1,90,128]{2,1,0:T(8,128)(2,1)S(1)}, u32[]{:S(2)}, u32[]{:S(2)}) collective-permute-start(bf16[1,90,128]{2,1,0:T(8,128)(2,1)S(1)} %get-tuple-element.14), channel_id=1, source_target_pairs={{4,0},{8,4},{12,8},{16,12},{20,16},{24,20},{28,24},{5,1},{9,5},{13... | collective-permute-start | bytes 69128 | tf_op jit(solution)/shard_map/ppermute | solution.py:195
  48.1 0.6 pad_add_fusion.meta_ref
  48.7 0.0 collective-permute-done.4
  48.7 0.3 collective-permute-done.5
  49.1 7.8 %all-gather.1 = bf16[8,90,128]{2,1,0:T(8,128)(2,1)} all-gather(bf16[2,90,128]{2,1,0:T(8,128)(2,1)S(1)} %pad_maximum_fusion.1), channel_id=3, replica_groups=mesh['lat'=8,'lon'=4] {'lon'}, dimensions={0}, use_global_device_ids=true | all-gather | bytes 230400 | tf_op jit(solution)/shard_map/all_gather | solution.py:196
  56.8 6.5 %all-gather.4.cloned.1.call-done = bf16[80,90,128]{2,1,0:T(8,128)(2,1)} async-done(((bf16[20,90,128]{2,1,0:T(8,128)(2,1)}), bf16[80,90,128]{2,1,0:T(8,128)(2,1)}) %all-gather.4.cloned.1.call-update) | async-done | bytes 1843216 | tf_op jit(solution)/shard_map/all_gather | solution.py:193
  63.3 16.3 %heads.1 = bf16[2,20,360,128]{3,2,1,0:T(8,128)(2,1)} custom-call(s32[4]{0:T(128)} %pad_add_fusion.meta_ref, bf16[4,20,90,128]{3,2,1,0:T(8,128)(2,1)} %bitcast.21, bf16[4,2,90,128]{3,2,1,0:T(8,128)(2,1)} %bitcast.26, f32[720,128]{1,0:T(8,128)} %scale_ref.1, f32[720,128]{1,0:T(8,128)} %shift_ref.1, bf16[1152,128]{1,0:T(8,128)(2,1)} %bitcast.27, ...), custom_call_target="tpu_custom_call" | custom-call | tf_op jit(solution)/shard_map/heads/pallas_call | solution.py:149
  (16 shorter events, 0.1 us)
Async XLA Ops:
  6.5 8.2 %copy-start.1 = (bf16[3,3,256,256]{3,2,1,0:T(8,128)(2,1)S(1)}, bf16[3,3,256,256]{3,2,1,0:T(8,128)(2,1)}, u32[]{:S(2)}) copy-start(bf16[3,3,256,256]{3,2,1,0:T(8,128)(2,1)} %param.9) | copy-start | bytes 3538948
  6.5 56.7 %all-gather.4.cloned.1.call-start = ((), (), s32[]{:S(2)}) async-start(), calls=%async_computation | async-start | bytes 2457600 | tf_op jit(solution)/shard_map/all_gather | solution.py:193
  9.4 5.6 %copy-start = (bf16[40,180,256]{2,1,0:T(8,128)(2,1)}, bf16[40,180,256]{2,1,0:T(8,128)(2,1)S(1)}, u32[]{:S(2)}) copy-start(bf16[40,180,256]{2,1,0:T(8,128)(2,1)S(1)} %copy.14.x_ref) | copy-start | bytes 11059204
  9.5 6.6 %collective-permute-start.1 = (bf16[1,180,256]{2,1,0:T(8,128)(2,1)S(1)}, bf16[1,180,256]{2,1,0:T(8,128)(2,1)S(1)}, u32[]{:S(2)}, u32[]{:S(2)}) collective-permute-start(bf16[1,180,256]{2,1,0:T(8,128)(2,1)S(1)} %get-tuple-element.5), channel_id=1, source_target_pairs={{4,0},{8,4},{12,8},{16,12},{20,16},{24,20},{28,24},{5,1},{9,5},{13... | collective-permute-start | bytes 276488 | tf_op jit(solution)/shard_map/ppermute | solution.py:183
  12.5 6.2 %collective-permute-start = (bf16[1,180,256]{2,1,0:T(8,128)(2,1)S(1)}, bf16[1,180,256]{2,1,0:T(8,128)(2,1)S(1)}, u32[]{:S(2)}, u32[]{:S(2)}) collective-permute-start(bf16[1,180,256]{2,1,0:T(8,128)(2,1)S(1)} %get-tuple-element.6), channel_id=1, source_target_pairs={{0,4},{4,8},{8,12},{12,16},{16,20},{20,24},{24,28},{1,5},{5,9},{9,... | collective-permute-start | bytes 276488 | tf_op jit(solution)/shard_map/ppermute | solution.py:182
  16.0 7.4 %copy-start.2 = (bf16[1,180,256]{2,1,0:T(8,128)(2,1)}, bf16[1,180,256]{2,1,0:T(8,128)(2,1)S(1)}, u32[]{:S(2)}) copy-start(bf16[1,180,256]{2,1,0:T(8,128)(2,1)S(1)} %collective-permute-done.1.dn_ref) | copy-start | bytes 276484
  18.7 4.7 %copy-start.3 = (bf16[1,180,256]{2,1,0:T(8,128)(2,1)}, bf16[1,180,256]{2,1,0:T(8,128)(2,1)S(1)}, u32[]{:S(2)}) copy-start(bf16[1,180,256]{2,1,0:T(8,128)(2,1)S(1)} %collective-permute-done.up_ref) | copy-start | bytes 276484
  18.7 4.7 %collective-permute-start.2 = (bf16[42,256]{1,0:T(8,128)(2,1)S(1)}, bf16[42,256]{1,0:T(8,128)(2,1)S(1)}, u32[]{:S(2)}, u32[]{:S(2)}) collective-permute-start(bf16[42,256]{1,0:T(8,128)(2,1)S(1)} %pad_maximum_fusion.2), channel_id=1, source_target_pairs={{0,1},{1,2},{2,3},{3,0},{4,5},{5,6},{6,7},{7,4},{8,9},{9,10},{10,1... | collective-permute-start | bytes 64520 | tf_op jit(solution)/shard_map/ppermute | solution.py:186
  22.0 3.3 %collective-permute-start.3 = (bf16[42,256]{1,0:T(8,128)(2,1)S(1)}, bf16[42,256]{1,0:T(8,128)(2,1)S(1)}, u32[]{:S(2)}, u32[]{:S(2)}) collective-permute-start(bf16[42,256]{1,0:T(8,128)(2,1)S(1)} %pad_maximum_fusion.3), channel_id=1, source_target_pairs={{1,0},{2,1},{3,2},{0,3},{5,4},{6,5},{7,6},{4,7},{9,8},{10,9},{11,1... | collective-permute-start | bytes 64520 | tf_op jit(solution)/shard_map/ppermute | solution.py:187
  23.4 17.6 %copy-start.6 = (s32[8]{0:T(128)S(1)}, s32[8]{0:T(128)}, u32[]{:S(2)}) copy-start(s32[8]{0:T(128)} %param.13) | copy-start | bytes 100
  23.4 1.9 %copy-start.4 = (bf16[42,256]{1,0:T(8,128)(2,1)}, bf16[42,256]{1,0:T(8,128)(2,1)S(1)}, u32[]{:S(2)}) copy-start(bf16[42,256]{1,0:T(8,128)(2,1)S(1)} %collective-permute-done.2.west_ref) | copy-start | bytes 64516
  25.3 0.6 copy-start.5
  41.9 6.8 %collective-permute-start.4 = (bf16[1,90,128]{2,1,0:T(8,128)(2,1)S(1)}, bf16[1,90,128]{2,1,0:T(8,128)(2,1)S(1)}, u32[]{:S(2)}, u32[]{:S(2)}) collective-permute-start(bf16[1,90,128]{2,1,0:T(8,128)(2,1)S(1)} %get-tuple-element.13), channel_id=1, source_target_pairs={{0,4},{4,8},{8,12},{12,16},{16,20},{20,24},{24,28},{1,5},{5,9},{9,... | collective-permute-start | bytes 69128 | tf_op jit(solution)/shard_map/ppermute | solution.py:194
  43.9 5.2 %collective-permute-start.5 = (bf16[1,90,128]{2,1,0:T(8,128)(2,1)S(1)}, bf16[1,90,128]{2,1,0:T(8,128)(2,1)S(1)}, u32[]{:S(2)}, u32[]{:S(2)}) collective-permute-start(bf16[1,90,128]{2,1,0:T(8,128)(2,1)S(1)} %get-tuple-element.14), channel_id=1, source_target_pairs={{4,0},{8,4},{12,8},{16,12},{20,16},{24,20},{28,24},{5,1},{9,5},{13... | collective-permute-start | bytes 69128 | tf_op jit(solution)/shard_map/ppermute | solution.py:195
Sparse Core Ops, SparseCore 0:
  41.1 22.1 all-gather.3

commit v2 on v0

v2 whole, which is shorter than its diff:
```python
import functools

import jax
import jax.numpy as jnp
from jax import lax
from jax.experimental import pallas as pl
from jax.experimental.pallas import tpu as pltpu
from jax.sharding import PartitionSpec as P

BF = jnp.bfloat16
F32 = jnp.float32
VMEM_LIMIT = 36 * 1024 * 1024
EDGE = 2
STEP = 4
BIAS, GAIN, SHIFT = 0, 3, 4


def up_to(n, unit):
    return -(-n // unit) * unit


def gelu_twice(x):
    inner = x * (0.7978845608028654 + 0.035677408136300125 * (x * x))
    return x + x * jnp.tanh(inner)


def params():
    return pltpu.CompilerParams(vmem_limit_bytes=VMEM_LIMIT)


def weights_kernel(ids_ref, we_ref, wh_ref, scale_ref, shift_ref, z_ref, g_ref, ws_ref, vec_ref, zs_ref):
    ch = we_ref.shape[-1]
    head = wh_ref.shape[-1]
    leads = ws_ref.shape[1] // head
    cols = z_ref.shape[0]
    for dc in range(3):
        at = slice(dc * ch, (dc + 1) * ch)
        w = [we_ref[dr, dc].astype(F32) for dr in range(3)]
        half = 0.5 * (w[0] + w[2])
        g_ref[0, at] = we_ref[0, dc]
        g_ref[1, at] = (half + 0.5 * w[1]).astype(BF)
        g_ref[2, at] = (half - 0.5 * w[1]).astype(BF)
        g_ref[3, at] = we_ref[2, dc]
    zs_ref[...] = jnp.zeros(zs_ref.shape, BF)
    zs_ref[:cols, :cols] = z_ref[...]
    for lead in range(leads):
        lanes = slice(lead * head, (lead + 1) * head)
        gain = 1.0 + scale_ref[pl.ds(ids_ref[lead], 1), :]
        shift = shift_ref[pl.ds(ids_ref[lead], 1), :]
        vec_ref[GAIN : GAIN + 1, lanes] = gain
        vec_ref[SHIFT : SHIFT + 1, lanes] = shift
        gain_t = jnp.transpose(jnp.broadcast_to(gain, (head, head)))
        shift_t = jnp.transpose(jnp.broadcast_to(shift, (head, head)))
        for dr in range(3):
            total = jnp.zeros((head, head), F32)
            for dc in range(3):
                at = (dr * 3 + dc) * head
                w = wh_ref[dr, dc].astype(F32)
                ws_ref[at : at + head, lanes] = (w * gain_t).astype(BF)
                total = total + w * shift_t
            vec_ref[BIAS + dr : BIAS + dr + 1, lanes] = jnp.sum(total, axis=0, keepdims=True)


def prepare(ids, w_enc, w_head, scale, shift, z):
    leads = ids.shape[0]
    ch, head, cols = w_enc.shape[-1], w_head.shape[-1], z.shape[0]
    wide = up_to(cols, 16)
    vmem = pl.BlockSpec(memory_space=pltpu.VMEM)
    return pl.pallas_call(
        weights_kernel,
        in_specs=[pl.BlockSpec(memory_space=pltpu.SMEM)] + [vmem] * 5,
        out_specs=[vmem] * 4,
        out_shape=[
            jax.ShapeDtypeStruct((4, 3 * ch, ch), BF),
            jax.ShapeDtypeStruct((9 * head, leads * head), BF),
            jax.ShapeDtypeStruct((8, leads * head), F32),
            jax.ShapeDtypeStruct((wide, wide), BF),
        ],
        compiler_params=params(),
        name="weights",
    )(ids, w_enc, w_head, scale, shift, z)


def encoder_kernel(meta_ref, x_ref, west_ref, east_ref, above_ref, below_ref, g_ref, wp_ref, out_ref, xs, xr, ys, sem, *, first, runs, group):
    rows, cols, ch = x_ref.shape
    wide = xs.shape[1]
    halfw = wide // 2
    here = [(max(a, 0), min(b, rows)) for a, b in runs]
    copies, at = [], 0
    for i, (a, b) in enumerate(here):
        copies.append(pltpu.make_async_copy(x_ref.at[a:b], xr.at[at : at + b - a], sem.at[i]))
        at += b - a
    for c in copies:
        c.start()
    if wide > cols:
        xs[:, cols:, :] = jnp.zeros((xs.shape[0], wide - cols, 3 * ch), BF)
    at = lax.broadcasted_iota(jnp.int32, (halfw, wide), 0)
    of = lax.broadcasted_iota(jnp.int32, (halfw, wide), 1)
    pool = jnp.where((of == 2 * at) | (of == 2 * at + 1), 0.125, 0.0).astype(BF)

    def put(slot, left, center, right):
        xs[slot, :cols, :ch] = left
        xs[slot, :cols, ch : 2 * ch] = center
        xs[slot, :cols, 2 * ch :] = right

    slot = held = 0
    for (a, b), copy in zip(runs, copies):
        waited = False
        for r in range(a, b):
            if r < 0 or r >= rows:
                halo = above_ref if r < 0 else below_ref
                row = halo[r + halo.shape[0] if r < 0 else r - rows]
                put(slot, row[:cols], row[1 : cols + 1], row[2:])
            else:
                if not waited:
                    copy.wait()
                    waited = True
                row = xr[held]
                held += 1
                west, east = west_ref[r : r + 1, :], east_ref[r : r + 1, :]
                put(slot, jnp.concatenate([west, row[:-1]], axis=0), row, jnp.concatenate([row[1:], east], axis=0))
            slot += 1

    per_run = (runs[0][1] - runs[0][0] - 2) // 2
    pairs = per_run * len(runs)

    def multiply(c):
        d = []
        for q in range(c * group, (c + 1) * group):
            base = (q // per_run) * (2 * per_run + 2) + 2 * (q % per_run)
            d.append([xs.at[base + i] for i in range(4)])
        t = [
            [e[0][...] - e[2][...] for e in d],
            [e[1][...] + e[2][...] for e in d],
            [e[2][...] - e[1][...] for e in d],
            [e[1][...] - e[3][...] for e in d],
        ]
        for k in range(4):
            ys[c % 2, k] = jnp.dot(jnp.concatenate(t[k], axis=0), g_ref[k], preferred_element_type=F32)

    def finish(c):
        for i in range(group):
            part = slice(i * wide, (i + 1) * wide)
            m = [ys.at[c % 2, k, part] for k in range(4)]
            both = gelu_twice(m[0][...] + m[1][...] + m[2][...])
            both = both + gelu_twice(m[1][...] - m[2][...] - m[3][...])
            pooled = jnp.dot(pool, both.astype(BF), preferred_element_type=F32).astype(BF)
            proj = jnp.dot(pooled, wp_ref[...], preferred_element_type=F32)[: cols // 2]
            q = c * group + i
            row = (runs[q // per_run][0] + 1) // 2 + q % per_run
            if row < 0:
                proj = jnp.where(meta_ref[0] == 0, proj, 0.0)
            elif row >= rows // 2:
                proj = jnp.where(meta_ref[1] == 0, proj, 0.0)
            out_ref[q] = proj.astype(BF)

    for c in range(pairs // group):
        multiply(c)
        if c:
            finish(c - 1)
    finish(pairs // group - 1)


def encode(meta, x, west, east, above, below, g, wp, runs, group):
    rows, cols, ch = x.shape
    head = wp.shape[1]
    wide = up_to(cols, 32)
    slots = sum(b - a for a, b in runs)
    held = sum(min(b, rows) - max(a, 0) for a, b in runs)
    vmem = pl.BlockSpec(memory_space=pltpu.VMEM)
    return pl.pallas_call(
        functools.partial(encoder_kernel, first=0, runs=runs, group=group),
        in_specs=[pl.BlockSpec(memory_space=pltpu.SMEM), pl.BlockSpec(memory_space=pl.ANY)] + [vmem] * 6,
        out_specs=vmem,
        out_shape=jax.ShapeDtypeStruct(((slots - 2 * len(runs)) // 2, cols // 2, head), BF),
        scratch_shapes=[
            pltpu.VMEM((slots, wide, 3 * ch), BF),
            pltpu.VMEM((held, cols, ch), BF),
            pltpu.VMEM((2, 4, group * wide, ch), F32),
            pltpu.SemaphoreType.DMA((len(runs),)),
        ],
        compiler_params=params(),
        name="encode",
    )(meta, x, west, east, above, below, g, wp)


def head_kernel(meta_ref, *refs, moves, blocks, rows, shards):
    sources = refs[: len(moves)]
    ws_ref, vec_ref, zs_ref = refs[len(moves) : len(moves) + 3]
    out_ref, band, ps, sem = refs[-4:]
    ch = ps.shape[2] // 3
    wide = ps.shape[1]
    leads = out_ref.shape[0]
    cols = out_ref.shape[2]
    step = pl.program_id(0)
    block = blocks[0] + step * (blocks[1] - blocks[0] if len(blocks) > 1 else 0)

    @pl.when(step == 0)
    def _():
        copies = []
        for source, (slot, pieces) in zip(sources, moves):
            for a, b, to in pieces:
                copies.append(
                    pltpu.make_async_copy(
                        source.at[:, a:b],
                        band.at[pl.ds(meta_ref[slot], source.shape[0]), to : to + b - a],
                        sem.at[len(copies)],
                    )
                )
        for c in copies:
            c.start()
        if wide > cols:
            ps[:, cols:, :] = jnp.zeros((ps.shape[0], wide - cols, 3 * ch), BF)
        for c in copies:
            c.wait()

    base = block * STEP
    for i in range(STEP + 2):
        row = jnp.concatenate([band[s, base + i] for s in range(shards)], axis=0)
        ps[i, :cols, ch : 2 * ch] = row
        ps[i, :cols, :ch] = jnp.concatenate([row[-1:], row[:-1]], axis=0)
        ps[i, :cols, 2 * ch :] = jnp.concatenate([row[1:], row[:1]], axis=0)

    first = jnp.where(block == 0, meta_ref[0], 0).astype(F32)
    last = jnp.where(block == rows // STEP - 1, meta_ref[1], 0).astype(F32)
    bias = vec_ref[BIAS : BIAS + 1, :] + vec_ref[BIAS + 1 : BIAS + 2, :] + vec_ref[BIAS + 2 : BIAS + 3, :]
    bias_first = bias - first * vec_ref[BIAS : BIAS + 1, :]
    bias_last = bias - last * vec_ref[BIAS + 2 : BIAS + 3, :]

    def conv(i):
        lhs = jnp.concatenate([ps[i], ps[i + 1], ps[i + 2]], axis=1)
        return jnp.dot(lhs, ws_ref[...], preferred_element_type=F32)

    def finish(i, y):
        y = y + (bias_first if i == 0 else (bias_last if i == STEP - 1 else bias))
        hidden = (0.5 * gelu_twice(y)).astype(BF)
        mixed = jnp.dot(zs_ref[...], hidden, preferred_element_type=F32)
        center = ps[i + 1, :, ch : 2 * ch].astype(F32)
        for lead in range(leads):
            lanes = slice(lead * ch, (lead + 1) * ch)
            mod = center * vec_ref[GAIN : GAIN + 1, lanes] + vec_ref[SHIFT : SHIFT + 1, lanes]
            out_ref[lead, i] = (mod + mixed[:, lanes]).astype(BF)[:cols]

    before = None
    for i in range(STEP):
        y = conv(i)
        if before is not None:
            finish(i - 1, before)
        before = y
    finish(STEP - 1, before)


def forecast_heads(meta, sources, moves, ws, vec, zs, so_far, blocks, shape):
    leads, rows, cols, ch = shape
    shards = cols // sources[0].shape[2]
    wide = zs.shape[0]
    full = lambda a: pl.BlockSpec(a.shape, lambda i, m: (0,) * a.ndim)
    anywhere = pl.BlockSpec(memory_space=pl.ANY)
    operands = [*sources, ws, vec, zs]
    in_specs = [anywhere] * len(sources) + [full(a) for a in (ws, vec, zs)]
    alias = {}
    if so_far is not None:
        alias = {len(operands) + 1: 0}
        operands.append(so_far)
        in_specs.append(anywhere)
    stride = blocks[1] - blocks[0] if len(blocks) > 1 else 0
    start = blocks[0]
    return pl.pallas_call(
        functools.partial(head_kernel, moves=moves, blocks=blocks, rows=rows, shards=shards),
        grid_spec=pltpu.PrefetchScalarGridSpec(
            num_scalar_prefetch=1,
            grid=(len(blocks),),
            in_specs=in_specs,
            out_specs=pl.BlockSpec((leads, STEP, cols, ch), lambda i, m: (0, start + i * stride, 0, 0)),
            scratch_shapes=[
                pltpu.VMEM((shards, rows + 2, cols // shards, ch), BF),
                pltpu.VMEM((STEP + 2, wide, 3 * ch), BF),
                pltpu.SemaphoreType.DMA((sum(len(m[1]) for m in moves),)),
            ],
        ),
        out_shape=jax.ShapeDtypeStruct(shape, BF),
        input_output_aliases=alias,
        compiler_params=params(),
        name="heads",
    )(meta, *operands)


def neighbours(size, wrap):
    count = size if wrap else size - 1
    up = [(i, (i + 1) % size) for i in range(count)]
    return up, [(j, i) for i, j in up]


def swap(size, bit):
    return [(i, i ^ bit) for i in range(size)]


def shards(inputs, w_enc, w_proj, film_scale, film_shift, lead_ids, w_head, zonal_mix):
    rows, cols, ch = inputs.shape
    lat, lon = lax.axis_size("lat"), lax.axis_size("lon")
    lat_at, lon_at = lax.axis_index("lat"), lax.axis_index("lon")
    lat_up, lat_dn = neighbours(lat, False)
    lon_up, lon_dn = neighbours(lon, True)
    two_level = lon == 4
    reach = 2 * EDGE - 1
    leads = lead_ids.shape[0] // lon
    head = w_proj.shape[1]
    band_rows = rows // 2

    west = lax.ppermute(inputs[:, -1], "lon", lon_up)
    east = lax.ppermute(inputs[:, 0], "lon", lon_dn)

    def slab(part):
        return jnp.concatenate([west[part][:, None], inputs[part], east[part][:, None]], axis=1)

    above = lax.ppermute(slab(slice(rows - reach, rows)), "lat", lat_up)
    below = lax.ppermute(slab(slice(0, reach)), "lat", lat_dn)

    mine = lax.dynamic_slice_in_dim(lead_ids, lon_at * leads, leads)
    meta = jnp.stack(
        [lat_at == 0, lat_at == lat - 1, lon_at, lon_at ^ 2, lon_at ^ 1, lon_at ^ 3, 0]
    ).astype(jnp.int32)
    g, ws, vec, zs = prepare(mine, w_enc, w_head, film_scale, film_shift, zonal_mix)

    middle = band_rows // 2
    plan = [
        (((2 * EDGE - 1, 2 * middle + 1),), 2),
        (((2 * middle - 1, 2 * (band_rows - EDGE) + 1),), 2),
        (((-3, 2 * EDGE + 1), (rows - 2 * EDGE - 1, rows + 3)), EDGE + 1),
    ]
    none = jnp.zeros((reach, cols + 2, ch), BF)
    proj = []
    for k, (runs, group) in enumerate(plan):
        halos = (above, below) if k == 2 else (none, none)
        proj.append(encode(meta, inputs, west, east, *halos, g, w_proj, runs, group))

    sent = []
    for own in proj:
        if two_level:
            across = lax.ppermute(own, "lon", swap(lon, 2))
            beside = lax.ppermute(own, "lon", swap(lon, 1))
            both = lax.ppermute(across, "lon", swap(lon, 1))
            sent.append([(2, own[None]), (3, across[None]), (4, beside[None]), (5, both[None])])
        else:
            sent.append([(6, lax.all_gather(own, "lon", axis=0, tiled=False))])

    def sources(ranges):
        arrays, moves = [], []
        for group, pieces in zip(sent, ranges):
            for slot, a in group if pieces else ():
                arrays.append(a)
                moves.append((slot, pieces))
        return arrays, moves

    shape = (leads, band_rows, cols // 2 * lon, head)
    upper, lower = middle - EDGE, band_rows - EDGE - middle
    blocks = band_rows // STEP
    arrays, moves = sources([[(0, upper, EDGE + 1)], [(0, lower, middle + 1)], []])
    out = forecast_heads(meta, arrays, moves, ws, vec, zs, None, list(range(1, blocks - 1)), shape)
    keep = STEP + 1 - EDGE
    arrays, moves = sources(
        [
            [(0, keep, EDGE + 1)],
            [(lower - keep, lower, band_rows - EDGE + 1 - keep)],
            [(0, EDGE + 1, 0), (EDGE + 1, 2 * EDGE + 2, band_rows + 1 - EDGE)],
        ]
    )
    return forecast_heads(meta, arrays, moves, ws, vec, zs, out, [0, blocks - 1], shape)


def solution(mesh):
    in_specs = (P("lat", "lon", None), P(), P(), P(), P(), P(), P(), P())
    out_specs = P("lon", "lat", None, None)
    return jax.shard_map(shards, mesh=mesh, in_specs=in_specs, out_specs=out_specs, check_vma=False)
```

time: 150 us -> 71.1 us (0.47)
  Pallas kernels: 0 us -> 39.5 us
  waiting for transfers between devices: 35.1 us -> 3.8 us
  matrix products: 28.3 us -> 0 us
  other arithmetic: 27 us -> 1.59 us
  local copies, waits for them, and re-layouts: 28.8 us -> 12.3 us
  between operations: 13.7 us -> 0.41 us
  starting transfers between devices: 15.8 us -> 13.1 us
    pallas_call x0 -> x6, Pallas kernels: none -> 39.5 us  [the longest x2 23.9 us: forecast_heads(): pl.pallas_call(functools.partial(head_kernel, moves=moves, blocks=blocks,...]
    all_gather x1 -> x0, waiting for transfers between devices: 22.6 us -> none  [shards(): lax.all_gather(flat.astype(jnp.bfloat16).reshape(pooled.shape[0], pooled....]
    conv_general_dilated x2 -> x0, matrix products: 20.2 us -> none  [conv_three(): lax.conv_general_dilated(batched, weight, (1, 1), 'VALID', dimension_numb...]
    conv_general_dilated x5 -> x0, local copies, waits for them, and re-layouts: 12.4 us -> none  [conv_three(): lax.conv_general_dilated(batched, weight, (1, 1), 'VALID', dimension_numb...]
    unnamed x27 -> x23, local copies, waits for them, and re-layouts: 0.34 us -> 11.3 us
    convert_element_type x4 -> x0, local copies, waits for them, and re-layouts: 10.1 us -> none  [the longest x2 9.65 us: shards(): hidden = jax.nn.gelu(conv_three(padded_head, w_head)).astype(jnp.bfloat16)]
    ppermute x6 -> x13, waiting for transfers between devices: 12.5 us -> 3.8 us  [the longest x3 3.78 us: shards(): across = lax.ppermute(own, 'lon', swap(lon, 2))]
    another operation x1 -> x0, other arithmetic: 8.37 us -> none  [pool_pairs(): lax.reduce_window(field, jnp.array(0, field.dtype), lax.add, (2, 2, 1), (...]
  transfers between devices with their start and end apart: 7 -> 13, of which waited for: 6 -> 1; matrix products, arithmetic and copies ran while one was open for 1% -> 5% of each run, Pallas kernels for 0% -> 42%
where the time goes in v2:
time: 71.1 us; the launch traced here: 70.7 us
  Pallas kernels  39.5 us (56%)
  starting transfers between devices  13.1 us (18%)
  local copies, waits for them, and re-layouts  12.3 us (17%)
  waiting for transfers between devices  3.8 us (5%)
  other arithmetic  1.59 us (2%)
    pallas_call x2, Pallas kernels, forecast_heads(): pl.pallas_call(functools.partial(head_kernel, moves=moves, blocks=blocks,...  23.9 us
    pallas_call x3, Pallas kernels, encode(): pl.pallas_call(functools.partial(encoder_kernel, first=0, runs=runs, grou...  14.2 us
    unnamed x23, local copies, waits for them, and re-layouts  11.3 us
    ppermute x3, waiting for transfers between devices, shards(): across = lax.ppermute(own, 'lon', swap(lon, 2))  3.78 us
    ppermute x1, starting transfers between devices, shards(): above = lax.ppermute(slab(slice(rows - reach, rows)), 'lat', lat_up)  3.14 us
    ppermute x1, starting transfers between devices, shards(): below = lax.ppermute(slab(slice(0, reach)), 'lat', lat_dn)  3.02 us
    ppermute x3, starting transfers between devices, shards(): across = lax.ppermute(own, 'lon', swap(lon, 2))  2.34 us
    concatenate x2, other arithmetic, slab(): jnp.concatenate([west[part][:, None], inputs[part], east[part][:, None]],...  1.59 us
  transfers between devices with their start and end apart: 13, of which 1 were waited for; matrix products, arithmetic and copies ran while one was open for 5% of the time, Pallas kernels for 42%

profile of v2, /device:TPU:25, one launch (start us, length us, event | category | flops | bytes accessed | tf_op | source)
XLA Modules:
  0.0 70.7 jit_solution(14820820132870629107)
XLA Ops:
  0.0 0.7 %slice_bitcast_fusion = (bf16[40,256]{1,0:T(8,128)(2,1)S(1)}, bf16[40,256]{1,0:T(8,128)(2,1)S(1)}) fusion(bf16[40,180,256]{2,0,1:T(8,128)(2,1)} %param.8), kind=kLoop, calls=%fused_computation.2 | loop fusion | bytes 81920 | tf_op jit(solution)/shard_map/squeeze | solution.py:311
  0.7 0.7 collective-permute-start.1
  1.4 1.2 %collective-permute-start = (bf16[40,256]{1,0:T(8,128)(2,1)S(1)}, bf16[40,256]{1,0:T(8,128)(2,1)S(1)}, u32[]{:S(2)}, u32[]{:S(2)}) collective-permute-start(bf16[40,256]{1,0:T(8,128)(2,1)S(1)} %get-tuple-element.16), channel_id=1, source_target_pairs={{0,1},{1,2},{2,3},{3,0},{4,5},{5,6},{6,7},{7,4},{8,9},{9,10},{10,1... | collective-permute-start | bytes 61448 | tf_op jit(solution)/shard_map/ppermute | solution.py:310
  2.6 2.8 %copy.24.x_ref = bf16[40,180,256]{2,1,0:T(8,128)(2,1)S(1)} copy(bf16[40,180,256]{2,0,1:T(8,128)(2,1)} %param.8) | data formatting | bytes 7372800 | tf_op args[0]
  5.5 1.8 %copy-done = bf16[40,180,256]{2,1,0:T(8,128)(2,1)} copy-done((bf16[40,180,256]{2,1,0:T(8,128)(2,1)}, bf16[40,180,256]{2,1,0:T(8,128)(2,1)S(1)}, u32[]{:S(2)}) %copy-start) | copy-done | bytes 3686424
  7.3 0.8 %pad_maximum_fusion = bf16[3,182,256]{2,1,0:T(8,128)(2,1)} fusion(bf16[3,1,256]{2,1,0:T(2,128)(2,1)S(1)} %copy.28, bf16[3,180,256]{2,1,0:T(8,128)(2,1)S(1)} %get-tuple-element.14, bf16[3,1,256]{2,1,0:T(2,128)(2,1)S(1)} %copy.27), kind=kLoop, calls=%fused_computation | loop fusion | flops 838656 | bytes 559104 | tf_op jit(solution)/shard_map/concatenate | solution.py:314
  8.1 3.1 %collective-permute-start.8 = (bf16[3,182,256]{2,1,0:T(8,128)(2,1)}, bf16[3,182,256]{2,1,0:T(8,128)(2,1)}, u32[]{:S(2)}, u32[]{:S(2)}) collective-permute-start(bf16[3,182,256]{2,1,0:T(8,128)(2,1)} %pad_maximum_fusion), channel_id=1, source_target_pairs={{0,4},{4,8},{8,12},{12,16},{16,20},{20,24},{24,28},{1,5},{5,9},{9,... | collective-permute-start | bytes 838664 | tf_op jit(solution)/shard_map/ppermute | solution.py:316
  11.3 0.8 %pad_maximum_fusion.1 = bf16[3,182,256]{2,1,0:T(8,128)(2,1)} fusion(bf16[3,1,256]{2,1,0:T(2,128)(2,1)S(1)} %copy.31, bf16[3,180,256]{2,1,0:T(8,128)(2,1)S(1)} %get-tuple-element.13, bf16[3,1,256]{2,1,0:T(2,128)(2,1)S(1)} %copy.30), kind=kLoop, calls=%fused_computation.1 | loop fusion | flops 838656 | bytes 559104 | tf_op jit(solution)/shard_map/concatenate | solution.py:314
  12.1 3.0 %collective-permute-start.9 = (bf16[3,182,256]{2,1,0:T(8,128)(2,1)}, bf16[3,182,256]{2,1,0:T(8,128)(2,1)}, u32[]{:S(2)}, u32[]{:S(2)}) collective-permute-start(bf16[3,182,256]{2,1,0:T(8,128)(2,1)} %pad_maximum_fusion.1), channel_id=1, source_target_pairs={{4,0},{8,4},{12,8},{16,12},{20,16},{24,20},{28,24},{5,1},{9,5},{13... | collective-permute-start | bytes 838664 | tf_op jit(solution)/shard_map/ppermute | solution.py:317
  15.2 1.0 %copy-done.6 = f32[720,128]{1,0:T(8,128)S(1)} copy-done((f32[720,128]{1,0:T(8,128)S(1)}, f32[720,128]{1,0:T(8,128)}, u32[]{:S(2)}) %copy-start.6) | copy-done | bytes 368664
  16.2 1.0 %copy-done.7 = f32[720,128]{1,0:T(8,128)S(1)} copy-done((f32[720,128]{1,0:T(8,128)S(1)}, f32[720,128]{1,0:T(8,128)}, u32[]{:S(2)}) %copy-start.7) | copy-done | bytes 368664
  17.2 1.0 %copy-done.8 = bf16[3,3,128,128]{3,2,1,0:T(8,128)(2,1)S(1)} copy-done((bf16[3,3,128,128]{3,2,1,0:T(8,128)(2,1)S(1)}, bf16[3,3,128,128]{3,2,1,0:T(8,128)(2,1)}, u32[]{:S(2)}) %copy-start.8) | copy-done | bytes 294936
  18.1 1.0 %copy-done.9 = bf16[360,360]{1,0:T(8,128)(2,1)S(1)} copy-done((bf16[360,360]{1,0:T(8,128)(2,1)S(1)}, bf16[360,360]{1,0:T(8,128)(2,1)}, u32[]{:S(2)}) %copy-start.9) | copy-done | bytes 259224
  19.1 1.3 %weights.1 = (bf16[4,768,256]{2,1,0:T(8,128)(2,1)S(1)}, bf16[1152,256]{1,0:T(8,128)(2,1)S(1)}, f32[8,256]{1,0:T(8,128)S(1)}, bf16[368,368]{1,0:T(8,128)(2,1)S(1)}) custom-call(s32[2]{0:T(128)S(1)} %dynamic_slice.3.ids_ref, bf16[3,3,256,256]{3,2,1,0:T(8,128)(2,1)S(1)} %copy-done.2, bf16[3,3,128,128]{3,2,1,0:T(8,128)(2,1)S(1)} %copy-done.8, ...), custom_call_target="tpu_custom_call" | custom-call | tf_op jit(solution)/shard_map/weights/pallas_call | solution.py:69
  20.4 0.7 copy-done.3
  21.1 0.1 stack.35.meta_ref
  21.3 2.1 %copy-done.1 = bf16[40,180,256]{2,1,0:T(8,128)(2,1)S(1)} copy-done((bf16[40,180,256]{2,1,0:T(8,128)(2,1)S(1)}, bf16[40,180,256]{2,1,0:T(8,128)(2,1)}, u32[]{:S(2)}) %copy-start.1) | copy-done | bytes 3686424
  23.3 4.8 %encode.3 = bf16[8,90,128]{2,1,0:T(8,128)(2,1)S(1)} custom-call(s32[7]{0:T(128)S(1)} %stack.35.meta_ref, bf16[40,180,256]{2,1,0:T(8,128)(2,1)S(1)} %copy-done.1, bf16[40,256]{1,0:T(8,128)(2,1)S(1)} %collective-permute-done.west_ref, bf16[40,256]{1,0:T(8,128)(2,1)S(1)} %collective-permute-done.1.east_ref, ...), custom_call_target="tpu_custom_call" | custom-call | tf_op jit(solution)/shard_map/encode/pallas_call | solution.py:171
  28.1 1.2 %collective-permute-start.2 = (bf16[8,90,128]{2,1,0:T(8,128)(2,1)S(1)}, bf16[8,90,128]{2,1,0:T(8,128)(2,1)S(1)}, u32[]{:S(2)}, u32[]{:S(2)}) collective-permute-start(bf16[8,90,128]{2,1,0:T(8,128)(2,1)S(1)} %encode.3), channel_id=1, source_target_pairs={{0,2},{1,3},{2,0},{3,1},{4,6},{5,7},{6,4},{7,5},{8,10},{9,11},{10,... | collective-permute-start | bytes 552968 | tf_op jit(solution)/shard_map/ppermute | solution.py:340
  29.3 4.6 %encode.4 = bf16[8,90,128]{2,1,0:T(8,128)(2,1)S(1)} custom-call(s32[7]{0:T(128)S(1)} %stack.35.meta_ref, bf16[40,180,256]{2,1,0:T(8,128)(2,1)S(1)} %copy-done.1, bf16[40,256]{1,0:T(8,128)(2,1)S(1)} %collective-permute-done.west_ref, bf16[40,256]{1,0:T(8,128)(2,1)S(1)} %collective-permute-done.1.east_ref, ...), custom_call_target="tpu_custom_call" | custom-call | tf_op jit(solution)/shard_map/encode/pallas_call | solution.py:171
  33.9 0.4 collective-permute-start.5
  34.3 1.0 %collective-permute-start.3 = (bf16[8,90,128]{2,1,0:T(8,128)(2,1)S(1)}, bf16[8,90,128]{2,1,0:T(8,128)(2,1)S(1)}, u32[]{:S(2)}, u32[]{:S(2)}) collective-permute-start(bf16[8,90,128]{2,1,0:T(8,128)(2,1)S(1)} %encode.3), channel_id=1, source_target_pairs={{0,1},{1,0},{2,3},{3,2},{4,5},{5,4},{6,7},{7,6},{8,9},{9,8},{10,11... | collective-permute-start | bytes 552968 | tf_op jit(solution)/shard_map/ppermute | solution.py:341
  35.4 4.9 %encode.5 = bf16[6,90,128]{2,1,0:T(8,128)(2,1)S(1)} custom-call(s32[7]{0:T(128)S(1)} %stack.35.meta_ref, bf16[40,180,256]{2,1,0:T(8,128)(2,1)S(1)} %copy-done.1, bf16[40,256]{1,0:T(8,128)(2,1)S(1)} %collective-permute-done.west_ref, bf16[40,256]{1,0:T(8,128)(2,1)S(1)} %collective-permute-done.1.east_ref, ...), custom_call_target="tpu_custom_call" | custom-call | tf_op jit(solution)/shard_map/encode/pallas_call | solution.py:171
  40.2 0.7 %collective-permute-start.10 = (bf16[6,90,128]{2,1,0:T(8,128)(2,1)S(1)}, bf16[6,90,128]{2,1,0:T(8,128)(2,1)S(1)}, u32[]{:S(2)}, u32[]{:S(2)}) collective-permute-start(bf16[6,90,128]{2,1,0:T(8,128)(2,1)S(1)} %encode.5), channel_id=1, source_target_pairs={{0,2},{1,3},{2,0},{3,1},{4,6},{5,7},{6,4},{7,5},{8,10},{9,11},{10,... | collective-permute-start | bytes 414728 | tf_op jit(solution)/shard_map/ppermute | solution.py:340
  41.0 0.3 collective-permute-start.6
  41.2 0.2 collective-permute-start.4
  41.5 0.3 collective-permute-start.7
  41.8 0.2 collective-permute-start.11
  42.0 3.8 %collective-permute-done.10 = bf16[6,90,128]{2,1,0:T(8,128)(2,1)S(1)} collective-permute-done((bf16[6,90,128]{2,1,0:T(8,128)(2,1)S(1)}, bf16[6,90,128]{2,1,0:T(8,128)(2,1)S(1)}, u32[]{:S(2)}, u32[]{:S(2)}) %collective-permute-start.10) | collective-permute-done | bytes 138272 | tf_op jit(solution)/shard_map/ppermute | solution.py:340
  45.8 0.8 %collective-permute-start.12 = (bf16[6,90,128]{2,1,0:T(8,128)(2,1)S(1)}, bf16[6,90,128]{2,1,0:T(8,128)(2,1)S(1)}, u32[]{:S(2)}, u32[]{:S(2)}) collective-permute-start(bf16[6,90,128]{2,1,0:T(8,128)(2,1)S(1)} %collective-permute-done.10), channel_id=1, source_target_pairs={{0,1},{1,0},{2,3},{3,2},{4,5},{5,4},{6,7},{7,6},{8,9},{9,8},{10,11... | collective-permute-start | bytes 414728 | tf_op jit(solution)/shard_map/ppermute | solution.py:342
  46.6 14.0 %heads.2.refs_15_ = bf16[2,20,360,128]{3,2,1,0:T(8,128)(2,1)} custom-call(s32[7]{0:T(128)S(1)} %stack.35.meta_ref, bf16[1,8,90,128]{3,2,1,0:T(8,128)(2,1)S(1)} %bitcast.30, bf16[1,8,90,128]{3,2,1,0:T(8,128)(2,1)S(1)} %bitcast.34, bf16[1,8,90,128]{3,2,1,0:T(8,128)(2,1)S(1)} %bitcast.38, bf16[1,8,90,128]{3,2,1,0:T(8,128)(2,1)S(1)} %bitcast.42, ...), custom_call_target="tpu_custom_call" | custom-call | tf_op jit(solution)/shard_map/heads/pallas_call | solution.py:268
  60.6 10.0 %heads.3 = bf16[2,20,360,128]{3,2,1,0:T(8,128)(2,1)} custom-call(s32[7]{0:T(128)S(1)} %stack.35.meta_ref, bf16[1,8,90,128]{3,2,1,0:T(8,128)(2,1)S(1)} %bitcast.31, bf16[1,8,90,128]{3,2,1,0:T(8,128)(2,1)S(1)} %bitcast.35, bf16[1,8,90,128]{3,2,1,0:T(8,128)(2,1)S(1)} %bitcast.39, bf16[1,8,90,128]{3,2,1,0:T(8,128)(2,1)S(1)} %bitcast.43, ...), custom_call_target="tpu_custom_call", output_to_operand_aliasing={{}: (16, {})} | custom-call | tf_op jit(solution)/shard_map/heads/pallas_call | solution.py:268
  (36 shorter events, 0.2 us)
Async XLA Ops:
  0.7 6.5 %collective-permute-start.1 = (bf16[40,256]{1,0:T(8,128)(2,1)S(1)}, bf16[40,256]{1,0:T(8,128)(2,1)S(1)}, u32[]{:S(2)}, u32[]{:S(2)}) collective-permute-start(bf16[40,256]{1,0:T(8,128)(2,1)S(1)} %get-tuple-element.15), channel_id=1, source_target_pairs={{1,0},{2,1},{3,2},{0,3},{5,4},{6,5},{7,6},{4,7},{9,8},{10,9},{11,1... | collective-permute-start | bytes 61448 | tf_op jit(solution)/shard_map/ppermute | solution.py:311
  1.4 13.7 %copy-start.10 = (s32[8]{0:T(128)S(1)}, s32[8]{0:T(128)}, u32[]{:S(2)}) copy-start(s32[8]{0:T(128)} %param.13) | copy-start | bytes 100
  1.4 13.8 %copy-start.2 = (bf16[3,3,256,256]{3,2,1,0:T(8,128)(2,1)S(1)}, bf16[3,3,256,256]{3,2,1,0:T(8,128)(2,1)}, u32[]{:S(2)}) copy-start(bf16[3,3,256,256]{3,2,1,0:T(8,128)(2,1)} %we_ref.1) | copy-start | bytes 3538948
  1.4 5.9 %collective-permute-start = (bf16[40,256]{1,0:T(8,128)(2,1)S(1)}, bf16[40,256]{1,0:T(8,128)(2,1)S(1)}, u32[]{:S(2)}, u32[]{:S(2)}) collective-permute-start(bf16[40,256]{1,0:T(8,128)(2,1)S(1)} %get-tuple-element.16), channel_id=1, source_target_pairs={{0,1},{1,2},{2,3},{3,0},{4,5},{5,6},{6,7},{7,4},{8,9},{9,10},{10,1... | collective-permute-start | bytes 61448 | tf_op jit(solution)/shard_map/ppermute | solution.py:310
  5.4 15.9 %copy-start.5 = (bf16[256,128]{1,0:T(8,128)(2,1)S(1)}, bf16[256,128]{1,0:T(8,128)(2,1)}, u32[]{:S(2)}) copy-start(bf16[256,128]{1,0:T(8,128)(2,1)} %wp_ref.5) | copy-start | bytes 196612
  5.4 1.8 %copy-start = (bf16[40,180,256]{2,1,0:T(8,128)(2,1)}, bf16[40,180,256]{2,1,0:T(8,128)(2,1)S(1)}, u32[]{:S(2)}) copy-start(bf16[40,180,256]{2,1,0:T(8,128)(2,1)S(1)} %copy.24.x_ref) | copy-start | bytes 11059204
  8.1 27.2 %collective-permute-start.8 = (bf16[3,182,256]{2,1,0:T(8,128)(2,1)}, bf16[3,182,256]{2,1,0:T(8,128)(2,1)}, u32[]{:S(2)}, u32[]{:S(2)}) collective-permute-start(bf16[3,182,256]{2,1,0:T(8,128)(2,1)} %pad_maximum_fusion), channel_id=1, source_target_pairs={{0,4},{4,8},{8,12},{12,16},{16,20},{20,24},{24,28},{1,5},{5,9},{9,... | collective-permute-start | bytes 838664 | tf_op jit(solution)/shard_map/ppermute | solution.py:316
  12.1 23.3 %collective-permute-start.9 = (bf16[3,182,256]{2,1,0:T(8,128)(2,1)}, bf16[3,182,256]{2,1,0:T(8,128)(2,1)}, u32[]{:S(2)}, u32[]{:S(2)}) collective-permute-start(bf16[3,182,256]{2,1,0:T(8,128)(2,1)} %pad_maximum_fusion.1), channel_id=1, source_target_pairs={{4,0},{8,4},{12,8},{16,12},{20,16},{24,20},{28,24},{5,1},{9,5},{13... | collective-permute-start | bytes 838664 | tf_op jit(solution)/shard_map/ppermute | solution.py:317
  15.2 1.0 %copy-start.6 = (f32[720,128]{1,0:T(8,128)S(1)}, f32[720,128]{1,0:T(8,128)}, u32[]{:S(2)}) copy-start(f32[720,128]{1,0:T(8,128)} %scale_ref.1) | copy-start | bytes 1105924
  16.2 1.0 %copy-start.7 = (f32[720,128]{1,0:T(8,128)S(1)}, f32[720,128]{1,0:T(8,128)}, u32[]{:S(2)}) copy-start(f32[720,128]{1,0:T(8,128)} %shift_ref.1) | copy-start | bytes 1105924
  17.2 1.0 %copy-start.8 = (bf16[3,3,128,128]{3,2,1,0:T(8,128)(2,1)S(1)}, bf16[3,3,128,128]{3,2,1,0:T(8,128)(2,1)}, u32[]{:S(2)}) copy-start(bf16[3,3,128,128]{3,2,1,0:T(8,128)(2,1)} %wh_ref.1) | copy-start | bytes 884740
  18.1 1.0 %copy-start.9 = (bf16[360,360]{1,0:T(8,128)(2,1)S(1)}, bf16[360,360]{1,0:T(8,128)(2,1)}, u32[]{:S(2)}) copy-start(bf16[360,360]{1,0:T(8,128)(2,1)} %z_ref.1) | copy-start | bytes 777604
  20.4 0.7 %copy-start.3 = (bf16[368,368]{1,0:T(8,128)(2,1)}, bf16[368,368]{1,0:T(8,128)(2,1)S(1)}, u32[]{:S(2)}) copy-start(bf16[368,368]{1,0:T(8,128)(2,1)S(1)} %get-tuple-element.12.refs_10_.refs_14_) | copy-start | bytes 812548
  21.3 2.1 %copy-start.1 = (bf16[40,180,256]{2,1,0:T(8,128)(2,1)S(1)}, bf16[40,180,256]{2,1,0:T(8,128)(2,1)}, u32[]{:S(2)}) copy-start(bf16[40,180,256]{2,1,0:T(8,128)(2,1)} %copy-done) | copy-start | bytes 11059204
  28.1 13.1 %collective-permute-start.2 = (bf16[8,90,128]{2,1,0:T(8,128)(2,1)S(1)}, bf16[8,90,128]{2,1,0:T(8,128)(2,1)S(1)}, u32[]{:S(2)}, u32[]{:S(2)}) collective-permute-start(bf16[8,90,128]{2,1,0:T(8,128)(2,1)S(1)} %encode.3), channel_id=1, source_target_pairs={{0,2},{1,3},{2,0},{3,1},{4,6},{5,7},{6,4},{7,5},{8,10},{9,11},{10,... | collective-permute-start | bytes 552968 | tf_op jit(solution)/shard_map/ppermute | solution.py:340
  33.9 12.6 %copy-start.4 = (bf16[368,368]{1,0:T(8,128)(2,1)S(1)}, bf16[368,368]{1,0:T(8,128)(2,1)}, u32[]{:S(2)}) copy-start(bf16[368,368]{1,0:T(8,128)(2,1)} %copy-done.3) | copy-start | bytes 812548
  33.9 7.5 %collective-permute-start.5 = (bf16[8,90,128]{2,1,0:T(8,128)(2,1)S(1)}, bf16[8,90,128]{2,1,0:T(8,128)(2,1)S(1)}, u32[]{:S(2)}, u32[]{:S(2)}) collective-permute-start(bf16[8,90,128]{2,1,0:T(8,128)(2,1)S(1)} %encode.4), channel_id=1, source_target_pairs={{0,2},{1,3},{2,0},{3,1},{4,6},{5,7},{6,4},{7,5},{8,10},{9,11},{10,... | collective-permute-start | bytes 552968 | tf_op jit(solution)/shard_map/ppermute | solution.py:340
  34.3 7.4 %collective-permute-start.3 = (bf16[8,90,128]{2,1,0:T(8,128)(2,1)S(1)}, bf16[8,90,128]{2,1,0:T(8,128)(2,1)S(1)}, u32[]{:S(2)}, u32[]{:S(2)}) collective-permute-start(bf16[8,90,128]{2,1,0:T(8,128)(2,1)S(1)} %encode.3), channel_id=1, source_target_pairs={{0,1},{1,0},{2,3},{3,2},{4,5},{5,4},{6,7},{7,6},{8,9},{9,8},{10,11... | collective-permute-start | bytes 552968 | tf_op jit(solution)/shard_map/ppermute | solution.py:341
  40.2 5.5 %collective-permute-start.10 = (bf16[6,90,128]{2,1,0:T(8,128)(2,1)S(1)}, bf16[6,90,128]{2,1,0:T(8,128)(2,1)S(1)}, u32[]{:S(2)}, u32[]{:S(2)}) collective-permute-start(bf16[6,90,128]{2,1,0:T(8,128)(2,1)S(1)} %encode.5), channel_id=1, source_target_pairs={{0,2},{1,3},{2,0},{3,1},{4,6},{5,7},{6,4},{7,5},{8,10},{9,11},{10,... | collective-permute-start | bytes 414728 | tf_op jit(solution)/shard_map/ppermute | solution.py:340
  41.0 5.6 %collective-permute-start.6 = (bf16[8,90,128]{2,1,0:T(8,128)(2,1)S(1)}, bf16[8,90,128]{2,1,0:T(8,128)(2,1)S(1)}, u32[]{:S(2)}, u32[]{:S(2)}) collective-permute-start(bf16[8,90,128]{2,1,0:T(8,128)(2,1)S(1)} %encode.4), channel_id=1, source_target_pairs={{0,1},{1,0},{2,3},{3,2},{4,5},{5,4},{6,7},{7,6},{8,9},{9,8},{10,11... | collective-permute-start | bytes 552968 | tf_op jit(solution)/shard_map/ppermute | solution.py:341
  41.2 5.3 %collective-permute-start.4 = (bf16[8,90,128]{2,1,0:T(8,128)(2,1)S(1)}, bf16[8,90,128]{2,1,0:T(8,128)(2,1)S(1)}, u32[]{:S(2)}, u32[]{:S(2)}) collective-permute-start(bf16[8,90,128]{2,1,0:T(8,128)(2,1)S(1)} %collective-permute-done.2), channel_id=1, source_target_pairs={{0,1},{1,0},{2,3},{3,2},{4,5},{5,4},{6,7},{7,6},{8,9},{9,8},{10,11... | collective-permute-start | bytes 552968 | tf_op jit(solution)/shard_map/ppermute | solution.py:342
  41.5 5.1 %collective-permute-start.7 = (bf16[8,90,128]{2,1,0:T(8,128)(2,1)S(1)}, bf16[8,90,128]{2,1,0:T(8,128)(2,1)S(1)}, u32[]{:S(2)}, u32[]{:S(2)}) collective-permute-start(bf16[8,90,128]{2,1,0:T(8,128)(2,1)S(1)} %collective-permute-done.5), channel_id=1, source_target_pairs={{0,1},{1,0},{2,3},{3,2},{4,5},{5,4},{6,7},{7,6},{8,9},{9,8},{10,11... | collective-permute-start | bytes 552968 | tf_op jit(solution)/shard_map/ppermute | solution.py:342
  41.8 18.8 %collective-permute-start.11 = (bf16[6,90,128]{2,1,0:T(8,128)(2,1)S(1)}, bf16[6,90,128]{2,1,0:T(8,128)(2,1)S(1)}, u32[]{:S(2)}, u32[]{:S(2)}) collective-permute-start(bf16[6,90,128]{2,1,0:T(8,128)(2,1)S(1)} %encode.5), channel_id=1, source_target_pairs={{0,1},{1,0},{2,3},{3,2},{4,5},{5,4},{6,7},{7,6},{8,9},{9,8},{10,11... | collective-permute-start | bytes 414728 | tf_op jit(solution)/shard_map/ppermute | solution.py:341
  45.8 14.8 %collective-permute-start.12 = (bf16[6,90,128]{2,1,0:T(8,128)(2,1)S(1)}, bf16[6,90,128]{2,1,0:T(8,128)(2,1)S(1)}, u32[]{:S(2)}, u32[]{:S(2)}) collective-permute-start(bf16[6,90,128]{2,1,0:T(8,128)(2,1)S(1)} %collective-permute-done.10), channel_id=1, source_target_pairs={{0,1},{1,0},{2,3},{3,2},{4,5},{5,4},{6,7},{7,6},{8,9},{9,8},{10,11... | collective-permute-start | bytes 414728 | tf_op jit(solution)/shard_map/ppermute | solution.py:342

commit v3 on v2

v3 whole, which is shorter than its diff:
```python
import functools

import jax
import jax.numpy as jnp
from jax import lax
from jax.experimental import pallas as pl
from jax.experimental.pallas import tpu as pltpu
from jax.sharding import PartitionSpec as P

BF = jnp.bfloat16
F32 = jnp.float32
MIB = 1024 * 1024
EDGE = 2
STEP = 4
BIAS, GAIN, SHIFT = 0, 3, 4


def up_to(n, unit):
    return -(-n // unit) * unit


def gelu_twice(x):
    inner = x * (0.7978845608028654 + 0.035677408136300125 * (x * x))
    return x + x * jnp.tanh(inner)


def params(mib):
    return pltpu.CompilerParams(vmem_limit_bytes=mib * MIB)


def weights_kernel(
    ids_ref, x_ref, west_ref, east_ref, we_hbm, wh_hbm, scale_hbm, shift_hbm, z_hbm,
    g_ref, ws_ref, vec_ref, zs_ref, up_ref, dn_ref,
    edge, we_ref, wh_ref, tab, z_ref, sem,
):
    ch = we_ref.shape[-1]
    head = wh_ref.shape[-1]
    leads = ws_ref.shape[1] // head
    cols = z_ref.shape[0]
    rows, xcols, _ = x_ref.shape
    reach = up_ref.shape[0]
    copies = [
        (x_ref.at[:reach], edge.at[:reach]),
        (x_ref.at[rows - reach :], edge.at[reach:]),
        (we_hbm, we_ref),
        (z_hbm, z_ref),
        (wh_hbm, wh_ref),
    ]
    for lead in range(leads):
        block = pl.multiple_of((ids_ref[lead] // 8) * 8, 8)
        copies.append((scale_hbm.at[pl.ds(block, 8)], tab.at[lead, 0]))
        copies.append((shift_hbm.at[pl.ds(block, 8)], tab.at[lead, 1]))
    copies = [pltpu.make_async_copy(one, two, sem.at[i]) for i, (one, two) in enumerate(copies)]
    for c in copies:
        c.start()
    copies[0].wait()
    copies[1].wait()
    for i in range(reach):
        for slab, r, at in ((dn_ref, i, i), (up_ref, rows - reach + i, reach + i)):
            slab[i] = jnp.concatenate([west_ref[r : r + 1, :], edge[at], east_ref[r : r + 1, :]], axis=0)
    copies[2].wait()
    for dc in range(3):
        at = slice(dc * ch, (dc + 1) * ch)
        w = [we_ref[dr, dc].astype(F32) for dr in range(3)]
        half = 0.5 * (w[0] + w[2])
        g_ref[0, at] = we_ref[0, dc]
        g_ref[1, at] = (half + 0.5 * w[1]).astype(BF)
        g_ref[2, at] = (half - 0.5 * w[1]).astype(BF)
        g_ref[3, at] = we_ref[2, dc]
    for c in copies[3:]:
        c.wait()
    zs_ref[...] = jnp.zeros(zs_ref.shape, BF)
    zs_ref[:cols, :cols] = z_ref[...] * jnp.asarray(0.5, BF)
    for lead in range(leads):
        lanes = slice(lead * head, (lead + 1) * head)
        at = ids_ref[lead] % 8
        gain = 1.0 + tab[lead, 0, pl.ds(at, 1), :]
        shift = tab[lead, 1, pl.ds(at, 1), :]
        vec_ref[GAIN : GAIN + 1, lanes] = gain
        vec_ref[SHIFT : SHIFT + 1, lanes] = shift
        gain_t = jnp.transpose(jnp.broadcast_to(gain, (head, head)))
        shift_t = jnp.transpose(jnp.broadcast_to(shift, (head, head)))
        for dr in range(3):
            total = jnp.zeros((head, head), F32)
            for dc in range(3):
                at = (dr * 3 + dc) * head
                w = wh_ref[dr, dc].astype(F32)
                ws_ref[at : at + head, lanes] = (w * gain_t).astype(BF)
                total = total + w * shift_t
            vec_ref[BIAS + dr : BIAS + dr + 1, lanes] = jnp.sum(total, axis=0, keepdims=True)


def prepare(ids, x, west, east, w_enc, w_head, scale, shift, z, reach):
    leads = ids.shape[0]
    ch, head, cols = w_enc.shape[-1], w_head.shape[-1], z.shape[0]
    xcols = x.shape[1]
    wide = up_to(cols, 16)
    vmem = pl.BlockSpec(memory_space=pltpu.VMEM)
    anywhere = pl.BlockSpec(memory_space=pl.ANY)
    return pl.pallas_call(
        weights_kernel,
        in_specs=[pl.BlockSpec(memory_space=pltpu.SMEM), anywhere, vmem, vmem] + [anywhere] * 5,
        out_specs=[vmem] * 6,
        out_shape=[
            jax.ShapeDtypeStruct((4, 3 * ch, ch), BF),
            jax.ShapeDtypeStruct((9 * head, leads * head), BF),
            jax.ShapeDtypeStruct((8, leads * head), F32),
            jax.ShapeDtypeStruct((wide, wide), BF),
            jax.ShapeDtypeStruct((reach, xcols + 2, ch), BF),
            jax.ShapeDtypeStruct((reach, xcols + 2, ch), BF),
        ],
        scratch_shapes=[
            pltpu.VMEM((2 * reach, xcols, ch), BF),
            pltpu.VMEM(w_enc.shape, BF),
            pltpu.VMEM(w_head.shape, BF),
            pltpu.VMEM((leads, 2, 8, head), F32),
            pltpu.VMEM(z.shape, BF),
            pltpu.SemaphoreType.DMA((5 + 2 * leads,)),
        ],
        compiler_params=params(16),
        name="weights",
    )(ids, x, west, east, w_enc, w_head, scale, shift, z)


def encoder_kernel(meta_ref, x_ref, west_ref, east_ref, above_ref, below_ref, g_ref, wp_ref, out_ref, xs, xr, ys, st, sem, *, runs, group):
    rows, cols, ch = x_ref.shape
    wide = xs.shape[1]
    halfw = wide // 2
    here = [(max(a, 0), min(b, rows)) for a, b in runs]
    copies, at = [], 0
    for i, (a, b) in enumerate(here):
        copies.append(pltpu.make_async_copy(x_ref.at[a:b], xr.at[at : at + b - a], sem.at[i]))
        at += b - a
    for c in copies:
        c.start()
    if wide > cols:
        xs[:, cols:, :] = jnp.zeros((xs.shape[0], wide - cols, 3 * ch), BF)
    def put(slot, left, center, right):
        xs[slot, :cols, :ch] = left
        xs[slot, :cols, ch : 2 * ch] = center
        xs[slot, :cols, 2 * ch :] = right

    slot = held = 0
    for (a, b), copy in zip(runs, copies):
        waited = False
        for r in range(a, b):
            if r < 0 or r >= rows:
                halo = above_ref if r < 0 else below_ref
                row = halo[r + halo.shape[0] if r < 0 else r - rows]
                put(slot, row[:cols], row[1 : cols + 1], row[2:])
            else:
                if not waited:
                    copy.wait()
                    waited = True
                row = xr[held]
                held += 1
                west, east = west_ref[r : r + 1, :], east_ref[r : r + 1, :]
                put(slot, jnp.concatenate([west, row[:-1]], axis=0), row, jnp.concatenate([row[1:], east], axis=0))
            slot += 1

    per_run = (runs[0][1] - runs[0][0] - 2) // 2
    pairs = per_run * len(runs)

    def multiply(c):
        d = []
        for q in range(c * group, (c + 1) * group):
            base = (q // per_run) * (2 * per_run + 2) + 2 * (q % per_run)
            d.append([xs.at[base + i] for i in range(4)])
        t = [
            [e[0][...] - e[2][...] for e in d],
            [e[1][...] + e[2][...] for e in d],
            [e[2][...] - e[1][...] for e in d],
            [e[1][...] - e[3][...] for e in d],
        ]
        for k in range(4):
            ys[c % 2, k] = jnp.dot(jnp.concatenate(t[k], axis=0), g_ref[k], preferred_element_type=F32)

    def finish(c):
        n = group * wide
        for i in range(group):
            part = slice(i * wide, (i + 1) * wide)
            m = [ys.at[c % 2, k, part] for k in range(4)]
            both = gelu_twice(m[0][...] + m[1][...] + m[2][...])
            both = both + gelu_twice(m[1][...] - m[2][...] - m[3][...])
            for j in range(ch // 128):
                st[j, part] = both[:, j * 128 : (j + 1) * 128]
        pooled = [
            st[j, pl.ds(0, n // 2, stride=2), :] + st[j, pl.ds(1, n // 2, stride=2), :] for j in range(ch // 128)
        ]
        pooled = (jnp.concatenate(pooled, axis=1) * 0.125).astype(BF)
        proj = jnp.dot(pooled, wp_ref[...], preferred_element_type=F32)
        for i in range(group):
            part = proj[i * halfw : i * halfw + cols // 2]
            q = c * group + i
            row = (runs[q // per_run][0] + 1) // 2 + q % per_run
            if row < 0:
                part = jnp.where(meta_ref[0] == 0, part, 0.0)
            elif row >= rows // 2:
                part = jnp.where(meta_ref[1] == 0, part, 0.0)
            out_ref[q] = part.astype(BF)

    for c in range(pairs // group):
        multiply(c)
        if c:
            finish(c - 1)
    finish(pairs // group - 1)


def encode(meta, x, west, east, above, below, g, wp, runs, group):
    rows, cols, ch = x.shape
    head = wp.shape[1]
    wide = up_to(cols, 32)
    slots = sum(b - a for a, b in runs)
    held = sum(min(b, rows) - max(a, 0) for a, b in runs)
    vmem = pl.BlockSpec(memory_space=pltpu.VMEM)
    return pl.pallas_call(
        functools.partial(encoder_kernel, runs=runs, group=group),
        in_specs=[pl.BlockSpec(memory_space=pltpu.SMEM), pl.BlockSpec(memory_space=pl.ANY)] + [vmem] * 6,
        out_specs=vmem,
        out_shape=jax.ShapeDtypeStruct(((slots - 2 * len(runs)) // 2, cols // 2, head), BF),
        scratch_shapes=[
            pltpu.VMEM((slots, wide, 3 * ch), BF),
            pltpu.VMEM((held, cols, ch), BF),
            pltpu.VMEM((2, 4, group * wide, ch), F32),
            pltpu.VMEM((ch // 128, group * wide, 128), F32),
            pltpu.SemaphoreType.DMA((len(runs),)),
        ],
        compiler_params=params(24),
        name="encode",
    )(meta, x, west, east, above, below, g, wp)


def head_kernel(meta_ref, *refs, moves, blocks, shards, aliased):
    sources = refs[: len(moves)]
    ws_ref, vec_ref, zs_ref = refs[len(moves) : len(moves) + 3]
    out_ref, band, ps, cs, outs, sem, out_sem = refs[len(moves) + 3 + aliased :]
    ch = ps.shape[3] // 3
    wide = ps.shape[2]
    leads, rows, cols, _ = out_ref.shape

    copies = []
    for source, (slot, pieces) in zip(sources, moves):
        for a, b, to in pieces:
            copies.append(
                pltpu.make_async_copy(
                    source.at[:, a:b],
                    band.at[pl.ds(meta_ref[slot], source.shape[0]), to : to + b - a],
                    sem.at[len(copies)],
                )
            )
    for c in copies:
        c.start()
    if wide > cols:
        ps[:, :, cols:, :] = jnp.zeros((*ps.shape[:2], wide - cols, 3 * ch), BF)
    for c in copies:
        c.wait()

    bias = vec_ref[BIAS : BIAS + 1, :] + vec_ref[BIAS + 1 : BIAS + 2, :] + vec_ref[BIAS + 2 : BIAS + 3, :]
    first = (meta_ref[0] == 1).astype(F32) * vec_ref[BIAS : BIAS + 1, :]
    last = (meta_ref[1] == 1).astype(F32) * vec_ref[BIAS + 2 : BIAS + 3, :]

    def stage(n):
        for i in range(STEP + 2):
            row = jnp.concatenate([band[s, blocks[n] * STEP + i] for s in range(shards)], axis=0)
            ps[n % 2, i, :cols, ch : 2 * ch] = row
            ps[n % 2, i, :cols, :ch] = jnp.concatenate([row[-1:], row[:-1]], axis=0)
            ps[n % 2, i, :cols, 2 * ch :] = jnp.concatenate([row[1:], row[:1]], axis=0)

    def conv(n):
        p = [ps[n % 2, i] for i in range(STEP + 2)]
        lhs = [jnp.concatenate(p[i : i + 3], axis=1) for i in range(STEP)]
        cs[n % 2] = jnp.dot(jnp.concatenate(lhs, axis=0), ws_ref[...], preferred_element_type=F32)

    def finish(n, i):
        row = blocks[n] * STEP + i
        y = cs[n % 2, i * wide : (i + 1) * wide] + (bias - first if row == 0 else (bias - last if row == rows - 1 else bias))
        mixed = jnp.dot(zs_ref[...], gelu_twice(y).astype(BF), preferred_element_type=F32)
        center = ps[n % 2, i + 1, :, ch : 2 * ch].astype(F32)
        for lead in range(leads):
            lanes = slice(lead * ch, (lead + 1) * ch)
            mod = center * vec_ref[GAIN : GAIN + 1, lanes] + vec_ref[SHIFT : SHIFT + 1, lanes]
            outs[n, lead, i] = (mod + mixed[:, lanes]).astype(BF)[:cols]

    sends = []

    def send(n):
        for lead in range(leads):
            sends.append(
                pltpu.make_async_copy(
                    outs.at[n, lead],
                    out_ref.at[lead, blocks[n] * STEP : (blocks[n] + 1) * STEP],
                    out_sem.at[n, lead],
                )
            )
            sends[-1].start()

    for n in range(len(blocks) + 1):
        if n < len(blocks):
            stage(n)
            conv(n)
        if n:
            for i in range(STEP):
                finish(n - 1, i)
            send(n - 1)
    for c in sends:
        c.wait()


def forecast_heads(meta, sources, moves, ws, vec, zs, so_far, blocks, shape):
    leads, rows, cols, ch = shape
    shards = cols // sources[0].shape[2]
    wide = zs.shape[0]
    vmem = pl.BlockSpec(memory_space=pltpu.VMEM)
    anywhere = pl.BlockSpec(memory_space=pl.ANY)
    operands = [meta, *sources, ws, vec, zs]
    in_specs = [pl.BlockSpec(memory_space=pltpu.SMEM)] + [anywhere] * len(sources) + [vmem] * 3
    alias = {}
    if so_far is not None:
        alias = {len(operands): 0}
        operands.append(so_far)
        in_specs.append(anywhere)
    return pl.pallas_call(
        functools.partial(head_kernel, moves=moves, blocks=blocks, shards=shards, aliased=len(alias)),
        in_specs=in_specs,
        out_specs=anywhere,
        out_shape=jax.ShapeDtypeStruct(shape, BF),
        scratch_shapes=[
            pltpu.VMEM((shards, rows + 2, cols // shards, ch), BF),
            pltpu.VMEM((2, STEP + 2, wide, 3 * ch), BF),
            pltpu.VMEM((2, STEP * wide, leads * ch), F32),
            pltpu.VMEM((len(blocks), leads, STEP, cols, ch), BF),
            pltpu.SemaphoreType.DMA((sum(len(m[1]) for m in moves),)),
            pltpu.SemaphoreType.DMA((len(blocks), leads)),
        ],
        input_output_aliases=alias,
        compiler_params=params(24 * -(-cols // 360)),
        name="heads",
    )(*operands)


def neighbours(size, wrap):
    count = size if wrap else size - 1
    up = [(i, (i + 1) % size) for i in range(count)]
    return up, [(j, i) for i, j in up]


def swap(size, bit):
    return [(i, i ^ bit) for i in range(size)]


def shards(inputs, w_enc, w_proj, film_scale, film_shift, lead_ids, w_head, zonal_mix):
    rows, cols, ch = inputs.shape
    lat, lon = lax.axis_size("lat"), lax.axis_size("lon")
    lat_at, lon_at = lax.axis_index("lat"), lax.axis_index("lon")
    lat_up, lat_dn = neighbours(lat, False)
    lon_up, lon_dn = neighbours(lon, True)
    two_level = lon == 4
    reach = 2 * EDGE - 1
    leads = lead_ids.shape[0] // lon
    head = w_proj.shape[1]
    band_rows = rows // 2

    west = lax.ppermute(inputs[:, -1], "lon", lon_up)
    east = lax.ppermute(inputs[:, 0], "lon", lon_dn)

    mine = lax.dynamic_slice_in_dim(lead_ids, lon_at * leads, leads)
    meta = jnp.stack(
        [lat_at == 0, lat_at == lat - 1, lon_at, lon_at ^ 2, lon_at ^ 1, lon_at ^ 3, 0]
    ).astype(jnp.int32)
    g, ws, vec, zs, up, dn = prepare(
        mine, inputs, west, east, w_enc, w_head, film_scale, film_shift, zonal_mix, reach
    )
    above = lax.ppermute(up, "lat", lat_up)
    below = lax.ppermute(dn, "lat", lat_dn)

    middle = band_rows // 2
    plan = [
        (((2 * EDGE - 1, 2 * middle + 1),), 4),
        (((2 * middle - 1, 2 * (band_rows - EDGE) + 1),), 4),
        (((-3, 2 * EDGE + 1), (rows - 2 * EDGE - 1, rows + 3)), EDGE + 1),
    ]
    none = jnp.zeros((reach, cols + 2, ch), BF)
    proj = []
    for k, (runs, group) in enumerate(plan):
        halos = (above, below) if k == 2 else (none, none)
        proj.append(encode(meta, inputs, west, east, *halos, g, w_proj, runs, group))

    sent = []
    for k, own in enumerate(proj):
        if two_level:
            across = lax.ppermute(own, "lon", swap(lon, 2))
            beside = lax.ppermute(own, "lon", swap(lon, 1))
            both = lax.ppermute(own, "lon", swap(lon, 3)) if k == 2 else lax.ppermute(across, "lon", swap(lon, 1))
            sent.append([(2, own[None]), (3, across[None]), (4, beside[None]), (5, both[None])])
        else:
            sent.append([(6, lax.all_gather(own, "lon", axis=0, tiled=False))])

    def sources(ranges):
        arrays, moves = [], []
        for group, pieces in zip(sent, ranges):
            for slot, a in group if pieces else ():
                arrays.append(a)
                moves.append((slot, pieces))
        return arrays, moves

    shape = (leads, band_rows, cols // 2 * lon, head)
    upper, lower = middle - EDGE, band_rows - EDGE - middle
    blocks = band_rows // STEP
    arrays, moves = sources([[(0, upper, EDGE + 1)], [(0, lower, middle + 1)], []])
    out = forecast_heads(meta, arrays, moves, ws, vec, zs, None, list(range(1, blocks - 1)), shape)
    keep = STEP + 1 - EDGE
    arrays, moves = sources(
        [
            [(0, keep, EDGE + 1)],
            [(lower - keep, lower, band_rows - EDGE + 1 - keep)],
            [(0, EDGE + 1, 0), (EDGE + 1, 2 * EDGE + 2, band_rows + 1 - EDGE)],
        ]
    )
    return forecast_heads(meta, arrays, moves, ws, vec, zs, out, [0, blocks - 1], shape)


def solution(mesh):
    in_specs = (P("lat", "lon", None), P(), P(), P(), P(), P(), P(), P())
    out_specs = P("lon", "lat", None, None)
    return jax.shard_map(shards, mesh=mesh, in_specs=in_specs, out_specs=out_specs, check_vma=False)
```

time: 71.1 us -> 58.9 us (0.83)
  Pallas kernels: 39.5 us -> 31.5 us
  local copies, waits for them, and re-layouts: 12.3 us -> 7.96 us
  other arithmetic: 1.59 us -> 0 us
  waiting for transfers between devices: 3.8 us -> 4.96 us
    pallas_call x2, Pallas kernels: 23.9 us -> 16.3 us  [forecast_heads(): pl.pallas_call(functools.partial(head_kernel, moves=moves, blocks=blocks,...]
    unnamed x23 -> x19, local copies, waits for them, and re-layouts: 11.3 us -> 7.03 us
    concatenate x2 -> x0, other arithmetic: 1.59 us -> none  [slab(): jnp.concatenate([west[part][:, None], inputs[part], east[part][:, None]],...]
    ppermute x3, waiting for transfers between devices: 3.78 us -> 4.93 us  [shards(): across = lax.ppermute(own, 'lon', swap(lon, 2))]
    pallas_call x3, Pallas kernels: 14.2 us -> 13.3 us  [encode(): pl.pallas_call(functools.partial(encoder_kernel, runs=runs, group=group),...]
    ppermute x5, starting transfers between devices: 7.46 us -> 8.21 us  [the longest x1 3.21 us: shards(): below = lax.ppermute(dn, 'lat', lat_dn)]
  transfers between devices with their start and end apart: 13 -> 13, of which waited for: 1 -> 1; matrix products, arithmetic and copies ran while one was open for 5% -> 8% of each run, Pallas kernels for 42% -> 31%
where the time goes in v3:
time: 58.9 us; the launch traced here: 58.6 us
  Pallas kernels  31.5 us (53%)
  starting transfers between devices  13.8 us (23%)
  local copies, waits for them, and re-layouts  7.96 us (14%)
  waiting for transfers between devices  4.96 us (8%)
    pallas_call x2, Pallas kernels, forecast_heads(): pl.pallas_call(functools.partial(head_kernel, moves=moves, blocks=blocks,...  16.3 us
    pallas_call x3, Pallas kernels, encode(): pl.pallas_call(functools.partial(encoder_kernel, runs=runs, group=group),...  13.3 us
    unnamed x19, local copies, waits for them, and re-layouts  7.03 us
    ppermute x3, waiting for transfers between devices, shards(): across = lax.ppermute(own, 'lon', swap(lon, 2))  4.93 us
    ppermute x1, starting transfers between devices, shards(): below = lax.ppermute(dn, 'lat', lat_dn)  3.21 us
    ppermute x1, starting transfers between devices, shards(): above = lax.ppermute(up, 'lat', lat_up)  3.14 us
    ppermute x3, starting transfers between devices, shards(): across = lax.ppermute(own, 'lon', swap(lon, 2))  2.84 us
    pallas_call x1, Pallas kernels, prepare(): pl.pallas_call(weights_kernel, in_specs=[pl.BlockSpec(memory_space=pltpu....  1.83 us
  transfers between devices with their start and end apart: 13, of which 1 were waited for; matrix products, arithmetic and copies ran while one was open for 8% of the time, Pallas kernels for 31%

profile of v3, /device:TPU:25, one launch (start us, length us, event | category | flops | bytes accessed | tf_op | source)
XLA Modules:
  0.0 58.6 jit_solution(7596726794479796969)
XLA Ops:
  0.0 0.7 %slice_bitcast_fusion = (bf16[40,256]{1,0:T(8,128)(2,1)S(1)}, bf16[40,256]{1,0:T(8,128)(2,1)S(1)}) fusion(bf16[40,180,256]{2,0,1:T(8,128)(2,1)} %param.8), kind=kLoop, calls=%fused_computation | loop fusion | bytes 81920 | tf_op jit(solution)/shard_map/squeeze | solution.py:364
  0.7 0.7 %collective-permute-start.1 = (bf16[40,256]{1,0:T(8,128)(2,1)S(1)}, bf16[40,256]{1,0:T(8,128)(2,1)S(1)}, u32[]{:S(2)}, u32[]{:S(2)}) collective-permute-start(bf16[40,256]{1,0:T(8,128)(2,1)S(1)} %get-tuple-element.17), channel_id=1, source_target_pairs={{1,0},{2,1},{3,2},{0,3},{5,4},{6,5},{7,6},{4,7},{9,8},{10,9},{11,1... | collective-permute-start | bytes 61448 | tf_op jit(solution)/shard_map/ppermute | solution.py:364
  1.4 1.1 %collective-permute-start = (bf16[40,256]{1,0:T(8,128)(2,1)S(1)}, bf16[40,256]{1,0:T(8,128)(2,1)S(1)}, u32[]{:S(2)}, u32[]{:S(2)}) collective-permute-start(bf16[40,256]{1,0:T(8,128)(2,1)S(1)} %get-tuple-element.18), channel_id=1, source_target_pairs={{0,1},{1,2},{2,3},{3,0},{4,5},{5,6},{6,7},{7,4},{8,9},{9,10},{10,1... | collective-permute-start | bytes 61448 | tf_op jit(solution)/shard_map/ppermute | solution.py:363
  2.5 0.0 copy-start.6
  2.5 0.0 copy-start.7
  2.6 0.0 copy-start.3
  2.6 4.7 %copy.11.x_ref = bf16[40,180,256]{2,1,0:T(8,128)(2,1)} copy(bf16[40,180,256]{2,0,1:T(8,128)(2,1)} %param.8) | data formatting | bytes 7372800 | tf_op args[0]
  7.3 0.1 dynamic_slice.3.ids_ref
  7.4 0.1 stack.35.meta_ref
  7.5 0.0 collective-permute-done.west_ref
  7.5 2.1 %copy-done = bf16[40,180,256]{2,1,0:T(8,128)(2,1)S(1)} copy-done((bf16[40,180,256]{2,1,0:T(8,128)(2,1)S(1)}, bf16[40,180,256]{2,1,0:T(8,128)(2,1)}, u32[]{:S(2)}) %copy-start) | copy-done | bytes 3686424
  9.6 1.8 %weights.1 = (bf16[4,768,256]{2,1,0:T(8,128)(2,1)S(1)}, bf16[1152,256]{1,0:T(8,128)(2,1)S(1)}, f32[8,256]{1,0:T(8,128)S(1)}, bf16[368,368]{1,0:T(8,128)(2,1)S(1)...) custom-call(s32[2]{0:T(128)S(1)} %dynamic_slice.3.ids_ref, bf16[40,180,256]{2,1,0:T(8,128)(2,1)S(1)} %copy-done, ...), custom_call_target="tpu_custom_call" | custom-call | tf_op jit(solution)/shard_map/weights/pallas_call | solution.py:100
  11.5 0.2 copy-done.1
  11.7 4.5 %encode.3 = bf16[8,90,128]{2,1,0:T(8,128)(2,1)S(1)} custom-call(s32[7]{0:T(128)S(1)} %stack.35.meta_ref, bf16[40,180,256]{2,1,0:T(8,128)(2,1)S(1)} %copy-done.1, bf16[40,256]{1,0:T(8,128)(2,1)S(1)} %collective-permute-done.west_ref, bf16[40,256]{1,0:T(8,128)(2,1)S(1)} %collective-permute-done.1.east_ref, ...), custom_call_target="tpu_custom_call" | custom-call | tf_op jit(solution)/shard_map/encode/pallas_call | solution.py:216
  16.2 1.2 %collective-permute-start.2 = (bf16[8,90,128]{2,1,0:T(8,128)(2,1)S(1)}, bf16[8,90,128]{2,1,0:T(8,128)(2,1)S(1)}, u32[]{:S(2)}, u32[]{:S(2)}) collective-permute-start(bf16[8,90,128]{2,1,0:T(8,128)(2,1)S(1)} %encode.3), channel_id=1, source_target_pairs={{0,2},{1,3},{2,0},{3,1},{4,6},{5,7},{6,4},{7,5},{8,10},{9,11},{10,... | collective-permute-start | bytes 552968 | tf_op jit(solution)/shard_map/ppermute | solution.py:391
  17.5 3.1 %collective-permute-start.8 = (bf16[3,182,256]{2,1,0:T(8,128)(2,1)S(1)}, bf16[3,182,256]{2,1,0:T(8,128)(2,1)S(1)}, u32[]{:S(2)}, u32[]{:S(2)}) collective-permute-start(bf16[3,182,256]{2,1,0:T(8,128)(2,1)S(1)} %get-tuple-element.12), channel_id=1, source_target_pairs={{0,4},{4,8},{8,12},{12,16},{16,20},{20,24},{24,28},{1,5},{5,9},{9,... | collective-permute-start | bytes 838664 | tf_op jit(solution)/shard_map/ppermute | solution.py:373
  20.6 3.2 %collective-permute-start.9 = (bf16[3,182,256]{2,1,0:T(8,128)(2,1)S(1)}, bf16[3,182,256]{2,1,0:T(8,128)(2,1)S(1)}, u32[]{:S(2)}, u32[]{:S(2)}) collective-permute-start(bf16[3,182,256]{2,1,0:T(8,128)(2,1)S(1)} %get-tuple-element.13), channel_id=1, source_target_pairs={{4,0},{8,4},{12,8},{16,12},{20,16},{24,20},{28,24},{5,1},{9,5},{13... | collective-permute-start | bytes 838664 | tf_op jit(solution)/shard_map/ppermute | solution.py:374
  23.8 4.5 %encode.4 = bf16[8,90,128]{2,1,0:T(8,128)(2,1)S(1)} custom-call(s32[7]{0:T(128)S(1)} %stack.35.meta_ref, bf16[40,180,256]{2,1,0:T(8,128)(2,1)S(1)} %copy-done.1, bf16[40,256]{1,0:T(8,128)(2,1)S(1)} %collective-permute-done.west_ref, bf16[40,256]{1,0:T(8,128)(2,1)S(1)} %collective-permute-done.1.east_ref, ...), custom_call_target="tpu_custom_call" | custom-call | tf_op jit(solution)/shard_map/encode/pallas_call | solution.py:216
  28.4 0.3 collective-permute-start.5
  28.7 1.0 %collective-permute-start.3 = (bf16[8,90,128]{2,1,0:T(8,128)(2,1)S(1)}, bf16[8,90,128]{2,1,0:T(8,128)(2,1)S(1)}, u32[]{:S(2)}, u32[]{:S(2)}) collective-permute-start(bf16[8,90,128]{2,1,0:T(8,128)(2,1)S(1)} %encode.3), channel_id=1, source_target_pairs={{0,1},{1,0},{2,3},{3,2},{4,5},{5,4},{6,7},{7,6},{8,9},{9,8},{10,11... | collective-permute-start | bytes 552968 | tf_op jit(solution)/shard_map/ppermute | solution.py:392
  29.7 0.0 collective-permute-done.2
  29.7 0.0 collective-permute-start.6
  29.7 4.9 %collective-permute-done.5 = bf16[8,90,128]{2,1,0:T(8,128)(2,1)S(1)} collective-permute-done((bf16[8,90,128]{2,1,0:T(8,128)(2,1)S(1)}, bf16[8,90,128]{2,1,0:T(8,128)(2,1)S(1)}, u32[]{:S(2)}, u32[]{:S(2)}) %collective-permute-start.5) | collective-permute-done | bytes 184352 | tf_op jit(solution)/shard_map/ppermute | solution.py:391
  34.6 1.1 %collective-permute-start.4 = (bf16[8,90,128]{2,1,0:T(8,128)(2,1)S(1)}, bf16[8,90,128]{2,1,0:T(8,128)(2,1)S(1)}, u32[]{:S(2)}, u32[]{:S(2)}) collective-permute-start(bf16[8,90,128]{2,1,0:T(8,128)(2,1)S(1)} %collective-permute-done.2), channel_id=1, source_target_pairs={{0,1},{1,0},{2,3},{3,2},{4,5},{5,4},{6,7},{7,6},{8,9},{9,8},{10,11... | collective-permute-start | bytes 552968 | tf_op jit(solution)/shard_map/ppermute | solution.py:393
  35.7 0.0 collective-permute-done.8.above_ref
  35.7 0.0 collective-permute-start.7
  35.8 4.3 %encode.5 = bf16[6,90,128]{2,1,0:T(8,128)(2,1)S(1)} custom-call(s32[7]{0:T(128)S(1)} %stack.35.meta_ref, bf16[40,180,256]{2,1,0:T(8,128)(2,1)S(1)} %copy-done.1, bf16[40,256]{1,0:T(8,128)(2,1)S(1)} %collective-permute-done.west_ref, bf16[40,256]{1,0:T(8,128)(2,1)S(1)} %collective-permute-done.1.east_ref, ...), custom_call_target="tpu_custom_call" | custom-call | tf_op jit(solution)/shard_map/encode/pallas_call | solution.py:216
  40.0 0.7 %collective-permute-start.12 = (bf16[6,90,128]{2,1,0:T(8,128)(2,1)S(1)}, bf16[6,90,128]{2,1,0:T(8,128)(2,1)S(1)}, u32[]{:S(2)}, u32[]{:S(2)}) collective-permute-start(bf16[6,90,128]{2,1,0:T(8,128)(2,1)S(1)} %encode.5), channel_id=1, source_target_pairs={{0,3},{1,2},{2,1},{3,0},{4,7},{5,6},{6,5},{7,4},{8,11},{9,10},{10,... | collective-permute-start | bytes 414728 | tf_op jit(solution)/shard_map/ppermute | solution.py:393
  40.8 0.0 collective-permute-start.11
  40.8 1.2 %collective-permute-start.10 = (bf16[6,90,128]{2,1,0:T(8,128)(2,1)S(1)}, bf16[6,90,128]{2,1,0:T(8,128)(2,1)S(1)}, u32[]{:S(2)}, u32[]{:S(2)}) collective-permute-start(bf16[6,90,128]{2,1,0:T(8,128)(2,1)S(1)} %encode.5), channel_id=1, source_target_pairs={{0,2},{1,3},{2,0},{3,1},{4,6},{5,7},{6,4},{7,5},{8,10},{9,11},{10,... | collective-permute-start | bytes 414728 | tf_op jit(solution)/shard_map/ppermute | solution.py:391
  42.0 9.7 %heads.2.refs_15_ = bf16[2,20,360,128]{3,2,1,0:T(8,128)(2,1)} custom-call(s32[7]{0:T(128)S(1)} %stack.35.meta_ref, bf16[1,8,90,128]{3,2,1,0:T(8,128)(2,1)S(1)} %bitcast.22, bf16[1,8,90,128]{3,2,1,0:T(8,128)(2,1)S(1)} %bitcast.26, bf16[1,8,90,128]{3,2,1,0:T(8,128)(2,1)S(1)} %bitcast.30, bf16[1,8,90,128]{3,2,1,0:T(8,128)(2,1)S(1)} %bitcast.34, ...), custom_call_target="tpu_custom_call" | custom-call | tf_op jit(solution)/shard_map/heads/pallas_call | solution.py:322
  51.7 6.7 %heads.3 = bf16[2,20,360,128]{3,2,1,0:T(8,128)(2,1)} custom-call(s32[7]{0:T(128)S(1)} %stack.35.meta_ref, bf16[1,8,90,128]{3,2,1,0:T(8,128)(2,1)S(1)} %bitcast.23, bf16[1,8,90,128]{3,2,1,0:T(8,128)(2,1)S(1)} %bitcast.27, bf16[1,8,90,128]{3,2,1,0:T(8,128)(2,1)S(1)} %bitcast.31, bf16[1,8,90,128]{3,2,1,0:T(8,128)(2,1)S(1)} %bitcast.35, ...), custom_call_target="tpu_custom_call", output_to_operand_aliasing={{}: (16, {})} | custom-call | tf_op jit(solution)/shard_map/heads/pallas_call | solution.py:322
  (23 shorter events, 0.1 us)
Async XLA Ops:
  0.7 6.7 %collective-permute-start.1 = (bf16[40,256]{1,0:T(8,128)(2,1)S(1)}, bf16[40,256]{1,0:T(8,128)(2,1)S(1)}, u32[]{:S(2)}, u32[]{:S(2)}) collective-permute-start(bf16[40,256]{1,0:T(8,128)(2,1)S(1)} %get-tuple-element.17), channel_id=1, source_target_pairs={{1,0},{2,1},{3,2},{0,3},{5,4},{6,5},{7,6},{4,7},{9,8},{10,9},{11,1... | collective-permute-start | bytes 61448 | tf_op jit(solution)/shard_map/ppermute | solution.py:364
  1.4 6.1 %collective-permute-start = (bf16[40,256]{1,0:T(8,128)(2,1)S(1)}, bf16[40,256]{1,0:T(8,128)(2,1)S(1)}, u32[]{:S(2)}, u32[]{:S(2)}) collective-permute-start(bf16[40,256]{1,0:T(8,128)(2,1)S(1)} %get-tuple-element.18), channel_id=1, source_target_pairs={{0,1},{1,2},{2,3},{3,0},{4,5},{5,6},{6,7},{7,4},{8,9},{9,10},{10,1... | collective-permute-start | bytes 61448 | tf_op jit(solution)/shard_map/ppermute | solution.py:363
  2.5 4.8 %copy-start.8 = (s32[8]{0:T(128)S(1)}, s32[8]{0:T(128)}, u32[]{:S(2)}) copy-start(s32[8]{0:T(128)} %param.13) | copy-start | bytes 100
  2.5 5.0 %copy-start.2 = (bf16[3,3,256,256]{3,2,1,0:T(8,128)(2,1)S(1)}, bf16[3,3,256,256]{3,2,1,0:T(8,128)(2,1)}, u32[]{:S(2)}) copy-start(bf16[3,3,256,256]{3,2,1,0:T(8,128)(2,1)} %we_hbm.1) | copy-start | bytes 3538948
  2.5 5.0 %copy-start.4 = (f32[720,128]{1,0:T(8,128)S(1)}, f32[720,128]{1,0:T(8,128)}, u32[]{:S(2)}) copy-start(f32[720,128]{1,0:T(8,128)} %scale_hbm.1) | copy-start | bytes 1105924
  2.5 5.0 %copy-start.5 = (f32[720,128]{1,0:T(8,128)S(1)}, f32[720,128]{1,0:T(8,128)}, u32[]{:S(2)}) copy-start(f32[720,128]{1,0:T(8,128)} %shift_hbm.1) | copy-start | bytes 1105924
  2.5 5.0 %copy-start.6 = (bf16[3,3,128,128]{3,2,1,0:T(8,128)(2,1)S(1)}, bf16[3,3,128,128]{3,2,1,0:T(8,128)(2,1)}, u32[]{:S(2)}) copy-start(bf16[3,3,128,128]{3,2,1,0:T(8,128)(2,1)} %wh_hbm.1) | copy-start | bytes 884740
  2.5 5.0 %copy-start.7 = (bf16[360,360]{1,0:T(8,128)(2,1)S(1)}, bf16[360,360]{1,0:T(8,128)(2,1)}, u32[]{:S(2)}) copy-start(bf16[360,360]{1,0:T(8,128)(2,1)} %z_hbm.1) | copy-start | bytes 777604
  2.6 8.9 %copy-start.3 = (bf16[256,128]{1,0:T(8,128)(2,1)S(1)}, bf16[256,128]{1,0:T(8,128)(2,1)}, u32[]{:S(2)}) copy-start(bf16[256,128]{1,0:T(8,128)(2,1)} %wp_ref.5) | copy-start | bytes 196612
  7.5 2.1 %copy-start = (bf16[40,180,256]{2,1,0:T(8,128)(2,1)S(1)}, bf16[40,180,256]{2,1,0:T(8,128)(2,1)}, u32[]{:S(2)}) copy-start(bf16[40,180,256]{2,1,0:T(8,128)(2,1)} %copy.11.x_ref) | copy-start | bytes 11059204
  9.6 2.1 %copy-start.1 = (bf16[40,180,256]{2,1,0:T(8,128)(2,1)S(1)}, bf16[40,180,256]{2,1,0:T(8,128)(2,1)}, u32[]{:S(2)}) copy-start(bf16[40,180,256]{2,1,0:T(8,128)(2,1)} %copy.11.x_ref) | copy-start | bytes 11059204
  16.2 13.5 %collective-permute-start.2 = (bf16[8,90,128]{2,1,0:T(8,128)(2,1)S(1)}, bf16[8,90,128]{2,1,0:T(8,128)(2,1)S(1)}, u32[]{:S(2)}, u32[]{:S(2)}) collective-permute-start(bf16[8,90,128]{2,1,0:T(8,128)(2,1)S(1)} %encode.3), channel_id=1, source_target_pairs={{0,2},{1,3},{2,0},{3,1},{4,6},{5,7},{6,4},{7,5},{8,10},{9,11},{10,... | collective-permute-start | bytes 552968 | tf_op jit(solution)/shard_map/ppermute | solution.py:391
  17.5 18.3 %collective-permute-start.8 = (bf16[3,182,256]{2,1,0:T(8,128)(2,1)S(1)}, bf16[3,182,256]{2,1,0:T(8,128)(2,1)S(1)}, u32[]{:S(2)}, u32[]{:S(2)}) collective-permute-start(bf16[3,182,256]{2,1,0:T(8,128)(2,1)S(1)} %get-tuple-element.12), channel_id=1, source_target_pairs={{0,4},{4,8},{8,12},{12,16},{16,20},{20,24},{24,28},{1,5},{5,9},{9,... | collective-permute-start | bytes 838664 | tf_op jit(solution)/shard_map/ppermute | solution.py:373
  20.6 15.2 %collective-permute-start.9 = (bf16[3,182,256]{2,1,0:T(8,128)(2,1)S(1)}, bf16[3,182,256]{2,1,0:T(8,128)(2,1)S(1)}, u32[]{:S(2)}, u32[]{:S(2)}) collective-permute-start(bf16[3,182,256]{2,1,0:T(8,128)(2,1)S(1)} %get-tuple-element.13), channel_id=1, source_target_pairs={{4,0},{8,4},{12,8},{16,12},{20,16},{24,20},{28,24},{5,1},{9,5},{13... | collective-permute-start | bytes 838664 | tf_op jit(solution)/shard_map/ppermute | solution.py:374
  28.4 6.3 %collective-permute-start.5 = (bf16[8,90,128]{2,1,0:T(8,128)(2,1)S(1)}, bf16[8,90,128]{2,1,0:T(8,128)(2,1)S(1)}, u32[]{:S(2)}, u32[]{:S(2)}) collective-permute-start(bf16[8,90,128]{2,1,0:T(8,128)(2,1)S(1)} %encode.4), channel_id=1, source_target_pairs={{0,2},{1,3},{2,0},{3,1},{4,6},{5,7},{6,4},{7,5},{8,10},{9,11},{10,... | collective-permute-start | bytes 552968 | tf_op jit(solution)/shard_map/ppermute | solution.py:391
  28.7 12.1 %collective-permute-start.3 = (bf16[8,90,128]{2,1,0:T(8,128)(2,1)S(1)}, bf16[8,90,128]{2,1,0:T(8,128)(2,1)S(1)}, u32[]{:S(2)}, u32[]{:S(2)}) collective-permute-start(bf16[8,90,128]{2,1,0:T(8,128)(2,1)S(1)} %encode.3), channel_id=1, source_target_pairs={{0,1},{1,0},{2,3},{3,2},{4,5},{5,4},{6,7},{7,6},{8,9},{9,8},{10,11... | collective-permute-start | bytes 552968 | tf_op jit(solution)/shard_map/ppermute | solution.py:392
  29.7 11.1 %collective-permute-start.6 = (bf16[8,90,128]{2,1,0:T(8,128)(2,1)S(1)}, bf16[8,90,128]{2,1,0:T(8,128)(2,1)S(1)}, u32[]{:S(2)}, u32[]{:S(2)}) collective-permute-start(bf16[8,90,128]{2,1,0:T(8,128)(2,1)S(1)} %encode.4), channel_id=1, source_target_pairs={{0,1},{1,0},{2,3},{3,2},{4,5},{5,4},{6,7},{7,6},{8,9},{9,8},{10,11... | collective-permute-start | bytes 552968 | tf_op jit(solution)/shard_map/ppermute | solution.py:392
  34.6 7.4 %collective-permute-start.4 = (bf16[8,90,128]{2,1,0:T(8,128)(2,1)S(1)}, bf16[8,90,128]{2,1,0:T(8,128)(2,1)S(1)}, u32[]{:S(2)}, u32[]{:S(2)}) collective-permute-start(bf16[8,90,128]{2,1,0:T(8,128)(2,1)S(1)} %collective-permute-done.2), channel_id=1, source_target_pairs={{0,1},{1,0},{2,3},{3,2},{4,5},{5,4},{6,7},{7,6},{8,9},{9,8},{10,11... | collective-permute-start | bytes 552968 | tf_op jit(solution)/shard_map/ppermute | solution.py:393
  35.7 6.3 %collective-permute-start.7 = (bf16[8,90,128]{2,1,0:T(8,128)(2,1)S(1)}, bf16[8,90,128]{2,1,0:T(8,128)(2,1)S(1)}, u32[]{:S(2)}, u32[]{:S(2)}) collective-permute-start(bf16[8,90,128]{2,1,0:T(8,128)(2,1)S(1)} %collective-permute-done.5), channel_id=1, source_target_pairs={{0,1},{1,0},{2,3},{3,2},{4,5},{5,4},{6,7},{7,6},{8,9},{9,8},{10,11... | collective-permute-start | bytes 552968 | tf_op jit(solution)/shard_map/ppermute | solution.py:393
  40.0 11.7 %collective-permute-start.12 = (bf16[6,90,128]{2,1,0:T(8,128)(2,1)S(1)}, bf16[6,90,128]{2,1,0:T(8,128)(2,1)S(1)}, u32[]{:S(2)}, u32[]{:S(2)}) collective-permute-start(bf16[6,90,128]{2,1,0:T(8,128)(2,1)S(1)} %encode.5), channel_id=1, source_target_pairs={{0,3},{1,2},{2,1},{3,0},{4,7},{5,6},{6,5},{7,4},{8,11},{9,10},{10,... | collective-permute-start | bytes 414728 | tf_op jit(solution)/shard_map/ppermute | solution.py:393
  40.8 10.9 %collective-permute-start.11 = (bf16[6,90,128]{2,1,0:T(8,128)(2,1)S(1)}, bf16[6,90,128]{2,1,0:T(8,128)(2,1)S(1)}, u32[]{:S(2)}, u32[]{:S(2)}) collective-permute-start(bf16[6,90,128]{2,1,0:T(8,128)(2,1)S(1)} %encode.5), channel_id=1, source_target_pairs={{0,1},{1,0},{2,3},{3,2},{4,5},{5,4},{6,7},{7,6},{8,9},{9,8},{10,11... | collective-permute-start | bytes 414728 | tf_op jit(solution)/shard_map/ppermute | solution.py:392
  40.8 10.9 %collective-permute-start.10 = (bf16[6,90,128]{2,1,0:T(8,128)(2,1)S(1)}, bf16[6,90,128]{2,1,0:T(8,128)(2,1)S(1)}, u32[]{:S(2)}, u32[]{:S(2)}) collective-permute-start(bf16[6,90,128]{2,1,0:T(8,128)(2,1)S(1)} %encode.5), channel_id=1, source_target_pairs={{0,2},{1,3},{2,0},{3,1},{4,6},{5,7},{6,4},{7,5},{8,10},{9,11},{10,... | collective-permute-start | bytes 414728 | tf_op jit(solution)/shard_map/ppermute | solution.py:391

commit v4 on v3

--- a/solution.py
+++ b/solution.py
@@ -31,17 +31,17 @@
 def weights_kernel(
     ids_ref, x_ref, west_ref, east_ref, we_hbm, wh_hbm, scale_hbm, shift_hbm, z_hbm,
     g_ref, ws_ref, vec_ref, zs_ref, up_ref, dn_ref,
-    edge, we_ref, wh_ref, tab, z_ref, sem,
+    edge, flat, we_ref, wh_ref, tab, z_ref, sem,
 ):
     ch = we_ref.shape[-1]
     head = wh_ref.shape[-1]
     leads = ws_ref.shape[1] // head
     cols = z_ref.shape[0]
-    rows, xcols, _ = x_ref.shape
+    xcols, rows, _ = x_ref.shape
     reach = up_ref.shape[0]
     copies = [
-        (x_ref.at[:reach], edge.at[:reach]),
-        (x_ref.at[rows - reach :], edge.at[reach:]),
+        (x_ref.at[:, :8], edge.at[0]),
+        (x_ref.at[:, rows - 8 :], edge.at[1]),
         (we_hbm, we_ref),
         (z_hbm, z_ref),
         (wh_hbm, wh_ref),
@@ -55,18 +55,24 @@
         c.start()
     copies[0].wait()
     copies[1].wait()
-    for i in range(reach):
-        for slab, r, at in ((dn_ref, i, i), (up_ref, rows - reach + i, reach + i)):
-            slab[i] = jnp.concatenate([west_ref[r : r + 1, :], edge[at], east_ref[r : r + 1, :]], axis=0)
+    for k, (slab, start, r) in enumerate(((dn_ref, 0, 0), (up_ref, 8 - reach, rows - reach))):
+        parts = []
+        for j in range(ch // 128):
+            lanes = slice(j * 128, (j + 1) * 128)
+            flat[k, j] = edge[k, :, :, lanes].astype(F32).reshape(xcols * 8, 128)
+            parts.append([flat[k, j, pl.ds(start + i, xcols, stride=8), :] for i in range(reach)])
+        for i in range(reach):
+            row = jnp.concatenate([p[i] for p in parts], axis=1).astype(BF)
+            slab[i] = jnp.concatenate([west_ref[r + i : r + i + 1, :], row, east_ref[r + i : r + i + 1, :]], axis=0)
     copies[2].wait()
-    for dc in range(3):
-        at = slice(dc * ch, (dc + 1) * ch)
-        w = [we_ref[dr, dc].astype(F32) for dr in range(3)]
+    for dr in range(3):
+        at = slice(dr * ch, (dr + 1) * ch)
+        w = [we_ref[dr, dc].astype(F32) for dc in range(3)]
         half = 0.5 * (w[0] + w[2])
-        g_ref[0, at] = we_ref[0, dc]
+        g_ref[0, at] = we_ref[dr, 0]
         g_ref[1, at] = (half + 0.5 * w[1]).astype(BF)
         g_ref[2, at] = (half - 0.5 * w[1]).astype(BF)
-        g_ref[3, at] = we_ref[2, dc]
+        g_ref[3, at] = we_ref[dr, 2]
     for c in copies[3:]:
         c.wait()
     zs_ref[...] = jnp.zeros(zs_ref.shape, BF)
@@ -93,7 +99,7 @@
 def prepare(ids, x, west, east, w_enc, w_head, scale, shift, z, reach):
     leads = ids.shape[0]
     ch, head, cols = w_enc.shape[-1], w_head.shape[-1], z.shape[0]
-    xcols = x.shape[1]
+    xcols = x.shape[0]
     wide = up_to(cols, 16)
     vmem = pl.BlockSpec(memory_space=pltpu.VMEM)
     anywhere = pl.BlockSpec(memory_space=pl.ANY)
@@ -110,7 +116,8 @@
             jax.ShapeDtypeStruct((reach, xcols + 2, ch), BF),
         ],
         scratch_shapes=[
-            pltpu.VMEM((2 * reach, xcols, ch), BF),
+            pltpu.VMEM((2, xcols, 8, ch), BF),
+            pltpu.VMEM((2, ch // 128, xcols * 8, 128), F32),
             pltpu.VMEM(w_enc.shape, BF),
             pltpu.VMEM(w_head.shape, BF),
             pltpu.VMEM((leads, 2, 8, head), F32),
@@ -122,63 +129,71 @@
     )(ids, x, west, east, w_enc, w_head, scale, shift, z)
 
 
-def encoder_kernel(meta_ref, x_ref, west_ref, east_ref, above_ref, below_ref, g_ref, wp_ref, out_ref, xs, xr, ys, st, sem, *, runs, group):
-    rows, cols, ch = x_ref.shape
-    wide = xs.shape[1]
-    halfw = wide // 2
-    here = [(max(a, 0), min(b, rows)) for a, b in runs]
-    copies, at = [], 0
-    for i, (a, b) in enumerate(here):
-        copies.append(pltpu.make_async_copy(x_ref.at[a:b], xr.at[at : at + b - a], sem.at[i]))
-        at += b - a
+def encoder_kernel(
+    meta_ref, x_ref, west_ref, east_ref, *refs, first, group
+):
+    halos, refs = (refs[:2], refs[2:]) if first is None else ((), refs)
+    g_ref, wp_ref, out_ref, xs, xr, ys, st, pt, sem = refs[:9]
+    cols, rows, ch = x_ref.shape
+    reach = 2 * EDGE - 1
+    starts = (0, rows - 8) if first is None else ((first - 1) // 8 * 8,)
+    tall = xr.shape[2]
+    copies = [
+        pltpu.make_async_copy(x_ref.at[:, a : a + tall], xr.at[i, 1 : cols + 1], sem.at[i])
+        for i, a in enumerate(starts)
+    ]
     for c in copies:
         c.start()
-    if wide > cols:
-        xs[:, cols:, :] = jnp.zeros((xs.shape[0], wide - cols, 3 * ch), BF)
-    def put(slot, left, center, right):
-        xs[slot, :cols, :ch] = left
-        xs[slot, :cols, ch : 2 * ch] = center
-        xs[slot, :cols, 2 * ch :] = right
-
-    slot = held = 0
-    for (a, b), copy in zip(runs, copies):
-        waited = False
-        for r in range(a, b):
-            if r < 0 or r >= rows:
-                halo = above_ref if r < 0 else below_ref
-                row = halo[r + halo.shape[0] if r < 0 else r - rows]
-                put(slot, row[:cols], row[1 : cols + 1], row[2:])
-            else:
-                if not waited:
-                    copy.wait()
-                    waited = True
-                row = xr[held]
-                held += 1
-                west, east = west_ref[r : r + 1, :], east_ref[r : r + 1, :]
-                put(slot, jnp.concatenate([west, row[:-1]], axis=0), row, jnp.concatenate([row[1:], east], axis=0))
-            slot += 1
-
-    per_run = (runs[0][1] - runs[0][0] - 2) // 2
-    pairs = per_run * len(runs)
+    for i, a in enumerate(starts):
+        xr[i, 0] = west_ref[a : a + tall, :]
+        xr[i, cols + 1] = east_ref[a : a + tall, :]
+    block = next(n for n in range(32, 0, -1) if (cols + 2) % n == 0)
+    if first is None:
+        hf = refs[9]
+        for k, halo in enumerate(halos):
+            for j in range(ch // 128):
+                lanes = slice(j * 128, (j + 1) * 128)
+                for i in range(reach):
+                    at = 8 - reach + i if k == 0 else i
+                    hf[k, j, pl.ds(at, cols + 2, stride=8), :] = halo[i, :, lanes].astype(F32)
+    for c in copies:
+        c.wait()
+    for a in range(0, cols + 2, block):
+        at = slice(a, a + block)
+        if first is None:
+            far = []
+            for k in range(2):
+                h = [hf[k, j, a * 8 : (a + block) * 8].astype(BF).reshape(block, 8, 128) for j in range(ch // 128)]
+                far.append(jnp.concatenate(h, axis=2))
+            top = jnp.concatenate([far[0], xr[0, at]], axis=1)
+            low = jnp.concatenate([xr[1, at], far[1]], axis=1)
+            pad = jnp.zeros((block, 16 - 4 * (EDGE + 1), ch), BF)
+            n = 2 * (EDGE + 1)
+            for dr in range(3):
+                t = top[:, 8 - reach + dr : 8 - reach + dr + n]
+                b = low[:, 8 - reach - 2 + dr : 8 - reach - 2 + dr + n]
+                xs[at, :, dr * ch : (dr + 1) * ch] = jnp.concatenate([t, b, pad], axis=1)
+        else:
+            rows_here = xr[0, at]
+            for dr in range(3):
+                off = first - 1 - starts[0] + dr
+                xs[at, :, dr * ch : (dr + 1) * ch] = rows_here[:, off : off + 16]
+
+    pairs = cols // 2
 
     def multiply(c):
-        d = []
-        for q in range(c * group, (c + 1) * group):
-            base = (q // per_run) * (2 * per_run + 2) + 2 * (q % per_run)
-            d.append([xs.at[base + i] for i in range(4)])
-        t = [
-            [e[0][...] - e[2][...] for e in d],
-            [e[1][...] + e[2][...] for e in d],
-            [e[2][...] - e[1][...] for e in d],
-            [e[1][...] - e[3][...] for e in d],
-        ]
-        for k in range(4):
-            ys[c % 2, k] = jnp.dot(jnp.concatenate(t[k], axis=0), g_ref[k], preferred_element_type=F32)
+        for k, (i, j) in enumerate(((0, 2), (1, 2), (2, 1), (1, 3))):
+            t = []
+            for q in range(c * group, (c + 1) * group):
+                one, two = xs[2 * q + i], xs[2 * q + j]
+                t.append(one + two if k == 1 else one - two)
+            ys[c % 2, k] = jnp.dot(jnp.concatenate(t, axis=0), g_ref[k], preferred_element_type=F32)
 
     def finish(c):
-        n = group * wide
-        for i in range(group):
-            part = slice(i * wide, (i + 1) * wide)
+        n = group * 16
+        sub = next(v for v in range(12, 0, -1) if group % v == 0) * 16
+        for a in range(0, n, sub):
+            part = slice(a, a + sub)
             m = [ys.at[c % 2, k, part] for k in range(4)]
             both = gelu_twice(m[0][...] + m[1][...] + m[2][...])
             both = both + gelu_twice(m[1][...] - m[2][...] - m[3][...])
@@ -188,46 +203,50 @@
             st[j, pl.ds(0, n // 2, stride=2), :] + st[j, pl.ds(1, n // 2, stride=2), :] for j in range(ch // 128)
         ]
         pooled = (jnp.concatenate(pooled, axis=1) * 0.125).astype(BF)
-        proj = jnp.dot(pooled, wp_ref[...], preferred_element_type=F32)
-        for i in range(group):
-            part = proj[i * halfw : i * halfw + cols // 2]
-            q = c * group + i
-            row = (runs[q // per_run][0] + 1) // 2 + q % per_run
-            if row < 0:
-                part = jnp.where(meta_ref[0] == 0, part, 0.0)
-            elif row >= rows // 2:
-                part = jnp.where(meta_ref[1] == 0, part, 0.0)
-            out_ref[q] = part.astype(BF)
+        pt[c * (n // 2) : (c + 1) * (n // 2)] = jnp.dot(pooled, wp_ref[...], preferred_element_type=F32)
 
     for c in range(pairs // group):
         multiply(c)
         if c:
             finish(c - 1)
     finish(pairs // group - 1)
-
-
-def encode(meta, x, west, east, above, below, g, wp, runs, group):
-    rows, cols, ch = x.shape
+    count = out_ref.shape[0]
+    for r in range(count):
+        row = pt[pl.ds(r, pairs, stride=8), :]
+        if first is None and r in (0, count - 1):
+            row = jnp.where(meta_ref[0 if r == 0 else 1] == 0, row, 0.0)
+        out_ref[r] = row.astype(BF)
+
+
+def encode(meta, x, west, east, halos, g, wp, first, count, group):
+    cols, rows, ch = x.shape
     head = wp.shape[1]
-    wide = up_to(cols, 32)
-    slots = sum(b - a for a, b in runs)
-    held = sum(min(b, rows) - max(a, 0) for a, b in runs)
+    blocks = 1 if halos is None else 2
+    tall = 24 if halos is None else 8
     vmem = pl.BlockSpec(memory_space=pltpu.VMEM)
+    scratch = [
+        pltpu.VMEM((cols + 2, 16, 3 * ch), BF),
+        pltpu.VMEM((blocks, cols + 2, tall, ch), BF),
+        pltpu.VMEM((2, 4, group * 16, ch), F32),
+        pltpu.VMEM((ch // 128, group * 16, 128), F32),
+        pltpu.VMEM((cols // 2 * 8, head), F32),
+        pltpu.SemaphoreType.DMA((blocks,)),
+    ]
+    if halos is not None:
+        scratch.append(pltpu.VMEM((2, ch // 128, (cols + 2) * 8, 128), F32))
+    operands = [meta, x, west, east, *(halos or ()), g, wp]
+    flops = 2 * cols * 16 * 6 * ch * ch
     return pl.pallas_call(
-        functools.partial(encoder_kernel, runs=runs, group=group),
-        in_specs=[pl.BlockSpec(memory_space=pltpu.SMEM), pl.BlockSpec(memory_space=pl.ANY)] + [vmem] * 6,
+        functools.partial(encoder_kernel, first=first, group=group),
+        in_specs=[pl.BlockSpec(memory_space=pltpu.SMEM), pl.BlockSpec(memory_space=pl.ANY)]
+        + [vmem] * (len(operands) - 2),
         out_specs=vmem,
-        out_shape=jax.ShapeDtypeStruct(((slots - 2 * len(runs)) // 2, cols // 2, head), BF),
-        scratch_shapes=[
-            pltpu.VMEM((slots, wide, 3 * ch), BF),
-            pltpu.VMEM((held, cols, ch), BF),
-            pltpu.VMEM((2, 4, group * wide, ch), F32),
-            pltpu.VMEM((ch // 128, group * wide, 128), F32),
-            pltpu.SemaphoreType.DMA((len(runs),)),
-        ],
-        compiler_params=params(24),
+        out_shape=jax.ShapeDtypeStruct((count, cols // 2, head), BF),
+        scratch_shapes=scratch,
+        compiler_params=params(28),
+        cost_estimate=pl.CostEstimate(flops=flops, transcendentals=cols * 16 * ch, bytes_accessed=8 * 1024 * 1024),
         name="encode",
-    )(meta, x, west, east, above, below, g, wp)
+    )(*operands)
 
 
 def head_kernel(meta_ref, *refs, moves, blocks, shards, aliased):
@@ -334,6 +353,11 @@
         ],
         input_output_aliases=alias,
         compiler_params=params(24 * -(-cols // 360)),
+        cost_estimate=pl.CostEstimate(
+            flops=len(blocks) * STEP * cols * leads * ch * 2 * (9 * ch + cols),
+            transcendentals=len(blocks) * STEP * cols * leads * ch,
+            bytes_accessed=len(blocks) * 8 * 1024 * 1024,
+        ),
         name="heads",
     )(*operands)
 
@@ -350,6 +374,7 @@
 
 def shards(inputs, w_enc, w_proj, film_scale, film_shift, lead_ids, w_head, zonal_mix):
     rows, cols, ch = inputs.shape
+    tile = jnp.transpose(inputs, (1, 0, 2))
     lat, lon = lax.axis_size("lat"), lax.axis_size("lon")
     lat_at, lon_at = lax.axis_index("lat"), lax.axis_index("lon")
     lat_up, lat_dn = neighbours(lat, False)
@@ -360,37 +385,38 @@
     head = w_proj.shape[1]
     band_rows = rows // 2
 
-    west = lax.ppermute(inputs[:, -1], "lon", lon_up)
-    east = lax.ppermute(inputs[:, 0], "lon", lon_dn)
+    west = lax.ppermute(tile[-1], "lon", lon_up)
+    east = lax.ppermute(tile[0], "lon", lon_dn)
 
     mine = lax.dynamic_slice_in_dim(lead_ids, lon_at * leads, leads)
     meta = jnp.stack(
         [lat_at == 0, lat_at == lat - 1, lon_at, lon_at ^ 2, lon_at ^ 1, lon_at ^ 3, 0]
     ).astype(jnp.int32)
     g, ws, vec, zs, up, dn = prepare(
-        mine, inputs, west, east, w_enc, w_head, film_scale, film_shift, zonal_mix, reach
+        mine, tile, west, east, w_enc, w_head, film_scale, film_shift, zonal_mix, reach
     )
     above = lax.ppermute(up, "lat", lat_up)
     below = lax.ppermute(dn, "lat", lat_dn)
 
     middle = band_rows // 2
+    group = cols // 4
     plan = [
-        (((2 * EDGE - 1, 2 * middle + 1),), 4),
-        (((2 * middle - 1, 2 * (band_rows - EDGE) + 1),), 4),
-        (((-3, 2 * EDGE + 1), (rows - 2 * EDGE - 1, rows + 3)), EDGE + 1),
+        (2 * EDGE, middle - EDGE, None),
+        (2 * middle, band_rows - EDGE - middle, None),
+        (None, 2 * (EDGE + 1), (above, below)),
     ]
-    none = jnp.zeros((reach, cols + 2, ch), BF)
-    proj = []
-    for k, (runs, group) in enumerate(plan):
-        halos = (above, below) if k == 2 else (none, none)
-        proj.append(encode(meta, inputs, west, east, *halos, g, w_proj, runs, group))
+    proj = [encode(meta, tile, west, east, halos, g, w_proj, first, n, group) for first, n, halos in plan]
 
     sent = []
     for k, own in enumerate(proj):
         if two_level:
             across = lax.ppermute(own, "lon", swap(lon, 2))
             beside = lax.ppermute(own, "lon", swap(lon, 1))
-            both = lax.ppermute(own, "lon", swap(lon, 3)) if k == 2 else lax.ppermute(across, "lon", swap(lon, 1))
+            if k == 2:
+                both = lax.ppermute(own, "lon", swap(lon, 3))
+            else:
+                ready, _ = lax.optimization_barrier((across, proj[k + 1]))
+                both = lax.ppermute(ready, "lon", swap(lon, 1))
             sent.append([(2, own[None]), (3, across[None]), (4, beside[None]), (5, both[None])])
         else:
             sent.append([(6, lax.all_gather(own, "lon", axis=0, tiled=False))])

time: 58.9 us -> 58.6 us (level)
  waiting for transfers between devices: 4.96 us -> 1.97 us
  starting transfers between devices: 13.8 us -> 14.9 us
  local copies, waits for them, and re-layouts: 7.96 us -> 8.8 us
  Pallas kernels: 31.5 us -> 32.3 us
    ppermute x3, waiting for transfers between devices: 4.93 us -> 1.3 us  [shards(): across = lax.ppermute(own, 'lon', swap(lon, 2))]
    ppermute x3, starting transfers between devices: 1 us -> 2.69 us  [shards(): beside = lax.ppermute(own, 'lon', swap(lon, 1))]
    ppermute x3, starting transfers between devices: 2.84 us -> 1.67 us  [shards(): across = lax.ppermute(own, 'lon', swap(lon, 2))]
    ppermute x5, starting transfers between devices: 3.63 us -> 4.34 us  [the longest x2 1.47 us: shards(): both = lax.ppermute(ready, 'lon', swap(lon, 1))]
    dynamic_slice x1, local copies, waits for them, and re-layouts: 0.07 us -> 0.73 us  [shards(): mine = lax.dynamic_slice_in_dim(lead_ids, lon_at * leads, leads)]
    ppermute x5, waiting for transfers between devices: 0.01 us -> 0.66 us  [the longest x1 0.65 us: shards(): east = lax.ppermute(tile[0], 'lon', lon_dn)]
    unnamed x19 -> x16, local copies, waits for them, and re-layouts: 7.03 us -> 7.21 us
  transfers between devices with their start and end apart: 13 -> 13, of which waited for: 1 -> 2; matrix products, arithmetic and copies ran while one was open for 8% -> 1% of each run, Pallas kernels for 31% -> 40%
where the time goes in v4:
time: 58.6 us; the launch traced here: 58.2 us
  Pallas kernels  32.3 us (55%)
  starting transfers between devices  14.9 us (25%)
  local copies, waits for them, and re-layouts  8.8 us (15%)
  waiting for transfers between devices  1.97 us (3%)
    pallas_call x2, Pallas kernels, forecast_heads(): pl.pallas_call(functools.partial(head_kernel, moves=moves, blocks=blocks,...  16.1 us
    pallas_call x3, Pallas kernels, encode(): pl.pallas_call(functools.partial(encoder_kernel, first=first, group=group...  13.9 us
    unnamed x16, local copies, waits for them, and re-layouts  7.21 us
    ppermute x1, starting transfers between devices, shards(): above = lax.ppermute(up, 'lat', lat_up)  3.15 us
    ppermute x1, starting transfers between devices, shards(): below = lax.ppermute(dn, 'lat', lat_dn)  3.03 us
    ppermute x3, starting transfers between devices, shards(): beside = lax.ppermute(own, 'lon', swap(lon, 1))  2.69 us
    pallas_call x1, Pallas kernels, prepare(): pl.pallas_call(weights_kernel, in_specs=[pl.BlockSpec(memory_space=pltpu....  2.24 us
    ppermute x3, starting transfers between devices, shards(): across = lax.ppermute(own, 'lon', swap(lon, 2))  1.67 us
  transfers between devices with their start and end apart: 13, of which 2 were waited for; matrix products, arithmetic and copies ran while one was open for 1% of the time, Pallas kernels for 40%

profile of v4, /device:TPU:25, one launch (start us, length us, event | category | flops | bytes accessed | tf_op | source)
XLA Modules:
  0.0 58.2 jit_solution(7539462707374963112)
XLA Ops:
  0.0 0.8 %slice_bitcast_fusion = (bf16[40,256]{1,0:T(8,128)(2,1)S(1)}, bf16[40,256]{1,0:T(8,128)(2,1)S(1)}) fusion(bf16[180,40,256]{2,1,0:T(8,128)(2,1)} %bitcast.23), kind=kLoop, calls=%fused_computation | loop fusion | bytes 81920 | tf_op jit(solution)/shard_map/squeeze | solution.py:389
  0.8 0.7 %collective-permute-start.1 = (bf16[40,256]{1,0:T(8,128)(2,1)S(1)}, bf16[40,256]{1,0:T(8,128)(2,1)S(1)}, u32[]{:S(2)}, u32[]{:S(2)}) collective-permute-start(bf16[40,256]{1,0:T(8,128)(2,1)S(1)} %get-tuple-element.21), channel_id=1, source_target_pairs={{1,0},{2,1},{3,2},{0,3},{5,4},{6,5},{7,6},{4,7},{9,8},{10,9},{11,1... | collective-permute-start | bytes 61448 | tf_op jit(solution)/shard_map/ppermute | solution.py:389
  1.5 1.1 %collective-permute-start = (bf16[40,256]{1,0:T(8,128)(2,1)S(1)}, bf16[40,256]{1,0:T(8,128)(2,1)S(1)}, u32[]{:S(2)}, u32[]{:S(2)}) collective-permute-start(bf16[40,256]{1,0:T(8,128)(2,1)S(1)} %get-tuple-element.22), channel_id=1, source_target_pairs={{0,1},{1,2},{2,3},{3,0},{4,5},{5,6},{6,7},{7,4},{8,9},{9,10},{10,1... | collective-permute-start | bytes 61448 | tf_op jit(solution)/shard_map/ppermute | solution.py:388
  2.6 0.7 %dynamic_slice.3.ids_ref = s32[2]{0:T(128)S(1)} dynamic-slice(s32[8]{0:T(128)} %param.13, s32[]{:T(128)S(6)} %select_n.3), dynamic_slice_sizes={2} | dynamic-slice | bytes 20 | tf_op jit(solution)/shard_map/dynamic_slice | solution.py:391
  3.3 0.1 stack.35.meta_ref
  3.4 0.6 %collective-permute-done.1.east_ref = bf16[40,256]{1,0:T(8,128)(2,1)S(1)} collective-permute-done((bf16[40,256]{1,0:T(8,128)(2,1)S(1)}, bf16[40,256]{1,0:T(8,128)(2,1)S(1)}, u32[]{:S(2)}, u32[]{:S(2)}) %collective-permute-start.1) | collective-permute-done | bytes 20512 | tf_op jit(solution)/shard_map/ppermute | solution.py:389
  4.0 0.0 collective-permute-done.west_ref
  4.0 2.0 %copy-done = bf16[40,180,256]{2,0,1:T(8,128)(2,1)S(1)} copy-done((bf16[40,180,256]{2,0,1:T(8,128)(2,1)S(1)}, bf16[40,180,256]{2,0,1:T(8,128)(2,1)}, u32[]{:S(2)}) %copy-start) | copy-done | bytes 3686424
  6.1 1.3 %copy-done.2 = bf16[3,3,256,256]{3,2,1,0:T(8,128)(2,1)S(1)} copy-done((bf16[3,3,256,256]{3,2,1,0:T(8,128)(2,1)S(1)}, bf16[3,3,256,256]{3,2,1,0:T(8,128)(2,1)}, u32[]{:S(2)}) %copy-start.2) | copy-done | bytes 1179672
  7.3 1.0 %copy-done.3 = f32[720,128]{1,0:T(8,128)S(1)} copy-done((f32[720,128]{1,0:T(8,128)S(1)}, f32[720,128]{1,0:T(8,128)}, u32[]{:S(2)}) %copy-start.3) | copy-done | bytes 368664
  8.3 1.0 %copy-done.4 = f32[720,128]{1,0:T(8,128)S(1)} copy-done((f32[720,128]{1,0:T(8,128)S(1)}, f32[720,128]{1,0:T(8,128)}, u32[]{:S(2)}) %copy-start.4) | copy-done | bytes 368664
  9.3 1.0 %copy-done.5 = bf16[3,3,128,128]{3,2,1,0:T(8,128)(2,1)S(1)} copy-done((bf16[3,3,128,128]{3,2,1,0:T(8,128)(2,1)S(1)}, bf16[3,3,128,128]{3,2,1,0:T(8,128)(2,1)}, u32[]{:S(2)}) %copy-start.5) | copy-done | bytes 294936
  10.3 1.0 %copy-done.6 = bf16[360,360]{1,0:T(8,128)(2,1)S(1)} copy-done((bf16[360,360]{1,0:T(8,128)(2,1)S(1)}, bf16[360,360]{1,0:T(8,128)(2,1)}, u32[]{:S(2)}) %copy-start.6) | copy-done | bytes 259224
  11.2 2.2 %weights.1 = (bf16[4,768,256]{2,1,0:T(8,128)(2,1)S(1)}, bf16[1152,256]{1,0:T(8,128)(2,1)S(1)}, f32[8,256]{1,0:T(8,128)S(1)}, bf16[368,368]{1,0:T(8,128)(2,1)S(1)...) custom-call(s32[2]{0:T(128)S(1)} %dynamic_slice.3.ids_ref, bf16[180,40,256]{2,1,0:T(8,128)(2,1)S(1)} %bitcast.24, ...), custom_call_target="tpu_custom_call" | custom-call | tf_op jit(solution)/shard_map/weights/pallas_call | solution.py:106
  13.5 3.1 %collective-permute-start.7 = (bf16[3,182,256]{2,1,0:T(8,128)(2,1)S(1)}, bf16[3,182,256]{2,1,0:T(8,128)(2,1)S(1)}, u32[]{:S(2)}, u32[]{:S(2)}) collective-permute-start(bf16[3,182,256]{2,1,0:T(8,128)(2,1)S(1)} %get-tuple-element.15), channel_id=1, source_target_pairs={{0,4},{4,8},{8,12},{12,16},{16,20},{20,24},{24,28},{1,5},{5,9},{9,... | collective-permute-start | bytes 838664 | tf_op jit(solution)/shard_map/ppermute | solution.py:398
  16.6 3.0 %collective-permute-start.8 = (bf16[3,182,256]{2,1,0:T(8,128)(2,1)S(1)}, bf16[3,182,256]{2,1,0:T(8,128)(2,1)S(1)}, u32[]{:S(2)}, u32[]{:S(2)}) collective-permute-start(bf16[3,182,256]{2,1,0:T(8,128)(2,1)S(1)} %get-tuple-element.16), channel_id=1, source_target_pairs={{4,0},{8,4},{12,8},{16,12},{20,16},{24,20},{28,24},{5,1},{9,5},{13... | collective-permute-start | bytes 838664 | tf_op jit(solution)/shard_map/ppermute | solution.py:399
  19.7 4.3 %encode.3 = bf16[8,90,128]{2,1,0:T(8,128)(2,1)S(1)} custom-call(s32[7]{0:T(128)S(1)} %stack.35.meta_ref, bf16[180,40,256]{2,1,0:T(8,128)(2,1)S(1)} %bitcast.25, bf16[40,256]{1,0:T(8,128)(2,1)S(1)} %collective-permute-done.west_ref, bf16[40,256]{1,0:T(8,128)(2,1)S(1)} %collective-permute-done.1.east_ref, ...), custom_call_target="tpu_custom_call" | custom-call | flops 2264924160 | bytes 8388608 | tf_op jit(solution)/shard_map/encode/pallas_call | solution.py:239
  24.0 2.2 %collective-permute-start.3 = (bf16[8,90,128]{2,1,0:T(8,128)(2,1)S(1)}, bf16[8,90,128]{2,1,0:T(8,128)(2,1)S(1)}, u32[]{:S(2)}, u32[]{:S(2)}) collective-permute-start(bf16[8,90,128]{2,1,0:T(8,128)(2,1)S(1)} %encode.3), channel_id=1, source_target_pairs={{0,1},{1,0},{2,3},{3,2},{4,5},{5,4},{6,7},{7,6},{8,9},{9,8},{10,11... | collective-permute-start | bytes 552968 | tf_op jit(solution)/shard_map/ppermute | solution.py:414
  26.2 0.5 collective-permute-start.2
  26.7 4.3 %encode.4 = bf16[8,90,128]{2,1,0:T(8,128)(2,1)S(1)} custom-call(s32[7]{0:T(128)S(1)} %stack.35.meta_ref, bf16[180,40,256]{2,1,0:T(8,128)(2,1)S(1)} %bitcast.26, bf16[40,256]{1,0:T(8,128)(2,1)S(1)} %collective-permute-done.west_ref, bf16[40,256]{1,0:T(8,128)(2,1)S(1)} %collective-permute-done.1.east_ref, ...), custom_call_target="tpu_custom_call" | custom-call | flops 2264924160 | bytes 8388608 | tf_op jit(solution)/shard_map/encode/pallas_call | solution.py:239
  31.0 0.4 collective-permute-start.6
  31.4 1.3 %collective-permute-done.2 = bf16[8,90,128]{2,1,0:T(8,128)(2,1)S(1)} collective-permute-done((bf16[8,90,128]{2,1,0:T(8,128)(2,1)S(1)}, bf16[8,90,128]{2,1,0:T(8,128)(2,1)S(1)}, u32[]{:S(2)}, u32[]{:S(2)}) %collective-permute-start.2) | collective-permute-done | bytes 184352 | tf_op jit(solution)/shard_map/ppermute | solution.py:413
  32.7 0.5 collective-permute-start.5
  33.2 1.1 %collective-permute-start.4 = (bf16[8,90,128]{2,1,0:T(8,128)(2,1)S(1)}, bf16[8,90,128]{2,1,0:T(8,128)(2,1)S(1)}, u32[]{:S(2)}, u32[]{:S(2)}) collective-permute-start(bf16[8,90,128]{2,1,0:T(8,128)(2,1)S(1)} %collective-permute-done.2), channel_id=1, source_target_pairs={{0,1},{1,0},{2,3},{3,2},{4,5},{5,4},{6,7},{7,6},{8,9},{9,8},{10,11... | collective-permute-start | bytes 552968 | tf_op jit(solution)/shard_map/ppermute | solution.py:419
  34.3 0.0 collective-permute-done.8.refs_1_
  34.3 5.3 %encode.5 = bf16[6,90,128]{2,1,0:T(8,128)(2,1)S(1)} custom-call(s32[7]{0:T(128)S(1)} %stack.35.meta_ref, bf16[180,40,256]{2,1,0:T(8,128)(2,1)S(1)} %bitcast.27, bf16[40,256]{1,0:T(8,128)(2,1)S(1)} %collective-permute-done.west_ref, bf16[40,256]{1,0:T(8,128)(2,1)S(1)} %collective-permute-done.1.east_ref, ...), custom_call_target="tpu_custom_call" | custom-call | flops 2264924160 | bytes 8388608 | tf_op jit(solution)/shard_map/encode/pallas_call | solution.py:239
  39.6 0.3 collective-permute-start.9
  40.0 1.1 %collective-permute-start.12 = (bf16[6,90,128]{2,1,0:T(8,128)(2,1)S(1)}, bf16[6,90,128]{2,1,0:T(8,128)(2,1)S(1)}, u32[]{:S(2)}, u32[]{:S(2)}) collective-permute-start(bf16[6,90,128]{2,1,0:T(8,128)(2,1)S(1)} %encode.5), channel_id=1, source_target_pairs={{0,3},{1,2},{2,1},{3,0},{4,7},{5,6},{6,5},{7,4},{8,11},{9,10},{10,... | collective-permute-start | bytes 414728 | tf_op jit(solution)/shard_map/ppermute | solution.py:416
  41.1 0.1 collective-permute-start.11
  41.2 0.7 %collective-permute-start.10 = (bf16[6,90,128]{2,1,0:T(8,128)(2,1)S(1)}, bf16[6,90,128]{2,1,0:T(8,128)(2,1)S(1)}, u32[]{:S(2)}, u32[]{:S(2)}) collective-permute-start(bf16[6,90,128]{2,1,0:T(8,128)(2,1)S(1)} %encode.5), channel_id=1, source_target_pairs={{0,2},{1,3},{2,0},{3,1},{4,6},{5,7},{6,4},{7,5},{8,10},{9,11},{10,... | collective-permute-start | bytes 414728 | tf_op jit(solution)/shard_map/ppermute | solution.py:413
  41.9 9.3 %heads.2.refs_15_ = bf16[2,20,360,128]{3,2,1,0:T(8,128)(2,1)} custom-call(s32[7]{0:T(128)S(1)} %stack.35.meta_ref, bf16[1,8,90,128]{3,2,1,0:T(8,128)(2,1)S(1)} %bitcast.28, bf16[1,8,90,128]{3,2,1,0:T(8,128)(2,1)S(1)} %bitcast.32, bf16[1,8,90,128]{3,2,1,0:T(8,128)(2,1)S(1)} %bitcast.30, bf16[1,8,90,128]{3,2,1,0:T(8,128)(2,1)S(1)} %bitcast.40, ...), custom_call_target="tpu_custom_call" | custom-call | flops 3344302080 | bytes 25165824 | tf_op jit(solution)/shard_map/heads/pallas_call | solution.py:341
  51.2 6.8 %heads.3 = bf16[2,20,360,128]{3,2,1,0:T(8,128)(2,1)} custom-call(s32[7]{0:T(128)S(1)} %stack.35.meta_ref, bf16[1,8,90,128]{3,2,1,0:T(8,128)(2,1)S(1)} %bitcast.29, bf16[1,8,90,128]{3,2,1,0:T(8,128)(2,1)S(1)} %bitcast.33, bf16[1,8,90,128]{3,2,1,0:T(8,128)(2,1)S(1)} %bitcast.31, bf16[1,8,90,128]{3,2,1,0:T(8,128)(2,1)S(1)} %bitcast.41, ...), custom_call_target="tpu_custom_call", output_to_operand_aliasing={{}: (16, {})} | custom-call | flops 2229534720 | bytes 16777216 | tf_op jit(solution)/shard_map/heads/pallas_call | solution.py:341
  (19 shorter events, 0.0 us)
Async XLA Ops:
  0.0 19.7 %copy-start.7 = (bf16[256,128]{1,0:T(8,128)(2,1)S(1)}, bf16[256,128]{1,0:T(8,128)(2,1)}, u32[]{:S(2)}) copy-start(bf16[256,128]{1,0:T(8,128)(2,1)} %refs_3_.1) | copy-start | bytes 196612
  0.8 3.2 %collective-permute-start.1 = (bf16[40,256]{1,0:T(8,128)(2,1)S(1)}, bf16[40,256]{1,0:T(8,128)(2,1)S(1)}, u32[]{:S(2)}, u32[]{:S(2)}) collective-permute-start(bf16[40,256]{1,0:T(8,128)(2,1)S(1)} %get-tuple-element.21), channel_id=1, source_target_pairs={{1,0},{2,1},{3,2},{0,3},{5,4},{6,5},{7,6},{4,7},{9,8},{10,9},{11,1... | collective-permute-start | bytes 61448 | tf_op jit(solution)/shard_map/ppermute | solution.py:389
  1.5 2.6 %collective-permute-start = (bf16[40,256]{1,0:T(8,128)(2,1)S(1)}, bf16[40,256]{1,0:T(8,128)(2,1)S(1)}, u32[]{:S(2)}, u32[]{:S(2)}) collective-permute-start(bf16[40,256]{1,0:T(8,128)(2,1)S(1)} %get-tuple-element.22), channel_id=1, source_target_pairs={{0,1},{1,2},{2,3},{3,0},{4,5},{5,6},{6,7},{7,4},{8,9},{9,10},{10,1... | collective-permute-start | bytes 61448 | tf_op jit(solution)/shard_map/ppermute | solution.py:388
  4.0 2.0 %copy-start = (bf16[40,180,256]{2,0,1:T(8,128)(2,1)S(1)}, bf16[40,180,256]{2,0,1:T(8,128)(2,1)}, u32[]{:S(2)}) copy-start(bf16[40,180,256]{2,0,1:T(8,128)(2,1)} %param.8) | copy-start | bytes 11059204
  6.1 1.3 %copy-start.2 = (bf16[3,3,256,256]{3,2,1,0:T(8,128)(2,1)S(1)}, bf16[3,3,256,256]{3,2,1,0:T(8,128)(2,1)}, u32[]{:S(2)}) copy-start(bf16[3,3,256,256]{3,2,1,0:T(8,128)(2,1)} %we_hbm.1) | copy-start | bytes 3538948
  7.3 1.0 %copy-start.3 = (f32[720,128]{1,0:T(8,128)S(1)}, f32[720,128]{1,0:T(8,128)}, u32[]{:S(2)}) copy-start(f32[720,128]{1,0:T(8,128)} %scale_hbm.1) | copy-start | bytes 1105924
  8.3 1.0 %copy-start.4 = (f32[720,128]{1,0:T(8,128)S(1)}, f32[720,128]{1,0:T(8,128)}, u32[]{:S(2)}) copy-start(f32[720,128]{1,0:T(8,128)} %shift_hbm.1) | copy-start | bytes 1105924
  9.3 1.0 %copy-start.5 = (bf16[3,3,128,128]{3,2,1,0:T(8,128)(2,1)S(1)}, bf16[3,3,128,128]{3,2,1,0:T(8,128)(2,1)}, u32[]{:S(2)}) copy-start(bf16[3,3,128,128]{3,2,1,0:T(8,128)(2,1)} %wh_hbm.1) | copy-start | bytes 884740
  10.3 1.0 %copy-start.6 = (bf16[360,360]{1,0:T(8,128)(2,1)S(1)}, bf16[360,360]{1,0:T(8,128)(2,1)}, u32[]{:S(2)}) copy-start(bf16[360,360]{1,0:T(8,128)(2,1)} %z_hbm.1) | copy-start | bytes 777604
  11.2 8.5 %copy-start.1 = (bf16[40,180,256]{2,0,1:T(8,128)(2,1)S(1)}, bf16[40,180,256]{2,0,1:T(8,128)(2,1)}, u32[]{:S(2)}) copy-start(bf16[40,180,256]{2,0,1:T(8,128)(2,1)} %param.8) | copy-start | bytes 11059204
  13.5 19.7 %collective-permute-start.7 = (bf16[3,182,256]{2,1,0:T(8,128)(2,1)S(1)}, bf16[3,182,256]{2,1,0:T(8,128)(2,1)S(1)}, u32[]{:S(2)}, u32[]{:S(2)}) collective-permute-start(bf16[3,182,256]{2,1,0:T(8,128)(2,1)S(1)} %get-tuple-element.15), channel_id=1, source_target_pairs={{0,4},{4,8},{8,12},{12,16},{16,20},{20,24},{24,28},{1,5},{5,9},{9,... | collective-permute-start | bytes 838664 | tf_op jit(solution)/shard_map/ppermute | solution.py:398
  16.6 17.6 %collective-permute-start.8 = (bf16[3,182,256]{2,1,0:T(8,128)(2,1)S(1)}, bf16[3,182,256]{2,1,0:T(8,128)(2,1)S(1)}, u32[]{:S(2)}, u32[]{:S(2)}) collective-permute-start(bf16[3,182,256]{2,1,0:T(8,128)(2,1)S(1)} %get-tuple-element.16), channel_id=1, source_target_pairs={{4,0},{8,4},{12,8},{16,12},{20,16},{24,20},{28,24},{5,1},{9,5},{13... | collective-permute-start | bytes 838664 | tf_op jit(solution)/shard_map/ppermute | solution.py:399
  24.0 17.1 %collective-permute-start.3 = (bf16[8,90,128]{2,1,0:T(8,128)(2,1)S(1)}, bf16[8,90,128]{2,1,0:T(8,128)(2,1)S(1)}, u32[]{:S(2)}, u32[]{:S(2)}) collective-permute-start(bf16[8,90,128]{2,1,0:T(8,128)(2,1)S(1)} %encode.3), channel_id=1, source_target_pairs={{0,1},{1,0},{2,3},{3,2},{4,5},{5,4},{6,7},{7,6},{8,9},{9,8},{10,11... | collective-permute-start | bytes 552968 | tf_op jit(solution)/shard_map/ppermute | solution.py:414
  26.2 6.5 %collective-permute-start.2 = (bf16[8,90,128]{2,1,0:T(8,128)(2,1)S(1)}, bf16[8,90,128]{2,1,0:T(8,128)(2,1)S(1)}, u32[]{:S(2)}, u32[]{:S(2)}) collective-permute-start(bf16[8,90,128]{2,1,0:T(8,128)(2,1)S(1)} %encode.3), channel_id=1, source_target_pairs={{0,2},{1,3},{2,0},{3,1},{4,6},{5,7},{6,4},{7,5},{8,10},{9,11},{10,... | collective-permute-start | bytes 552968 | tf_op jit(solution)/shard_map/ppermute | solution.py:413
  31.0 10.2 %collective-permute-start.6 = (bf16[8,90,128]{2,1,0:T(8,128)(2,1)S(1)}, bf16[8,90,128]{2,1,0:T(8,128)(2,1)S(1)}, u32[]{:S(2)}, u32[]{:S(2)}) collective-permute-start(bf16[8,90,128]{2,1,0:T(8,128)(2,1)S(1)} %encode.4), channel_id=1, source_target_pairs={{0,1},{1,0},{2,3},{3,2},{4,5},{5,4},{6,7},{7,6},{8,9},{9,8},{10,11... | collective-permute-start | bytes 552968 | tf_op jit(solution)/shard_map/ppermute | solution.py:414
  32.7 7.0 %collective-permute-start.5 = (bf16[8,90,128]{2,1,0:T(8,128)(2,1)S(1)}, bf16[8,90,128]{2,1,0:T(8,128)(2,1)S(1)}, u32[]{:S(2)}, u32[]{:S(2)}) collective-permute-start(bf16[8,90,128]{2,1,0:T(8,128)(2,1)S(1)} %encode.4), channel_id=1, source_target_pairs={{0,2},{1,3},{2,0},{3,1},{4,6},{5,7},{6,4},{7,5},{8,10},{9,11},{10,... | collective-permute-start | bytes 552968 | tf_op jit(solution)/shard_map/ppermute | solution.py:413
  33.2 8.7 %collective-permute-start.4 = (bf16[8,90,128]{2,1,0:T(8,128)(2,1)S(1)}, bf16[8,90,128]{2,1,0:T(8,128)(2,1)S(1)}, u32[]{:S(2)}, u32[]{:S(2)}) collective-permute-start(bf16[8,90,128]{2,1,0:T(8,128)(2,1)S(1)} %collective-permute-done.2), channel_id=1, source_target_pairs={{0,1},{1,0},{2,3},{3,2},{4,5},{5,4},{6,7},{7,6},{8,9},{9,8},{10,11... | collective-permute-start | bytes 552968 | tf_op jit(solution)/shard_map/ppermute | solution.py:419
  39.6 2.2 %collective-permute-start.9 = (bf16[8,90,128]{2,1,0:T(8,128)(2,1)S(1)}, bf16[8,90,128]{2,1,0:T(8,128)(2,1)S(1)}, u32[]{:S(2)}, u32[]{:S(2)}) collective-permute-start(bf16[8,90,128]{2,1,0:T(8,128)(2,1)S(1)} %collective-permute-done.5), channel_id=1, source_target_pairs={{0,1},{1,0},{2,3},{3,2},{4,5},{5,4},{6,7},{7,6},{8,9},{9,8},{10,11... | collective-permute-start | bytes 552968 | tf_op jit(solution)/shard_map/ppermute | solution.py:419
  40.0 11.2 %collective-permute-start.12 = (bf16[6,90,128]{2,1,0:T(8,128)(2,1)S(1)}, bf16[6,90,128]{2,1,0:T(8,128)(2,1)S(1)}, u32[]{:S(2)}, u32[]{:S(2)}) collective-permute-start(bf16[6,90,128]{2,1,0:T(8,128)(2,1)S(1)} %encode.5), channel_id=1, source_target_pairs={{0,3},{1,2},{2,1},{3,0},{4,7},{5,6},{6,5},{7,4},{8,11},{9,10},{10,... | collective-permute-start | bytes 414728 | tf_op jit(solution)/shard_map/ppermute | solution.py:416
  41.1 10.1 %collective-permute-start.11 = (bf16[6,90,128]{2,1,0:T(8,128)(2,1)S(1)}, bf16[6,90,128]{2,1,0:T(8,128)(2,1)S(1)}, u32[]{:S(2)}, u32[]{:S(2)}) collective-permute-start(bf16[6,90,128]{2,1,0:T(8,128)(2,1)S(1)} %encode.5), channel_id=1, source_target_pairs={{0,1},{1,0},{2,3},{3,2},{4,5},{5,4},{6,7},{7,6},{8,9},{9,8},{10,11... | collective-permute-start | bytes 414728 | tf_op jit(solution)/shard_map/ppermute | solution.py:414
  41.2 10.0 %collective-permute-start.10 = (bf16[6,90,128]{2,1,0:T(8,128)(2,1)S(1)}, bf16[6,90,128]{2,1,0:T(8,128)(2,1)S(1)}, u32[]{:S(2)}, u32[]{:S(2)}) collective-permute-start(bf16[6,90,128]{2,1,0:T(8,128)(2,1)S(1)} %encode.5), channel_id=1, source_target_pairs={{0,2},{1,3},{2,0},{3,1},{4,6},{5,7},{6,4},{7,5},{8,10},{9,11},{10,... | collective-permute-start | bytes 414728 | tf_op jit(solution)/shard_map/ppermute | solution.py:413

commit v5 on v4

--- a/solution.py
+++ b/solution.py
@@ -29,42 +29,25 @@
 
 
 def weights_kernel(
-    ids_ref, x_ref, west_ref, east_ref, we_hbm, wh_hbm, scale_hbm, shift_hbm, z_hbm,
-    g_ref, ws_ref, vec_ref, zs_ref, up_ref, dn_ref,
-    edge, flat, we_ref, wh_ref, tab, z_ref, sem,
+    meta_ref, ids_ref, we_hbm, wh_hbm, scale_hbm, shift_hbm, z_hbm,
+    g_ref, ws_ref, vec_ref, zs_ref,
+    we_ref, wh_ref, tab, z_ref, sem,
 ):
     ch = we_ref.shape[-1]
     head = wh_ref.shape[-1]
     leads = ws_ref.shape[1] // head
     cols = z_ref.shape[0]
-    xcols, rows, _ = x_ref.shape
-    reach = up_ref.shape[0]
-    copies = [
-        (x_ref.at[:, :8], edge.at[0]),
-        (x_ref.at[:, rows - 8 :], edge.at[1]),
-        (we_hbm, we_ref),
-        (z_hbm, z_ref),
-        (wh_hbm, wh_ref),
-    ]
+    ids = [ids_ref[meta_ref[2] * leads + lead] for lead in range(leads)]
+    copies = [(we_hbm, we_ref), (z_hbm, z_ref), (wh_hbm, wh_ref)]
     for lead in range(leads):
-        block = pl.multiple_of((ids_ref[lead] // 8) * 8, 8)
+        block = pl.multiple_of((ids[lead] // 8) * 8, 8)
         copies.append((scale_hbm.at[pl.ds(block, 8)], tab.at[lead, 0]))
         copies.append((shift_hbm.at[pl.ds(block, 8)], tab.at[lead, 1]))
     copies = [pltpu.make_async_copy(one, two, sem.at[i]) for i, (one, two) in enumerate(copies)]
     for c in copies:
         c.start()
+    zs_ref[...] = jnp.zeros(zs_ref.shape, BF)
     copies[0].wait()
-    copies[1].wait()
-    for k, (slab, start, r) in enumerate(((dn_ref, 0, 0), (up_ref, 8 - reach, rows - reach))):
-        parts = []
-        for j in range(ch // 128):
-            lanes = slice(j * 128, (j + 1) * 128)
-            flat[k, j] = edge[k, :, :, lanes].astype(F32).reshape(xcols * 8, 128)
-            parts.append([flat[k, j, pl.ds(start + i, xcols, stride=8), :] for i in range(reach)])
-        for i in range(reach):
-            row = jnp.concatenate([p[i] for p in parts], axis=1).astype(BF)
-            slab[i] = jnp.concatenate([west_ref[r + i : r + i + 1, :], row, east_ref[r + i : r + i + 1, :]], axis=0)
-    copies[2].wait()
     for dr in range(3):
         at = slice(dr * ch, (dr + 1) * ch)
         w = [we_ref[dr, dc].astype(F32) for dc in range(3)]
@@ -73,13 +56,12 @@
         g_ref[1, at] = (half + 0.5 * w[1]).astype(BF)
         g_ref[2, at] = (half - 0.5 * w[1]).astype(BF)
         g_ref[3, at] = we_ref[dr, 2]
-    for c in copies[3:]:
+    for c in copies[1:]:
         c.wait()
-    zs_ref[...] = jnp.zeros(zs_ref.shape, BF)
     zs_ref[:cols, :cols] = z_ref[...] * jnp.asarray(0.5, BF)
     for lead in range(leads):
         lanes = slice(lead * head, (lead + 1) * head)
-        at = ids_ref[lead] % 8
+        at = ids[lead] % 8
         gain = 1.0 + tab[lead, 0, pl.ds(at, 1), :]
         shift = tab[lead, 1, pl.ds(at, 1), :]
         vec_ref[GAIN : GAIN + 1, lanes] = gain
@@ -96,37 +78,70 @@
             vec_ref[BIAS + dr : BIAS + dr + 1, lanes] = jnp.sum(total, axis=0, keepdims=True)
 
 
-def prepare(ids, x, west, east, w_enc, w_head, scale, shift, z, reach):
-    leads = ids.shape[0]
+def prepare(meta, ids, w_enc, w_head, scale, shift, z, leads):
     ch, head, cols = w_enc.shape[-1], w_head.shape[-1], z.shape[0]
-    xcols = x.shape[0]
     wide = up_to(cols, 16)
     vmem = pl.BlockSpec(memory_space=pltpu.VMEM)
-    anywhere = pl.BlockSpec(memory_space=pl.ANY)
+    smem = pl.BlockSpec(memory_space=pltpu.SMEM)
+    hbm = pl.BlockSpec(memory_space=pltpu.HBM)
     return pl.pallas_call(
         weights_kernel,
-        in_specs=[pl.BlockSpec(memory_space=pltpu.SMEM), anywhere, vmem, vmem] + [anywhere] * 5,
-        out_specs=[vmem] * 6,
+        in_specs=[smem, smem] + [hbm] * 5,
+        out_specs=[vmem] * 4,
         out_shape=[
             jax.ShapeDtypeStruct((4, 3 * ch, ch), BF),
             jax.ShapeDtypeStruct((9 * head, leads * head), BF),
             jax.ShapeDtypeStruct((8, leads * head), F32),
             jax.ShapeDtypeStruct((wide, wide), BF),
-            jax.ShapeDtypeStruct((reach, xcols + 2, ch), BF),
-            jax.ShapeDtypeStruct((reach, xcols + 2, ch), BF),
         ],
         scratch_shapes=[
-            pltpu.VMEM((2, xcols, 8, ch), BF),
-            pltpu.VMEM((2, ch // 128, xcols * 8, 128), F32),
             pltpu.VMEM(w_enc.shape, BF),
             pltpu.VMEM(w_head.shape, BF),
             pltpu.VMEM((leads, 2, 8, head), F32),
             pltpu.VMEM(z.shape, BF),
-            pltpu.SemaphoreType.DMA((5 + 2 * leads,)),
+            pltpu.SemaphoreType.DMA((3 + 2 * leads,)),
         ],
-        compiler_params=params(16),
+        compiler_params=params(58),
         name="weights",
-    )(ids, x, west, east, w_enc, w_head, scale, shift, z)
+    )(meta, ids, w_enc, w_head, scale, shift, z)
+
+
+def slabs_kernel(x_ref, west_ref, east_ref, up_ref, dn_ref, edge, flat, sem):
+    xcols, rows, ch = x_ref.shape
+    reach = up_ref.shape[0]
+    copies = [
+        pltpu.make_async_copy(x_ref.at[:, a : a + 8], edge.at[k], sem.at[k]) for k, a in enumerate((0, rows - 8))
+    ]
+    for c in copies:
+        c.start()
+    for k, (slab, start, r) in enumerate(((dn_ref, 0, 0), (up_ref, 8 - reach, rows - reach))):
+        copies[k].wait()
+        parts = []
+        for j in range(ch // 128):
+            lanes = slice(j * 128, (j + 1) * 128)
+            flat[k, j] = edge[k, :, :, lanes].astype(F32).reshape(xcols * 8, 128)
+            parts.append([flat[k, j, pl.ds(start + i, xcols, stride=8), :] for i in range(reach)])
+        for i in range(reach):
+            row = jnp.concatenate([p[i] for p in parts], axis=1).astype(BF)
+            slab[i] = jnp.concatenate([west_ref[r + i : r + i + 1, :], row, east_ref[r + i : r + i + 1, :]], axis=0)
+
+
+def row_slabs(x, west, east, reach):
+    xcols, _, ch = x.shape
+    vmem = pl.BlockSpec(memory_space=pltpu.VMEM)
+    return pl.pallas_call(
+        slabs_kernel,
+        in_specs=[pl.BlockSpec(memory_space=pltpu.HBM), vmem, vmem],
+        out_specs=[vmem] * 2,
+        out_shape=[jax.ShapeDtypeStruct((reach, xcols + 2, ch), BF)] * 2,
+        scratch_shapes=[
+            pltpu.VMEM((2, xcols, 8, ch), BF),
+            pltpu.VMEM((2, ch // 128, xcols * 8, 128), F32),
+            pltpu.SemaphoreType.DMA((2,)),
+        ],
+        compiler_params=params(48),
+        name="slabs",
+    )(x, west, east)
 
 
 def encoder_kernel(
@@ -138,16 +153,20 @@
     reach = 2 * EDGE - 1
     starts = (0, rows - 8) if first is None else ((first - 1) // 8 * 8,)
     tall = xr.shape[2]
-    copies = [
-        pltpu.make_async_copy(x_ref.at[:, a : a + tall], xr.at[i, 1 : cols + 1], sem.at[i])
-        for i, a in enumerate(starts)
-    ]
-    for c in copies:
-        c.start()
+    block = next(n for n in range(32, 0, -1) if (cols + 2) % n == 0)
+    copies = []
+    for p in range(0, cols, block):
+        to = min(p + block, cols)
+        for i, a in enumerate(starts):
+            copies.append(
+                pltpu.make_async_copy(
+                    x_ref.at[p:to, a : a + tall], xr.at[i, p + 1 : to + 1], sem.at[i, p // block]
+                )
+            )
+            copies[-1].start()
     for i, a in enumerate(starts):
         xr[i, 0] = west_ref[a : a + tall, :]
         xr[i, cols + 1] = east_ref[a : a + tall, :]
-    block = next(n for n in range(32, 0, -1) if (cols + 2) % n == 0)
     if first is None:
         hf = refs[9]
         for k, halo in enumerate(halos):
@@ -156,10 +175,11 @@
                 for i in range(reach):
                     at = 8 - reach + i if k == 0 else i
                     hf[k, j, pl.ds(at, cols + 2, stride=8), :] = halo[i, :, lanes].astype(F32)
-    for c in copies:
-        c.wait()
     for a in range(0, cols + 2, block):
         at = slice(a, a + block)
+        for c in copies[: len(starts)]:
+            c.wait()
+        copies = copies[len(starts) :]
         if first is None:
             far = []
             for k in range(2):
@@ -230,7 +250,7 @@
         pltpu.VMEM((2, 4, group * 16, ch), F32),
         pltpu.VMEM((ch // 128, group * 16, 128), F32),
         pltpu.VMEM((cols // 2 * 8, head), F32),
-        pltpu.SemaphoreType.DMA((blocks,)),
+        pltpu.SemaphoreType.DMA((blocks, cols)),
     ]
     if halos is not None:
         scratch.append(pltpu.VMEM((2, ch // 128, (cols + 2) * 8, 128), F32))
@@ -238,7 +258,7 @@
     flops = 2 * cols * 16 * 6 * ch * ch
     return pl.pallas_call(
         functools.partial(encoder_kernel, first=first, group=group),
-        in_specs=[pl.BlockSpec(memory_space=pltpu.SMEM), pl.BlockSpec(memory_space=pl.ANY)]
+        in_specs=[pl.BlockSpec(memory_space=pltpu.SMEM), pl.BlockSpec(memory_space=pltpu.HBM)]
         + [vmem] * (len(operands) - 2),
         out_specs=vmem,
         out_shape=jax.ShapeDtypeStruct((count, cols // 2, head), BF),
@@ -253,8 +273,8 @@
     sources = refs[: len(moves)]
     ws_ref, vec_ref, zs_ref = refs[len(moves) : len(moves) + 3]
     out_ref, band, ps, cs, outs, sem, out_sem = refs[len(moves) + 3 + aliased :]
-    ch = ps.shape[3] // 3
-    wide = ps.shape[2]
+    ch = ps.shape[2] // 3
+    wide = ps.shape[1]
     leads, rows, cols, _ = out_ref.shape
 
     copies = []
@@ -270,7 +290,7 @@
     for c in copies:
         c.start()
     if wide > cols:
-        ps[:, :, cols:, :] = jnp.zeros((*ps.shape[:2], wide - cols, 3 * ch), BF)
+        ps[:, cols:, :] = jnp.zeros((ps.shape[0], wide - cols, 3 * ch), BF)
     for c in copies:
         c.wait()
 
@@ -278,15 +298,23 @@
     first = (meta_ref[0] == 1).astype(F32) * vec_ref[BIAS : BIAS + 1, :]
     last = (meta_ref[1] == 1).astype(F32) * vec_ref[BIAS + 2 : BIAS + 3, :]
 
+    wanted = [sorted({n * STEP + i for i in range(STEP + 2)}) for n in blocks]
+    slots = {r: k for k, r in enumerate(sorted(set(sum(wanted, []))))}
+    staged = set()
+
     def stage(n):
-        for i in range(STEP + 2):
-            row = jnp.concatenate([band[s, blocks[n] * STEP + i] for s in range(shards)], axis=0)
-            ps[n % 2, i, :cols, ch : 2 * ch] = row
-            ps[n % 2, i, :cols, :ch] = jnp.concatenate([row[-1:], row[:-1]], axis=0)
-            ps[n % 2, i, :cols, 2 * ch :] = jnp.concatenate([row[1:], row[:1]], axis=0)
+        for r in wanted[n]:
+            if r in staged:
+                continue
+            staged.add(r)
+            k = slots[r]
+            row = jnp.concatenate([band[s, r] for s in range(shards)], axis=0)
+            ps[k, :cols, ch : 2 * ch] = row
+            ps[k, :cols, :ch] = jnp.concatenate([row[-1:], row[:-1]], axis=0)
+            ps[k, :cols, 2 * ch :] = jnp.concatenate([row[1:], row[:1]], axis=0)
 
     def conv(n):
-        p = [ps[n % 2, i] for i in range(STEP + 2)]
+        p = [ps[slots[r]] for r in wanted[n]]
         lhs = [jnp.concatenate(p[i : i + 3], axis=1) for i in range(STEP)]
         cs[n % 2] = jnp.dot(jnp.concatenate(lhs, axis=0), ws_ref[...], preferred_element_type=F32)
 
@@ -294,7 +322,7 @@
         row = blocks[n] * STEP + i
         y = cs[n % 2, i * wide : (i + 1) * wide] + (bias - first if row == 0 else (bias - last if row == rows - 1 else bias))
         mixed = jnp.dot(zs_ref[...], gelu_twice(y).astype(BF), preferred_element_type=F32)
-        center = ps[n % 2, i + 1, :, ch : 2 * ch].astype(F32)
+        center = ps[slots[row + 1], :, ch : 2 * ch].astype(F32)
         for lead in range(leads):
             lanes = slice(lead * ch, (lead + 1) * ch)
             mod = center * vec_ref[GAIN : GAIN + 1, lanes] + vec_ref[SHIFT : SHIFT + 1, lanes]
@@ -331,21 +359,22 @@
     wide = zs.shape[0]
     vmem = pl.BlockSpec(memory_space=pltpu.VMEM)
     anywhere = pl.BlockSpec(memory_space=pl.ANY)
+    staged = len({n * STEP + i for n in blocks for i in range(STEP + 2)})
     operands = [meta, *sources, ws, vec, zs]
     in_specs = [pl.BlockSpec(memory_space=pltpu.SMEM)] + [anywhere] * len(sources) + [vmem] * 3
     alias = {}
     if so_far is not None:
         alias = {len(operands): 0}
         operands.append(so_far)
-        in_specs.append(anywhere)
+        in_specs.append(pl.BlockSpec(memory_space=pltpu.HBM))
     return pl.pallas_call(
         functools.partial(head_kernel, moves=moves, blocks=blocks, shards=shards, aliased=len(alias)),
         in_specs=in_specs,
-        out_specs=anywhere,
+        out_specs=pl.BlockSpec(memory_space=pltpu.HBM),
         out_shape=jax.ShapeDtypeStruct(shape, BF),
         scratch_shapes=[
             pltpu.VMEM((shards, rows + 2, cols // shards, ch), BF),
-            pltpu.VMEM((2, STEP + 2, wide, 3 * ch), BF),
+            pltpu.VMEM((staged, wide, 3 * ch), BF),
             pltpu.VMEM((2, STEP * wide, leads * ch), F32),
             pltpu.VMEM((len(blocks), leads, STEP, cols, ch), BF),
             pltpu.SemaphoreType.DMA((sum(len(m[1]) for m in moves),)),
@@ -388,13 +417,11 @@
     west = lax.ppermute(tile[-1], "lon", lon_up)
     east = lax.ppermute(tile[0], "lon", lon_dn)
 
-    mine = lax.dynamic_slice_in_dim(lead_ids, lon_at * leads, leads)
     meta = jnp.stack(
         [lat_at == 0, lat_at == lat - 1, lon_at, lon_at ^ 2, lon_at ^ 1, lon_at ^ 3, 0]
     ).astype(jnp.int32)
-    g, ws, vec, zs, up, dn = prepare(
-        mine, tile, west, east, w_enc, w_head, film_scale, film_shift, zonal_mix, reach
-    )
+    g, ws, vec, zs = prepare(meta, lead_ids, w_enc, w_head, film_scale, film_shift, zonal_mix, leads)
+    up, dn = row_slabs(tile, west, east, reach)
     above = lax.ppermute(up, "lat", lat_up)
     below = lax.ppermute(dn, "lat", lat_dn)
 
@@ -415,7 +442,7 @@
             if k == 2:
                 both = lax.ppermute(own, "lon", swap(lon, 3))
             else:
-                ready, _ = lax.optimization_barrier((across, proj[k + 1]))
+                ready, _ = lax.optimization_barrier((across, proj[2]))
                 both = lax.ppermute(ready, "lon", swap(lon, 1))
             sent.append([(2, own[None]), (3, across[None]), (4, beside[None]), (5, both[None])])
         else:

time: 58.6 us -> 60 us (1.024)
  Pallas kernels: 32.3 us -> 43.1 us
  local copies, waits for them, and re-layouts: 8.8 us -> 3.43 us
  starting transfers between devices: 14.9 us -> 12.8 us
  waiting for transfers between devices: 1.97 us -> 0.03 us
    pallas_call x3, Pallas kernels: 13.9 us -> 22.7 us  [encode(): pl.pallas_call(functools.partial(encoder_kernel, first=first, group=group...]
    unnamed x16 -> x14, local copies, waits for them, and re-layouts: 7.21 us -> 2.06 us
    pallas_call x1 -> x2, Pallas kernels: 2.24 us -> 4.46 us  [the longest x1 3.82 us: prepare(): pl.pallas_call(weights_kernel, in_specs=[smem, smem] + [hbm] * 5, out_spe...]
    ppermute x3, starting transfers between devices: 2.69 us -> 1.36 us  [shards(): beside = lax.ppermute(own, 'lon', swap(lon, 1))]
    ppermute x3, waiting for transfers between devices: 1.3 us -> 0.01 us  [shards(): across = lax.ppermute(own, 'lon', swap(lon, 2))]
    ppermute x2, starting transfers between devices: 1.47 us -> 0.58 us  [shards(): both = lax.ppermute(ready, 'lon', swap(lon, 1))]
    dynamic_slice x1 -> x0, local copies, waits for them, and re-layouts: 0.73 us -> none  [shards(): mine = lax.dynamic_slice_in_dim(lead_ids, lon_at * leads, leads)]
    ppermute x1, waiting for transfers between devices: 0.65 us -> 0.01 us  [shards(): east = lax.ppermute(tile[0], 'lon', lon_dn)]
  transfers between devices with their start and end apart: 13 -> 13, of which waited for: 2 -> 0; matrix products, arithmetic and copies ran while one was open for 1% -> 1% of each run, Pallas kernels for 40% -> 60%
where the time goes in v5:
time: 60 us; the launch traced here: 59.7 us
  Pallas kernels  43.1 us (72%)
  starting transfers between devices  12.8 us (21%)
  local copies, waits for them, and re-layouts  3.43 us (6%)
    pallas_call x3, Pallas kernels, encode(): pl.pallas_call(functools.partial(encoder_kernel, first=first, group=group...  22.7 us
    pallas_call x2, Pallas kernels, forecast_heads(): pl.pallas_call(functools.partial(head_kernel, moves=moves, blocks=blocks,...  15.9 us
    pallas_call x1, Pallas kernels, prepare(): pl.pallas_call(weights_kernel, in_specs=[smem, smem] + [hbm] * 5, out_spe...  3.82 us
    ppermute x1, starting transfers between devices, shards(): above = lax.ppermute(up, 'lat', lat_up)  3.15 us
    ppermute x1, starting transfers between devices, shards(): below = lax.ppermute(dn, 'lat', lat_dn)  3.07 us
    unnamed x14, local copies, waits for them, and re-layouts  2.06 us
    ppermute x3, starting transfers between devices, shards(): across = lax.ppermute(own, 'lon', swap(lon, 2))  1.54 us
    ppermute x1, starting transfers between devices, shards(): both = lax.ppermute(own, 'lon', swap(lon, 3))  1.37 us
  transfers between devices with their start and end apart: 13, of which 0 were waited for; matrix products, arithmetic and copies ran while one was open for 1% of the time, Pallas kernels for 60%

profile of v5, /device:TPU:25, one launch (start us, length us, event | category | flops | bytes accessed | tf_op | source)
XLA Modules:
  0.0 59.7 jit_solution(3072682031965728338)
XLA Ops:
  0.0 0.8 %slice_bitcast_fusion = (bf16[40,256]{1,0:T(8,128)(2,1)S(1)}, bf16[40,256]{1,0:T(8,128)(2,1)S(1)}) fusion(bf16[180,40,256]{2,1,0:T(8,128)(2,1)} %bitcast.23), kind=kLoop, calls=%fused_computation | loop fusion | bytes 81920 | tf_op jit(solution)/shard_map/squeeze | solution.py:418
  0.8 0.7 %collective-permute-start.1 = (bf16[40,256]{1,0:T(8,128)(2,1)S(1)}, bf16[40,256]{1,0:T(8,128)(2,1)S(1)}, u32[]{:S(2)}, u32[]{:S(2)}) collective-permute-start(bf16[40,256]{1,0:T(8,128)(2,1)S(1)} %get-tuple-element.21), channel_id=1, source_target_pairs={{1,0},{2,1},{3,2},{0,3},{5,4},{6,5},{7,6},{4,7},{9,8},{10,9},{11,1... | collective-permute-start | bytes 61448 | tf_op jit(solution)/shard_map/ppermute | solution.py:418
  1.5 1.1 %collective-permute-start = (bf16[40,256]{1,0:T(8,128)(2,1)S(1)}, bf16[40,256]{1,0:T(8,128)(2,1)S(1)}, u32[]{:S(2)}, u32[]{:S(2)}) collective-permute-start(bf16[40,256]{1,0:T(8,128)(2,1)S(1)} %get-tuple-element.22), channel_id=1, source_target_pairs={{0,1},{1,2},{2,3},{3,0},{4,5},{5,6},{6,7},{7,4},{8,9},{9,10},{10,1... | collective-permute-start | bytes 61448 | tf_op jit(solution)/shard_map/ppermute | solution.py:417
  2.6 0.6 stack.35.meta_ref
  3.2 3.8 %weights.1 = (bf16[4,768,256]{2,1,0:T(8,128)(2,1)}, bf16[1152,256]{1,0:T(8,128)(2,1)}, f32[8,256]{1,0:T(8,128)}, bf16[368,368]{1,0:T(8,128)(2,1)}) custom-call(s32[7]{0:T(128)} %stack.35.meta_ref, s32[8]{0:T(128)} %ids_ref.1, bf16[3,3,256,256]{3,2,1,0:T(8,128)(2,1)} %we_hbm.1, bf16[3,3,128,128]{3,2,1,0:T(8,128)(2,1)} %wh_hbm.1, f32[720,128]{1,0:T(8,128)} %scale_hbm.1, ...), custom_call_target="tpu_custom_call" | custom-call | tf_op jit(solution)/shard_map/weights/pallas_call | solution.py:87
  7.0 0.0 collective-permute-done.1.east_ref
  7.0 0.0 collective-permute-done.west_ref
  7.0 0.0 copy-start
  7.0 2.0 %copy-done = bf16[40,180,256]{2,0,1:T(8,128)(2,1)S(1)} copy-done((bf16[40,180,256]{2,0,1:T(8,128)(2,1)S(1)}, bf16[40,180,256]{2,0,1:T(8,128)(2,1)}, u32[]{:S(2)}) %copy-start) | copy-done | bytes 3686424
  9.1 0.6 %slabs.1 = (bf16[3,182,256]{2,1,0:T(8,128)(2,1)S(1)}, bf16[3,182,256]{2,1,0:T(8,128)(2,1)S(1)}) custom-call(bf16[180,40,256]{2,1,0:T(8,128)(2,1)S(1)} %bitcast.24, bf16[40,256]{1,0:T(8,128)(2,1)S(1)} %collective-permute-done.west_ref, bf16[40,256]{1,0:T(8,128)(2,1)S(1)} %collective-permute-done.1.east_ref), custom_call_target="tpu_custom_call" | custom-call | tf_op jit(solution)/shard_map/slabs/pallas_call | solution.py:132
  9.7 3.1 %collective-permute-start.4 = (bf16[3,182,256]{2,1,0:T(8,128)(2,1)S(1)}, bf16[3,182,256]{2,1,0:T(8,128)(2,1)S(1)}, u32[]{:S(2)}, u32[]{:S(2)}) collective-permute-start(bf16[3,182,256]{2,1,0:T(8,128)(2,1)S(1)} %get-tuple-element.14), channel_id=1, source_target_pairs={{0,4},{4,8},{8,12},{12,16},{16,20},{20,24},{24,28},{1,5},{5,9},{9,... | collective-permute-start | bytes 838664 | tf_op jit(solution)/shard_map/ppermute | solution.py:425
  12.9 3.1 %collective-permute-start.5 = (bf16[3,182,256]{2,1,0:T(8,128)(2,1)S(1)}, bf16[3,182,256]{2,1,0:T(8,128)(2,1)S(1)}, u32[]{:S(2)}, u32[]{:S(2)}) collective-permute-start(bf16[3,182,256]{2,1,0:T(8,128)(2,1)S(1)} %get-tuple-element.15), channel_id=1, source_target_pairs={{4,0},{8,4},{12,8},{16,12},{20,16},{24,20},{28,24},{5,1},{9,5},{13... | collective-permute-start | bytes 838664 | tf_op jit(solution)/shard_map/ppermute | solution.py:426
  16.0 6.6 %encode.3 = bf16[8,90,128]{2,1,0:T(8,128)(2,1)S(1)} custom-call(s32[7]{0:T(128)S(1)} %copy-done.4, bf16[180,40,256]{2,1,0:T(8,128)(2,1)S(1)} %bitcast.25, bf16[40,256]{1,0:T(8,128)(2,1)S(1)} %collective-permute-done.west_ref, bf16[40,256]{1,0:T(8,128)(2,1)S(1)} %collective-permute-done.1.east_ref, bf16[4,768,256]{2,1,0:T(8,128)(2,1)S(1)} %copy-done.5, ...), custom_call_target="tpu_custom_call" | custom-call | flops 2264924160 | bytes 8388608 | tf_op jit(solution)/shard_map/encode/pallas_call | solution.py:259
  22.5 0.4 collective-permute-start.3
  22.9 0.9 %collective-permute-start.2 = (bf16[8,90,128]{2,1,0:T(8,128)(2,1)S(1)}, bf16[8,90,128]{2,1,0:T(8,128)(2,1)S(1)}, u32[]{:S(2)}, u32[]{:S(2)}) collective-permute-start(bf16[8,90,128]{2,1,0:T(8,128)(2,1)S(1)} %encode.3), channel_id=1, source_target_pairs={{0,2},{1,3},{2,0},{3,1},{4,6},{5,7},{6,4},{7,5},{8,10},{9,11},{10,... | collective-permute-start | bytes 552968 | tf_op jit(solution)/shard_map/ppermute | solution.py:440
  23.8 6.6 %encode.5 = bf16[8,90,128]{2,1,0:T(8,128)(2,1)S(1)} custom-call(s32[7]{0:T(128)S(1)} %copy-done.4, bf16[180,40,256]{2,1,0:T(8,128)(2,1)S(1)} %bitcast.26, bf16[40,256]{1,0:T(8,128)(2,1)S(1)} %collective-permute-done.west_ref, bf16[40,256]{1,0:T(8,128)(2,1)S(1)} %collective-permute-done.1.east_ref, bf16[4,768,256]{2,1,0:T(8,128)(2,1)S(1)} %copy-done.5, ...), custom_call_target="tpu_custom_call" | custom-call | flops 2264924160 | bytes 8388608 | tf_op jit(solution)/shard_map/encode/pallas_call | solution.py:259
  30.4 0.8 %collective-permute-start.8 = (bf16[8,90,128]{2,1,0:T(8,128)(2,1)S(1)}, bf16[8,90,128]{2,1,0:T(8,128)(2,1)S(1)}, u32[]{:S(2)}, u32[]{:S(2)}) collective-permute-start(bf16[8,90,128]{2,1,0:T(8,128)(2,1)S(1)} %encode.5), channel_id=1, source_target_pairs={{0,1},{1,0},{2,3},{3,2},{4,5},{5,4},{6,7},{7,6},{8,9},{9,8},{10,11... | collective-permute-start | bytes 552968 | tf_op jit(solution)/shard_map/ppermute | solution.py:441
  31.2 0.0 collective-permute-done.4.refs_0_
  31.2 0.3 collective-permute-start.7
  31.5 0.0 collective-permute-done.5.refs_1_
  31.5 9.6 %encode.4 = bf16[6,90,128]{2,1,0:T(8,128)(2,1)S(1)} custom-call(s32[7]{0:T(128)S(1)} %copy-done.4, bf16[180,40,256]{2,1,0:T(8,128)(2,1)S(1)} %bitcast.27, bf16[40,256]{1,0:T(8,128)(2,1)S(1)} %collective-permute-done.west_ref, bf16[40,256]{1,0:T(8,128)(2,1)S(1)} %collective-permute-done.1.east_ref, bf16[3,182,256]{2,1,0:T(8,128)(2,1)S(1)} %collective-permute-done.4.refs_0_, ...), custom_call_target="tpu_custom_call" | custom-call | flops 2264924160 | bytes 8388608 | tf_op jit(solution)/shard_map/encode/pallas_call | solution.py:259
  41.2 0.4 collective-permute-start.6
  41.6 0.0 collective-permute-done.7
  41.6 0.1 collective-permute-start.9
  41.8 1.4 %collective-permute-start.12 = (bf16[6,90,128]{2,1,0:T(8,128)(2,1)S(1)}, bf16[6,90,128]{2,1,0:T(8,128)(2,1)S(1)}, u32[]{:S(2)}, u32[]{:S(2)}) collective-permute-start(bf16[6,90,128]{2,1,0:T(8,128)(2,1)S(1)} %encode.4), channel_id=1, source_target_pairs={{0,3},{1,2},{2,1},{3,0},{4,7},{5,6},{6,5},{7,4},{8,11},{9,10},{10,... | collective-permute-start | bytes 414728 | tf_op jit(solution)/shard_map/ppermute | solution.py:443
  43.1 0.2 collective-permute-start.11
  43.3 0.0 collective-permute-done.8
  43.3 0.3 collective-permute-start.10
  43.7 9.0 %heads.2.refs_15_ = bf16[2,20,360,128]{3,2,1,0:T(8,128)(2,1)} custom-call(s32[7]{0:T(128)S(1)} %copy-done.4, bf16[1,8,90,128]{3,2,1,0:T(8,128)(2,1)S(1)} %bitcast.28, bf16[1,8,90,128]{3,2,1,0:T(8,128)(2,1)S(1)} %bitcast.32, bf16[1,8,90,128]{3,2,1,0:T(8,128)(2,1)S(1)} %bitcast.30, bf16[1,8,90,128]{3,2,1,0:T(8,128)(2,1)S(1)} %bitcast.40, ...), custom_call_target="tpu_custom_call" | custom-call | flops 3344302080 | bytes 25165824 | tf_op jit(solution)/shard_map/heads/pallas_call | solution.py:370
  52.6 0.0 collective-permute-done.12
  52.6 0.0 collective-permute-done.11
  52.7 6.9 %heads.3 = bf16[2,20,360,128]{3,2,1,0:T(8,128)(2,1)} custom-call(s32[7]{0:T(128)S(1)} %copy-done.4, bf16[1,8,90,128]{3,2,1,0:T(8,128)(2,1)S(1)} %bitcast.29, bf16[1,8,90,128]{3,2,1,0:T(8,128)(2,1)S(1)} %bitcast.33, bf16[1,8,90,128]{3,2,1,0:T(8,128)(2,1)S(1)} %bitcast.31, bf16[1,8,90,128]{3,2,1,0:T(8,128)(2,1)S(1)} %bitcast.41, ...), custom_call_target="tpu_custom_call", output_to_operand_aliasing={{}: (16, {})} | custom-call | flops 2229534720 | bytes 16777216 | tf_op jit(solution)/shard_map/heads/pallas_call | solution.py:370
  (17 shorter events, 0.0 us)
Async XLA Ops:
  0.0 15.9 %copy-start.6 = (bf16[256,128]{1,0:T(8,128)(2,1)S(1)}, bf16[256,128]{1,0:T(8,128)(2,1)}, u32[]{:S(2)}) copy-start(bf16[256,128]{1,0:T(8,128)(2,1)} %refs_1_.3) | copy-start | bytes 196612
  0.8 6.2 %collective-permute-start.1 = (bf16[40,256]{1,0:T(8,128)(2,1)S(1)}, bf16[40,256]{1,0:T(8,128)(2,1)S(1)}, u32[]{:S(2)}, u32[]{:S(2)}) collective-permute-start(bf16[40,256]{1,0:T(8,128)(2,1)S(1)} %get-tuple-element.21), channel_id=1, source_target_pairs={{1,0},{2,1},{3,2},{0,3},{5,4},{6,5},{7,6},{4,7},{9,8},{10,9},{11,1... | collective-permute-start | bytes 61448 | tf_op jit(solution)/shard_map/ppermute | solution.py:418
  1.5 5.5 %collective-permute-start = (bf16[40,256]{1,0:T(8,128)(2,1)S(1)}, bf16[40,256]{1,0:T(8,128)(2,1)S(1)}, u32[]{:S(2)}, u32[]{:S(2)}) collective-permute-start(bf16[40,256]{1,0:T(8,128)(2,1)S(1)} %get-tuple-element.22), channel_id=1, source_target_pairs={{0,1},{1,2},{2,3},{3,0},{4,5},{5,6},{6,7},{7,4},{8,9},{9,10},{10,1... | collective-permute-start | bytes 61448 | tf_op jit(solution)/shard_map/ppermute | solution.py:417
  3.1 12.8 %copy-start.4 = (s32[7]{0:T(128)S(1)}, s32[7]{0:T(128)}, u32[]{:S(2)}) copy-start(s32[7]{0:T(128)} %stack.35.meta_ref) | copy-start | bytes 88
  7.0 2.0 %copy-start = (bf16[40,180,256]{2,0,1:T(8,128)(2,1)S(1)}, bf16[40,180,256]{2,0,1:T(8,128)(2,1)}, u32[]{:S(2)}) copy-start(bf16[40,180,256]{2,0,1:T(8,128)(2,1)} %param.8) | copy-start | bytes 11059204
  9.1 6.9 %copy-start.5 = (bf16[4,768,256]{2,1,0:T(8,128)(2,1)S(1)}, bf16[4,768,256]{2,1,0:T(8,128)(2,1)}, u32[]{:S(2)}) copy-start(bf16[4,768,256]{2,1,0:T(8,128)(2,1)} %get-tuple-element.13.refs_0_.refs_2_) | copy-start | bytes 4718596
  9.7 21.5 %collective-permute-start.4 = (bf16[3,182,256]{2,1,0:T(8,128)(2,1)S(1)}, bf16[3,182,256]{2,1,0:T(8,128)(2,1)S(1)}, u32[]{:S(2)}, u32[]{:S(2)}) collective-permute-start(bf16[3,182,256]{2,1,0:T(8,128)(2,1)S(1)} %get-tuple-element.14), channel_id=1, source_target_pairs={{0,4},{4,8},{8,12},{12,16},{16,20},{20,24},{24,28},{1,5},{5,9},{9,... | collective-permute-start | bytes 838664 | tf_op jit(solution)/shard_map/ppermute | solution.py:425
  12.9 18.7 %collective-permute-start.5 = (bf16[3,182,256]{2,1,0:T(8,128)(2,1)S(1)}, bf16[3,182,256]{2,1,0:T(8,128)(2,1)S(1)}, u32[]{:S(2)}, u32[]{:S(2)}) collective-permute-start(bf16[3,182,256]{2,1,0:T(8,128)(2,1)S(1)} %get-tuple-element.15), channel_id=1, source_target_pairs={{4,0},{8,4},{12,8},{16,12},{20,16},{24,20},{28,24},{5,1},{9,5},{13... | collective-permute-start | bytes 838664 | tf_op jit(solution)/shard_map/ppermute | solution.py:426
  22.5 20.6 %collective-permute-start.3 = (bf16[8,90,128]{2,1,0:T(8,128)(2,1)S(1)}, bf16[8,90,128]{2,1,0:T(8,128)(2,1)S(1)}, u32[]{:S(2)}, u32[]{:S(2)}) collective-permute-start(bf16[8,90,128]{2,1,0:T(8,128)(2,1)S(1)} %encode.3), channel_id=1, source_target_pairs={{0,1},{1,0},{2,3},{3,2},{4,5},{5,4},{6,7},{7,6},{8,9},{9,8},{10,11... | collective-permute-start | bytes 552968 | tf_op jit(solution)/shard_map/ppermute | solution.py:441
  22.9 18.2 %collective-permute-start.2 = (bf16[8,90,128]{2,1,0:T(8,128)(2,1)S(1)}, bf16[8,90,128]{2,1,0:T(8,128)(2,1)S(1)}, u32[]{:S(2)}, u32[]{:S(2)}) collective-permute-start(bf16[8,90,128]{2,1,0:T(8,128)(2,1)S(1)} %encode.3), channel_id=1, source_target_pairs={{0,2},{1,3},{2,0},{3,1},{4,6},{5,7},{6,4},{7,5},{8,10},{9,11},{10,... | collective-permute-start | bytes 552968 | tf_op jit(solution)/shard_map/ppermute | solution.py:440
  30.4 13.3 %copy-start.1 = (bf16[1152,256]{1,0:T(8,128)(2,1)S(1)}, bf16[1152,256]{1,0:T(8,128)(2,1)}, u32[]{:S(2)}) copy-start(bf16[1152,256]{1,0:T(8,128)(2,1)} %get-tuple-element.18.refs_8_.refs_12_) | copy-start | bytes 1769476
  30.4 13.3 %copy-start.2 = (bf16[368,368]{1,0:T(8,128)(2,1)S(1)}, bf16[368,368]{1,0:T(8,128)(2,1)}, u32[]{:S(2)}) copy-start(bf16[368,368]{1,0:T(8,128)(2,1)} %get-tuple-element.20.refs_10_.refs_14_) | copy-start | bytes 812548
  30.4 13.3 %copy-start.3 = (f32[8,256]{1,0:T(8,128)S(1)}, f32[8,256]{1,0:T(8,128)}, u32[]{:S(2)}) copy-start(f32[8,256]{1,0:T(8,128)} %get-tuple-element.19.refs_9_.refs_13_) | copy-start | bytes 24580
  30.4 12.9 %collective-permute-start.8 = (bf16[8,90,128]{2,1,0:T(8,128)(2,1)S(1)}, bf16[8,90,128]{2,1,0:T(8,128)(2,1)S(1)}, u32[]{:S(2)}, u32[]{:S(2)}) collective-permute-start(bf16[8,90,128]{2,1,0:T(8,128)(2,1)S(1)} %encode.5), channel_id=1, source_target_pairs={{0,1},{1,0},{2,3},{3,2},{4,5},{5,4},{6,7},{7,6},{8,9},{9,8},{10,11... | collective-permute-start | bytes 552968 | tf_op jit(solution)/shard_map/ppermute | solution.py:441
  31.2 10.4 %collective-permute-start.7 = (bf16[8,90,128]{2,1,0:T(8,128)(2,1)S(1)}, bf16[8,90,128]{2,1,0:T(8,128)(2,1)S(1)}, u32[]{:S(2)}, u32[]{:S(2)}) collective-permute-start(bf16[8,90,128]{2,1,0:T(8,128)(2,1)S(1)} %encode.5), channel_id=1, source_target_pairs={{0,2},{1,3},{2,0},{3,1},{4,6},{5,7},{6,4},{7,5},{8,10},{9,11},{10,... | collective-permute-start | bytes 552968 | tf_op jit(solution)/shard_map/ppermute | solution.py:440
  41.2 2.5 %collective-permute-start.6 = (bf16[8,90,128]{2,1,0:T(8,128)(2,1)S(1)}, bf16[8,90,128]{2,1,0:T(8,128)(2,1)S(1)}, u32[]{:S(2)}, u32[]{:S(2)}) collective-permute-start(bf16[8,90,128]{2,1,0:T(8,128)(2,1)S(1)} %collective-permute-done.2), channel_id=1, source_target_pairs={{0,1},{1,0},{2,3},{3,2},{4,5},{5,4},{6,7},{7,6},{8,9},{9,8},{10,11... | collective-permute-start | bytes 552968 | tf_op jit(solution)/shard_map/ppermute | solution.py:446
  41.6 2.0 %collective-permute-start.9 = (bf16[8,90,128]{2,1,0:T(8,128)(2,1)S(1)}, bf16[8,90,128]{2,1,0:T(8,128)(2,1)S(1)}, u32[]{:S(2)}, u32[]{:S(2)}) collective-permute-start(bf16[8,90,128]{2,1,0:T(8,128)(2,1)S(1)} %collective-permute-done.7), channel_id=1, source_target_pairs={{0,1},{1,0},{2,3},{3,2},{4,5},{5,4},{6,7},{7,6},{8,9},{9,8},{10,11... | collective-permute-start | bytes 552968 | tf_op jit(solution)/shard_map/ppermute | solution.py:446
  41.8 10.9 %collective-permute-start.12 = (bf16[6,90,128]{2,1,0:T(8,128)(2,1)S(1)}, bf16[6,90,128]{2,1,0:T(8,128)(2,1)S(1)}, u32[]{:S(2)}, u32[]{:S(2)}) collective-permute-start(bf16[6,90,128]{2,1,0:T(8,128)(2,1)S(1)} %encode.4), channel_id=1, source_target_pairs={{0,3},{1,2},{2,1},{3,0},{4,7},{5,6},{6,5},{7,4},{8,11},{9,10},{10,... | collective-permute-start | bytes 414728 | tf_op jit(solution)/shard_map/ppermute | solution.py:443
  43.1 9.5 %collective-permute-start.11 = (bf16[6,90,128]{2,1,0:T(8,128)(2,1)S(1)}, bf16[6,90,128]{2,1,0:T(8,128)(2,1)S(1)}, u32[]{:S(2)}, u32[]{:S(2)}) collective-permute-start(bf16[6,90,128]{2,1,0:T(8,128)(2,1)S(1)} %encode.4), channel_id=1, source_target_pairs={{0,1},{1,0},{2,3},{3,2},{4,5},{5,4},{6,7},{7,6},{8,9},{9,8},{10,11... | collective-permute-start | bytes 414728 | tf_op jit(solution)/shard_map/ppermute | solution.py:441
  43.3 9.3 %collective-permute-start.10 = (bf16[6,90,128]{2,1,0:T(8,128)(2,1)S(1)}, bf16[6,90,128]{2,1,0:T(8,128)(2,1)S(1)}, u32[]{:S(2)}, u32[]{:S(2)}) collective-permute-start(bf16[6,90,128]{2,1,0:T(8,128)(2,1)S(1)} %encode.4), channel_id=1, source_target_pairs={{0,2},{1,3},{2,0},{3,1},{4,6},{5,7},{6,4},{7,5},{8,10},{9,11},{10,... | collective-permute-start | bytes 414728 | tf_op jit(solution)/shard_map/ppermute | solution.py:440

commit v6 on v5

--- a/solution.py
+++ b/solution.py
@@ -106,20 +106,17 @@
     )(meta, ids, w_enc, w_head, scale, shift, z)
 
 
-def slabs_kernel(x_ref, west_ref, east_ref, up_ref, dn_ref, edge, flat, sem):
-    xcols, rows, ch = x_ref.shape
+def slabs_kernel(first_ref, last_ref, west_ref, east_ref, up_ref, dn_ref, flat):
+    xcols, _, ch = first_ref.shape
+    rows = west_ref.shape[0]
     reach = up_ref.shape[0]
-    copies = [
-        pltpu.make_async_copy(x_ref.at[:, a : a + 8], edge.at[k], sem.at[k]) for k, a in enumerate((0, rows - 8))
-    ]
-    for c in copies:
-        c.start()
-    for k, (slab, start, r) in enumerate(((dn_ref, 0, 0), (up_ref, 8 - reach, rows - reach))):
-        copies[k].wait()
+    for k, (edge, slab, start, r) in enumerate(
+        ((first_ref, dn_ref, 0, 0), (last_ref, up_ref, 8 - reach, rows - reach))
+    ):
         parts = []
         for j in range(ch // 128):
             lanes = slice(j * 128, (j + 1) * 128)
-            flat[k, j] = edge[k, :, :, lanes].astype(F32).reshape(xcols * 8, 128)
+            flat[k, j] = edge[:, :, lanes].astype(F32).reshape(xcols * 8, 128)
             parts.append([flat[k, j, pl.ds(start + i, xcols, stride=8), :] for i in range(reach)])
         for i in range(reach):
             row = jnp.concatenate([p[i] for p in parts], axis=1).astype(BF)
@@ -127,77 +124,62 @@
 
 
 def row_slabs(x, west, east, reach):
-    xcols, _, ch = x.shape
+    xcols, rows, ch = x.shape
     vmem = pl.BlockSpec(memory_space=pltpu.VMEM)
     return pl.pallas_call(
         slabs_kernel,
-        in_specs=[pl.BlockSpec(memory_space=pltpu.HBM), vmem, vmem],
+        in_specs=[vmem] * 4,
         out_specs=[vmem] * 2,
         out_shape=[jax.ShapeDtypeStruct((reach, xcols + 2, ch), BF)] * 2,
-        scratch_shapes=[
-            pltpu.VMEM((2, xcols, 8, ch), BF),
-            pltpu.VMEM((2, ch // 128, xcols * 8, 128), F32),
-            pltpu.SemaphoreType.DMA((2,)),
-        ],
-        compiler_params=params(48),
+        scratch_shapes=[pltpu.VMEM((2, ch // 128, xcols * 8, 128), F32)],
+        compiler_params=params(16),
         name="slabs",
-    )(x, west, east)
+    )(x[:, :8], x[:, rows - 8 :], west, east)
 
 
 def encoder_kernel(
     meta_ref, x_ref, west_ref, east_ref, *refs, first, group
 ):
     halos, refs = (refs[:2], refs[2:]) if first is None else ((), refs)
-    g_ref, wp_ref, out_ref, xs, xr, ys, st, pt, sem = refs[:9]
+    g_ref, wp_ref, out_ref, xs, ys, st, pt = refs[:7]
     cols, rows, ch = x_ref.shape
     reach = 2 * EDGE - 1
-    starts = (0, rows - 8) if first is None else ((first - 1) // 8 * 8,)
-    tall = xr.shape[2]
-    block = next(n for n in range(32, 0, -1) if (cols + 2) % n == 0)
-    copies = []
-    for p in range(0, cols, block):
-        to = min(p + block, cols)
-        for i, a in enumerate(starts):
-            copies.append(
-                pltpu.make_async_copy(
-                    x_ref.at[p:to, a : a + tall], xr.at[i, p + 1 : to + 1], sem.at[i, p // block]
-                )
-            )
-            copies[-1].start()
-    for i, a in enumerate(starts):
-        xr[i, 0] = west_ref[a : a + tall, :]
-        xr[i, cols + 1] = east_ref[a : a + tall, :]
     if first is None:
-        hf = refs[9]
+        hf = refs[7]
         for k, halo in enumerate(halos):
             for j in range(ch // 128):
                 lanes = slice(j * 128, (j + 1) * 128)
                 for i in range(reach):
                     at = 8 - reach + i if k == 0 else i
                     hf[k, j, pl.ds(at, cols + 2, stride=8), :] = halo[i, :, lanes].astype(F32)
-    for a in range(0, cols + 2, block):
-        at = slice(a, a + block)
-        for c in copies[: len(starts)]:
-            c.wait()
-        copies = copies[len(starts) :]
+    low = 0 if first is None else (first - 1) // 8 * 8
+
+    def stage(at, tile_rows):
         if first is None:
             far = []
             for k in range(2):
-                h = [hf[k, j, a * 8 : (a + block) * 8].astype(BF).reshape(block, 8, 128) for j in range(ch // 128)]
+                h = [hf[k, j, at.start * 8 : at.stop * 8] for j in range(ch // 128)]
+                h = [v.astype(BF).reshape(at.stop - at.start, 8, 128) for v in h]
                 far.append(jnp.concatenate(h, axis=2))
-            top = jnp.concatenate([far[0], xr[0, at]], axis=1)
-            low = jnp.concatenate([xr[1, at], far[1]], axis=1)
-            pad = jnp.zeros((block, 16 - 4 * (EDGE + 1), ch), BF)
+            top = jnp.concatenate([far[0], tile_rows(0, 8)], axis=1)
+            end = jnp.concatenate([tile_rows(rows - 8, 8), far[1]], axis=1)
+            pad = jnp.zeros((at.stop - at.start, 16 - 4 * (EDGE + 1), ch), BF)
             n = 2 * (EDGE + 1)
             for dr in range(3):
                 t = top[:, 8 - reach + dr : 8 - reach + dr + n]
-                b = low[:, 8 - reach - 2 + dr : 8 - reach - 2 + dr + n]
+                b = end[:, 8 - reach - 2 + dr : 8 - reach - 2 + dr + n]
                 xs[at, :, dr * ch : (dr + 1) * ch] = jnp.concatenate([t, b, pad], axis=1)
         else:
-            rows_here = xr[0, at]
+            here = tile_rows(low, 24)
             for dr in range(3):
-                off = first - 1 - starts[0] + dr
-                xs[at, :, dr * ch : (dr + 1) * ch] = rows_here[:, off : off + 16]
+                off = first - 1 - low + dr
+                xs[at, :, dr * ch : (dr + 1) * ch] = here[:, off : off + 16]
+
+    stage(slice(0, 1), lambda a, n: west_ref[a : a + n, :].reshape(1, n, ch))
+    stage(slice(cols + 1, cols + 2), lambda a, n: east_ref[a : a + n, :].reshape(1, n, ch))
+    block = next(n for n in range(32, 0, -1) if cols % n == 0)
+    for c in range(0, cols, block):
+        stage(slice(c + 1, c + 1 + block), lambda a, n: x_ref[c : c + block, a : a + n, :])
 
     pairs = cols // 2
 
@@ -241,16 +223,12 @@
 def encode(meta, x, west, east, halos, g, wp, first, count, group):
     cols, rows, ch = x.shape
     head = wp.shape[1]
-    blocks = 1 if halos is None else 2
-    tall = 24 if halos is None else 8
     vmem = pl.BlockSpec(memory_space=pltpu.VMEM)
     scratch = [
         pltpu.VMEM((cols + 2, 16, 3 * ch), BF),
-        pltpu.VMEM((blocks, cols + 2, tall, ch), BF),
         pltpu.VMEM((2, 4, group * 16, ch), F32),
         pltpu.VMEM((ch // 128, group * 16, 128), F32),
         pltpu.VMEM((cols // 2 * 8, head), F32),
-        pltpu.SemaphoreType.DMA((blocks, cols)),
     ]
     if halos is not None:
         scratch.append(pltpu.VMEM((2, ch // 128, (cols + 2) * 8, 128), F32))
@@ -258,8 +236,7 @@
     flops = 2 * cols * 16 * 6 * ch * ch
     return pl.pallas_call(
         functools.partial(encoder_kernel, first=first, group=group),
-        in_specs=[pl.BlockSpec(memory_space=pltpu.SMEM), pl.BlockSpec(memory_space=pltpu.HBM)]
-        + [vmem] * (len(operands) - 2),
+        in_specs=[pl.BlockSpec(memory_space=pltpu.SMEM)] + [vmem] * (len(operands) - 1),
         out_specs=vmem,
         out_shape=jax.ShapeDtypeStruct((count, cols // 2, head), BF),
         scratch_shapes=scratch,
@@ -269,30 +246,31 @@
     )(*operands)
 
 
-def head_kernel(meta_ref, *refs, moves, blocks, shards, aliased):
-    sources = refs[: len(moves)]
-    ws_ref, vec_ref, zs_ref = refs[len(moves) : len(moves) + 3]
-    out_ref, band, ps, cs, outs, sem, out_sem = refs[len(moves) + 3 + aliased :]
+def head_kernel(meta_ref, *refs, chunks, blocks, shards, aliased):
+    arrays = refs[: sum(n for n, _ in chunks)]
+    ws_ref, vec_ref, zs_ref = refs[len(arrays) : len(arrays) + 3]
+    out_ref, ps, cs, outs, out_sem = refs[len(arrays) + 3 + aliased :]
     ch = ps.shape[2] // 3
     wide = ps.shape[1]
     leads, rows, cols, _ = out_ref.shape
-
-    copies = []
-    for source, (slot, pieces) in zip(sources, moves):
-        for a, b, to in pieces:
-            copies.append(
-                pltpu.make_async_copy(
-                    source.at[:, a:b],
-                    band.at[pl.ds(meta_ref[slot], source.shape[0]), to : to + b - a],
-                    sem.at[len(copies)],
-                )
-            )
-    for c in copies:
-        c.start()
+    odd = meta_ref[2] % 2 == 1
+    high = meta_ref[2] // 2 == 1
     if wide > cols:
         ps[:, cols:, :] = jnp.zeros((ps.shape[0], wide - cols, 3 * ch), BF)
-    for c in copies:
-        c.wait()
+
+    def pieces(r):
+        taken = 0
+        for count, at in chunks:
+            if r in at:
+                mine = arrays[taken : taken + count]
+                if count == 1:
+                    return [mine[0][s, at[r]] for s in range(shards)]
+                own, beside, across, both = [a[at[r]] for a in mine]
+                here = [jnp.where(odd, beside, own), jnp.where(odd, own, beside)]
+                there = [jnp.where(odd, both, across), jnp.where(odd, across, both)]
+                lower = [jnp.where(high, t, h) for h, t in zip(here, there)]
+                return lower + [jnp.where(high, h, t) for h, t in zip(here, there)]
+            taken += count
 
     bias = vec_ref[BIAS : BIAS + 1, :] + vec_ref[BIAS + 1 : BIAS + 2, :] + vec_ref[BIAS + 2 : BIAS + 3, :]
     first = (meta_ref[0] == 1).astype(F32) * vec_ref[BIAS : BIAS + 1, :]
@@ -308,7 +286,7 @@
                 continue
             staged.add(r)
             k = slots[r]
-            row = jnp.concatenate([band[s, r] for s in range(shards)], axis=0)
+            row = jnp.concatenate(pieces(r), axis=0)
             ps[k, :cols, ch : 2 * ch] = row
             ps[k, :cols, :ch] = jnp.concatenate([row[-1:], row[:-1]], axis=0)
             ps[k, :cols, 2 * ch :] = jnp.concatenate([row[1:], row[:1]], axis=0)
@@ -353,31 +331,28 @@
         c.wait()
 
 
-def forecast_heads(meta, sources, moves, ws, vec, zs, so_far, blocks, shape):
+def forecast_heads(meta, arrays, chunks, ws, vec, zs, so_far, blocks, shape):
     leads, rows, cols, ch = shape
-    shards = cols // sources[0].shape[2]
+    shards = cols // arrays[0].shape[-2]
     wide = zs.shape[0]
     vmem = pl.BlockSpec(memory_space=pltpu.VMEM)
-    anywhere = pl.BlockSpec(memory_space=pl.ANY)
     staged = len({n * STEP + i for n in blocks for i in range(STEP + 2)})
-    operands = [meta, *sources, ws, vec, zs]
-    in_specs = [pl.BlockSpec(memory_space=pltpu.SMEM)] + [anywhere] * len(sources) + [vmem] * 3
+    operands = [meta, *arrays, ws, vec, zs]
+    in_specs = [pl.BlockSpec(memory_space=pltpu.SMEM)] + [vmem] * (len(operands) - 1)
     alias = {}
     if so_far is not None:
         alias = {len(operands): 0}
         operands.append(so_far)
         in_specs.append(pl.BlockSpec(memory_space=pltpu.HBM))
     return pl.pallas_call(
-        functools.partial(head_kernel, moves=moves, blocks=blocks, shards=shards, aliased=len(alias)),
+        functools.partial(head_kernel, chunks=chunks, blocks=blocks, shards=shards, aliased=len(alias)),
         in_specs=in_specs,
         out_specs=pl.BlockSpec(memory_space=pltpu.HBM),
         out_shape=jax.ShapeDtypeStruct(shape, BF),
         scratch_shapes=[
-            pltpu.VMEM((shards, rows + 2, cols // shards, ch), BF),
             pltpu.VMEM((staged, wide, 3 * ch), BF),
             pltpu.VMEM((2, STEP * wide, leads * ch), F32),
             pltpu.VMEM((len(blocks), leads, STEP, cols, ch), BF),
-            pltpu.SemaphoreType.DMA((sum(len(m[1]) for m in moves),)),
             pltpu.SemaphoreType.DMA((len(blocks), leads)),
         ],
         input_output_aliases=alias,
@@ -418,7 +393,7 @@
     east = lax.ppermute(tile[0], "lon", lon_dn)
 
     meta = jnp.stack(
-        [lat_at == 0, lat_at == lat - 1, lon_at, lon_at ^ 2, lon_at ^ 1, lon_at ^ 3, 0]
+        [lat_at == 0, lat_at == lat - 1, lon_at]
     ).astype(jnp.int32)
     g, ws, vec, zs = prepare(meta, lead_ids, w_enc, w_head, film_scale, film_shift, zonal_mix, leads)
     up, dn = row_slabs(tile, west, east, reach)
@@ -444,32 +419,25 @@
             else:
                 ready, _ = lax.optimization_barrier((across, proj[2]))
                 both = lax.ppermute(ready, "lon", swap(lon, 1))
-            sent.append([(2, own[None]), (3, across[None]), (4, beside[None]), (5, both[None])])
+            sent.append([own, beside, across, both])
         else:
-            sent.append([(6, lax.all_gather(own, "lon", axis=0, tiled=False))])
-
-    def sources(ranges):
-        arrays, moves = [], []
-        for group, pieces in zip(sent, ranges):
-            for slot, a in group if pieces else ():
-                arrays.append(a)
-                moves.append((slot, pieces))
-        return arrays, moves
+            sent.append([lax.all_gather(own, "lon", axis=0, tiled=False)])
 
     shape = (leads, band_rows, cols // 2 * lon, head)
     upper, lower = middle - EDGE, band_rows - EDGE - middle
     blocks = band_rows // STEP
-    arrays, moves = sources([[(0, upper, EDGE + 1)], [(0, lower, middle + 1)], []])
-    out = forecast_heads(meta, arrays, moves, ws, vec, zs, None, list(range(1, blocks - 1)), shape)
-    keep = STEP + 1 - EDGE
-    arrays, moves = sources(
-        [
-            [(0, keep, EDGE + 1)],
-            [(lower - keep, lower, band_rows - EDGE + 1 - keep)],
-            [(0, EDGE + 1, 0), (EDGE + 1, 2 * EDGE + 2, band_rows + 1 - EDGE)],
-        ]
+    at = [
+        {EDGE + 1 + r: r for r in range(upper)},
+        {middle + 1 + r: r for r in range(lower)},
+        {(r if r <= EDGE else band_rows - EDGE - EDGE - 1 + r + 1): r for r in range(2 * EDGE + 2)},
+    ]
+    chunks = [(len(a), rows_at) for a, rows_at in zip(sent, at)]
+    inner = forecast_heads(
+        meta, sent[0] + sent[1], chunks[:2], ws, vec, zs, None, list(range(1, blocks - 1)), shape
     )
-    return forecast_heads(meta, arrays, moves, ws, vec, zs, out, [0, blocks - 1], shape)
+    return forecast_heads(
+        meta, sent[0] + sent[1] + sent[2], chunks, ws, vec, zs, inner, [0, blocks - 1], shape
+    )
 
 
 def solution(mesh):

time: 60 us -> 51.1 us (0.85)
  Pallas kernels: 43.1 us -> 29.9 us
  local copies, waits for them, and re-layouts: 3.43 us -> 5.69 us
  starting transfers between devices: 12.8 us -> 14 us
  other arithmetic: 0 us -> 0.67 us
    pallas_call x3, Pallas kernels: 22.7 us -> 13.2 us  [encode(): pl.pallas_call(functools.partial(encoder_kernel, first=first, group=group...]
    pallas_call x3, Pallas kernels: 16.5 us -> 12.8 us  [the longest x2 12.3 us: forecast_heads(): pl.pallas_call(functools.partial(head_kernel, chunks=chunks, blocks=block...]
    slice x0 -> x1, local copies, waits for them, and re-layouts: none -> 1.45 us  [row_slabs(): x[:, rows - 8:]]
    unnamed x14, local copies, waits for them, and re-layouts: 2.06 us -> 3.47 us
    ppermute x3, starting transfers between devices: 1.54 us -> 2.75 us  [shards(): across = lax.ppermute(own, 'lon', swap(lon, 2))]
    ppermute x1, starting transfers between devices: 1.37 us -> 0.57 us  [shards(): both = lax.ppermute(own, 'lon', swap(lon, 3))]
    ppermute x2, starting transfers between devices: 0.58 us -> 1.33 us  [shards(): both = lax.ppermute(ready, 'lon', swap(lon, 1))]
    another operation x0 -> x1, other arithmetic: none -> 0.67 us  [shards(): meta = jnp.stack([lat_at == 0, lat_at == lat - 1, lon_at]).astype(jnp.int32)]
  transfers between devices with their start and end apart: 13 -> 13, of which waited for: 0 -> 1; matrix products, arithmetic and copies ran while one was open for 1% -> 4% of each run, Pallas kernels for 60% -> 47%
where the time goes in v6:
time: 51.1 us; the launch traced here: 50.8 us
  Pallas kernels  29.9 us (59%)
  starting transfers between devices  14 us (27%)
  local copies, waits for them, and re-layouts  5.69 us (11%)
  other arithmetic  0.67 us (1%)
    pallas_call x3, Pallas kernels, encode(): pl.pallas_call(functools.partial(encoder_kernel, first=first, group=group...  13.2 us
    pallas_call x2, Pallas kernels, forecast_heads(): pl.pallas_call(functools.partial(head_kernel, chunks=chunks, blocks=block...  12.3 us
    pallas_call x1, Pallas kernels, prepare(): pl.pallas_call(weights_kernel, in_specs=[smem, smem] + [hbm] * 5, out_spe...  3.83 us
    unnamed x14, local copies, waits for them, and re-layouts  3.47 us
    ppermute x1, starting transfers between devices, shards(): above = lax.ppermute(up, 'lat', lat_up)  3.15 us
    ppermute x1, starting transfers between devices, shards(): below = lax.ppermute(dn, 'lat', lat_dn)  3.07 us
    ppermute x3, starting transfers between devices, shards(): across = lax.ppermute(own, 'lon', swap(lon, 2))  2.75 us
    slice x1, local copies, waits for them, and re-layouts, row_slabs(): x[:, rows - 8:]  1.45 us
  transfers between devices with their start and end apart: 13, of which 1 were waited for; matrix products, arithmetic and copies ran while one was open for 4% of the time, Pallas kernels for 47%

profile of v6, /device:TPU:25, one launch (start us, length us, event | category | flops | bytes accessed | tf_op | source)
XLA Modules:
  0.0 50.8 jit_solution(18314056330594005909)
XLA Ops:
  0.0 0.8 %slice_bitcast_fusion = (bf16[40,256]{1,0:T(8,128)(2,1)S(1)}, bf16[40,256]{1,0:T(8,128)(2,1)S(1)}) fusion(bf16[180,40,256]{2,1,0:T(8,128)(2,1)} %bitcast.8), kind=kLoop, calls=%fused_computation | loop fusion | bytes 81920 | tf_op jit(solution)/shard_map/squeeze | solution.py:393
  0.8 0.7 %collective-permute-start.1 = (bf16[40,256]{1,0:T(8,128)(2,1)S(1)}, bf16[40,256]{1,0:T(8,128)(2,1)S(1)}, u32[]{:S(2)}, u32[]{:S(2)}) collective-permute-start(bf16[40,256]{1,0:T(8,128)(2,1)S(1)} %get-tuple-element.23), channel_id=1, source_target_pairs={{1,0},{2,1},{3,2},{0,3},{5,4},{6,5},{7,6},{4,7},{9,8},{10,9},{11,1... | collective-permute-start | bytes 61448 | tf_op jit(solution)/shard_map/ppermute | solution.py:393
  1.5 1.1 %collective-permute-start = (bf16[40,256]{1,0:T(8,128)(2,1)S(1)}, bf16[40,256]{1,0:T(8,128)(2,1)S(1)}, u32[]{:S(2)}, u32[]{:S(2)}) collective-permute-start(bf16[40,256]{1,0:T(8,128)(2,1)S(1)} %get-tuple-element.24), channel_id=1, source_target_pairs={{0,1},{1,2},{2,3},{3,0},{4,5},{5,6},{6,7},{7,4},{8,9},{9,10},{10,1... | collective-permute-start | bytes 61448 | tf_op jit(solution)/shard_map/ppermute | solution.py:392
  2.6 1.4 %fusion = (bf16[180,8,256]{2,1,0:T(8,128)(2,1)S(1)}, bf16[180,8,256]{2,1,0:T(8,128)(2,1)S(1)}) fusion(bf16[180,40,256]{2,1,0:T(8,128)(2,1)} %bitcast.9), kind=kLoop, calls=%fused_computation.3 | loop fusion | bytes 2949120 | tf_op jit(solution)/shard_map/slice | solution.py:137
  4.0 0.7 %pad_add_fusion.meta_ref = s32[3]{0:T(128)} fusion(s32[1]{0:T(128)} %bitcast.2, s32[1]{0:T(128)} %bitcast.1, s32[1]{0:T(128)} %bitcast), kind=kLoop, calls=%fused_computation.2 | loop fusion | flops 6 | bytes 24 | tf_op jit(solution)/shard_map/stack | solution.py:395
  4.7 3.8 %weights.1 = (bf16[4,768,256]{2,1,0:T(8,128)(2,1)}, bf16[1152,256]{1,0:T(8,128)(2,1)}, f32[8,256]{1,0:T(8,128)}, bf16[368,368]{1,0:T(8,128)(2,1)}) custom-call(s32[3]{0:T(128)} %pad_add_fusion.meta_ref, s32[8]{0:T(128)} %ids_ref.1, bf16[3,3,256,256]{3,2,1,0:T(8,128)(2,1)} %we_hbm.1, bf16[3,3,128,128]{3,2,1,0:T(8,128)(2,1)} %wh_hbm.1, f32[720,128]{1,0:T(8,128)} %scale_hbm.1, ...), custom_call_target="tpu_custom_call" | custom-call | tf_op jit(solution)/shard_map/weights/pallas_call | solution.py:87
  8.5 0.0 collective-permute-done.1.east_ref
  8.5 0.0 collective-permute-done.west_ref
  8.5 0.5 %slabs.1 = (bf16[3,182,256]{2,1,0:T(8,128)(2,1)S(1)}, bf16[3,182,256]{2,1,0:T(8,128)(2,1)S(1)}) custom-call(bf16[180,8,256]{2,1,0:T(8,128)(2,1)S(1)} %get-tuple-element.22.first_ref, bf16[180,8,256]{2,1,0:T(8,128)(2,1)S(1)} %get-tuple-element.21.last_ref, bf16[40,256]{1,0:T(8,128)(2,1)S(1)} %collective-permute-done.west_ref, ...), custom_call_target="tpu_custom_call" | custom-call | tf_op jit(solution)/shard_map/slabs/pallas_call | solution.py:129
  9.1 3.1 %collective-permute-start.4 = (bf16[3,182,256]{2,1,0:T(8,128)(2,1)S(1)}, bf16[3,182,256]{2,1,0:T(8,128)(2,1)S(1)}, u32[]{:S(2)}, u32[]{:S(2)}) collective-permute-start(bf16[3,182,256]{2,1,0:T(8,128)(2,1)S(1)} %get-tuple-element.14), channel_id=1, source_target_pairs={{0,4},{4,8},{8,12},{12,16},{16,20},{20,24},{24,28},{1,5},{5,9},{9,... | collective-permute-start | bytes 838664 | tf_op jit(solution)/shard_map/ppermute | solution.py:400
  12.2 3.1 %collective-permute-start.5 = (bf16[3,182,256]{2,1,0:T(8,128)(2,1)S(1)}, bf16[3,182,256]{2,1,0:T(8,128)(2,1)S(1)}, u32[]{:S(2)}, u32[]{:S(2)}) collective-permute-start(bf16[3,182,256]{2,1,0:T(8,128)(2,1)S(1)} %get-tuple-element.15), channel_id=1, source_target_pairs={{4,0},{8,4},{12,8},{16,12},{20,16},{24,20},{28,24},{5,1},{9,5},{13... | collective-permute-start | bytes 838664 | tf_op jit(solution)/shard_map/ppermute | solution.py:401
  15.3 0.0 copy-start
  15.3 2.0 %copy-done = bf16[40,180,256]{2,0,1:T(8,128)(2,1)S(1)} copy-done((bf16[40,180,256]{2,0,1:T(8,128)(2,1)S(1)}, bf16[40,180,256]{2,0,1:T(8,128)(2,1)}, u32[]{:S(2)}) %copy-start) | copy-done | bytes 3686424
  17.4 1.4 %copy-done.5 = bf16[4,768,256]{2,1,0:T(8,128)(2,1)S(1)} copy-done((bf16[4,768,256]{2,1,0:T(8,128)(2,1)S(1)}, bf16[4,768,256]{2,1,0:T(8,128)(2,1)}, u32[]{:S(2)}) %copy-start.5) | copy-done | bytes 1572888
  18.8 4.2 %encode.3.refs_0_ = bf16[8,90,128]{2,1,0:T(8,128)(2,1)S(1)} custom-call(s32[3]{0:T(128)S(1)} %copy-done.4, bf16[180,40,256]{2,1,0:T(8,128)(2,1)S(1)} %bitcast.10, bf16[40,256]{1,0:T(8,128)(2,1)S(1)} %collective-permute-done.west_ref, bf16[40,256]{1,0:T(8,128)(2,1)S(1)} %collective-permute-done.1.east_ref, bf16[4,768,256]{2,1,0:T(8,128)(2,1)S(1)} %copy-done.5, ...), custom_call_target="tpu_custom_call" | custom-call | flops 2264924160 | bytes 8388608 | tf_op jit(solution)/shard_map/encode/pallas_call | solution.py:237
  23.0 1.2 %collective-permute-start.3 = (bf16[8,90,128]{2,1,0:T(8,128)(2,1)S(1)}, bf16[8,90,128]{2,1,0:T(8,128)(2,1)S(1)}, u32[]{:S(2)}, u32[]{:S(2)}) collective-permute-start(bf16[8,90,128]{2,1,0:T(8,128)(2,1)S(1)} %encode.3.refs_0_), channel_id=1, source_target_pairs={{0,2},{1,3},{2,0},{3,1},{4,6},{5,7},{6,4},{7,5},{8,10},{9,11},{10,... | collective-permute-start | bytes 552968 | tf_op jit(solution)/shard_map/ppermute | solution.py:415
  24.2 0.3 collective-permute-start.2
  24.5 4.2 %encode.5.refs_4_ = bf16[8,90,128]{2,1,0:T(8,128)(2,1)S(1)} custom-call(s32[3]{0:T(128)S(1)} %copy-done.4, bf16[180,40,256]{2,1,0:T(8,128)(2,1)S(1)} %bitcast.11, bf16[40,256]{1,0:T(8,128)(2,1)S(1)} %collective-permute-done.west_ref, bf16[40,256]{1,0:T(8,128)(2,1)S(1)} %collective-permute-done.1.east_ref, bf16[4,768,256]{2,1,0:T(8,128)(2,1)S(1)} %copy-done.5, ...), custom_call_target="tpu_custom_call" | custom-call | flops 2264924160 | bytes 8388608 | tf_op jit(solution)/shard_map/encode/pallas_call | solution.py:237
  28.7 0.7 %collective-permute-start.8 = (bf16[8,90,128]{2,1,0:T(8,128)(2,1)S(1)}, bf16[8,90,128]{2,1,0:T(8,128)(2,1)S(1)}, u32[]{:S(2)}, u32[]{:S(2)}) collective-permute-start(bf16[8,90,128]{2,1,0:T(8,128)(2,1)S(1)} %encode.5.refs_4_), channel_id=1, source_target_pairs={{0,2},{1,3},{2,0},{3,1},{4,6},{5,7},{6,4},{7,5},{8,10},{9,11},{10,... | collective-permute-start | bytes 552968 | tf_op jit(solution)/shard_map/ppermute | solution.py:415
  29.4 0.0 collective-permute-done.4.refs_0_
  29.5 0.3 collective-permute-start.7
  29.7 0.0 collective-permute-done.5.refs_1_
  29.7 4.8 %encode.4.refs_8_ = bf16[6,90,128]{2,1,0:T(8,128)(2,1)S(1)} custom-call(s32[3]{0:T(128)S(1)} %copy-done.4, bf16[180,40,256]{2,1,0:T(8,128)(2,1)S(1)} %bitcast.12, bf16[40,256]{1,0:T(8,128)(2,1)S(1)} %collective-permute-done.west_ref, bf16[40,256]{1,0:T(8,128)(2,1)S(1)} %collective-permute-done.1.east_ref, ...), custom_call_target="tpu_custom_call" | custom-call | flops 2264924160 | bytes 8388608 | tf_op jit(solution)/shard_map/encode/pallas_call | solution.py:237
  34.6 0.3 collective-permute-start.6
  34.9 0.2 collective-permute-done.8.refs_6_
  35.0 1.0 %collective-permute-start.9 = (bf16[8,90,128]{2,1,0:T(8,128)(2,1)S(1)}, bf16[8,90,128]{2,1,0:T(8,128)(2,1)S(1)}, u32[]{:S(2)}, u32[]{:S(2)}) collective-permute-start(bf16[8,90,128]{2,1,0:T(8,128)(2,1)S(1)} %collective-permute-done.8.refs_6_), channel_id=1, source_target_pairs={{0,1},{1,0},{2,3},{3,2},{4,5},{5,4},{6,7},{7,6},{8,9},{9,8},{10,11... | collective-permute-start | bytes 552968 | tf_op jit(solution)/shard_map/ppermute | solution.py:421
  36.1 0.6 %collective-permute-start.12 = (bf16[6,90,128]{2,1,0:T(8,128)(2,1)S(1)}, bf16[6,90,128]{2,1,0:T(8,128)(2,1)S(1)}, u32[]{:S(2)}, u32[]{:S(2)}) collective-permute-start(bf16[6,90,128]{2,1,0:T(8,128)(2,1)S(1)} %encode.4.refs_8_), channel_id=1, source_target_pairs={{0,3},{1,2},{2,1},{3,0},{4,7},{5,6},{6,5},{7,4},{8,11},{9,10},{10,... | collective-permute-start | bytes 414728 | tf_op jit(solution)/shard_map/ppermute | solution.py:418
  36.7 0.0 collective-permute-done.2.refs_1_
  36.7 0.8 %collective-permute-start.11 = (bf16[6,90,128]{2,1,0:T(8,128)(2,1)S(1)}, bf16[6,90,128]{2,1,0:T(8,128)(2,1)S(1)}, u32[]{:S(2)}, u32[]{:S(2)}) collective-permute-start(bf16[6,90,128]{2,1,0:T(8,128)(2,1)S(1)} %encode.4.refs_8_), channel_id=1, source_target_pairs={{0,2},{1,3},{2,0},{3,1},{4,6},{5,7},{6,4},{7,5},{8,10},{9,11},{10,... | collective-permute-start | bytes 414728 | tf_op jit(solution)/shard_map/ppermute | solution.py:415
  37.4 0.8 %collective-permute-start.10 = (bf16[6,90,128]{2,1,0:T(8,128)(2,1)S(1)}, bf16[6,90,128]{2,1,0:T(8,128)(2,1)S(1)}, u32[]{:S(2)}, u32[]{:S(2)}) collective-permute-start(bf16[6,90,128]{2,1,0:T(8,128)(2,1)S(1)} %encode.4.refs_8_), channel_id=1, source_target_pairs={{0,1},{1,0},{2,3},{3,2},{4,5},{5,4},{6,7},{7,6},{8,9},{9,8},{10,11... | collective-permute-start | bytes 414728 | tf_op jit(solution)/shard_map/ppermute | solution.py:416
  38.3 7.1 %heads.2.refs_15_ = bf16[2,20,360,128]{3,2,1,0:T(8,128)(2,1)} custom-call(s32[3]{0:T(128)S(1)} %copy-done.4, bf16[8,90,128]{2,1,0:T(8,128)(2,1)S(1)} %encode.3.refs_0_, bf16[8,90,128]{2,1,0:T(8,128)(2,1)S(1)} %collective-permute-done.2.refs_1_, bf16[8,90,128]{2,1,0:T(8,128)(2,1)S(1)} %collective-permute-done.3.refs_2_, ...), custom_call_target="tpu_custom_call" | custom-call | flops 3344302080 | bytes 25165824 | tf_op jit(solution)/shard_map/heads/pallas_call | solution.py:347
  45.4 5.2 %heads.3 = bf16[2,20,360,128]{3,2,1,0:T(8,128)(2,1)} custom-call(s32[3]{0:T(128)S(1)} %copy-done.4, bf16[8,90,128]{2,1,0:T(8,128)(2,1)S(1)} %encode.3.refs_0_, bf16[8,90,128]{2,1,0:T(8,128)(2,1)S(1)} %collective-permute-done.2.refs_1_, bf16[8,90,128]{2,1,0:T(8,128)(2,1)S(1)} %collective-permute-done.3.refs_2_, ...), custom_call_target="tpu_custom_call", output_to_operand_aliasing={{}: (16, {})} | custom-call | flops 2229534720 | bytes 16777216 | tf_op jit(solution)/shard_map/heads/pallas_call | solution.py:347
  (18 shorter events, 0.0 us)
Async XLA Ops:
  0.0 15.3 %copy-start.6 = (bf16[256,128]{1,0:T(8,128)(2,1)S(1)}, bf16[256,128]{1,0:T(8,128)(2,1)}, u32[]{:S(2)}) copy-start(bf16[256,128]{1,0:T(8,128)(2,1)} %refs_1_.3) | copy-start | bytes 196612
  0.8 7.7 %collective-permute-start.1 = (bf16[40,256]{1,0:T(8,128)(2,1)S(1)}, bf16[40,256]{1,0:T(8,128)(2,1)S(1)}, u32[]{:S(2)}, u32[]{:S(2)}) collective-permute-start(bf16[40,256]{1,0:T(8,128)(2,1)S(1)} %get-tuple-element.23), channel_id=1, source_target_pairs={{1,0},{2,1},{3,2},{0,3},{5,4},{6,5},{7,6},{4,7},{9,8},{10,9},{11,1... | collective-permute-start | bytes 61448 | tf_op jit(solution)/shard_map/ppermute | solution.py:393
  1.5 7.1 %collective-permute-start = (bf16[40,256]{1,0:T(8,128)(2,1)S(1)}, bf16[40,256]{1,0:T(8,128)(2,1)S(1)}, u32[]{:S(2)}, u32[]{:S(2)}) collective-permute-start(bf16[40,256]{1,0:T(8,128)(2,1)S(1)} %get-tuple-element.24), channel_id=1, source_target_pairs={{0,1},{1,2},{2,3},{3,0},{4,5},{5,6},{6,7},{7,4},{8,9},{9,10},{10,1... | collective-permute-start | bytes 61448 | tf_op jit(solution)/shard_map/ppermute | solution.py:392
  4.7 10.6 %copy-start.4 = (s32[3]{0:T(128)S(1)}, s32[3]{0:T(128)}, u32[]{:S(2)}) copy-start(s32[3]{0:T(128)} %pad_add_fusion.meta_ref) | copy-start | bytes 40
  9.1 20.4 %collective-permute-start.4 = (bf16[3,182,256]{2,1,0:T(8,128)(2,1)S(1)}, bf16[3,182,256]{2,1,0:T(8,128)(2,1)S(1)}, u32[]{:S(2)}, u32[]{:S(2)}) collective-permute-start(bf16[3,182,256]{2,1,0:T(8,128)(2,1)S(1)} %get-tuple-element.14), channel_id=1, source_target_pairs={{0,4},{4,8},{8,12},{12,16},{16,20},{20,24},{24,28},{1,5},{5,9},{9,... | collective-permute-start | bytes 838664 | tf_op jit(solution)/shard_map/ppermute | solution.py:400
  12.2 17.5 %collective-permute-start.5 = (bf16[3,182,256]{2,1,0:T(8,128)(2,1)S(1)}, bf16[3,182,256]{2,1,0:T(8,128)(2,1)S(1)}, u32[]{:S(2)}, u32[]{:S(2)}) collective-permute-start(bf16[3,182,256]{2,1,0:T(8,128)(2,1)S(1)} %get-tuple-element.15), channel_id=1, source_target_pairs={{4,0},{8,4},{12,8},{16,12},{20,16},{24,20},{28,24},{5,1},{9,5},{13... | collective-permute-start | bytes 838664 | tf_op jit(solution)/shard_map/ppermute | solution.py:401
  15.3 2.0 %copy-start = (bf16[40,180,256]{2,0,1:T(8,128)(2,1)S(1)}, bf16[40,180,256]{2,0,1:T(8,128)(2,1)}, u32[]{:S(2)}) copy-start(bf16[40,180,256]{2,0,1:T(8,128)(2,1)} %param.8) | copy-start | bytes 11059204
  17.4 1.4 %copy-start.5 = (bf16[4,768,256]{2,1,0:T(8,128)(2,1)S(1)}, bf16[4,768,256]{2,1,0:T(8,128)(2,1)}, u32[]{:S(2)}) copy-start(bf16[4,768,256]{2,1,0:T(8,128)(2,1)} %get-tuple-element.13.refs_0_.refs_2_) | copy-start | bytes 4718596
  23.0 11.6 %collective-permute-start.3 = (bf16[8,90,128]{2,1,0:T(8,128)(2,1)S(1)}, bf16[8,90,128]{2,1,0:T(8,128)(2,1)S(1)}, u32[]{:S(2)}, u32[]{:S(2)}) collective-permute-start(bf16[8,90,128]{2,1,0:T(8,128)(2,1)S(1)} %encode.3.refs_0_), channel_id=1, source_target_pairs={{0,2},{1,3},{2,0},{3,1},{4,6},{5,7},{6,4},{7,5},{8,10},{9,11},{10,... | collective-permute-start | bytes 552968 | tf_op jit(solution)/shard_map/ppermute | solution.py:415
  24.2 12.5 %collective-permute-start.2 = (bf16[8,90,128]{2,1,0:T(8,128)(2,1)S(1)}, bf16[8,90,128]{2,1,0:T(8,128)(2,1)S(1)}, u32[]{:S(2)}, u32[]{:S(2)}) collective-permute-start(bf16[8,90,128]{2,1,0:T(8,128)(2,1)S(1)} %encode.3.refs_0_), channel_id=1, source_target_pairs={{0,1},{1,0},{2,3},{3,2},{4,5},{5,4},{6,7},{7,6},{8,9},{9,8},{10,11... | collective-permute-start | bytes 552968 | tf_op jit(solution)/shard_map/ppermute | solution.py:416
  28.7 9.6 %copy-start.1 = (bf16[1152,256]{1,0:T(8,128)(2,1)S(1)}, bf16[1152,256]{1,0:T(8,128)(2,1)}, u32[]{:S(2)}) copy-start(bf16[1152,256]{1,0:T(8,128)(2,1)} %get-tuple-element.18.refs_8_.refs_12_) | copy-start | bytes 1769476
  28.7 9.6 %copy-start.2 = (bf16[368,368]{1,0:T(8,128)(2,1)S(1)}, bf16[368,368]{1,0:T(8,128)(2,1)}, u32[]{:S(2)}) copy-start(bf16[368,368]{1,0:T(8,128)(2,1)} %get-tuple-element.20.refs_10_.refs_14_) | copy-start | bytes 812548
  28.7 9.6 %copy-start.3 = (f32[8,256]{1,0:T(8,128)S(1)}, f32[8,256]{1,0:T(8,128)}, u32[]{:S(2)}) copy-start(f32[8,256]{1,0:T(8,128)} %get-tuple-element.19.refs_9_.refs_13_) | copy-start | bytes 24580
  28.7 6.3 %collective-permute-start.8 = (bf16[8,90,128]{2,1,0:T(8,128)(2,1)S(1)}, bf16[8,90,128]{2,1,0:T(8,128)(2,1)S(1)}, u32[]{:S(2)}, u32[]{:S(2)}) collective-permute-start(bf16[8,90,128]{2,1,0:T(8,128)(2,1)S(1)} %encode.5.refs_4_), channel_id=1, source_target_pairs={{0,2},{1,3},{2,0},{3,1},{4,6},{5,7},{6,4},{7,5},{8,10},{9,11},{10,... | collective-permute-start | bytes 552968 | tf_op jit(solution)/shard_map/ppermute | solution.py:415
  29.5 8.0 %collective-permute-start.7 = (bf16[8,90,128]{2,1,0:T(8,128)(2,1)S(1)}, bf16[8,90,128]{2,1,0:T(8,128)(2,1)S(1)}, u32[]{:S(2)}, u32[]{:S(2)}) collective-permute-start(bf16[8,90,128]{2,1,0:T(8,128)(2,1)S(1)} %encode.5.refs_4_), channel_id=1, source_target_pairs={{0,1},{1,0},{2,3},{3,2},{4,5},{5,4},{6,7},{7,6},{8,9},{9,8},{10,11... | collective-permute-start | bytes 552968 | tf_op jit(solution)/shard_map/ppermute | solution.py:416
  34.6 3.7 %collective-permute-start.6 = (bf16[8,90,128]{2,1,0:T(8,128)(2,1)S(1)}, bf16[8,90,128]{2,1,0:T(8,128)(2,1)S(1)}, u32[]{:S(2)}, u32[]{:S(2)}) collective-permute-start(bf16[8,90,128]{2,1,0:T(8,128)(2,1)S(1)} %collective-permute-done.3.refs_2_), channel_id=1, source_target_pairs={{0,1},{1,0},{2,3},{3,2},{4,5},{5,4},{6,7},{7,6},{8,9},{9,8},{10,11... | collective-permute-start | bytes 552968 | tf_op jit(solution)/shard_map/ppermute | solution.py:421
  35.0 3.2 %collective-permute-start.9 = (bf16[8,90,128]{2,1,0:T(8,128)(2,1)S(1)}, bf16[8,90,128]{2,1,0:T(8,128)(2,1)S(1)}, u32[]{:S(2)}, u32[]{:S(2)}) collective-permute-start(bf16[8,90,128]{2,1,0:T(8,128)(2,1)S(1)} %collective-permute-done.8.refs_6_), channel_id=1, source_target_pairs={{0,1},{1,0},{2,3},{3,2},{4,5},{5,4},{6,7},{7,6},{8,9},{9,8},{10,11... | collective-permute-start | bytes 552968 | tf_op jit(solution)/shard_map/ppermute | solution.py:421
  36.1 9.2 %collective-permute-start.12 = (bf16[6,90,128]{2,1,0:T(8,128)(2,1)S(1)}, bf16[6,90,128]{2,1,0:T(8,128)(2,1)S(1)}, u32[]{:S(2)}, u32[]{:S(2)}) collective-permute-start(bf16[6,90,128]{2,1,0:T(8,128)(2,1)S(1)} %encode.4.refs_8_), channel_id=1, source_target_pairs={{0,3},{1,2},{2,1},{3,0},{4,7},{5,6},{6,5},{7,4},{8,11},{9,10},{10,... | collective-permute-start | bytes 414728 | tf_op jit(solution)/shard_map/ppermute | solution.py:418
  36.7 8.7 %collective-permute-start.11 = (bf16[6,90,128]{2,1,0:T(8,128)(2,1)S(1)}, bf16[6,90,128]{2,1,0:T(8,128)(2,1)S(1)}, u32[]{:S(2)}, u32[]{:S(2)}) collective-permute-start(bf16[6,90,128]{2,1,0:T(8,128)(2,1)S(1)} %encode.4.refs_8_), channel_id=1, source_target_pairs={{0,2},{1,3},{2,0},{3,1},{4,6},{5,7},{6,4},{7,5},{8,10},{9,11},{10,... | collective-permute-start | bytes 414728 | tf_op jit(solution)/shard_map/ppermute | solution.py:415
  37.4 7.9 %collective-permute-start.10 = (bf16[6,90,128]{2,1,0:T(8,128)(2,1)S(1)}, bf16[6,90,128]{2,1,0:T(8,128)(2,1)S(1)}, u32[]{:S(2)}, u32[]{:S(2)}) collective-permute-start(bf16[6,90,128]{2,1,0:T(8,128)(2,1)S(1)} %encode.4.refs_8_), channel_id=1, source_target_pairs={{0,1},{1,0},{2,3},{3,2},{4,5},{5,4},{6,7},{7,6},{8,9},{9,8},{10,11... | collective-permute-start | bytes 414728 | tf_op jit(solution)/shard_map/ppermute | solution.py:416

commit v7 on v6

--- a/solution.py
+++ b/solution.py
@@ -29,16 +29,15 @@
 
 
 def weights_kernel(
-    meta_ref, ids_ref, we_hbm, wh_hbm, scale_hbm, shift_hbm, z_hbm,
-    g_ref, ws_ref, vec_ref, zs_ref,
-    we_ref, wh_ref, tab, z_ref, sem,
+    meta_ref, ids_ref, wh_hbm, scale_hbm, shift_hbm, z_hbm,
+    ws_ref, vec_ref, zs_ref,
+    wh_ref, tab, z_ref, sem,
 ):
-    ch = we_ref.shape[-1]
     head = wh_ref.shape[-1]
     leads = ws_ref.shape[1] // head
     cols = z_ref.shape[0]
     ids = [ids_ref[meta_ref[2] * leads + lead] for lead in range(leads)]
-    copies = [(we_hbm, we_ref), (z_hbm, z_ref), (wh_hbm, wh_ref)]
+    copies = [(z_hbm, z_ref), (wh_hbm, wh_ref)]
     for lead in range(leads):
         block = pl.multiple_of((ids[lead] // 8) * 8, 8)
         copies.append((scale_hbm.at[pl.ds(block, 8)], tab.at[lead, 0]))
@@ -47,16 +46,7 @@
     for c in copies:
         c.start()
     zs_ref[...] = jnp.zeros(zs_ref.shape, BF)
-    copies[0].wait()
-    for dr in range(3):
-        at = slice(dr * ch, (dr + 1) * ch)
-        w = [we_ref[dr, dc].astype(F32) for dc in range(3)]
-        half = 0.5 * (w[0] + w[2])
-        g_ref[0, at] = we_ref[dr, 0]
-        g_ref[1, at] = (half + 0.5 * w[1]).astype(BF)
-        g_ref[2, at] = (half - 0.5 * w[1]).astype(BF)
-        g_ref[3, at] = we_ref[dr, 2]
-    for c in copies[1:]:
+    for c in copies:
         c.wait()
     zs_ref[:cols, :cols] = z_ref[...] * jnp.asarray(0.5, BF)
     for lead in range(leads):
@@ -78,45 +68,46 @@
             vec_ref[BIAS + dr : BIAS + dr + 1, lanes] = jnp.sum(total, axis=0, keepdims=True)
 
 
-def prepare(meta, ids, w_enc, w_head, scale, shift, z, leads):
-    ch, head, cols = w_enc.shape[-1], w_head.shape[-1], z.shape[0]
+def prepare(meta, ids, w_head, scale, shift, z, leads):
+    head, cols = w_head.shape[-1], z.shape[0]
     wide = up_to(cols, 16)
     vmem = pl.BlockSpec(memory_space=pltpu.VMEM)
     smem = pl.BlockSpec(memory_space=pltpu.SMEM)
     hbm = pl.BlockSpec(memory_space=pltpu.HBM)
     return pl.pallas_call(
         weights_kernel,
-        in_specs=[smem, smem] + [hbm] * 5,
-        out_specs=[vmem] * 4,
+        in_specs=[smem, smem] + [hbm] * 4,
+        out_specs=[vmem] * 3,
         out_shape=[
-            jax.ShapeDtypeStruct((4, 3 * ch, ch), BF),
             jax.ShapeDtypeStruct((9 * head, leads * head), BF),
             jax.ShapeDtypeStruct((8, leads * head), F32),
             jax.ShapeDtypeStruct((wide, wide), BF),
         ],
         scratch_shapes=[
-            pltpu.VMEM(w_enc.shape, BF),
             pltpu.VMEM(w_head.shape, BF),
             pltpu.VMEM((leads, 2, 8, head), F32),
             pltpu.VMEM(z.shape, BF),
-            pltpu.SemaphoreType.DMA((3 + 2 * leads,)),
+            pltpu.SemaphoreType.DMA((2 + 2 * leads,)),
         ],
         compiler_params=params(58),
         name="weights",
-    )(meta, ids, w_enc, w_head, scale, shift, z)
-
-
-def slabs_kernel(first_ref, last_ref, west_ref, east_ref, up_ref, dn_ref, flat):
-    xcols, _, ch = first_ref.shape
-    rows = west_ref.shape[0]
+    )(meta, ids, w_head, scale, shift, z)
+
+
+def slabs_kernel(x_ref, west_ref, east_ref, up_ref, dn_ref, edge, flat, sem):
+    xcols, rows, ch = x_ref.shape
     reach = up_ref.shape[0]
-    for k, (edge, slab, start, r) in enumerate(
-        ((first_ref, dn_ref, 0, 0), (last_ref, up_ref, 8 - reach, rows - reach))
-    ):
+    copies = [
+        pltpu.make_async_copy(x_ref.at[:, a : a + 8], edge.at[k], sem.at[k]) for k, a in enumerate((0, rows - 8))
+    ]
+    for c in copies:
+        c.start()
+    for k, (slab, start, r) in enumerate(((dn_ref, 0, 0), (up_ref, 8 - reach, rows - reach))):
+        copies[k].wait()
         parts = []
         for j in range(ch // 128):
             lanes = slice(j * 128, (j + 1) * 128)
-            flat[k, j] = edge[:, :, lanes].astype(F32).reshape(xcols * 8, 128)
+            flat[k, j] = edge[k, :, :, lanes].astype(F32).reshape(xcols * 8, 128)
             parts.append([flat[k, j, pl.ds(start + i, xcols, stride=8), :] for i in range(reach)])
         for i in range(reach):
             row = jnp.concatenate([p[i] for p in parts], axis=1).astype(BF)
@@ -124,26 +115,57 @@
 
 
 def row_slabs(x, west, east, reach):
-    xcols, rows, ch = x.shape
+    xcols, _, ch = x.shape
     vmem = pl.BlockSpec(memory_space=pltpu.VMEM)
     return pl.pallas_call(
         slabs_kernel,
-        in_specs=[vmem] * 4,
+        in_specs=[pl.BlockSpec(memory_space=pltpu.HBM), vmem, vmem],
         out_specs=[vmem] * 2,
         out_shape=[jax.ShapeDtypeStruct((reach, xcols + 2, ch), BF)] * 2,
-        scratch_shapes=[pltpu.VMEM((2, ch // 128, xcols * 8, 128), F32)],
-        compiler_params=params(16),
+        scratch_shapes=[
+            pltpu.VMEM((2, xcols, 8, ch), BF),
+            pltpu.VMEM((2, ch // 128, xcols * 8, 128), F32),
+            pltpu.SemaphoreType.DMA((2,)),
+        ],
+        compiler_params=params(53),
         name="slabs",
-    )(x[:, :8], x[:, rows - 8 :], west, east)
-
-
-def encoder_kernel(
-    meta_ref, x_ref, west_ref, east_ref, *refs, first, group
-):
+    )(x, west, east)
+
+
+def encoder_kernel(meta_ref, x_hbm, west_ref, east_ref, *refs, first, group, makes):
     halos, refs = (refs[:2], refs[2:]) if first is None else ((), refs)
-    g_ref, wp_ref, out_ref, xs, ys, st, pt = refs[:7]
-    cols, rows, ch = x_ref.shape
+    w_hbm, wp_ref, out_ref = refs[:3]
+    if makes:
+        g_out, w_ref, refs = refs[3], refs[4], refs[5:]
+    else:
+        refs = refs[3:]
+    g_ref, x_ref, xs, ys, st, pt, sem = refs[:7]
+    cols, rows, ch = x_hbm.shape
     reach = 2 * EDGE - 1
+    low = (0, rows - 8) if first is None else ((first - 1) // 8 * 8,)
+    tall = x_ref.shape[2]
+    copies = [
+        pltpu.make_async_copy(x_hbm.at[:, a : a + tall], x_ref.at[i], sem.at[i]) for i, a in enumerate(low)
+    ]
+    weights = pltpu.make_async_copy(w_hbm, w_ref if makes else g_ref, sem.at[2])
+    if makes:
+        weights.start()
+    for c in copies:
+        c.start()
+    if not makes:
+        weights.start()
+    if makes:
+        weights.wait()
+        for dr in range(3):
+            at = slice(dr * ch, (dr + 1) * ch)
+            w = [w_ref[dr, dc].astype(F32) for dc in range(3)]
+            half = 0.5 * (w[0] + w[2])
+            g_ref[0, at] = w_ref[dr, 0]
+            g_ref[1, at] = (half + 0.5 * w[1]).astype(BF)
+            g_ref[2, at] = (half - 0.5 * w[1]).astype(BF)
+            g_ref[3, at] = w_ref[dr, 2]
+        weights = pltpu.make_async_copy(g_ref, g_out, sem.at[3])
+        weights.start()
     if first is None:
         hf = refs[7]
         for k, halo in enumerate(halos):
@@ -152,7 +174,8 @@
                 for i in range(reach):
                     at = 8 - reach + i if k == 0 else i
                     hf[k, j, pl.ds(at, cols + 2, stride=8), :] = halo[i, :, lanes].astype(F32)
-    low = 0 if first is None else (first - 1) // 8 * 8
+    for c in copies:
+        c.wait()
 
     def stage(at, tile_rows):
         if first is None:
@@ -161,8 +184,8 @@
                 h = [hf[k, j, at.start * 8 : at.stop * 8] for j in range(ch // 128)]
                 h = [v.astype(BF).reshape(at.stop - at.start, 8, 128) for v in h]
                 far.append(jnp.concatenate(h, axis=2))
-            top = jnp.concatenate([far[0], tile_rows(0, 8)], axis=1)
-            end = jnp.concatenate([tile_rows(rows - 8, 8), far[1]], axis=1)
+            top = jnp.concatenate([far[0], tile_rows(0)], axis=1)
+            end = jnp.concatenate([tile_rows(1), far[1]], axis=1)
             pad = jnp.zeros((at.stop - at.start, 16 - 4 * (EDGE + 1), ch), BF)
             n = 2 * (EDGE + 1)
             for dr in range(3):
@@ -170,16 +193,16 @@
                 b = end[:, 8 - reach - 2 + dr : 8 - reach - 2 + dr + n]
                 xs[at, :, dr * ch : (dr + 1) * ch] = jnp.concatenate([t, b, pad], axis=1)
         else:
-            here = tile_rows(low, 24)
+            here = tile_rows(0)
             for dr in range(3):
-                off = first - 1 - low + dr
+                off = first - 1 - low[0] + dr
                 xs[at, :, dr * ch : (dr + 1) * ch] = here[:, off : off + 16]
 
-    stage(slice(0, 1), lambda a, n: west_ref[a : a + n, :].reshape(1, n, ch))
-    stage(slice(cols + 1, cols + 2), lambda a, n: east_ref[a : a + n, :].reshape(1, n, ch))
+    stage(slice(0, 1), lambda i: west_ref[low[i] : low[i] + tall, :].reshape(1, tall, ch))
+    stage(slice(cols + 1, cols + 2), lambda i: east_ref[low[i] : low[i] + tall, :].reshape(1, tall, ch))
     block = next(n for n in range(32, 0, -1) if cols % n == 0)
     for c in range(0, cols, block):
-        stage(slice(c + 1, c + 1 + block), lambda a, n: x_ref[c : c + block, a : a + n, :])
+        stage(slice(c + 1, c + 1 + block), lambda i: x_ref[i, c : c + block])
 
     pairs = cols // 2
 
@@ -207,6 +230,8 @@
         pooled = (jnp.concatenate(pooled, axis=1) * 0.125).astype(BF)
         pt[c * (n // 2) : (c + 1) * (n // 2)] = jnp.dot(pooled, wp_ref[...], preferred_element_type=F32)
 
+    if not makes:
+        weights.wait()
     for c in range(pairs // group):
         multiply(c)
         if c:
@@ -218,32 +243,49 @@
         if first is None and r in (0, count - 1):
             row = jnp.where(meta_ref[0 if r == 0 else 1] == 0, row, 0.0)
         out_ref[r] = row.astype(BF)
-
-
-def encode(meta, x, west, east, halos, g, wp, first, count, group):
+    if makes:
+        weights.wait()
+
+
+def encode(meta, x, west, east, halos, w, wp, first, count, group):
     cols, rows, ch = x.shape
     head = wp.shape[1]
+    makes = w.ndim == 4
+    blocks, tall = (1, 24) if halos is None else (2, 8)
     vmem = pl.BlockSpec(memory_space=pltpu.VMEM)
+    hbm = pl.BlockSpec(memory_space=pltpu.HBM)
+    form = (4, 3 * ch, ch)
     scratch = [
+        pltpu.VMEM(form, BF),
+        pltpu.VMEM((blocks, cols, tall, ch), BF),
         pltpu.VMEM((cols + 2, 16, 3 * ch), BF),
         pltpu.VMEM((2, 4, group * 16, ch), F32),
         pltpu.VMEM((ch // 128, group * 16, 128), F32),
         pltpu.VMEM((cols // 2 * 8, head), F32),
+        pltpu.SemaphoreType.DMA((4,)),
     ]
+    if makes:
+        scratch = [pltpu.VMEM(w.shape, BF), *scratch]
     if halos is not None:
         scratch.append(pltpu.VMEM((2, ch // 128, (cols + 2) * 8, 128), F32))
-    operands = [meta, x, west, east, *(halos or ()), g, wp]
-    flops = 2 * cols * 16 * 6 * ch * ch
+    near = [west, east, *(halos or ())]
+    out_shape = [jax.ShapeDtypeStruct((count, cols // 2, head), BF)]
+    out_specs = [vmem]
+    if makes:
+        out_shape.append(jax.ShapeDtypeStruct(form, BF))
+        out_specs.append(hbm)
     return pl.pallas_call(
-        functools.partial(encoder_kernel, first=first, group=group),
-        in_specs=[pl.BlockSpec(memory_space=pltpu.SMEM)] + [vmem] * (len(operands) - 1),
-        out_specs=vmem,
-        out_shape=jax.ShapeDtypeStruct((count, cols // 2, head), BF),
+        functools.partial(encoder_kernel, first=first, group=group, makes=makes),
+        in_specs=[pl.BlockSpec(memory_space=pltpu.SMEM), hbm] + [vmem] * len(near) + [hbm, vmem],
+        out_specs=out_specs,
+        out_shape=out_shape,
         scratch_shapes=scratch,
-        compiler_params=params(28),
-        cost_estimate=pl.CostEstimate(flops=flops, transcendentals=cols * 16 * ch, bytes_accessed=8 * 1024 * 1024),
+        compiler_params=params(53),
+        cost_estimate=pl.CostEstimate(
+            flops=2 * cols * 16 * 6 * ch * ch, transcendentals=cols * 16 * ch, bytes_accessed=8 * MIB
+        ),
         name="encode",
-    )(*operands)
+    )(meta, x, *near, w, wp)
 
 
 def head_kernel(meta_ref, *refs, chunks, blocks, shards, aliased):
@@ -395,7 +437,8 @@
     meta = jnp.stack(
         [lat_at == 0, lat_at == lat - 1, lon_at]
     ).astype(jnp.int32)
-    g, ws, vec, zs = prepare(meta, lead_ids, w_enc, w_head, film_scale, film_shift, zonal_mix, leads)
+    ws, vec, zs = prepare(meta, lead_ids, w_head, film_scale, film_shift, zonal_mix, leads)
+    west, east, ws, vec, zs = lax.optimization_barrier((west, east, ws, vec, zs))
     up, dn = row_slabs(tile, west, east, reach)
     above = lax.ppermute(up, "lat", lat_up)
     below = lax.ppermute(dn, "lat", lat_dn)
@@ -407,7 +450,11 @@
         (2 * middle, band_rows - EDGE - middle, None),
         (None, 2 * (EDGE + 1), (above, below)),
     ]
-    proj = [encode(meta, tile, west, east, halos, g, w_proj, first, n, group) for first, n, halos in plan]
+    proj, weights = [], w_enc
+    for first, count, halos in plan:
+        own, *made = encode(meta, tile, west, east, halos, weights, w_proj, first, count, group)
+        proj.append(own)
+        weights = made[0] if made else weights
 
     sent = []
     for k, own in enumerate(proj):

time: 51.1 us -> 53.4 us (1.045)
  Pallas kernels: 29.9 us -> 37.4 us
  local copies, waits for them, and re-layouts: 5.69 us -> 0.8 us
    pallas_call x3, Pallas kernels: 13.2 us -> 20.4 us  [encode(): pl.pallas_call(functools.partial(encoder_kernel, first=first, group=group...]
    unnamed x14 -> x10, local copies, waits for them, and re-layouts: 3.47 us -> 0.02 us
    slice x1 -> x0, local copies, waits for them, and re-layouts: 1.45 us -> none  [row_slabs(): x[:, rows - 8:]]
    ppermute x3, starting transfers between devices: 2.75 us -> 2.21 us  [shards(): across = lax.ppermute(own, 'lon', swap(lon, 2))]
  transfers between devices with their start and end apart: 13 -> 13, of which waited for: 1 -> 0; matrix products, arithmetic and copies ran while one was open for 4% -> 1% of each run, Pallas kernels for 47% -> 57%
where the time goes in v7:
time: 53.4 us; the launch traced here: 53.1 us
  Pallas kernels  37.4 us (70%)
  starting transfers between devices  13.9 us (26%)
  local copies, waits for them, and re-layouts  0.8 us (1%)
  other arithmetic  0.66 us (1%)
    pallas_call x3, Pallas kernels, encode(): pl.pallas_call(functools.partial(encoder_kernel, first=first, group=group...  20.4 us
    pallas_call x2, Pallas kernels, forecast_heads(): pl.pallas_call(functools.partial(head_kernel, chunks=chunks, blocks=block...  12.3 us
    ppermute x1, starting transfers between devices, shards(): above = lax.ppermute(up, 'lat', lat_up)  3.15 us
    ppermute x1, starting transfers between devices, shards(): below = lax.ppermute(dn, 'lat', lat_dn)  3.07 us
    pallas_call x1, Pallas kernels, prepare(): pl.pallas_call(weights_kernel, in_specs=[smem, smem] + [hbm] * 4, out_spe...  3.05 us
    ppermute x3, starting transfers between devices, shards(): across = lax.ppermute(own, 'lon', swap(lon, 2))  2.21 us
    pallas_call x1, Pallas kernels, row_slabs(): pl.pallas_call(slabs_kernel, in_specs=[pl.BlockSpec(memory_space=pltpu.HB...  1.66 us
    ppermute x3, starting transfers between devices, shards(): beside = lax.ppermute(own, 'lon', swap(lon, 1))  1.42 us
  transfers between devices with their start and end apart: 13, of which 0 were waited for; matrix products, arithmetic and copies ran while one was open for 1% of the time, Pallas kernels for 57%

profile of v7, /device:TPU:25, one launch (start us, length us, event | category | flops | bytes accessed | tf_op | source)
XLA Modules:
  0.0 53.1 jit_solution(5299547044532834620)
XLA Ops:
  0.0 0.8 %slice_bitcast_fusion = (bf16[40,256]{1,0:T(8,128)(2,1)S(1)}, bf16[40,256]{1,0:T(8,128)(2,1)S(1)}) fusion(bf16[180,40,256]{2,1,0:T(8,128)(2,1)} %bitcast.8), kind=kLoop, calls=%fused_computation | loop fusion | bytes 81920 | tf_op jit(solution)/shard_map/squeeze | solution.py:435
  0.8 0.7 %collective-permute-start.1 = (bf16[40,256]{1,0:T(8,128)(2,1)S(1)}, bf16[40,256]{1,0:T(8,128)(2,1)S(1)}, u32[]{:S(2)}, u32[]{:S(2)}) collective-permute-start(bf16[40,256]{1,0:T(8,128)(2,1)S(1)} %get-tuple-element.33), channel_id=1, source_target_pairs={{1,0},{2,1},{3,2},{0,3},{5,4},{6,5},{7,6},{4,7},{9,8},{10,9},{11,1... | collective-permute-start | bytes 61448 | tf_op jit(solution)/shard_map/ppermute | solution.py:435
  1.5 1.1 %collective-permute-start = (bf16[40,256]{1,0:T(8,128)(2,1)S(1)}, bf16[40,256]{1,0:T(8,128)(2,1)S(1)}, u32[]{:S(2)}, u32[]{:S(2)}) collective-permute-start(bf16[40,256]{1,0:T(8,128)(2,1)S(1)} %get-tuple-element.34), channel_id=1, source_target_pairs={{0,1},{1,2},{2,3},{3,0},{4,5},{5,6},{6,7},{7,4},{8,9},{9,10},{10,1... | collective-permute-start | bytes 61448 | tf_op jit(solution)/shard_map/ppermute | solution.py:434
  2.6 0.7 %pad_add_fusion.meta_ref = s32[3]{0:T(128)} fusion(s32[1]{0:T(128)} %bitcast.2, s32[1]{0:T(128)} %bitcast.1, s32[1]{0:T(128)} %bitcast), kind=kLoop, calls=%fused_computation.2 | loop fusion | flops 6 | bytes 24 | tf_op jit(solution)/shard_map/stack | solution.py:437
  3.2 3.1 %weights.1 = (bf16[1152,256]{1,0:T(8,128)(2,1)}, f32[8,256]{1,0:T(8,128)}, bf16[368,368]{1,0:T(8,128)(2,1)}) custom-call(s32[3]{0:T(128)} %pad_add_fusion.meta_ref, s32[8]{0:T(128)} %ids_ref.1, bf16[3,3,128,128]{3,2,1,0:T(8,128)(2,1)} %wh_hbm.1, f32[720,128]{1,0:T(8,128)} %scale_hbm.1, f32[720,128]{1,0:T(8,128)} %shift_hbm.1, bf16[360,360]{1,0:T(8,128)(2,1)} %z_hbm.1), custom_call_target="tpu_custom_call" | custom-call | tf_op jit(solution)/shard_map/weights/pallas_call | solution.py:77
  6.3 0.0 collective-permute-done.1.east_ref
  6.3 0.0 collective-permute-done.west_ref
  6.3 1.7 %slabs.1 = (bf16[3,182,256]{2,1,0:T(8,128)(2,1)S(1)}, bf16[3,182,256]{2,1,0:T(8,128)(2,1)S(1)}) custom-call(bf16[180,40,256]{2,1,0:T(8,128)(2,1)} %bitcast.9, bf16[40,256]{1,0:T(8,128)(2,1)S(1)} %collective-permute-done.west_ref, bf16[40,256]{1,0:T(8,128)(2,1)S(1)} %collective-permute-done.1.east_ref), custom_call_target="tpu_custom_call" | custom-call | tf_op jit(solution)/shard_map/slabs/pallas_call | solution.py:120
  8.0 3.1 %collective-permute-start.4 = (bf16[3,182,256]{2,1,0:T(8,128)(2,1)S(1)}, bf16[3,182,256]{2,1,0:T(8,128)(2,1)S(1)}, u32[]{:S(2)}, u32[]{:S(2)}) collective-permute-start(bf16[3,182,256]{2,1,0:T(8,128)(2,1)S(1)} %get-tuple-element.25), channel_id=1, source_target_pairs={{0,4},{4,8},{8,12},{12,16},{16,20},{20,24},{24,28},{1,5},{5,9},{9,... | collective-permute-start | bytes 838664 | tf_op jit(solution)/shard_map/ppermute | solution.py:443
  11.1 3.1 %collective-permute-start.5 = (bf16[3,182,256]{2,1,0:T(8,128)(2,1)S(1)}, bf16[3,182,256]{2,1,0:T(8,128)(2,1)S(1)}, u32[]{:S(2)}, u32[]{:S(2)}) collective-permute-start(bf16[3,182,256]{2,1,0:T(8,128)(2,1)S(1)} %get-tuple-element.26), channel_id=1, source_target_pairs={{4,0},{8,4},{12,8},{16,12},{20,16},{24,20},{28,24},{5,1},{9,5},{13... | collective-permute-start | bytes 838664 | tf_op jit(solution)/shard_map/ppermute | solution.py:444
  14.2 6.1 %encode.3 = (bf16[8,90,128]{2,1,0:T(8,128)(2,1)S(1)}, bf16[4,768,256]{2,1,0:T(8,128)(2,1)}) custom-call(s32[3]{0:T(128)S(1)} %copy-done.3, bf16[180,40,256]{2,1,0:T(8,128)(2,1)} %bitcast.10, bf16[40,256]{1,0:T(8,128)(2,1)S(1)} %collective-permute-done.west_ref, bf16[40,256]{1,0:T(8,128)(2,1)S(1)} %collective-permute-done.1.east_ref, ...), custom_call_target="tpu_custom_call" | custom-call | flops 2264924160 | bytes 8388608 | tf_op jit(solution)/shard_map/encode/pallas_call | solution.py:277
  20.3 6.5 %encode.5.refs_4_ = bf16[8,90,128]{2,1,0:T(8,128)(2,1)S(1)} custom-call(s32[3]{0:T(128)S(1)} %copy-done.3, bf16[180,40,256]{2,1,0:T(8,128)(2,1)} %bitcast.11, bf16[40,256]{1,0:T(8,128)(2,1)S(1)} %collective-permute-done.west_ref, bf16[40,256]{1,0:T(8,128)(2,1)S(1)} %collective-permute-done.1.east_ref, ...), custom_call_target="tpu_custom_call" | custom-call | flops 2264924160 | bytes 8388608 | tf_op jit(solution)/shard_map/encode/pallas_call | solution.py:277
  26.8 1.2 %collective-permute-start.8 = (bf16[8,90,128]{2,1,0:T(8,128)(2,1)S(1)}, bf16[8,90,128]{2,1,0:T(8,128)(2,1)S(1)}, u32[]{:S(2)}, u32[]{:S(2)}) collective-permute-start(bf16[8,90,128]{2,1,0:T(8,128)(2,1)S(1)} %encode.5.refs_4_), channel_id=1, source_target_pairs={{0,2},{1,3},{2,0},{3,1},{4,6},{5,7},{6,4},{7,5},{8,10},{9,11},{10,... | collective-permute-start | bytes 552968 | tf_op jit(solution)/shard_map/ppermute | solution.py:462
  28.1 0.3 collective-permute-start.7
  28.4 0.7 %collective-permute-start.3 = (bf16[8,90,128]{2,1,0:T(8,128)(2,1)S(1)}, bf16[8,90,128]{2,1,0:T(8,128)(2,1)S(1)}, u32[]{:S(2)}, u32[]{:S(2)}) collective-permute-start(bf16[8,90,128]{2,1,0:T(8,128)(2,1)S(1)} %get-tuple-element.24.refs_0_), channel_id=1, source_target_pairs={{0,2},{1,3},{2,0},{3,1},{4,6},{5,7},{6,4},{7,5},{8,10},{9,11},{10,... | collective-permute-start | bytes 552968 | tf_op jit(solution)/shard_map/ppermute | solution.py:462
  29.0 0.0 collective-permute-done.4.refs_0_
  29.0 0.4 collective-permute-start.2
  29.4 0.0 collective-permute-done.5.refs_1_
  29.4 7.8 %encode.4.refs_8_ = bf16[6,90,128]{2,1,0:T(8,128)(2,1)S(1)} custom-call(s32[3]{0:T(128)S(1)} %copy-done.3, bf16[180,40,256]{2,1,0:T(8,128)(2,1)} %bitcast.12, bf16[40,256]{1,0:T(8,128)(2,1)S(1)} %collective-permute-done.west_ref, bf16[40,256]{1,0:T(8,128)(2,1)S(1)} %collective-permute-done.1.east_ref, ...), custom_call_target="tpu_custom_call" | custom-call | flops 2264924160 | bytes 8388608 | tf_op jit(solution)/shard_map/encode/pallas_call | solution.py:277
  37.2 0.0 collective-permute-done.8.refs_6_
  37.2 0.2 collective-permute-start.9
  37.4 0.0 collective-permute-done.3.refs_2_
  37.4 1.0 %collective-permute-start.6 = (bf16[8,90,128]{2,1,0:T(8,128)(2,1)S(1)}, bf16[8,90,128]{2,1,0:T(8,128)(2,1)S(1)}, u32[]{:S(2)}, u32[]{:S(2)}) collective-permute-start(bf16[8,90,128]{2,1,0:T(8,128)(2,1)S(1)} %collective-permute-done.3.refs_2_), channel_id=1, source_target_pairs={{0,1},{1,0},{2,3},{3,2},{4,5},{5,4},{6,7},{7,6},{8,9},{9,8},{10,11... | collective-permute-start | bytes 552968 | tf_op jit(solution)/shard_map/ppermute | solution.py:468
  38.4 1.0 %collective-permute-start.12 = (bf16[6,90,128]{2,1,0:T(8,128)(2,1)S(1)}, bf16[6,90,128]{2,1,0:T(8,128)(2,1)S(1)}, u32[]{:S(2)}, u32[]{:S(2)}) collective-permute-start(bf16[6,90,128]{2,1,0:T(8,128)(2,1)S(1)} %encode.4.refs_8_), channel_id=1, source_target_pairs={{0,3},{1,2},{2,1},{3,0},{4,7},{5,6},{6,5},{7,4},{8,11},{9,10},{10,... | collective-permute-start | bytes 414728 | tf_op jit(solution)/shard_map/ppermute | solution.py:465
  39.5 0.0 collective-permute-done.7.refs_5_
  39.5 0.3 collective-permute-start.11
  39.8 0.0 collective-permute-done.2.refs_1_
  39.8 0.8 %collective-permute-start.10 = (bf16[6,90,128]{2,1,0:T(8,128)(2,1)S(1)}, bf16[6,90,128]{2,1,0:T(8,128)(2,1)S(1)}, u32[]{:S(2)}, u32[]{:S(2)}) collective-permute-start(bf16[6,90,128]{2,1,0:T(8,128)(2,1)S(1)} %encode.4.refs_8_), channel_id=1, source_target_pairs={{0,1},{1,0},{2,3},{3,2},{4,5},{5,4},{6,7},{7,6},{8,9},{9,8},{10,11... | collective-permute-start | bytes 414728 | tf_op jit(solution)/shard_map/ppermute | solution.py:463
  40.6 0.0 collective-permute-done.9.refs_7_
  40.6 0.0 collective-permute-done.6.refs_3_
  40.6 7.1 %heads.2.refs_15_ = bf16[2,20,360,128]{3,2,1,0:T(8,128)(2,1)} custom-call(s32[3]{0:T(128)S(1)} %copy-done.3, bf16[8,90,128]{2,1,0:T(8,128)(2,1)S(1)} %get-tuple-element.24.refs_0_, bf16[8,90,128]{2,1,0:T(8,128)(2,1)S(1)} %collective-permute-done.2.refs_1_, bf16[8,90,128]{2,1,0:T(8,128)(2,1)S(1)} %collective-permute-done.3.refs_2_, ...), custom_call_target="tpu_custom_call" | custom-call | flops 3344302080 | bytes 25165824 | tf_op jit(solution)/shard_map/heads/pallas_call | solution.py:389
  47.7 5.2 %heads.3 = bf16[2,20,360,128]{3,2,1,0:T(8,128)(2,1)} custom-call(s32[3]{0:T(128)S(1)} %copy-done.3, bf16[8,90,128]{2,1,0:T(8,128)(2,1)S(1)} %get-tuple-element.24.refs_0_, bf16[8,90,128]{2,1,0:T(8,128)(2,1)S(1)} %collective-permute-done.2.refs_1_, bf16[8,90,128]{2,1,0:T(8,128)(2,1)S(1)} %collective-permute-done.3.refs_2_, ...), custom_call_target="tpu_custom_call", output_to_operand_aliasing={{}: (16, {})} | custom-call | flops 2229534720 | bytes 16777216 | tf_op jit(solution)/shard_map/heads/pallas_call | solution.py:389
  (13 shorter events, 0.0 us)
Async XLA Ops:
  0.0 14.2 %copy-start.4 = (bf16[256,128]{1,0:T(8,128)(2,1)S(1)}, bf16[256,128]{1,0:T(8,128)(2,1)}, u32[]{:S(2)}) copy-start(bf16[256,128]{1,0:T(8,128)(2,1)} %refs_1_.3) | copy-start | bytes 196612
  0.8 5.5 %collective-permute-start.1 = (bf16[40,256]{1,0:T(8,128)(2,1)S(1)}, bf16[40,256]{1,0:T(8,128)(2,1)S(1)}, u32[]{:S(2)}, u32[]{:S(2)}) collective-permute-start(bf16[40,256]{1,0:T(8,128)(2,1)S(1)} %get-tuple-element.33), channel_id=1, source_target_pairs={{1,0},{2,1},{3,2},{0,3},{5,4},{6,5},{7,6},{4,7},{9,8},{10,9},{11,1... | collective-permute-start | bytes 61448 | tf_op jit(solution)/shard_map/ppermute | solution.py:435
  1.5 4.8 %collective-permute-start = (bf16[40,256]{1,0:T(8,128)(2,1)S(1)}, bf16[40,256]{1,0:T(8,128)(2,1)S(1)}, u32[]{:S(2)}, u32[]{:S(2)}) collective-permute-start(bf16[40,256]{1,0:T(8,128)(2,1)S(1)} %get-tuple-element.34), channel_id=1, source_target_pairs={{0,1},{1,2},{2,3},{3,0},{4,5},{5,6},{6,7},{7,4},{8,9},{9,10},{10,1... | collective-permute-start | bytes 61448 | tf_op jit(solution)/shard_map/ppermute | solution.py:434
  3.2 11.0 %copy-start.3 = (s32[3]{0:T(128)S(1)}, s32[3]{0:T(128)}, u32[]{:S(2)}) copy-start(s32[3]{0:T(128)} %pad_add_fusion.meta_ref) | copy-start | bytes 40
  8.0 21.1 %collective-permute-start.4 = (bf16[3,182,256]{2,1,0:T(8,128)(2,1)S(1)}, bf16[3,182,256]{2,1,0:T(8,128)(2,1)S(1)}, u32[]{:S(2)}, u32[]{:S(2)}) collective-permute-start(bf16[3,182,256]{2,1,0:T(8,128)(2,1)S(1)} %get-tuple-element.25), channel_id=1, source_target_pairs={{0,4},{4,8},{8,12},{12,16},{16,20},{20,24},{24,28},{1,5},{5,9},{9,... | collective-permute-start | bytes 838664 | tf_op jit(solution)/shard_map/ppermute | solution.py:443
  11.1 18.3 %collective-permute-start.5 = (bf16[3,182,256]{2,1,0:T(8,128)(2,1)S(1)}, bf16[3,182,256]{2,1,0:T(8,128)(2,1)S(1)}, u32[]{:S(2)}, u32[]{:S(2)}) collective-permute-start(bf16[3,182,256]{2,1,0:T(8,128)(2,1)S(1)} %get-tuple-element.26), channel_id=1, source_target_pairs={{4,0},{8,4},{12,8},{16,12},{20,16},{24,20},{28,24},{5,1},{9,5},{13... | collective-permute-start | bytes 838664 | tf_op jit(solution)/shard_map/ppermute | solution.py:444
  26.8 10.3 %collective-permute-start.8 = (bf16[8,90,128]{2,1,0:T(8,128)(2,1)S(1)}, bf16[8,90,128]{2,1,0:T(8,128)(2,1)S(1)}, u32[]{:S(2)}, u32[]{:S(2)}) collective-permute-start(bf16[8,90,128]{2,1,0:T(8,128)(2,1)S(1)} %encode.5.refs_4_), channel_id=1, source_target_pairs={{0,2},{1,3},{2,0},{3,1},{4,6},{5,7},{6,4},{7,5},{8,10},{9,11},{10,... | collective-permute-start | bytes 552968 | tf_op jit(solution)/shard_map/ppermute | solution.py:462
  28.1 11.4 %collective-permute-start.7 = (bf16[8,90,128]{2,1,0:T(8,128)(2,1)S(1)}, bf16[8,90,128]{2,1,0:T(8,128)(2,1)S(1)}, u32[]{:S(2)}, u32[]{:S(2)}) collective-permute-start(bf16[8,90,128]{2,1,0:T(8,128)(2,1)S(1)} %encode.5.refs_4_), channel_id=1, source_target_pairs={{0,1},{1,0},{2,3},{3,2},{4,5},{5,4},{6,7},{7,6},{8,9},{9,8},{10,11... | collective-permute-start | bytes 552968 | tf_op jit(solution)/shard_map/ppermute | solution.py:463
  28.3 12.3 %copy-start = (bf16[1152,256]{1,0:T(8,128)(2,1)S(1)}, bf16[1152,256]{1,0:T(8,128)(2,1)}, u32[]{:S(2)}) copy-start(bf16[1152,256]{1,0:T(8,128)(2,1)} %get-tuple-element.30.refs_8_.refs_12_) | copy-start | bytes 1769476
  28.3 12.3 %copy-start.1 = (bf16[368,368]{1,0:T(8,128)(2,1)S(1)}, bf16[368,368]{1,0:T(8,128)(2,1)}, u32[]{:S(2)}) copy-start(bf16[368,368]{1,0:T(8,128)(2,1)} %get-tuple-element.32.refs_10_.refs_14_) | copy-start | bytes 812548
  28.4 12.3 %copy-start.2 = (f32[8,256]{1,0:T(8,128)S(1)}, f32[8,256]{1,0:T(8,128)}, u32[]{:S(2)}) copy-start(f32[8,256]{1,0:T(8,128)} %get-tuple-element.31.refs_9_.refs_13_) | copy-start | bytes 24580
  28.4 9.1 %collective-permute-start.3 = (bf16[8,90,128]{2,1,0:T(8,128)(2,1)S(1)}, bf16[8,90,128]{2,1,0:T(8,128)(2,1)S(1)}, u32[]{:S(2)}, u32[]{:S(2)}) collective-permute-start(bf16[8,90,128]{2,1,0:T(8,128)(2,1)S(1)} %get-tuple-element.24.refs_0_), channel_id=1, source_target_pairs={{0,2},{1,3},{2,0},{3,1},{4,6},{5,7},{6,4},{7,5},{8,10},{9,11},{10,... | collective-permute-start | bytes 552968 | tf_op jit(solution)/shard_map/ppermute | solution.py:462
  29.0 10.8 %collective-permute-start.2 = (bf16[8,90,128]{2,1,0:T(8,128)(2,1)S(1)}, bf16[8,90,128]{2,1,0:T(8,128)(2,1)S(1)}, u32[]{:S(2)}, u32[]{:S(2)}) collective-permute-start(bf16[8,90,128]{2,1,0:T(8,128)(2,1)S(1)} %get-tuple-element.24.refs_0_), channel_id=1, source_target_pairs={{0,1},{1,0},{2,3},{3,2},{4,5},{5,4},{6,7},{7,6},{8,9},{9,8},{10,11... | collective-permute-start | bytes 552968 | tf_op jit(solution)/shard_map/ppermute | solution.py:463
  37.2 3.4 %collective-permute-start.9 = (bf16[8,90,128]{2,1,0:T(8,128)(2,1)S(1)}, bf16[8,90,128]{2,1,0:T(8,128)(2,1)S(1)}, u32[]{:S(2)}, u32[]{:S(2)}) collective-permute-start(bf16[8,90,128]{2,1,0:T(8,128)(2,1)S(1)} %collective-permute-done.8.refs_6_), channel_id=1, source_target_pairs={{0,1},{1,0},{2,3},{3,2},{4,5},{5,4},{6,7},{7,6},{8,9},{9,8},{10,11... | collective-permute-start | bytes 552968 | tf_op jit(solution)/shard_map/ppermute | solution.py:468
  37.4 3.2 %collective-permute-start.6 = (bf16[8,90,128]{2,1,0:T(8,128)(2,1)S(1)}, bf16[8,90,128]{2,1,0:T(8,128)(2,1)S(1)}, u32[]{:S(2)}, u32[]{:S(2)}) collective-permute-start(bf16[8,90,128]{2,1,0:T(8,128)(2,1)S(1)} %collective-permute-done.3.refs_2_), channel_id=1, source_target_pairs={{0,1},{1,0},{2,3},{3,2},{4,5},{5,4},{6,7},{7,6},{8,9},{9,8},{10,11... | collective-permute-start | bytes 552968 | tf_op jit(solution)/shard_map/ppermute | solution.py:468
  38.4 9.2 %collective-permute-start.12 = (bf16[6,90,128]{2,1,0:T(8,128)(2,1)S(1)}, bf16[6,90,128]{2,1,0:T(8,128)(2,1)S(1)}, u32[]{:S(2)}, u32[]{:S(2)}) collective-permute-start(bf16[6,90,128]{2,1,0:T(8,128)(2,1)S(1)} %encode.4.refs_8_), channel_id=1, source_target_pairs={{0,3},{1,2},{2,1},{3,0},{4,7},{5,6},{6,5},{7,4},{8,11},{9,10},{10,... | collective-permute-start | bytes 414728 | tf_op jit(solution)/shard_map/ppermute | solution.py:465
  39.5 8.2 %collective-permute-start.11 = (bf16[6,90,128]{2,1,0:T(8,128)(2,1)S(1)}, bf16[6,90,128]{2,1,0:T(8,128)(2,1)S(1)}, u32[]{:S(2)}, u32[]{:S(2)}) collective-permute-start(bf16[6,90,128]{2,1,0:T(8,128)(2,1)S(1)} %encode.4.refs_8_), channel_id=1, source_target_pairs={{0,2},{1,3},{2,0},{3,1},{4,6},{5,7},{6,4},{7,5},{8,10},{9,11},{10,... | collective-permute-start | bytes 414728 | tf_op jit(solution)/shard_map/ppermute | solution.py:462
  39.8 7.9 %collective-permute-start.10 = (bf16[6,90,128]{2,1,0:T(8,128)(2,1)S(1)}, bf16[6,90,128]{2,1,0:T(8,128)(2,1)S(1)}, u32[]{:S(2)}, u32[]{:S(2)}) collective-permute-start(bf16[6,90,128]{2,1,0:T(8,128)(2,1)S(1)} %encode.4.refs_8_), channel_id=1, source_target_pairs={{0,1},{1,0},{2,3},{3,2},{4,5},{5,4},{6,7},{7,6},{8,9},{9,8},{10,11... | collective-permute-start | bytes 414728 | tf_op jit(solution)/shard_map/ppermute | solution.py:463

commit v8 on v6

--- a/solution.py
+++ b/solution.py
@@ -29,16 +29,19 @@
 
 
 def weights_kernel(
-    meta_ref, ids_ref, we_hbm, wh_hbm, scale_hbm, shift_hbm, z_hbm,
-    g_ref, ws_ref, vec_ref, zs_ref,
-    we_ref, wh_ref, tab, z_ref, sem,
+    meta_ref, ids_ref, x_hbm, we_hbm, wh_hbm, scale_hbm, shift_hbm, z_hbm,
+    g_hbm, ws_ref, vec_ref, zs_ref, edge_ref,
+    g_ref, we_ref, wh_ref, tab, z_ref, near, flat, sem,
 ):
     ch = we_ref.shape[-1]
     head = wh_ref.shape[-1]
     leads = ws_ref.shape[1] // head
     cols = z_ref.shape[0]
+    xcols, rows, _ = x_hbm.shape
+    reach = edge_ref.shape[1]
     ids = [ids_ref[meta_ref[2] * leads + lead] for lead in range(leads)]
-    copies = [(we_hbm, we_ref), (z_hbm, z_ref), (wh_hbm, wh_ref)]
+    copies = [(we_hbm, we_ref), (x_hbm.at[:, :8], near.at[0]), (x_hbm.at[:, rows - 8 :], near.at[1])]
+    copies += [(z_hbm, z_ref), (wh_hbm, wh_ref)]
     for lead in range(leads):
         block = pl.multiple_of((ids[lead] // 8) * 8, 8)
         copies.append((scale_hbm.at[pl.ds(block, 8)], tab.at[lead, 0]))
@@ -56,7 +59,18 @@
         g_ref[1, at] = (half + 0.5 * w[1]).astype(BF)
         g_ref[2, at] = (half - 0.5 * w[1]).astype(BF)
         g_ref[3, at] = we_ref[dr, 2]
-    for c in copies[1:]:
+    made = pltpu.make_async_copy(g_ref, g_hbm, sem.at[len(copies)])
+    made.start()
+    for k in range(2):
+        copies[1 + k].wait()
+        parts = []
+        for j in range(ch // 128):
+            flat[k, j] = near[k, :, :, j * 128 : (j + 1) * 128].astype(F32).reshape(xcols * 8, 128)
+            first = 0 if k == 0 else 8 - reach
+            parts.append([flat[k, j, pl.ds(first + i, xcols, stride=8), :] for i in range(reach)])
+        for i in range(reach):
+            edge_ref[k, i] = jnp.concatenate([p[i] for p in parts], axis=1).astype(BF)
+    for c in copies[3:]:
         c.wait()
     zs_ref[:cols, :cols] = z_ref[...] * jnp.asarray(0.5, BF)
     for lead in range(leads):
@@ -76,65 +90,65 @@
                 ws_ref[at : at + head, lanes] = (w * gain_t).astype(BF)
                 total = total + w * shift_t
             vec_ref[BIAS + dr : BIAS + dr + 1, lanes] = jnp.sum(total, axis=0, keepdims=True)
-
-
-def prepare(meta, ids, w_enc, w_head, scale, shift, z, leads):
+    made.wait()
+
+
+def prepare(meta, ids, x, w_enc, w_head, scale, shift, z, leads, reach):
     ch, head, cols = w_enc.shape[-1], w_head.shape[-1], z.shape[0]
+    xcols = x.shape[0]
     wide = up_to(cols, 16)
     vmem = pl.BlockSpec(memory_space=pltpu.VMEM)
     smem = pl.BlockSpec(memory_space=pltpu.SMEM)
     hbm = pl.BlockSpec(memory_space=pltpu.HBM)
+    form = (4, 3 * ch, ch)
     return pl.pallas_call(
         weights_kernel,
-        in_specs=[smem, smem] + [hbm] * 5,
-        out_specs=[vmem] * 4,
+        in_specs=[smem, smem] + [hbm] * 6,
+        out_specs=[hbm] + [vmem] * 4,
         out_shape=[
-            jax.ShapeDtypeStruct((4, 3 * ch, ch), BF),
+            jax.ShapeDtypeStruct(form, BF),
             jax.ShapeDtypeStruct((9 * head, leads * head), BF),
             jax.ShapeDtypeStruct((8, leads * head), F32),
             jax.ShapeDtypeStruct((wide, wide), BF),
+            jax.ShapeDtypeStruct((2, reach, xcols, ch), BF),
         ],
         scratch_shapes=[
+            pltpu.VMEM(form, BF),
             pltpu.VMEM(w_enc.shape, BF),
             pltpu.VMEM(w_head.shape, BF),
             pltpu.VMEM((leads, 2, 8, head), F32),
             pltpu.VMEM(z.shape, BF),
-            pltpu.SemaphoreType.DMA((3 + 2 * leads,)),
+            pltpu.VMEM((2, xcols, 8, ch), BF),
+            pltpu.VMEM((2, ch // 128, xcols * 8, 128), F32),
+            pltpu.SemaphoreType.DMA((6 + 2 * leads,)),
         ],
         compiler_params=params(58),
+        cost_estimate=pl.CostEstimate(flops=1 << 31, transcendentals=0, bytes_accessed=12 * MIB),
         name="weights",
-    )(meta, ids, w_enc, w_head, scale, shift, z)
-
-
-def slabs_kernel(first_ref, last_ref, west_ref, east_ref, up_ref, dn_ref, flat):
-    xcols, _, ch = first_ref.shape
+    )(meta, ids, x, w_enc, w_head, scale, shift, z)
+
+
+def slabs_kernel(edge_ref, west_ref, east_ref, up_ref, dn_ref):
     rows = west_ref.shape[0]
     reach = up_ref.shape[0]
-    for k, (edge, slab, start, r) in enumerate(
-        ((first_ref, dn_ref, 0, 0), (last_ref, up_ref, 8 - reach, rows - reach))
-    ):
-        parts = []
-        for j in range(ch // 128):
-            lanes = slice(j * 128, (j + 1) * 128)
-            flat[k, j] = edge[:, :, lanes].astype(F32).reshape(xcols * 8, 128)
-            parts.append([flat[k, j, pl.ds(start + i, xcols, stride=8), :] for i in range(reach)])
+    for k, (slab, r) in enumerate(((dn_ref, 0), (up_ref, rows - reach))):
         for i in range(reach):
-            row = jnp.concatenate([p[i] for p in parts], axis=1).astype(BF)
-            slab[i] = jnp.concatenate([west_ref[r + i : r + i + 1, :], row, east_ref[r + i : r + i + 1, :]], axis=0)
-
-
-def row_slabs(x, west, east, reach):
-    xcols, rows, ch = x.shape
+            ends = [side[r + i : r + i + 1, :] for side in (west_ref, east_ref)]
+            slab[i] = jnp.concatenate([ends[0], edge_ref[k, i], ends[1]], axis=0)
+
+
+def row_slabs(edge, west, east):
+    _, reach, xcols, ch = edge.shape
     vmem = pl.BlockSpec(memory_space=pltpu.VMEM)
     return pl.pallas_call(
         slabs_kernel,
-        in_specs=[vmem] * 4,
+        in_specs=[vmem] * 3,
         out_specs=[vmem] * 2,
         out_shape=[jax.ShapeDtypeStruct((reach, xcols + 2, ch), BF)] * 2,
-        scratch_shapes=[pltpu.VMEM((2, ch // 128, xcols * 8, 128), F32)],
-        compiler_params=params(16),
+        compiler_params=params(12),
+        cost_estimate=pl.CostEstimate(flops=1 << 32, transcendentals=0, bytes_accessed=12 * MIB),
         name="slabs",
-    )(x[:, :8], x[:, rows - 8 :], west, east)
+    )(edge, west, east)
 
 
 def encoder_kernel(
@@ -395,8 +409,10 @@
     meta = jnp.stack(
         [lat_at == 0, lat_at == lat - 1, lon_at]
     ).astype(jnp.int32)
-    g, ws, vec, zs = prepare(meta, lead_ids, w_enc, w_head, film_scale, film_shift, zonal_mix, leads)
-    up, dn = row_slabs(tile, west, east, reach)
+    g, ws, vec, zs, edge = prepare(
+        meta, lead_ids, tile, w_enc, w_head, film_scale, film_shift, zonal_mix, leads, reach
+    )
+    up, dn = row_slabs(edge, west, east)
     above = lax.ppermute(up, "lat", lat_up)
     below = lax.ppermute(dn, "lat", lat_dn)
 

time: 51.1 us -> 47.9 us (0.937)
  local copies, waits for them, and re-layouts: 5.69 us -> 1.82 us
    unnamed x14 -> x16, local copies, waits for them, and re-layouts: 3.47 us -> 1.08 us
    slice x1 -> x0, local copies, waits for them, and re-layouts: 1.45 us -> none  [row_slabs(): x[:, rows - 8:]]
  transfers between devices with their start and end apart: 13 -> 13, of which waited for: 1 -> 2; matrix products, arithmetic and copies ran while one was open for 4% -> 1% of each run, Pallas kernels for 47% -> 53%
where the time goes in v8:
time: 47.9 us; the launch traced here: 47.7 us
  Pallas kernels  30.4 us (63%)
  starting transfers between devices  14 us (29%)
  local copies, waits for them, and re-layouts  1.82 us (4%)
  other arithmetic  0.66 us (1%)
    pallas_call x3, Pallas kernels, encode(): pl.pallas_call(functools.partial(encoder_kernel, first=first, group=group...  13.4 us
    pallas_call x2, Pallas kernels, forecast_heads(): pl.pallas_call(functools.partial(head_kernel, chunks=chunks, blocks=block...  12.3 us
    pallas_call x1, Pallas kernels, prepare(): pl.pallas_call(weights_kernel, in_specs=[smem, smem] + [hbm] * 6, out_spe...  4.63 us
    ppermute x1, starting transfers between devices, shards(): above = lax.ppermute(up, 'lat', lat_up)  3.41 us
    ppermute x1, starting transfers between devices, shards(): below = lax.ppermute(dn, 'lat', lat_dn)  3.07 us
    ppermute x3, starting transfers between devices, shards(): across = lax.ppermute(own, 'lon', swap(lon, 2))  2.75 us
    ppermute x1, starting transfers between devices, shards(): west = lax.ppermute(tile[-1], 'lon', lon_up)  1.1 us
    unnamed x16, local copies, waits for them, and re-layouts  1.08 us
  transfers between devices with their start and end apart: 13, of which 2 were waited for; matrix products, arithmetic and copies ran while one was open for 1% of the time, Pallas kernels for 53%

profile of v8, /device:TPU:25, one launch (start us, length us, event | category | flops | bytes accessed | tf_op | source)
XLA Modules:
  0.0 47.7 jit_solution(10154876484095785115)
XLA Ops:
  0.0 0.7 %slice_bitcast_fusion = (bf16[40,256]{1,0:T(8,128)(2,1)S(1)}, bf16[40,256]{1,0:T(8,128)(2,1)S(1)}) fusion(bf16[180,40,256]{2,1,0:T(8,128)(2,1)} %bitcast.8), kind=kLoop, calls=%fused_computation | loop fusion | bytes 81920 | tf_op jit(solution)/shard_map/squeeze | solution.py:407
  0.7 0.7 %collective-permute-start.1 = (bf16[40,256]{1,0:T(8,128)(2,1)S(1)}, bf16[40,256]{1,0:T(8,128)(2,1)S(1)}, u32[]{:S(2)}, u32[]{:S(2)}) collective-permute-start(bf16[40,256]{1,0:T(8,128)(2,1)S(1)} %get-tuple-element.23), channel_id=1, source_target_pairs={{1,0},{2,1},{3,2},{0,3},{5,4},{6,5},{7,6},{4,7},{9,8},{10,9},{11,1... | collective-permute-start | bytes 61448 | tf_op jit(solution)/shard_map/ppermute | solution.py:407
  1.4 1.1 %collective-permute-start = (bf16[40,256]{1,0:T(8,128)(2,1)S(1)}, bf16[40,256]{1,0:T(8,128)(2,1)S(1)}, u32[]{:S(2)}, u32[]{:S(2)}) collective-permute-start(bf16[40,256]{1,0:T(8,128)(2,1)S(1)} %get-tuple-element.24), channel_id=1, source_target_pairs={{0,1},{1,2},{2,3},{3,0},{4,5},{5,6},{6,7},{7,4},{8,9},{9,10},{10,1... | collective-permute-start | bytes 61448 | tf_op jit(solution)/shard_map/ppermute | solution.py:406
  2.5 0.7 %pad_add_fusion.meta_ref = s32[3]{0:T(128)} fusion(s32[1]{0:T(128)} %bitcast.2, s32[1]{0:T(128)} %bitcast.1, s32[1]{0:T(128)} %bitcast), kind=kLoop, calls=%fused_computation.2 | loop fusion | flops 6 | bytes 24 | tf_op jit(solution)/shard_map/stack | solution.py:409
  3.2 4.6 %weights.1 = (bf16[4,768,256]{2,1,0:T(8,128)(2,1)}, bf16[1152,256]{1,0:T(8,128)(2,1)}, f32[8,256]{1,0:T(8,128)}, bf16[368,368]{1,0:T(8,128)(2,1)}, bf16[2,3,180,256]{3,2,1,0:T(8,128)(2,1)}) custom-call(s32[3]{0:T(128)} %pad_add_fusion.meta_ref, s32[8]{0:T(128)} %ids_ref.1, bf16[180,40,256]{2,1,0:T(8,128)(2,1)} %bitcast.9, bf16[3,3,256,256]{3,2,1,0:T(8,128)(2,1)} %we_hbm.1, ...), custom_call_target="tpu_custom_call" | custom-call | flops 2147483648 | bytes 12582912 | tf_op jit(solution)/shard_map/weights/pallas_call | solution.py:104
  7.8 0.0 collective-permute-done.west_ref
  7.9 1.0 %copy-done.7 = bf16[2,3,180,256]{3,2,1,0:T(8,128)(2,1)S(1)} copy-done((bf16[2,3,180,256]{3,2,1,0:T(8,128)(2,1)S(1)}, bf16[2,3,180,256]{3,2,1,0:T(8,128)(2,1)}, u32[]{:S(2)}) %copy-start.7) | copy-done | bytes 552984
  8.9 0.1 slabs.1
  9.0 3.4 %collective-permute-start.4 = (bf16[3,182,256]{2,1,0:T(8,128)(2,1)S(1)}, bf16[3,182,256]{2,1,0:T(8,128)(2,1)S(1)}, u32[]{:S(2)}, u32[]{:S(2)}) collective-permute-start(bf16[3,182,256]{2,1,0:T(8,128)(2,1)S(1)} %get-tuple-element.16), channel_id=1, source_target_pairs={{0,4},{4,8},{8,12},{12,16},{16,20},{20,24},{24,28},{1,5},{5,9},{9,... | collective-permute-start | bytes 838664 | tf_op jit(solution)/shard_map/ppermute | solution.py:416
  12.5 3.1 %collective-permute-start.5 = (bf16[3,182,256]{2,1,0:T(8,128)(2,1)S(1)}, bf16[3,182,256]{2,1,0:T(8,128)(2,1)S(1)}, u32[]{:S(2)}, u32[]{:S(2)}) collective-permute-start(bf16[3,182,256]{2,1,0:T(8,128)(2,1)S(1)} %get-tuple-element.17), channel_id=1, source_target_pairs={{4,0},{8,4},{12,8},{16,12},{20,16},{24,20},{28,24},{5,1},{9,5},{13... | collective-permute-start | bytes 838664 | tf_op jit(solution)/shard_map/ppermute | solution.py:417
  15.6 4.3 %encode.3.refs_0_ = bf16[8,90,128]{2,1,0:T(8,128)(2,1)S(1)} custom-call(s32[3]{0:T(128)S(1)} %copy-done.3, bf16[180,40,256]{2,1,0:T(8,128)(2,1)S(1)} %bitcast.10, bf16[40,256]{1,0:T(8,128)(2,1)S(1)} %collective-permute-done.west_ref, bf16[40,256]{1,0:T(8,128)(2,1)S(1)} %collective-permute-done.1.east_ref, bf16[4,768,256]{2,1,0:T(8,128)(2,1)S(1)} %copy-done.6, ...), custom_call_target="tpu_custom_call" | custom-call | flops 2264924160 | bytes 8388608 | tf_op jit(solution)/shard_map/encode/pallas_call | solution.py:251
  19.8 1.2 %collective-permute-start.3 = (bf16[8,90,128]{2,1,0:T(8,128)(2,1)S(1)}, bf16[8,90,128]{2,1,0:T(8,128)(2,1)S(1)}, u32[]{:S(2)}, u32[]{:S(2)}) collective-permute-start(bf16[8,90,128]{2,1,0:T(8,128)(2,1)S(1)} %encode.3.refs_0_), channel_id=1, source_target_pairs={{0,2},{1,3},{2,0},{3,1},{4,6},{5,7},{6,4},{7,5},{8,10},{9,11},{10,... | collective-permute-start | bytes 552968 | tf_op jit(solution)/shard_map/ppermute | solution.py:431
  21.0 0.3 collective-permute-start.2
  21.3 4.2 %encode.5.refs_4_ = bf16[8,90,128]{2,1,0:T(8,128)(2,1)S(1)} custom-call(s32[3]{0:T(128)S(1)} %copy-done.3, bf16[180,40,256]{2,1,0:T(8,128)(2,1)S(1)} %bitcast.11, bf16[40,256]{1,0:T(8,128)(2,1)S(1)} %collective-permute-done.west_ref, bf16[40,256]{1,0:T(8,128)(2,1)S(1)} %collective-permute-done.1.east_ref, bf16[4,768,256]{2,1,0:T(8,128)(2,1)S(1)} %copy-done.6, ...), custom_call_target="tpu_custom_call" | custom-call | flops 2264924160 | bytes 8388608 | tf_op jit(solution)/shard_map/encode/pallas_call | solution.py:251
  25.6 0.7 %collective-permute-start.8 = (bf16[8,90,128]{2,1,0:T(8,128)(2,1)S(1)}, bf16[8,90,128]{2,1,0:T(8,128)(2,1)S(1)}, u32[]{:S(2)}, u32[]{:S(2)}) collective-permute-start(bf16[8,90,128]{2,1,0:T(8,128)(2,1)S(1)} %encode.5.refs_4_), channel_id=1, source_target_pairs={{0,2},{1,3},{2,0},{3,1},{4,6},{5,7},{6,4},{7,5},{8,10},{9,11},{10,... | collective-permute-start | bytes 552968 | tf_op jit(solution)/shard_map/ppermute | solution.py:431
  26.3 0.0 collective-permute-done.4.refs_0_
  26.3 0.3 collective-permute-start.7
  26.6 0.2 collective-permute-done.5.refs_1_
  26.9 4.9 %encode.4.refs_8_ = bf16[6,90,128]{2,1,0:T(8,128)(2,1)S(1)} custom-call(s32[3]{0:T(128)S(1)} %copy-done.3, bf16[180,40,256]{2,1,0:T(8,128)(2,1)S(1)} %bitcast.12, bf16[40,256]{1,0:T(8,128)(2,1)S(1)} %collective-permute-done.west_ref, bf16[40,256]{1,0:T(8,128)(2,1)S(1)} %collective-permute-done.1.east_ref, ...), custom_call_target="tpu_custom_call" | custom-call | flops 2264924160 | bytes 8388608 | tf_op jit(solution)/shard_map/encode/pallas_call | solution.py:251
  31.8 0.2 collective-permute-done.8.refs_6_
  31.9 0.0 collective-permute-done.3.refs_2_
  31.9 1.0 %collective-permute-start.6 = (bf16[8,90,128]{2,1,0:T(8,128)(2,1)S(1)}, bf16[8,90,128]{2,1,0:T(8,128)(2,1)S(1)}, u32[]{:S(2)}, u32[]{:S(2)}) collective-permute-start(bf16[8,90,128]{2,1,0:T(8,128)(2,1)S(1)} %collective-permute-done.3.refs_2_), channel_id=1, source_target_pairs={{0,1},{1,0},{2,3},{3,2},{4,5},{5,4},{6,7},{7,6},{8,9},{9,8},{10,11... | collective-permute-start | bytes 552968 | tf_op jit(solution)/shard_map/ppermute | solution.py:437
  33.0 0.0 collective-permute-start.9
  33.0 1.1 %collective-permute-start.12 = (bf16[6,90,128]{2,1,0:T(8,128)(2,1)S(1)}, bf16[6,90,128]{2,1,0:T(8,128)(2,1)S(1)}, u32[]{:S(2)}, u32[]{:S(2)}) collective-permute-start(bf16[6,90,128]{2,1,0:T(8,128)(2,1)S(1)} %encode.4.refs_8_), channel_id=1, source_target_pairs={{0,3},{1,2},{2,1},{3,0},{4,7},{5,6},{6,5},{7,4},{8,11},{9,10},{10,... | collective-permute-start | bytes 414728 | tf_op jit(solution)/shard_map/ppermute | solution.py:434
  34.1 0.0 collective-permute-done.2.refs_1_
  34.1 0.8 %collective-permute-start.11 = (bf16[6,90,128]{2,1,0:T(8,128)(2,1)S(1)}, bf16[6,90,128]{2,1,0:T(8,128)(2,1)S(1)}, u32[]{:S(2)}, u32[]{:S(2)}) collective-permute-start(bf16[6,90,128]{2,1,0:T(8,128)(2,1)S(1)} %encode.4.refs_8_), channel_id=1, source_target_pairs={{0,2},{1,3},{2,0},{3,1},{4,6},{5,7},{6,4},{7,5},{8,10},{9,11},{10,... | collective-permute-start | bytes 414728 | tf_op jit(solution)/shard_map/ppermute | solution.py:431
  34.9 0.0 collective-permute-done.7.refs_5_
  34.9 0.3 collective-permute-start.10
  35.1 0.0 collective-permute-done.6.refs_3_
  35.1 0.0 collective-permute-done.9.refs_7_
  35.2 7.1 %heads.2.refs_15_ = bf16[2,20,360,128]{3,2,1,0:T(8,128)(2,1)} custom-call(s32[3]{0:T(128)S(1)} %copy-done.3, bf16[8,90,128]{2,1,0:T(8,128)(2,1)S(1)} %encode.3.refs_0_, bf16[8,90,128]{2,1,0:T(8,128)(2,1)S(1)} %collective-permute-done.2.refs_1_, bf16[8,90,128]{2,1,0:T(8,128)(2,1)S(1)} %collective-permute-done.3.refs_2_, ...), custom_call_target="tpu_custom_call" | custom-call | flops 3344302080 | bytes 25165824 | tf_op jit(solution)/shard_map/heads/pallas_call | solution.py:361
  42.3 5.2 %heads.3 = bf16[2,20,360,128]{3,2,1,0:T(8,128)(2,1)} custom-call(s32[3]{0:T(128)S(1)} %copy-done.3, bf16[8,90,128]{2,1,0:T(8,128)(2,1)S(1)} %encode.3.refs_0_, bf16[8,90,128]{2,1,0:T(8,128)(2,1)S(1)} %collective-permute-done.2.refs_1_, bf16[8,90,128]{2,1,0:T(8,128)(2,1)S(1)} %collective-permute-done.3.refs_2_, ...), custom_call_target="tpu_custom_call", output_to_operand_aliasing={{}: (16, {})} | custom-call | flops 2229534720 | bytes 16777216 | tf_op jit(solution)/shard_map/heads/pallas_call | solution.py:361
  (19 shorter events, 0.0 us)
Async XLA Ops:
  0.7 7.1 %collective-permute-start.1 = (bf16[40,256]{1,0:T(8,128)(2,1)S(1)}, bf16[40,256]{1,0:T(8,128)(2,1)S(1)}, u32[]{:S(2)}, u32[]{:S(2)}) collective-permute-start(bf16[40,256]{1,0:T(8,128)(2,1)S(1)} %get-tuple-element.23), channel_id=1, source_target_pairs={{1,0},{2,1},{3,2},{0,3},{5,4},{6,5},{7,6},{4,7},{9,8},{10,9},{11,1... | collective-permute-start | bytes 61448 | tf_op jit(solution)/shard_map/ppermute | solution.py:407
  1.4 6.4 %collective-permute-start = (bf16[40,256]{1,0:T(8,128)(2,1)S(1)}, bf16[40,256]{1,0:T(8,128)(2,1)S(1)}, u32[]{:S(2)}, u32[]{:S(2)}) collective-permute-start(bf16[40,256]{1,0:T(8,128)(2,1)S(1)} %get-tuple-element.24), channel_id=1, source_target_pairs={{0,1},{1,2},{2,3},{3,0},{4,5},{5,6},{6,7},{7,4},{8,9},{9,10},{10,1... | collective-permute-start | bytes 61448 | tf_op jit(solution)/shard_map/ppermute | solution.py:406
  7.8 1.1 %copy-start.7 = (bf16[2,3,180,256]{3,2,1,0:T(8,128)(2,1)S(1)}, bf16[2,3,180,256]{3,2,1,0:T(8,128)(2,1)}, u32[]{:S(2)}) copy-start(bf16[2,3,180,256]{3,2,1,0:T(8,128)(2,1)} %get-tuple-element.15.edge_ref) | copy-start | bytes 1658884
  8.9 6.6 %copy-start.3 = (s32[3]{0:T(128)S(1)}, s32[3]{0:T(128)}, u32[]{:S(2)}) copy-start(s32[3]{0:T(128)} %pad_add_fusion.meta_ref) | copy-start | bytes 40
  8.9 6.7 %copy-start.4 = (bf16[40,180,256]{2,0,1:T(8,128)(2,1)S(1)}, bf16[40,180,256]{2,0,1:T(8,128)(2,1)}, u32[]{:S(2)}) copy-start(bf16[40,180,256]{2,0,1:T(8,128)(2,1)} %param.8) | copy-start | bytes 11059204
  8.9 6.7 %copy-start.5 = (bf16[256,128]{1,0:T(8,128)(2,1)S(1)}, bf16[256,128]{1,0:T(8,128)(2,1)}, u32[]{:S(2)}) copy-start(bf16[256,128]{1,0:T(8,128)(2,1)} %refs_1_.3) | copy-start | bytes 196612
  8.9 6.7 %copy-start.6 = (bf16[4,768,256]{2,1,0:T(8,128)(2,1)S(1)}, bf16[4,768,256]{2,1,0:T(8,128)(2,1)}, u32[]{:S(2)}) copy-start(bf16[4,768,256]{2,1,0:T(8,128)(2,1)} %get-tuple-element.14.refs_0_.refs_2_) | copy-start | bytes 4718596
  9.0 17.3 %collective-permute-start.4 = (bf16[3,182,256]{2,1,0:T(8,128)(2,1)S(1)}, bf16[3,182,256]{2,1,0:T(8,128)(2,1)S(1)}, u32[]{:S(2)}, u32[]{:S(2)}) collective-permute-start(bf16[3,182,256]{2,1,0:T(8,128)(2,1)S(1)} %get-tuple-element.16), channel_id=1, source_target_pairs={{0,4},{4,8},{8,12},{12,16},{16,20},{20,24},{24,28},{1,5},{5,9},{9,... | collective-permute-start | bytes 838664 | tf_op jit(solution)/shard_map/ppermute | solution.py:416
  12.5 14.4 %collective-permute-start.5 = (bf16[3,182,256]{2,1,0:T(8,128)(2,1)S(1)}, bf16[3,182,256]{2,1,0:T(8,128)(2,1)S(1)}, u32[]{:S(2)}, u32[]{:S(2)}) collective-permute-start(bf16[3,182,256]{2,1,0:T(8,128)(2,1)S(1)} %get-tuple-element.17), channel_id=1, source_target_pairs={{4,0},{8,4},{12,8},{16,12},{20,16},{24,20},{28,24},{5,1},{9,5},{13... | collective-permute-start | bytes 838664 | tf_op jit(solution)/shard_map/ppermute | solution.py:417
  19.8 12.1 %collective-permute-start.3 = (bf16[8,90,128]{2,1,0:T(8,128)(2,1)S(1)}, bf16[8,90,128]{2,1,0:T(8,128)(2,1)S(1)}, u32[]{:S(2)}, u32[]{:S(2)}) collective-permute-start(bf16[8,90,128]{2,1,0:T(8,128)(2,1)S(1)} %encode.3.refs_0_), channel_id=1, source_target_pairs={{0,2},{1,3},{2,0},{3,1},{4,6},{5,7},{6,4},{7,5},{8,10},{9,11},{10,... | collective-permute-start | bytes 552968 | tf_op jit(solution)/shard_map/ppermute | solution.py:431
  21.0 13.0 %collective-permute-start.2 = (bf16[8,90,128]{2,1,0:T(8,128)(2,1)S(1)}, bf16[8,90,128]{2,1,0:T(8,128)(2,1)S(1)}, u32[]{:S(2)}, u32[]{:S(2)}) collective-permute-start(bf16[8,90,128]{2,1,0:T(8,128)(2,1)S(1)} %encode.3.refs_0_), channel_id=1, source_target_pairs={{0,1},{1,0},{2,3},{3,2},{4,5},{5,4},{6,7},{7,6},{8,9},{9,8},{10,11... | collective-permute-start | bytes 552968 | tf_op jit(solution)/shard_map/ppermute | solution.py:432
  25.6 9.6 %copy-start = (bf16[1152,256]{1,0:T(8,128)(2,1)S(1)}, bf16[1152,256]{1,0:T(8,128)(2,1)}, u32[]{:S(2)}) copy-start(bf16[1152,256]{1,0:T(8,128)(2,1)} %get-tuple-element.20.refs_8_.refs_12_) | copy-start | bytes 1769476
  25.6 9.6 %copy-start.1 = (bf16[368,368]{1,0:T(8,128)(2,1)S(1)}, bf16[368,368]{1,0:T(8,128)(2,1)}, u32[]{:S(2)}) copy-start(bf16[368,368]{1,0:T(8,128)(2,1)} %get-tuple-element.22.refs_10_.refs_14_) | copy-start | bytes 812548
  25.6 9.6 %copy-start.2 = (f32[8,256]{1,0:T(8,128)S(1)}, f32[8,256]{1,0:T(8,128)}, u32[]{:S(2)}) copy-start(f32[8,256]{1,0:T(8,128)} %get-tuple-element.21.refs_9_.refs_13_) | copy-start | bytes 24580
  25.6 6.3 %collective-permute-start.8 = (bf16[8,90,128]{2,1,0:T(8,128)(2,1)S(1)}, bf16[8,90,128]{2,1,0:T(8,128)(2,1)S(1)}, u32[]{:S(2)}, u32[]{:S(2)}) collective-permute-start(bf16[8,90,128]{2,1,0:T(8,128)(2,1)S(1)} %encode.5.refs_4_), channel_id=1, source_target_pairs={{0,2},{1,3},{2,0},{3,1},{4,6},{5,7},{6,4},{7,5},{8,10},{9,11},{10,... | collective-permute-start | bytes 552968 | tf_op jit(solution)/shard_map/ppermute | solution.py:431
  26.3 8.5 %collective-permute-start.7 = (bf16[8,90,128]{2,1,0:T(8,128)(2,1)S(1)}, bf16[8,90,128]{2,1,0:T(8,128)(2,1)S(1)}, u32[]{:S(2)}, u32[]{:S(2)}) collective-permute-start(bf16[8,90,128]{2,1,0:T(8,128)(2,1)S(1)} %encode.5.refs_4_), channel_id=1, source_target_pairs={{0,1},{1,0},{2,3},{3,2},{4,5},{5,4},{6,7},{7,6},{8,9},{9,8},{10,11... | collective-permute-start | bytes 552968 | tf_op jit(solution)/shard_map/ppermute | solution.py:432
  31.9 3.2 %collective-permute-start.6 = (bf16[8,90,128]{2,1,0:T(8,128)(2,1)S(1)}, bf16[8,90,128]{2,1,0:T(8,128)(2,1)S(1)}, u32[]{:S(2)}, u32[]{:S(2)}) collective-permute-start(bf16[8,90,128]{2,1,0:T(8,128)(2,1)S(1)} %collective-permute-done.3.refs_2_), channel_id=1, source_target_pairs={{0,1},{1,0},{2,3},{3,2},{4,5},{5,4},{6,7},{7,6},{8,9},{9,8},{10,11... | collective-permute-start | bytes 552968 | tf_op jit(solution)/shard_map/ppermute | solution.py:437
  33.0 2.2 %collective-permute-start.9 = (bf16[8,90,128]{2,1,0:T(8,128)(2,1)S(1)}, bf16[8,90,128]{2,1,0:T(8,128)(2,1)S(1)}, u32[]{:S(2)}, u32[]{:S(2)}) collective-permute-start(bf16[8,90,128]{2,1,0:T(8,128)(2,1)S(1)} %collective-permute-done.8.refs_6_), channel_id=1, source_target_pairs={{0,1},{1,0},{2,3},{3,2},{4,5},{5,4},{6,7},{7,6},{8,9},{9,8},{10,11... | collective-permute-start | bytes 552968 | tf_op jit(solution)/shard_map/ppermute | solution.py:437
  33.0 9.3 %collective-permute-start.12 = (bf16[6,90,128]{2,1,0:T(8,128)(2,1)S(1)}, bf16[6,90,128]{2,1,0:T(8,128)(2,1)S(1)}, u32[]{:S(2)}, u32[]{:S(2)}) collective-permute-start(bf16[6,90,128]{2,1,0:T(8,128)(2,1)S(1)} %encode.4.refs_8_), channel_id=1, source_target_pairs={{0,3},{1,2},{2,1},{3,0},{4,7},{5,6},{6,5},{7,4},{8,11},{9,10},{10,... | collective-permute-start | bytes 414728 | tf_op jit(solution)/shard_map/ppermute | solution.py:434
  34.1 8.2 %collective-permute-start.11 = (bf16[6,90,128]{2,1,0:T(8,128)(2,1)S(1)}, bf16[6,90,128]{2,1,0:T(8,128)(2,1)S(1)}, u32[]{:S(2)}, u32[]{:S(2)}) collective-permute-start(bf16[6,90,128]{2,1,0:T(8,128)(2,1)S(1)} %encode.4.refs_8_), channel_id=1, source_target_pairs={{0,2},{1,3},{2,0},{3,1},{4,6},{5,7},{6,4},{7,5},{8,10},{9,11},{10,... | collective-permute-start | bytes 414728 | tf_op jit(solution)/shard_map/ppermute | solution.py:431
  34.9 7.4 %collective-permute-start.10 = (bf16[6,90,128]{2,1,0:T(8,128)(2,1)S(1)}, bf16[6,90,128]{2,1,0:T(8,128)(2,1)S(1)}, u32[]{:S(2)}, u32[]{:S(2)}) collective-permute-start(bf16[6,90,128]{2,1,0:T(8,128)(2,1)S(1)} %encode.4.refs_8_), channel_id=1, source_target_pairs={{0,1},{1,0},{2,3},{3,2},{4,5},{5,4},{6,7},{7,6},{8,9},{9,8},{10,11... | collective-permute-start | bytes 414728 | tf_op jit(solution)/shard_map/ppermute | solution.py:432

commit v9 on v8

--- a/solution.py
+++ b/solution.py
@@ -20,7 +20,8 @@
 
 
 def gelu_twice(x):
-    inner = x * (0.7978845608028654 + 0.035677408136300125 * (x * x))
+    x = x.astype(BF)
+    inner = x * (jnp.asarray(0.7978845608028654, BF) + jnp.asarray(0.035677408136300125, BF) * (x * x))
     return x + x * jnp.tanh(inner)
 
 
@@ -29,18 +30,18 @@
 
 
 def weights_kernel(
-    meta_ref, ids_ref, x_hbm, we_hbm, wh_hbm, scale_hbm, shift_hbm, z_hbm,
-    g_hbm, ws_ref, vec_ref, zs_ref, edge_ref,
-    g_ref, we_ref, wh_ref, tab, z_ref, near, flat, sem,
+    ids_ref, x_hbm, wh_hbm, scale_hbm, shift_hbm, z_hbm,
+    ws_ref, vec_ref, zs_ref, edge_ref,
+    wh_ref, tab, z_ref, near, flat, sem,
 ):
-    ch = we_ref.shape[-1]
+    ch = x_hbm.shape[-1]
     head = wh_ref.shape[-1]
     leads = ws_ref.shape[1] // head
     cols = z_ref.shape[0]
     xcols, rows, _ = x_hbm.shape
     reach = edge_ref.shape[1]
-    ids = [ids_ref[meta_ref[2] * leads + lead] for lead in range(leads)]
-    copies = [(we_hbm, we_ref), (x_hbm.at[:, :8], near.at[0]), (x_hbm.at[:, rows - 8 :], near.at[1])]
+    ids = [ids_ref[lax.axis_index("lon") * leads + lead] for lead in range(leads)]
+    copies = [(x_hbm.at[:, :8], near.at[0]), (x_hbm.at[:, rows - 8 :], near.at[1])]
     copies += [(z_hbm, z_ref), (wh_hbm, wh_ref)]
     for lead in range(leads):
         block = pl.multiple_of((ids[lead] // 8) * 8, 8)
@@ -50,19 +51,8 @@
     for c in copies:
         c.start()
     zs_ref[...] = jnp.zeros(zs_ref.shape, BF)
-    copies[0].wait()
-    for dr in range(3):
-        at = slice(dr * ch, (dr + 1) * ch)
-        w = [we_ref[dr, dc].astype(F32) for dc in range(3)]
-        half = 0.5 * (w[0] + w[2])
-        g_ref[0, at] = we_ref[dr, 0]
-        g_ref[1, at] = (half + 0.5 * w[1]).astype(BF)
-        g_ref[2, at] = (half - 0.5 * w[1]).astype(BF)
-        g_ref[3, at] = we_ref[dr, 2]
-    made = pltpu.make_async_copy(g_ref, g_hbm, sem.at[len(copies)])
-    made.start()
     for k in range(2):
-        copies[1 + k].wait()
+        copies[k].wait()
         parts = []
         for j in range(ch // 128):
             flat[k, j] = near[k, :, :, j * 128 : (j + 1) * 128].astype(F32).reshape(xcols * 8, 128)
@@ -70,7 +60,7 @@
             parts.append([flat[k, j, pl.ds(first + i, xcols, stride=8), :] for i in range(reach)])
         for i in range(reach):
             edge_ref[k, i] = jnp.concatenate([p[i] for p in parts], axis=1).astype(BF)
-    for c in copies[3:]:
+    for c in copies[2:]:
         c.wait()
     zs_ref[:cols, :cols] = z_ref[...] * jnp.asarray(0.5, BF)
     for lead in range(leads):
@@ -90,42 +80,37 @@
                 ws_ref[at : at + head, lanes] = (w * gain_t).astype(BF)
                 total = total + w * shift_t
             vec_ref[BIAS + dr : BIAS + dr + 1, lanes] = jnp.sum(total, axis=0, keepdims=True)
-    made.wait()
-
-
-def prepare(meta, ids, x, w_enc, w_head, scale, shift, z, leads, reach):
-    ch, head, cols = w_enc.shape[-1], w_head.shape[-1], z.shape[0]
-    xcols = x.shape[0]
+
+
+def prepare(ids, x, w_head, scale, shift, z, leads, reach):
+    head, cols = w_head.shape[-1], z.shape[0]
+    xcols, _, ch = x.shape
     wide = up_to(cols, 16)
     vmem = pl.BlockSpec(memory_space=pltpu.VMEM)
     smem = pl.BlockSpec(memory_space=pltpu.SMEM)
     hbm = pl.BlockSpec(memory_space=pltpu.HBM)
-    form = (4, 3 * ch, ch)
     return pl.pallas_call(
         weights_kernel,
-        in_specs=[smem, smem] + [hbm] * 6,
-        out_specs=[hbm] + [vmem] * 4,
+        in_specs=[smem] + [hbm] * 5,
+        out_specs=[vmem] * 4,
         out_shape=[
-            jax.ShapeDtypeStruct(form, BF),
             jax.ShapeDtypeStruct((9 * head, leads * head), BF),
             jax.ShapeDtypeStruct((8, leads * head), F32),
             jax.ShapeDtypeStruct((wide, wide), BF),
             jax.ShapeDtypeStruct((2, reach, xcols, ch), BF),
         ],
         scratch_shapes=[
-            pltpu.VMEM(form, BF),
-            pltpu.VMEM(w_enc.shape, BF),
             pltpu.VMEM(w_head.shape, BF),
             pltpu.VMEM((leads, 2, 8, head), F32),
             pltpu.VMEM(z.shape, BF),
             pltpu.VMEM((2, xcols, 8, ch), BF),
             pltpu.VMEM((2, ch // 128, xcols * 8, 128), F32),
-            pltpu.SemaphoreType.DMA((6 + 2 * leads,)),
+            pltpu.SemaphoreType.DMA((4 + 2 * leads,)),
         ],
         compiler_params=params(58),
         cost_estimate=pl.CostEstimate(flops=1 << 31, transcendentals=0, bytes_accessed=12 * MIB),
         name="weights",
-    )(meta, ids, x, w_enc, w_head, scale, shift, z)
+    )(ids, x, w_head, scale, shift, z)
 
 
 def slabs_kernel(edge_ref, west_ref, east_ref, up_ref, dn_ref):
@@ -151,15 +136,24 @@
     )(edge, west, east)
 
 
-def encoder_kernel(
-    meta_ref, x_ref, west_ref, east_ref, *refs, first, group
-):
+def encoder_kernel(x_ref, west_ref, east_ref, *refs, first, group):
     halos, refs = (refs[:2], refs[2:]) if first is None else ((), refs)
-    g_ref, wp_ref, out_ref, xs, ys, st, pt = refs[:7]
+    w_ref, wp_ref, out_ref, g_ref, *refs = refs
+    ch = x_ref.shape[2]
+    for dr in range(3):
+        at = slice(dr * ch, (dr + 1) * ch)
+        w = [w_ref[dr, dc].astype(F32) for dc in range(3)]
+        half = 0.5 * (w[0] + w[2])
+        g_ref[0, at] = w_ref[dr, 0]
+        g_ref[1, at] = (half + 0.5 * w[1]).astype(BF)
+        g_ref[2, at] = (half - 0.5 * w[1]).astype(BF)
+        g_ref[3, at] = w_ref[dr, 2]
+    xs, ys0, ys1, st0, st1, pt = refs[:6]
+    ys, st = (ys0, ys1), (st0, st1)
     cols, rows, ch = x_ref.shape
     reach = 2 * EDGE - 1
     if first is None:
-        hf = refs[7]
+        hf = refs[6]
         for k, halo in enumerate(halos):
             for j in range(ch // 128):
                 lanes = slice(j * 128, (j + 1) * 128)
@@ -203,20 +197,21 @@
             for q in range(c * group, (c + 1) * group):
                 one, two = xs[2 * q + i], xs[2 * q + j]
                 t.append(one + two if k == 1 else one - two)
-            ys[c % 2, k] = jnp.dot(jnp.concatenate(t, axis=0), g_ref[k], preferred_element_type=F32)
+            ys[c % 2][k] = jnp.dot(jnp.concatenate(t, axis=0), g_ref[k], preferred_element_type=F32)
 
     def finish(c):
         n = group * 16
         sub = next(v for v in range(12, 0, -1) if group % v == 0) * 16
         for a in range(0, n, sub):
             part = slice(a, a + sub)
-            m = [ys.at[c % 2, k, part] for k in range(4)]
-            both = gelu_twice(m[0][...] + m[1][...] + m[2][...])
-            both = both + gelu_twice(m[1][...] - m[2][...] - m[3][...])
+            m = [ys[c % 2].at[k, part] for k in range(4)]
+            both = gelu_twice(m[0][...] + m[1][...] + m[2][...]).astype(F32)
+            both = both + gelu_twice(m[1][...] - m[2][...] - m[3][...]).astype(F32)
             for j in range(ch // 128):
-                st[j, part] = both[:, j * 128 : (j + 1) * 128]
+                st[c % 2][j, part] = both[:, j * 128 : (j + 1) * 128]
         pooled = [
-            st[j, pl.ds(0, n // 2, stride=2), :] + st[j, pl.ds(1, n // 2, stride=2), :] for j in range(ch // 128)
+            st[c % 2][j, pl.ds(0, n // 2, stride=2), :] + st[c % 2][j, pl.ds(1, n // 2, stride=2), :]
+            for j in range(ch // 128)
         ]
         pooled = (jnp.concatenate(pooled, axis=1) * 0.125).astype(BF)
         pt[c * (n // 2) : (c + 1) * (n // 2)] = jnp.dot(pooled, wp_ref[...], preferred_element_type=F32)
@@ -230,45 +225,53 @@
     for r in range(count):
         row = pt[pl.ds(r, pairs, stride=8), :]
         if first is None and r in (0, count - 1):
-            row = jnp.where(meta_ref[0 if r == 0 else 1] == 0, row, 0.0)
+            pole = 0 if r == 0 else lax.axis_size("lat") - 1
+            row = jnp.where(lax.axis_index("lat") == pole, 0.0, row)
         out_ref[r] = row.astype(BF)
 
 
-def encode(meta, x, west, east, halos, g, wp, first, count, group):
+def encode(x, west, east, halos, w, wp, first, count, group):
     cols, rows, ch = x.shape
     head = wp.shape[1]
     vmem = pl.BlockSpec(memory_space=pltpu.VMEM)
+    form = (4, 3 * ch, ch)
     scratch = [
+        pltpu.VMEM(form, BF),
         pltpu.VMEM((cols + 2, 16, 3 * ch), BF),
-        pltpu.VMEM((2, 4, group * 16, ch), F32),
+        pltpu.VMEM((4, group * 16, ch), F32),
+        pltpu.VMEM((4, group * 16, ch), F32),
+        pltpu.VMEM((ch // 128, group * 16, 128), F32),
         pltpu.VMEM((ch // 128, group * 16, 128), F32),
         pltpu.VMEM((cols // 2 * 8, head), F32),
     ]
     if halos is not None:
         scratch.append(pltpu.VMEM((2, ch // 128, (cols + 2) * 8, 128), F32))
-    operands = [meta, x, west, east, *(halos or ()), g, wp]
-    flops = 2 * cols * 16 * 6 * ch * ch
+    operands = [x, west, east, *(halos or ()), w, wp]
     return pl.pallas_call(
         functools.partial(encoder_kernel, first=first, group=group),
-        in_specs=[pl.BlockSpec(memory_space=pltpu.SMEM)] + [vmem] * (len(operands) - 1),
+        in_specs=[vmem] * len(operands),
         out_specs=vmem,
         out_shape=jax.ShapeDtypeStruct((count, cols // 2, head), BF),
         scratch_shapes=scratch,
         compiler_params=params(28),
-        cost_estimate=pl.CostEstimate(flops=flops, transcendentals=cols * 16 * ch, bytes_accessed=8 * 1024 * 1024),
+        cost_estimate=pl.CostEstimate(
+            flops=2 * cols * 16 * 6 * ch * ch, transcendentals=cols * 16 * ch, bytes_accessed=8 * MIB
+        ),
         name="encode",
     )(*operands)
 
 
-def head_kernel(meta_ref, *refs, chunks, blocks, shards, aliased):
+def head_kernel(*refs, chunks, blocks, shards, aliased):
     arrays = refs[: sum(n for n, _ in chunks)]
     ws_ref, vec_ref, zs_ref = refs[len(arrays) : len(arrays) + 3]
-    out_ref, ps, cs, outs, out_sem = refs[len(arrays) + 3 + aliased :]
+    out_ref, ps, cs0, cs1, outs, out_sem = refs[len(arrays) + 3 + aliased :]
     ch = ps.shape[2] // 3
     wide = ps.shape[1]
     leads, rows, cols, _ = out_ref.shape
-    odd = meta_ref[2] % 2 == 1
-    high = meta_ref[2] // 2 == 1
+    cs = (cs0, cs1)
+    lat, lon = lax.axis_index("lat"), lax.axis_index("lon")
+    odd = lon % 2 == 1
+    high = lon // 2 == 1
     if wide > cols:
         ps[:, cols:, :] = jnp.zeros((ps.shape[0], wide - cols, 3 * ch), BF)
 
@@ -287,8 +290,8 @@
             taken += count
 
     bias = vec_ref[BIAS : BIAS + 1, :] + vec_ref[BIAS + 1 : BIAS + 2, :] + vec_ref[BIAS + 2 : BIAS + 3, :]
-    first = (meta_ref[0] == 1).astype(F32) * vec_ref[BIAS : BIAS + 1, :]
-    last = (meta_ref[1] == 1).astype(F32) * vec_ref[BIAS + 2 : BIAS + 3, :]
+    first = (lat == 0).astype(F32) * vec_ref[BIAS : BIAS + 1, :]
+    last = (lat == lax.axis_size("lat") - 1).astype(F32) * vec_ref[BIAS + 2 : BIAS + 3, :]
 
     wanted = [sorted({n * STEP + i for i in range(STEP + 2)}) for n in blocks]
     slots = {r: k for k, r in enumerate(sorted(set(sum(wanted, []))))}
@@ -308,12 +311,12 @@
     def conv(n):
         p = [ps[slots[r]] for r in wanted[n]]
         lhs = [jnp.concatenate(p[i : i + 3], axis=1) for i in range(STEP)]
-        cs[n % 2] = jnp.dot(jnp.concatenate(lhs, axis=0), ws_ref[...], preferred_element_type=F32)
+        cs[n % 2][...] = jnp.dot(jnp.concatenate(lhs, axis=0), ws_ref[...], preferred_element_type=F32)
 
     def finish(n, i):
         row = blocks[n] * STEP + i
-        y = cs[n % 2, i * wide : (i + 1) * wide] + (bias - first if row == 0 else (bias - last if row == rows - 1 else bias))
-        mixed = jnp.dot(zs_ref[...], gelu_twice(y).astype(BF), preferred_element_type=F32)
+        y = cs[n % 2][i * wide : (i + 1) * wide] + (bias - first if row == 0 else (bias - last if row == rows - 1 else bias))
+        mixed = jnp.dot(zs_ref[...], gelu_twice(y), preferred_element_type=F32)
         center = ps[slots[row + 1], :, ch : 2 * ch].astype(F32)
         for lead in range(leads):
             lanes = slice(lead * ch, (lead + 1) * ch)
@@ -345,14 +348,14 @@
         c.wait()
 
 
-def forecast_heads(meta, arrays, chunks, ws, vec, zs, so_far, blocks, shape):
+def forecast_heads(arrays, chunks, ws, vec, zs, so_far, blocks, shape):
     leads, rows, cols, ch = shape
     shards = cols // arrays[0].shape[-2]
     wide = zs.shape[0]
     vmem = pl.BlockSpec(memory_space=pltpu.VMEM)
     staged = len({n * STEP + i for n in blocks for i in range(STEP + 2)})
-    operands = [meta, *arrays, ws, vec, zs]
-    in_specs = [pl.BlockSpec(memory_space=pltpu.SMEM)] + [vmem] * (len(operands) - 1)
+    operands = [*arrays, ws, vec, zs]
+    in_specs = [vmem] * len(operands)
     alias = {}
     if so_far is not None:
         alias = {len(operands): 0}
@@ -365,7 +368,8 @@
         out_shape=jax.ShapeDtypeStruct(shape, BF),
         scratch_shapes=[
             pltpu.VMEM((staged, wide, 3 * ch), BF),
-            pltpu.VMEM((2, STEP * wide, leads * ch), F32),
+            pltpu.VMEM((STEP * wide, leads * ch), F32),
+            pltpu.VMEM((STEP * wide, leads * ch), F32),
             pltpu.VMEM((len(blocks), leads, STEP, cols, ch), BF),
             pltpu.SemaphoreType.DMA((len(blocks), leads)),
         ],
@@ -394,7 +398,6 @@
     rows, cols, ch = inputs.shape
     tile = jnp.transpose(inputs, (1, 0, 2))
     lat, lon = lax.axis_size("lat"), lax.axis_size("lon")
-    lat_at, lon_at = lax.axis_index("lat"), lax.axis_index("lon")
     lat_up, lat_dn = neighbours(lat, False)
     lon_up, lon_dn = neighbours(lon, True)
     two_level = lon == 4
@@ -406,12 +409,7 @@
     west = lax.ppermute(tile[-1], "lon", lon_up)
     east = lax.ppermute(tile[0], "lon", lon_dn)
 
-    meta = jnp.stack(
-        [lat_at == 0, lat_at == lat - 1, lon_at]
-    ).astype(jnp.int32)
-    g, ws, vec, zs, edge = prepare(
-        meta, lead_ids, tile, w_enc, w_head, film_scale, film_shift, zonal_mix, leads, reach
-    )
+    ws, vec, zs, edge = prepare(lead_ids, tile, w_head, film_scale, film_shift, zonal_mix, leads, reach)
     up, dn = row_slabs(edge, west, east)
     above = lax.ppermute(up, "lat", lat_up)
     below = lax.ppermute(dn, "lat", lat_dn)
@@ -423,7 +421,7 @@
         (2 * middle, band_rows - EDGE - middle, None),
         (None, 2 * (EDGE + 1), (above, below)),
     ]
-    proj = [encode(meta, tile, west, east, halos, g, w_proj, first, n, group) for first, n, halos in plan]
+    proj = [encode(tile, west, east, halos, w_enc, w_proj, first, n, group) for first, n, halos in plan]
 
     sent = []
     for k, own in enumerate(proj):
@@ -449,10 +447,10 @@
     ]
     chunks = [(len(a), rows_at) for a, rows_at in zip(sent, at)]
     inner = forecast_heads(
-        meta, sent[0] + sent[1], chunks[:2], ws, vec, zs, None, list(range(1, blocks - 1)), shape
+        sent[0] + sent[1], chunks[:2], ws, vec, zs, None, list(range(1, blocks - 1)), shape
     )
     return forecast_heads(
-        meta, sent[0] + sent[1] + sent[2], chunks, ws, vec, zs, inner, [0, blocks - 1], shape
+        sent[0] + sent[1] + sent[2], chunks, ws, vec, zs, inner, [0, blocks - 1], shape
     )
 
 

time: 47.9 us -> 44 us (0.919)
  Pallas kernels: 30.4 us -> 25.7 us
  waiting for transfers between devices: 0.45 us -> 2.19 us
  other arithmetic: 0.66 us -> 0 us
    pallas_call x2, Pallas kernels: 12.3 us -> 10.2 us  [forecast_heads(): pl.pallas_call(functools.partial(head_kernel, chunks=chunks, blocks=block...]
    pallas_call x3, Pallas kernels: 13.4 us -> 11.9 us  [encode(): pl.pallas_call(functools.partial(encoder_kernel, first=first, group=group...]
    pallas_call x1, Pallas kernels: 4.63 us -> 3.46 us  [prepare(): pl.pallas_call(weights_kernel, in_specs=[smem] + [hbm] * 5, out_specs=[vm...]
    ppermute x1, waiting for transfers between devices: 0.24 us -> 1.28 us  [shards(): below = lax.ppermute(dn, 'lat', lat_dn)]
    ppermute x3, waiting for transfers between devices: 0.19 us -> 0.89 us  [shards(): across = lax.ppermute(own, 'lon', swap(lon, 2))]
    another operation x1 -> x0, other arithmetic: 0.66 us -> none  [shards(): meta = jnp.stack([lat_at == 0, lat_at == lat - 1, lon_at]).astype(jnp.int32)]
    unnamed x16 -> x14, local copies, waits for them, and re-layouts: 1.08 us -> 1.07 us
  transfers between devices with their start and end apart: 13 -> 13, of which waited for: 2 -> 2; matrix products, arithmetic and copies ran while one was open for 1% -> 0% of each run, Pallas kernels for 53% -> 49%
where the time goes in v9:
time: 44 us; the launch traced here: 43.7 us
  Pallas kernels  25.7 us (58%)
  starting transfers between devices  13.7 us (31%)
  waiting for transfers between devices  2.19 us (5%)
  local copies, waits for them, and re-layouts  1.82 us (4%)
    pallas_call x3, Pallas kernels, encode(): pl.pallas_call(functools.partial(encoder_kernel, first=first, group=group...  11.9 us
    pallas_call x2, Pallas kernels, forecast_heads(): pl.pallas_call(functools.partial(head_kernel, chunks=chunks, blocks=block...  10.2 us
    pallas_call x1, Pallas kernels, prepare(): pl.pallas_call(weights_kernel, in_specs=[smem] + [hbm] * 5, out_specs=[vm...  3.46 us
    ppermute x1, starting transfers between devices, shards(): above = lax.ppermute(up, 'lat', lat_up)  3.41 us
    ppermute x1, starting transfers between devices, shards(): below = lax.ppermute(dn, 'lat', lat_dn)  3.07 us
    ppermute x3, starting transfers between devices, shards(): across = lax.ppermute(own, 'lon', swap(lon, 2))  2.35 us
    ppermute x1, starting transfers between devices, shards(): both = lax.ppermute(own, 'lon', swap(lon, 3))  1.4 us
    ppermute x1, waiting for transfers between devices, shards(): below = lax.ppermute(dn, 'lat', lat_dn)  1.28 us
  transfers between devices with their start and end apart: 13, of which 2 were waited for; matrix products, arithmetic and copies ran while one was open for 0% of the time, Pallas kernels for 49%

profile of v9, /device:TPU:25, one launch (start us, length us, event | category | flops | bytes accessed | tf_op | source)
XLA Modules:
  0.0 43.7 jit_solution(5493196408558941907)
XLA Ops:
  0.0 0.7 %slice_bitcast_fusion = (bf16[40,256]{1,0:T(8,128)(2,1)S(1)}, bf16[40,256]{1,0:T(8,128)(2,1)S(1)}) fusion(bf16[180,40,256]{2,1,0:T(8,128)(2,1)} %bitcast.5), kind=kLoop, calls=%fused_computation | loop fusion | bytes 81920 | tf_op jit(solution)/shard_map/squeeze | solution.py:410
  0.7 0.7 %collective-permute-start.1 = (bf16[40,256]{1,0:T(8,128)(2,1)S(1)}, bf16[40,256]{1,0:T(8,128)(2,1)S(1)}, u32[]{:S(2)}, u32[]{:S(2)}) collective-permute-start(bf16[40,256]{1,0:T(8,128)(2,1)S(1)} %get-tuple-element.21), channel_id=1, source_target_pairs={{1,0},{2,1},{3,2},{0,3},{5,4},{6,5},{7,6},{4,7},{9,8},{10,9},{11,1... | collective-permute-start | bytes 61448 | tf_op jit(solution)/shard_map/ppermute | solution.py:410
  1.4 1.1 %collective-permute-start = (bf16[40,256]{1,0:T(8,128)(2,1)S(1)}, bf16[40,256]{1,0:T(8,128)(2,1)S(1)}, u32[]{:S(2)}, u32[]{:S(2)}) collective-permute-start(bf16[40,256]{1,0:T(8,128)(2,1)S(1)} %get-tuple-element.22), channel_id=1, source_target_pairs={{0,1},{1,2},{2,3},{3,0},{4,5},{5,6},{6,7},{7,4},{8,9},{9,10},{10,1... | collective-permute-start | bytes 61448 | tf_op jit(solution)/shard_map/ppermute | solution.py:409
  2.5 3.5 %weights.1 = (bf16[1152,256]{1,0:T(8,128)(2,1)}, f32[8,256]{1,0:T(8,128)}, bf16[368,368]{1,0:T(8,128)(2,1)}, bf16[2,3,180,256]{3,2,1,0:T(8,128)(2,1)}) custom-call(s32[8]{0:T(128)} %ids_ref.1, bf16[180,40,256]{2,1,0:T(8,128)(2,1)} %bitcast.6, bf16[3,3,128,128]{3,2,1,0:T(8,128)(2,1)} %wh_hbm.1, f32[720,128]{1,0:T(8,128)} %scale_hbm.1, f32[720,128]{1,0:T(8,128)} %shift_hbm.1, ...), custom_call_target="tpu_custom_call" | custom-call | flops 2147483648 | bytes 12582912 | tf_op jit(solution)/shard_map/weights/pallas_call | solution.py:92
  6.0 0.0 collective-permute-done.1.east_ref
  6.0 0.0 collective-permute-done.west_ref
  6.0 1.0 %copy-done.6 = bf16[2,3,180,256]{3,2,1,0:T(8,128)(2,1)S(1)} copy-done((bf16[2,3,180,256]{3,2,1,0:T(8,128)(2,1)S(1)}, bf16[2,3,180,256]{3,2,1,0:T(8,128)(2,1)}, u32[]{:S(2)}) %copy-start.6) | copy-done | bytes 552984
  7.1 0.1 slabs.1
  7.2 3.4 %collective-permute-start.4 = (bf16[3,182,256]{2,1,0:T(8,128)(2,1)S(1)}, bf16[3,182,256]{2,1,0:T(8,128)(2,1)S(1)}, u32[]{:S(2)}, u32[]{:S(2)}) collective-permute-start(bf16[3,182,256]{2,1,0:T(8,128)(2,1)S(1)} %get-tuple-element.14), channel_id=1, source_target_pairs={{0,4},{4,8},{8,12},{12,16},{16,20},{20,24},{24,28},{1,5},{5,9},{9,... | collective-permute-start | bytes 838664 | tf_op jit(solution)/shard_map/ppermute | solution.py:414
  10.6 3.1 %collective-permute-start.5 = (bf16[3,182,256]{2,1,0:T(8,128)(2,1)S(1)}, bf16[3,182,256]{2,1,0:T(8,128)(2,1)S(1)}, u32[]{:S(2)}, u32[]{:S(2)}) collective-permute-start(bf16[3,182,256]{2,1,0:T(8,128)(2,1)S(1)} %get-tuple-element.15), channel_id=1, source_target_pairs={{4,0},{8,4},{12,8},{16,12},{20,16},{24,20},{28,24},{5,1},{9,5},{13... | collective-permute-start | bytes 838664 | tf_op jit(solution)/shard_map/ppermute | solution.py:415
  13.7 3.7 %encode.3.refs_0_ = bf16[8,90,128]{2,1,0:T(8,128)(2,1)S(1)} custom-call(bf16[180,40,256]{2,1,0:T(8,128)(2,1)S(1)} %bitcast.7, bf16[40,256]{1,0:T(8,128)(2,1)S(1)} %collective-permute-done.west_ref, bf16[40,256]{1,0:T(8,128)(2,1)S(1)} %collective-permute-done.1.east_ref, bf16[3,3,256,256]{3,2,1,0:T(8,128)(2,1)S(1)} %copy-done.4, bf16[256,128]{1,0:T(8,128)(2,1)S(1)} %copy-done.5), custom_call_target="tpu_custom_call" | custom-call | flops 2264924160 | bytes 8388608 | tf_op jit(solution)/shard_map/encode/pallas_call | solution.py:250
  17.5 1.2 %collective-permute-start.3 = (bf16[8,90,128]{2,1,0:T(8,128)(2,1)S(1)}, bf16[8,90,128]{2,1,0:T(8,128)(2,1)S(1)}, u32[]{:S(2)}, u32[]{:S(2)}) collective-permute-start(bf16[8,90,128]{2,1,0:T(8,128)(2,1)S(1)} %encode.3.refs_0_), channel_id=1, source_target_pairs={{0,2},{1,3},{2,0},{3,1},{4,6},{5,7},{6,4},{7,5},{8,10},{9,11},{10,... | collective-permute-start | bytes 552968 | tf_op jit(solution)/shard_map/ppermute | solution.py:429
  18.7 0.3 collective-permute-start.2
  19.0 3.7 %encode.5.refs_4_ = bf16[8,90,128]{2,1,0:T(8,128)(2,1)S(1)} custom-call(bf16[180,40,256]{2,1,0:T(8,128)(2,1)S(1)} %bitcast.8, bf16[40,256]{1,0:T(8,128)(2,1)S(1)} %collective-permute-done.west_ref, bf16[40,256]{1,0:T(8,128)(2,1)S(1)} %collective-permute-done.1.east_ref, bf16[3,3,256,256]{3,2,1,0:T(8,128)(2,1)S(1)} %copy-done.4, bf16[256,128]{1,0:T(8,128)(2,1)S(1)} %copy-done.5), custom_call_target="tpu_custom_call" | custom-call | flops 2264924160 | bytes 8388608 | tf_op jit(solution)/shard_map/encode/pallas_call | solution.py:250
  22.7 0.0 copy-start
  22.7 0.7 %collective-permute-start.8 = (bf16[8,90,128]{2,1,0:T(8,128)(2,1)S(1)}, bf16[8,90,128]{2,1,0:T(8,128)(2,1)S(1)}, u32[]{:S(2)}, u32[]{:S(2)}) collective-permute-start(bf16[8,90,128]{2,1,0:T(8,128)(2,1)S(1)} %encode.5.refs_4_), channel_id=1, source_target_pairs={{0,2},{1,3},{2,0},{3,1},{4,6},{5,7},{6,4},{7,5},{8,10},{9,11},{10,... | collective-permute-start | bytes 552968 | tf_op jit(solution)/shard_map/ppermute | solution.py:429
  23.5 0.0 collective-permute-done.4.refs_0_
  23.5 0.3 collective-permute-start.7
  23.8 1.3 %collective-permute-done.5.refs_1_ = bf16[3,182,256]{2,1,0:T(8,128)(2,1)S(1)} collective-permute-done((bf16[3,182,256]{2,1,0:T(8,128)(2,1)S(1)}, bf16[3,182,256]{2,1,0:T(8,128)(2,1)S(1)}, u32[]{:S(2)}, u32[]{:S(2)}) %collective-permute-start.5) | collective-permute-done | bytes 279584 | tf_op jit(solution)/shard_map/ppermute | solution.py:415
  25.0 4.4 %encode.4.refs_8_ = bf16[6,90,128]{2,1,0:T(8,128)(2,1)S(1)} custom-call(bf16[180,40,256]{2,1,0:T(8,128)(2,1)S(1)} %bitcast.9, bf16[40,256]{1,0:T(8,128)(2,1)S(1)} %collective-permute-done.west_ref, bf16[40,256]{1,0:T(8,128)(2,1)S(1)} %collective-permute-done.1.east_ref, bf16[3,182,256]{2,1,0:T(8,128)(2,1)S(1)} %collective-permute-done.4.refs_0_, ...), custom_call_target="tpu_custom_call" | custom-call | flops 2264924160 | bytes 8388608 | tf_op jit(solution)/shard_map/encode/pallas_call | solution.py:250
  29.5 0.0 collective-permute-done.3.refs_2_
  29.5 0.7 %collective-permute-start.6 = (bf16[8,90,128]{2,1,0:T(8,128)(2,1)S(1)}, bf16[8,90,128]{2,1,0:T(8,128)(2,1)S(1)}, u32[]{:S(2)}, u32[]{:S(2)}) collective-permute-start(bf16[8,90,128]{2,1,0:T(8,128)(2,1)S(1)} %collective-permute-done.3.refs_2_), channel_id=1, source_target_pairs={{0,1},{1,0},{2,3},{3,2},{4,5},{5,4},{6,7},{7,6},{8,9},{9,8},{10,11... | collective-permute-start | bytes 552968 | tf_op jit(solution)/shard_map/ppermute | solution.py:435
  30.2 0.1 collective-permute-start.9
  30.3 1.4 %collective-permute-start.12 = (bf16[6,90,128]{2,1,0:T(8,128)(2,1)S(1)}, bf16[6,90,128]{2,1,0:T(8,128)(2,1)S(1)}, u32[]{:S(2)}, u32[]{:S(2)}) collective-permute-start(bf16[6,90,128]{2,1,0:T(8,128)(2,1)S(1)} %encode.4.refs_8_), channel_id=1, source_target_pairs={{0,3},{1,2},{2,1},{3,0},{4,7},{5,6},{6,5},{7,4},{8,11},{9,10},{10,... | collective-permute-start | bytes 414728 | tf_op jit(solution)/shard_map/ppermute | solution.py:432
  31.6 0.0 collective-permute-done.2.refs_1_
  31.7 0.4 collective-permute-start.11
  32.1 0.0 collective-permute-done.7.refs_5_
  32.1 0.3 collective-permute-start.10
  32.4 0.0 collective-permute-done.6.refs_3_
  32.4 6.0 %heads.2.refs_15_ = bf16[2,20,360,128]{3,2,1,0:T(8,128)(2,1)} custom-call(bf16[8,90,128]{2,1,0:T(8,128)(2,1)S(1)} %encode.3.refs_0_, bf16[8,90,128]{2,1,0:T(8,128)(2,1)S(1)} %collective-permute-done.2.refs_1_, bf16[8,90,128]{2,1,0:T(8,128)(2,1)S(1)} %collective-permute-done.3.refs_2_, bf16[8,90,128]{2,1,0:T(8,128)(2,1)S(1)} %collective-permute-done.6.refs_3_, ...), custom_call_target="tpu_custom_call" | custom-call | flops 3344302080 | bytes 25165824 | tf_op jit(solution)/shard_map/heads/pallas_call | solution.py:364
  38.4 0.9 %collective-permute-done.11.refs_10_ = bf16[6,90,128]{2,1,0:T(8,128)(2,1)S(1)} collective-permute-done((bf16[6,90,128]{2,1,0:T(8,128)(2,1)S(1)}, bf16[6,90,128]{2,1,0:T(8,128)(2,1)S(1)}, u32[]{:S(2)}, u32[]{:S(2)}) %collective-permute-start.11) | collective-permute-done | bytes 138272 | tf_op jit(solution)/shard_map/ppermute | solution.py:429
  39.3 4.2 %heads.3 = bf16[2,20,360,128]{3,2,1,0:T(8,128)(2,1)} custom-call(bf16[8,90,128]{2,1,0:T(8,128)(2,1)S(1)} %encode.3.refs_0_, bf16[8,90,128]{2,1,0:T(8,128)(2,1)S(1)} %collective-permute-done.2.refs_1_, bf16[8,90,128]{2,1,0:T(8,128)(2,1)S(1)} %collective-permute-done.3.refs_2_, ...), custom_call_target="tpu_custom_call", output_to_operand_aliasing={{}: (15, {})} | custom-call | flops 2229534720 | bytes 16777216 | tf_op jit(solution)/shard_map/heads/pallas_call | solution.py:364
  (16 shorter events, 0.0 us)
Async XLA Ops:
  0.7 5.2 %collective-permute-start.1 = (bf16[40,256]{1,0:T(8,128)(2,1)S(1)}, bf16[40,256]{1,0:T(8,128)(2,1)S(1)}, u32[]{:S(2)}, u32[]{:S(2)}) collective-permute-start(bf16[40,256]{1,0:T(8,128)(2,1)S(1)} %get-tuple-element.21), channel_id=1, source_target_pairs={{1,0},{2,1},{3,2},{0,3},{5,4},{6,5},{7,6},{4,7},{9,8},{10,9},{11,1... | collective-permute-start | bytes 61448 | tf_op jit(solution)/shard_map/ppermute | solution.py:410
  1.4 4.6 %collective-permute-start = (bf16[40,256]{1,0:T(8,128)(2,1)S(1)}, bf16[40,256]{1,0:T(8,128)(2,1)S(1)}, u32[]{:S(2)}, u32[]{:S(2)}) collective-permute-start(bf16[40,256]{1,0:T(8,128)(2,1)S(1)} %get-tuple-element.22), channel_id=1, source_target_pairs={{0,1},{1,2},{2,3},{3,0},{4,5},{5,6},{6,7},{7,4},{8,9},{9,10},{10,1... | collective-permute-start | bytes 61448 | tf_op jit(solution)/shard_map/ppermute | solution.py:409
  6.0 1.1 %copy-start.6 = (bf16[2,3,180,256]{3,2,1,0:T(8,128)(2,1)S(1)}, bf16[2,3,180,256]{3,2,1,0:T(8,128)(2,1)}, u32[]{:S(2)}) copy-start(bf16[2,3,180,256]{3,2,1,0:T(8,128)(2,1)} %get-tuple-element.13.edge_ref) | copy-start | bytes 1658884
  7.1 6.6 %copy-start.3 = (bf16[40,180,256]{2,0,1:T(8,128)(2,1)S(1)}, bf16[40,180,256]{2,0,1:T(8,128)(2,1)}, u32[]{:S(2)}) copy-start(bf16[40,180,256]{2,0,1:T(8,128)(2,1)} %param.8) | copy-start | bytes 11059204
  7.1 6.6 %copy-start.4 = (bf16[3,3,256,256]{3,2,1,0:T(8,128)(2,1)S(1)}, bf16[3,3,256,256]{3,2,1,0:T(8,128)(2,1)}, u32[]{:S(2)}) copy-start(bf16[3,3,256,256]{3,2,1,0:T(8,128)(2,1)} %refs_0_.3) | copy-start | bytes 3538948
  7.1 6.6 %copy-start.5 = (bf16[256,128]{1,0:T(8,128)(2,1)S(1)}, bf16[256,128]{1,0:T(8,128)(2,1)}, u32[]{:S(2)}) copy-start(bf16[256,128]{1,0:T(8,128)(2,1)} %refs_1_.3) | copy-start | bytes 196612
  7.2 16.3 %collective-permute-start.4 = (bf16[3,182,256]{2,1,0:T(8,128)(2,1)S(1)}, bf16[3,182,256]{2,1,0:T(8,128)(2,1)S(1)}, u32[]{:S(2)}, u32[]{:S(2)}) collective-permute-start(bf16[3,182,256]{2,1,0:T(8,128)(2,1)S(1)} %get-tuple-element.14), channel_id=1, source_target_pairs={{0,4},{4,8},{8,12},{12,16},{16,20},{20,24},{24,28},{1,5},{5,9},{9,... | collective-permute-start | bytes 838664 | tf_op jit(solution)/shard_map/ppermute | solution.py:414
  10.6 14.4 %collective-permute-start.5 = (bf16[3,182,256]{2,1,0:T(8,128)(2,1)S(1)}, bf16[3,182,256]{2,1,0:T(8,128)(2,1)S(1)}, u32[]{:S(2)}, u32[]{:S(2)}) collective-permute-start(bf16[3,182,256]{2,1,0:T(8,128)(2,1)S(1)} %get-tuple-element.15), channel_id=1, source_target_pairs={{4,0},{8,4},{12,8},{16,12},{20,16},{24,20},{28,24},{5,1},{9,5},{13... | collective-permute-start | bytes 838664 | tf_op jit(solution)/shard_map/ppermute | solution.py:415
  17.5 12.0 %collective-permute-start.3 = (bf16[8,90,128]{2,1,0:T(8,128)(2,1)S(1)}, bf16[8,90,128]{2,1,0:T(8,128)(2,1)S(1)}, u32[]{:S(2)}, u32[]{:S(2)}) collective-permute-start(bf16[8,90,128]{2,1,0:T(8,128)(2,1)S(1)} %encode.3.refs_0_), channel_id=1, source_target_pairs={{0,2},{1,3},{2,0},{3,1},{4,6},{5,7},{6,4},{7,5},{8,10},{9,11},{10,... | collective-permute-start | bytes 552968 | tf_op jit(solution)/shard_map/ppermute | solution.py:429
  18.7 13.0 %collective-permute-start.2 = (bf16[8,90,128]{2,1,0:T(8,128)(2,1)S(1)}, bf16[8,90,128]{2,1,0:T(8,128)(2,1)S(1)}, u32[]{:S(2)}, u32[]{:S(2)}) collective-permute-start(bf16[8,90,128]{2,1,0:T(8,128)(2,1)S(1)} %encode.3.refs_0_), channel_id=1, source_target_pairs={{0,1},{1,0},{2,3},{3,2},{4,5},{5,4},{6,7},{7,6},{8,9},{9,8},{10,11... | collective-permute-start | bytes 552968 | tf_op jit(solution)/shard_map/ppermute | solution.py:430
  22.7 9.7 %copy-start = (bf16[1152,256]{1,0:T(8,128)(2,1)S(1)}, bf16[1152,256]{1,0:T(8,128)(2,1)}, u32[]{:S(2)}) copy-start(bf16[1152,256]{1,0:T(8,128)(2,1)} %get-tuple-element.18.refs_8_.refs_12_) | copy-start | bytes 1769476
  22.7 9.7 %copy-start.1 = (bf16[368,368]{1,0:T(8,128)(2,1)S(1)}, bf16[368,368]{1,0:T(8,128)(2,1)}, u32[]{:S(2)}) copy-start(bf16[368,368]{1,0:T(8,128)(2,1)} %get-tuple-element.20.refs_10_.refs_14_) | copy-start | bytes 812548
  22.7 9.7 %copy-start.2 = (f32[8,256]{1,0:T(8,128)S(1)}, f32[8,256]{1,0:T(8,128)}, u32[]{:S(2)}) copy-start(f32[8,256]{1,0:T(8,128)} %get-tuple-element.19.refs_9_.refs_13_) | copy-start | bytes 24580
  22.7 6.7 %collective-permute-start.8 = (bf16[8,90,128]{2,1,0:T(8,128)(2,1)S(1)}, bf16[8,90,128]{2,1,0:T(8,128)(2,1)S(1)}, u32[]{:S(2)}, u32[]{:S(2)}) collective-permute-start(bf16[8,90,128]{2,1,0:T(8,128)(2,1)S(1)} %encode.5.refs_4_), channel_id=1, source_target_pairs={{0,2},{1,3},{2,0},{3,1},{4,6},{5,7},{6,4},{7,5},{8,10},{9,11},{10,... | collective-permute-start | bytes 552968 | tf_op jit(solution)/shard_map/ppermute | solution.py:429
  23.5 8.6 %collective-permute-start.7 = (bf16[8,90,128]{2,1,0:T(8,128)(2,1)S(1)}, bf16[8,90,128]{2,1,0:T(8,128)(2,1)S(1)}, u32[]{:S(2)}, u32[]{:S(2)}) collective-permute-start(bf16[8,90,128]{2,1,0:T(8,128)(2,1)S(1)} %encode.5.refs_4_), channel_id=1, source_target_pairs={{0,1},{1,0},{2,3},{3,2},{4,5},{5,4},{6,7},{7,6},{8,9},{9,8},{10,11... | collective-permute-start | bytes 552968 | tf_op jit(solution)/shard_map/ppermute | solution.py:430
  29.5 2.9 %collective-permute-start.6 = (bf16[8,90,128]{2,1,0:T(8,128)(2,1)S(1)}, bf16[8,90,128]{2,1,0:T(8,128)(2,1)S(1)}, u32[]{:S(2)}, u32[]{:S(2)}) collective-permute-start(bf16[8,90,128]{2,1,0:T(8,128)(2,1)S(1)} %collective-permute-done.3.refs_2_), channel_id=1, source_target_pairs={{0,1},{1,0},{2,3},{3,2},{4,5},{5,4},{6,7},{7,6},{8,9},{9,8},{10,11... | collective-permute-start | bytes 552968 | tf_op jit(solution)/shard_map/ppermute | solution.py:435
  30.2 2.2 %collective-permute-start.9 = (bf16[8,90,128]{2,1,0:T(8,128)(2,1)S(1)}, bf16[8,90,128]{2,1,0:T(8,128)(2,1)S(1)}, u32[]{:S(2)}, u32[]{:S(2)}) collective-permute-start(bf16[8,90,128]{2,1,0:T(8,128)(2,1)S(1)} %collective-permute-done.8.refs_6_), channel_id=1, source_target_pairs={{0,1},{1,0},{2,3},{3,2},{4,5},{5,4},{6,7},{7,6},{8,9},{9,8},{10,11... | collective-permute-start | bytes 552968 | tf_op jit(solution)/shard_map/ppermute | solution.py:435
  30.3 8.2 %collective-permute-start.12 = (bf16[6,90,128]{2,1,0:T(8,128)(2,1)S(1)}, bf16[6,90,128]{2,1,0:T(8,128)(2,1)S(1)}, u32[]{:S(2)}, u32[]{:S(2)}) collective-permute-start(bf16[6,90,128]{2,1,0:T(8,128)(2,1)S(1)} %encode.4.refs_8_), channel_id=1, source_target_pairs={{0,3},{1,2},{2,1},{3,0},{4,7},{5,6},{6,5},{7,4},{8,11},{9,10},{10,... | collective-permute-start | bytes 414728 | tf_op jit(solution)/shard_map/ppermute | solution.py:432
  31.7 7.7 %collective-permute-start.11 = (bf16[6,90,128]{2,1,0:T(8,128)(2,1)S(1)}, bf16[6,90,128]{2,1,0:T(8,128)(2,1)S(1)}, u32[]{:S(2)}, u32[]{:S(2)}) collective-permute-start(bf16[6,90,128]{2,1,0:T(8,128)(2,1)S(1)} %encode.4.refs_8_), channel_id=1, source_target_pairs={{0,2},{1,3},{2,0},{3,1},{4,6},{5,7},{6,4},{7,5},{8,10},{9,11},{10,... | collective-permute-start | bytes 414728 | tf_op jit(solution)/shard_map/ppermute | solution.py:429
  32.1 7.3 %collective-permute-start.10 = (bf16[6,90,128]{2,1,0:T(8,128)(2,1)S(1)}, bf16[6,90,128]{2,1,0:T(8,128)(2,1)S(1)}, u32[]{:S(2)}, u32[]{:S(2)}) collective-permute-start(bf16[6,90,128]{2,1,0:T(8,128)(2,1)S(1)} %encode.4.refs_8_), channel_id=1, source_target_pairs={{0,1},{1,0},{2,3},{3,2},{4,5},{5,4},{6,7},{7,6},{8,9},{9,8},{10,11... | collective-permute-start | bytes 414728 | tf_op jit(solution)/shard_map/ppermute | solution.py:430

commit v10 on v9

--- a/solution.py
+++ b/solution.py
@@ -23,6 +23,12 @@
     x = x.astype(BF)
     inner = x * (jnp.asarray(0.7978845608028654, BF) + jnp.asarray(0.035677408136300125, BF) * (x * x))
     return x + x * jnp.tanh(inner)
+
+
+def together(*parts):
+    parts = [iter(p) for p in parts]
+    while parts:
+        parts = [p for p in parts if next(p, parts) is not parts]
 
 
 def params(mib):
@@ -183,13 +189,21 @@
                 off = first - 1 - low + dr
                 xs[at, :, dr * ch : (dr + 1) * ch] = here[:, off : off + 16]
 
-    stage(slice(0, 1), lambda a, n: west_ref[a : a + n, :].reshape(1, n, ch))
-    stage(slice(cols + 1, cols + 2), lambda a, n: east_ref[a : a + n, :].reshape(1, n, ch))
-    block = next(n for n in range(32, 0, -1) if cols % n == 0)
-    for c in range(0, cols, block):
-        stage(slice(c + 1, c + 1 + block), lambda a, n: x_ref[c : c + block, a : a + n, :])
-
     pairs = cols // 2
+    groups = pairs // group
+
+    def stage_group(c):
+        start, stop = 2 * c * group + (2 if c else 1), 2 * (c + 1) * group + 2
+        if c == 0:
+            stage(slice(0, 1), lambda a, n: west_ref[a : a + n, :].reshape(1, n, ch))
+        if c == groups - 1:
+            stage(slice(cols + 1, cols + 2), lambda a, n: east_ref[a : a + n, :].reshape(1, n, ch))
+            stop = cols + 1
+        size = -(-(stop - start) // 4)
+        for p in range(start, stop, size):
+            e = min(p + size, stop)
+            stage(slice(p, e), lambda a, n: x_ref[p - 1 : e - 1, a : a + n, :])
+            yield
 
     def multiply(c):
         for k, (i, j) in enumerate(((0, 2), (1, 2), (2, 1), (1, 3))):
@@ -198,6 +212,7 @@
                 one, two = xs[2 * q + i], xs[2 * q + j]
                 t.append(one + two if k == 1 else one - two)
             ys[c % 2][k] = jnp.dot(jnp.concatenate(t, axis=0), g_ref[k], preferred_element_type=F32)
+            yield
 
     def finish(c):
         n = group * 16
@@ -209,18 +224,22 @@
             both = both + gelu_twice(m[1][...] - m[2][...] - m[3][...]).astype(F32)
             for j in range(ch // 128):
                 st[c % 2][j, part] = both[:, j * 128 : (j + 1) * 128]
+            yield
         pooled = [
             st[c % 2][j, pl.ds(0, n // 2, stride=2), :] + st[c % 2][j, pl.ds(1, n // 2, stride=2), :]
             for j in range(ch // 128)
         ]
         pooled = (jnp.concatenate(pooled, axis=1) * 0.125).astype(BF)
         pt[c * (n // 2) : (c + 1) * (n // 2)] = jnp.dot(pooled, wp_ref[...], preferred_element_type=F32)
-
-    for c in range(pairs // group):
-        multiply(c)
-        if c:
-            finish(c - 1)
-    finish(pairs // group - 1)
+        yield
+
+    together(stage_group(0))
+    for c in range(groups + 1):
+        together(
+            multiply(c) if c < groups else (),
+            finish(c - 1) if c else (),
+            stage_group(c + 1) if c + 1 < groups else (),
+        )
     count = out_ref.shape[0]
     for r in range(count):
         row = pt[pl.ds(r, pairs, stride=8), :]
@@ -307,21 +326,30 @@
             ps[k, :cols, ch : 2 * ch] = row
             ps[k, :cols, :ch] = jnp.concatenate([row[-1:], row[:-1]], axis=0)
             ps[k, :cols, 2 * ch :] = jnp.concatenate([row[1:], row[:1]], axis=0)
+            yield
 
     def conv(n):
-        p = [ps[slots[r]] for r in wanted[n]]
-        lhs = [jnp.concatenate(p[i : i + 3], axis=1) for i in range(STEP)]
-        cs[n % 2][...] = jnp.dot(jnp.concatenate(lhs, axis=0), ws_ref[...], preferred_element_type=F32)
-
-    def finish(n, i):
-        row = blocks[n] * STEP + i
-        y = cs[n % 2][i * wide : (i + 1) * wide] + (bias - first if row == 0 else (bias - last if row == rows - 1 else bias))
-        mixed = jnp.dot(zs_ref[...], gelu_twice(y), preferred_element_type=F32)
-        center = ps[slots[row + 1], :, ch : 2 * ch].astype(F32)
-        for lead in range(leads):
-            lanes = slice(lead * ch, (lead + 1) * ch)
-            mod = center * vec_ref[GAIN : GAIN + 1, lanes] + vec_ref[SHIFT : SHIFT + 1, lanes]
-            outs[n, lead, i] = (mod + mixed[:, lanes]).astype(BF)[:cols]
+        half = STEP // 2
+        for h in range(2):
+            p = [ps[slots[r]] for r in wanted[n][h * half : (h + 1) * half + 2]]
+            lhs = [jnp.concatenate(p[i : i + 3], axis=1) for i in range(half)]
+            at = slice(h * half * wide, (h + 1) * half * wide)
+            cs[n % 2][at] = jnp.dot(jnp.concatenate(lhs, axis=0), ws_ref[...], preferred_element_type=F32)
+            yield
+            yield
+
+    def finish(n):
+        for i in range(STEP):
+            row = blocks[n] * STEP + i
+            near = bias - first if row == 0 else (bias - last if row == rows - 1 else bias)
+            y = cs[n % 2][i * wide : (i + 1) * wide] + near
+            mixed = jnp.dot(zs_ref[...], gelu_twice(y), preferred_element_type=F32)
+            center = ps[slots[row + 1], :, ch : 2 * ch].astype(F32)
+            for lead in range(leads):
+                lanes = slice(lead * ch, (lead + 1) * ch)
+                mod = center * vec_ref[GAIN : GAIN + 1, lanes] + vec_ref[SHIFT : SHIFT + 1, lanes]
+                outs[n, lead, i] = (mod + mixed[:, lanes]).astype(BF)[:cols]
+            yield
 
     sends = []
 
@@ -336,13 +364,14 @@
             )
             sends[-1].start()
 
+    together(stage(0))
     for n in range(len(blocks) + 1):
-        if n < len(blocks):
-            stage(n)
-            conv(n)
+        together(
+            conv(n) if n < len(blocks) else (),
+            finish(n - 1) if n else (),
+            stage(n + 1) if n + 1 < len(blocks) else (),
+        )
         if n:
-            for i in range(STEP):
-                finish(n - 1, i)
             send(n - 1)
     for c in sends:
         c.wait()
@@ -415,7 +444,7 @@
     below = lax.ppermute(dn, "lat", lat_dn)
 
     middle = band_rows // 2
-    group = cols // 4
+    group = cols // 6
     plan = [
         (2 * EDGE, middle - EDGE, None),
         (2 * middle, band_rows - EDGE - middle, None),

time: 44 us -> 43.8 us (level)
  Pallas kernels: 25.7 us -> 24.9 us
  waiting for transfers between devices: 2.19 us -> 2.81 us
    pallas_call x2, Pallas kernels: 10.2 us -> 9.4 us  [forecast_heads(): pl.pallas_call(functools.partial(head_kernel, chunks=chunks, blocks=block...]
    ppermute x3, waiting for transfers between devices: 0.89 us -> 1.53 us  [shards(): across = lax.ppermute(own, 'lon', swap(lon, 2))]
  transfers between devices with their start and end apart: 13 -> 13, of which waited for: 2 -> 2; matrix products, arithmetic and copies ran while one was open for 0% -> 0% of each run, Pallas kernels for 49% -> 48%
where the time goes in v10:
time: 43.8 us; the launch traced here: 43.5 us
  Pallas kernels  24.9 us (57%)
  starting transfers between devices  13.7 us (31%)
  waiting for transfers between devices  2.81 us (6%)
  local copies, waits for them, and re-layouts  1.82 us (4%)
    pallas_call x3, Pallas kernels, encode(): pl.pallas_call(functools.partial(encoder_kernel, first=first, group=group...  11.9 us
    pallas_call x2, Pallas kernels, forecast_heads(): pl.pallas_call(functools.partial(head_kernel, chunks=chunks, blocks=block...  9.4 us
    pallas_call x1, Pallas kernels, prepare(): pl.pallas_call(weights_kernel, in_specs=[smem] + [hbm] * 5, out_specs=[vm...  3.46 us
    ppermute x1, starting transfers between devices, shards(): above = lax.ppermute(up, 'lat', lat_up)  3.41 us
    ppermute x1, starting transfers between devices, shards(): below = lax.ppermute(dn, 'lat', lat_dn)  3.07 us
    ppermute x3, starting transfers between devices, shards(): across = lax.ppermute(own, 'lon', swap(lon, 2))  2.36 us
    ppermute x3, waiting for transfers between devices, shards(): across = lax.ppermute(own, 'lon', swap(lon, 2))  1.53 us
    ppermute x1, starting transfers between devices, shards(): both = lax.ppermute(own, 'lon', swap(lon, 3))  1.4 us
  transfers between devices with their start and end apart: 13, of which 2 were waited for; matrix products, arithmetic and copies ran while one was open for 0% of the time, Pallas kernels for 48%

profile of v10, /device:TPU:25, one launch (start us, length us, event | category | flops | bytes accessed | tf_op | source)
XLA Modules:
  0.0 43.5 jit_solution(12458430562120720617)
XLA Ops:
  0.0 0.7 %slice_bitcast_fusion = (bf16[40,256]{1,0:T(8,128)(2,1)S(1)}, bf16[40,256]{1,0:T(8,128)(2,1)S(1)}) fusion(bf16[180,40,256]{2,1,0:T(8,128)(2,1)} %bitcast.5), kind=kLoop, calls=%fused_computation | loop fusion | bytes 81920 | tf_op jit(solution)/shard_map/squeeze | solution.py:439
  0.7 0.7 %collective-permute-start.1 = (bf16[40,256]{1,0:T(8,128)(2,1)S(1)}, bf16[40,256]{1,0:T(8,128)(2,1)S(1)}, u32[]{:S(2)}, u32[]{:S(2)}) collective-permute-start(bf16[40,256]{1,0:T(8,128)(2,1)S(1)} %get-tuple-element.21), channel_id=1, source_target_pairs={{1,0},{2,1},{3,2},{0,3},{5,4},{6,5},{7,6},{4,7},{9,8},{10,9},{11,1... | collective-permute-start | bytes 61448 | tf_op jit(solution)/shard_map/ppermute | solution.py:439
  1.4 1.1 %collective-permute-start = (bf16[40,256]{1,0:T(8,128)(2,1)S(1)}, bf16[40,256]{1,0:T(8,128)(2,1)S(1)}, u32[]{:S(2)}, u32[]{:S(2)}) collective-permute-start(bf16[40,256]{1,0:T(8,128)(2,1)S(1)} %get-tuple-element.22), channel_id=1, source_target_pairs={{0,1},{1,2},{2,3},{3,0},{4,5},{5,6},{6,7},{7,4},{8,9},{9,10},{10,1... | collective-permute-start | bytes 61448 | tf_op jit(solution)/shard_map/ppermute | solution.py:438
  2.5 3.5 %weights.1 = (bf16[1152,256]{1,0:T(8,128)(2,1)}, f32[8,256]{1,0:T(8,128)}, bf16[368,368]{1,0:T(8,128)(2,1)}, bf16[2,3,180,256]{3,2,1,0:T(8,128)(2,1)}) custom-call(s32[8]{0:T(128)} %ids_ref.1, bf16[180,40,256]{2,1,0:T(8,128)(2,1)} %bitcast.6, bf16[3,3,128,128]{3,2,1,0:T(8,128)(2,1)} %wh_hbm.1, f32[720,128]{1,0:T(8,128)} %scale_hbm.1, f32[720,128]{1,0:T(8,128)} %shift_hbm.1, ...), custom_call_target="tpu_custom_call" | custom-call | flops 2147483648 | bytes 12582912 | tf_op jit(solution)/shard_map/weights/pallas_call | solution.py:98
  6.0 0.0 collective-permute-done.1.east_ref
  6.0 0.0 collective-permute-done.west_ref
  6.0 1.0 %copy-done.6 = bf16[2,3,180,256]{3,2,1,0:T(8,128)(2,1)S(1)} copy-done((bf16[2,3,180,256]{3,2,1,0:T(8,128)(2,1)S(1)}, bf16[2,3,180,256]{3,2,1,0:T(8,128)(2,1)}, u32[]{:S(2)}) %copy-start.6) | copy-done | bytes 552984
  7.1 0.1 slabs.1
  7.2 3.4 %collective-permute-start.4 = (bf16[3,182,256]{2,1,0:T(8,128)(2,1)S(1)}, bf16[3,182,256]{2,1,0:T(8,128)(2,1)S(1)}, u32[]{:S(2)}, u32[]{:S(2)}) collective-permute-start(bf16[3,182,256]{2,1,0:T(8,128)(2,1)S(1)} %get-tuple-element.14), channel_id=1, source_target_pairs={{0,4},{4,8},{8,12},{12,16},{16,20},{20,24},{24,28},{1,5},{5,9},{9,... | collective-permute-start | bytes 838664 | tf_op jit(solution)/shard_map/ppermute | solution.py:443
  10.6 3.1 %collective-permute-start.5 = (bf16[3,182,256]{2,1,0:T(8,128)(2,1)S(1)}, bf16[3,182,256]{2,1,0:T(8,128)(2,1)S(1)}, u32[]{:S(2)}, u32[]{:S(2)}) collective-permute-start(bf16[3,182,256]{2,1,0:T(8,128)(2,1)S(1)} %get-tuple-element.15), channel_id=1, source_target_pairs={{4,0},{8,4},{12,8},{16,12},{20,16},{24,20},{28,24},{5,1},{9,5},{13... | collective-permute-start | bytes 838664 | tf_op jit(solution)/shard_map/ppermute | solution.py:444
  13.7 3.7 %encode.3.refs_0_ = bf16[8,90,128]{2,1,0:T(8,128)(2,1)S(1)} custom-call(bf16[180,40,256]{2,1,0:T(8,128)(2,1)S(1)} %bitcast.7, bf16[40,256]{1,0:T(8,128)(2,1)S(1)} %collective-permute-done.west_ref, bf16[40,256]{1,0:T(8,128)(2,1)S(1)} %collective-permute-done.1.east_ref, bf16[3,3,256,256]{3,2,1,0:T(8,128)(2,1)S(1)} %copy-done.4, bf16[256,128]{1,0:T(8,128)(2,1)S(1)} %copy-done.5), custom_call_target="tpu_custom_call" | custom-call | flops 2264924160 | bytes 8388608 | tf_op jit(solution)/shard_map/encode/pallas_call | solution.py:269
  17.5 1.2 %collective-permute-start.3 = (bf16[8,90,128]{2,1,0:T(8,128)(2,1)S(1)}, bf16[8,90,128]{2,1,0:T(8,128)(2,1)S(1)}, u32[]{:S(2)}, u32[]{:S(2)}) collective-permute-start(bf16[8,90,128]{2,1,0:T(8,128)(2,1)S(1)} %encode.3.refs_0_), channel_id=1, source_target_pairs={{0,2},{1,3},{2,0},{3,1},{4,6},{5,7},{6,4},{7,5},{8,10},{9,11},{10,... | collective-permute-start | bytes 552968 | tf_op jit(solution)/shard_map/ppermute | solution.py:458
  18.7 0.3 collective-permute-start.2
  19.0 3.7 %encode.5.refs_4_ = bf16[8,90,128]{2,1,0:T(8,128)(2,1)S(1)} custom-call(bf16[180,40,256]{2,1,0:T(8,128)(2,1)S(1)} %bitcast.8, bf16[40,256]{1,0:T(8,128)(2,1)S(1)} %collective-permute-done.west_ref, bf16[40,256]{1,0:T(8,128)(2,1)S(1)} %collective-permute-done.1.east_ref, bf16[3,3,256,256]{3,2,1,0:T(8,128)(2,1)S(1)} %copy-done.4, bf16[256,128]{1,0:T(8,128)(2,1)S(1)} %copy-done.5), custom_call_target="tpu_custom_call" | custom-call | flops 2264924160 | bytes 8388608 | tf_op jit(solution)/shard_map/encode/pallas_call | solution.py:269
  22.7 0.0 copy-start
  22.7 0.7 %collective-permute-start.8 = (bf16[8,90,128]{2,1,0:T(8,128)(2,1)S(1)}, bf16[8,90,128]{2,1,0:T(8,128)(2,1)S(1)}, u32[]{:S(2)}, u32[]{:S(2)}) collective-permute-start(bf16[8,90,128]{2,1,0:T(8,128)(2,1)S(1)} %encode.5.refs_4_), channel_id=1, source_target_pairs={{0,2},{1,3},{2,0},{3,1},{4,6},{5,7},{6,4},{7,5},{8,10},{9,11},{10,... | collective-permute-start | bytes 552968 | tf_op jit(solution)/shard_map/ppermute | solution.py:458
  23.5 0.0 collective-permute-done.4.refs_0_
  23.5 0.3 collective-permute-start.7
  23.8 1.3 %collective-permute-done.5.refs_1_ = bf16[3,182,256]{2,1,0:T(8,128)(2,1)S(1)} collective-permute-done((bf16[3,182,256]{2,1,0:T(8,128)(2,1)S(1)}, bf16[3,182,256]{2,1,0:T(8,128)(2,1)S(1)}, u32[]{:S(2)}, u32[]{:S(2)}) %collective-permute-start.5) | collective-permute-done | bytes 279584 | tf_op jit(solution)/shard_map/ppermute | solution.py:444
  25.0 4.4 %encode.4.refs_8_ = bf16[6,90,128]{2,1,0:T(8,128)(2,1)S(1)} custom-call(bf16[180,40,256]{2,1,0:T(8,128)(2,1)S(1)} %bitcast.9, bf16[40,256]{1,0:T(8,128)(2,1)S(1)} %collective-permute-done.west_ref, bf16[40,256]{1,0:T(8,128)(2,1)S(1)} %collective-permute-done.1.east_ref, bf16[3,182,256]{2,1,0:T(8,128)(2,1)S(1)} %collective-permute-done.4.refs_0_, ...), custom_call_target="tpu_custom_call" | custom-call | flops 2264924160 | bytes 8388608 | tf_op jit(solution)/shard_map/encode/pallas_call | solution.py:269
  29.5 0.0 collective-permute-done.8.refs_6_
  29.5 0.0 collective-permute-done.3.refs_2_
  29.5 0.7 %collective-permute-start.6 = (bf16[8,90,128]{2,1,0:T(8,128)(2,1)S(1)}, bf16[8,90,128]{2,1,0:T(8,128)(2,1)S(1)}, u32[]{:S(2)}, u32[]{:S(2)}) collective-permute-start(bf16[8,90,128]{2,1,0:T(8,128)(2,1)S(1)} %collective-permute-done.3.refs_2_), channel_id=1, source_target_pairs={{0,1},{1,0},{2,3},{3,2},{4,5},{5,4},{6,7},{7,6},{8,9},{9,8},{10,11... | collective-permute-start | bytes 552968 | tf_op jit(solution)/shard_map/ppermute | solution.py:464
  30.2 0.1 collective-permute-start.9
  30.2 1.4 %collective-permute-start.12 = (bf16[6,90,128]{2,1,0:T(8,128)(2,1)S(1)}, bf16[6,90,128]{2,1,0:T(8,128)(2,1)S(1)}, u32[]{:S(2)}, u32[]{:S(2)}) collective-permute-start(bf16[6,90,128]{2,1,0:T(8,128)(2,1)S(1)} %encode.4.refs_8_), channel_id=1, source_target_pairs={{0,3},{1,2},{2,1},{3,0},{4,7},{5,6},{6,5},{7,4},{8,11},{9,10},{10,... | collective-permute-start | bytes 414728 | tf_op jit(solution)/shard_map/ppermute | solution.py:461
  31.6 0.0 collective-permute-done.2.refs_1_
  31.6 0.4 collective-permute-start.11
  32.0 0.0 collective-permute-done.7.refs_5_
  32.0 0.3 collective-permute-start.10
  32.4 5.4 %heads.2.refs_15_ = bf16[2,20,360,128]{3,2,1,0:T(8,128)(2,1)} custom-call(bf16[8,90,128]{2,1,0:T(8,128)(2,1)S(1)} %encode.3.refs_0_, bf16[8,90,128]{2,1,0:T(8,128)(2,1)S(1)} %collective-permute-done.2.refs_1_, bf16[8,90,128]{2,1,0:T(8,128)(2,1)S(1)} %collective-permute-done.3.refs_2_, bf16[8,90,128]{2,1,0:T(8,128)(2,1)S(1)} %collective-permute-done.6.refs_3_, ...), custom_call_target="tpu_custom_call" | custom-call | flops 3344302080 | bytes 25165824 | tf_op jit(solution)/shard_map/heads/pallas_call | solution.py:393
  37.8 1.5 %collective-permute-done.11.refs_10_ = bf16[6,90,128]{2,1,0:T(8,128)(2,1)S(1)} collective-permute-done((bf16[6,90,128]{2,1,0:T(8,128)(2,1)S(1)}, bf16[6,90,128]{2,1,0:T(8,128)(2,1)S(1)}, u32[]{:S(2)}, u32[]{:S(2)}) %collective-permute-start.11) | collective-permute-done | bytes 138272 | tf_op jit(solution)/shard_map/ppermute | solution.py:458
  39.3 4.0 %heads.3 = bf16[2,20,360,128]{3,2,1,0:T(8,128)(2,1)} custom-call(bf16[8,90,128]{2,1,0:T(8,128)(2,1)S(1)} %encode.3.refs_0_, bf16[8,90,128]{2,1,0:T(8,128)(2,1)S(1)} %collective-permute-done.2.refs_1_, bf16[8,90,128]{2,1,0:T(8,128)(2,1)S(1)} %collective-permute-done.3.refs_2_, ...), custom_call_target="tpu_custom_call", output_to_operand_aliasing={{}: (15, {})} | custom-call | flops 2229534720 | bytes 16777216 | tf_op jit(solution)/shard_map/heads/pallas_call | solution.py:393
  (16 shorter events, 0.0 us)
Async XLA Ops:
  0.7 5.2 %collective-permute-start.1 = (bf16[40,256]{1,0:T(8,128)(2,1)S(1)}, bf16[40,256]{1,0:T(8,128)(2,1)S(1)}, u32[]{:S(2)}, u32[]{:S(2)}) collective-permute-start(bf16[40,256]{1,0:T(8,128)(2,1)S(1)} %get-tuple-element.21), channel_id=1, source_target_pairs={{1,0},{2,1},{3,2},{0,3},{5,4},{6,5},{7,6},{4,7},{9,8},{10,9},{11,1... | collective-permute-start | bytes 61448 | tf_op jit(solution)/shard_map/ppermute | solution.py:439
  1.4 4.6 %collective-permute-start = (bf16[40,256]{1,0:T(8,128)(2,1)S(1)}, bf16[40,256]{1,0:T(8,128)(2,1)S(1)}, u32[]{:S(2)}, u32[]{:S(2)}) collective-permute-start(bf16[40,256]{1,0:T(8,128)(2,1)S(1)} %get-tuple-element.22), channel_id=1, source_target_pairs={{0,1},{1,2},{2,3},{3,0},{4,5},{5,6},{6,7},{7,4},{8,9},{9,10},{10,1... | collective-permute-start | bytes 61448 | tf_op jit(solution)/shard_map/ppermute | solution.py:438
  6.0 1.1 %copy-start.6 = (bf16[2,3,180,256]{3,2,1,0:T(8,128)(2,1)S(1)}, bf16[2,3,180,256]{3,2,1,0:T(8,128)(2,1)}, u32[]{:S(2)}) copy-start(bf16[2,3,180,256]{3,2,1,0:T(8,128)(2,1)} %get-tuple-element.13.edge_ref) | copy-start | bytes 1658884
  7.1 6.6 %copy-start.3 = (bf16[40,180,256]{2,0,1:T(8,128)(2,1)S(1)}, bf16[40,180,256]{2,0,1:T(8,128)(2,1)}, u32[]{:S(2)}) copy-start(bf16[40,180,256]{2,0,1:T(8,128)(2,1)} %param.8) | copy-start | bytes 11059204
  7.1 6.6 %copy-start.4 = (bf16[3,3,256,256]{3,2,1,0:T(8,128)(2,1)S(1)}, bf16[3,3,256,256]{3,2,1,0:T(8,128)(2,1)}, u32[]{:S(2)}) copy-start(bf16[3,3,256,256]{3,2,1,0:T(8,128)(2,1)} %refs_0_.3) | copy-start | bytes 3538948
  7.1 6.6 %copy-start.5 = (bf16[256,128]{1,0:T(8,128)(2,1)S(1)}, bf16[256,128]{1,0:T(8,128)(2,1)}, u32[]{:S(2)}) copy-start(bf16[256,128]{1,0:T(8,128)(2,1)} %refs_1_.3) | copy-start | bytes 196612
  7.2 16.3 %collective-permute-start.4 = (bf16[3,182,256]{2,1,0:T(8,128)(2,1)S(1)}, bf16[3,182,256]{2,1,0:T(8,128)(2,1)S(1)}, u32[]{:S(2)}, u32[]{:S(2)}) collective-permute-start(bf16[3,182,256]{2,1,0:T(8,128)(2,1)S(1)} %get-tuple-element.14), channel_id=1, source_target_pairs={{0,4},{4,8},{8,12},{12,16},{16,20},{20,24},{24,28},{1,5},{5,9},{9,... | collective-permute-start | bytes 838664 | tf_op jit(solution)/shard_map/ppermute | solution.py:443
  10.6 14.4 %collective-permute-start.5 = (bf16[3,182,256]{2,1,0:T(8,128)(2,1)S(1)}, bf16[3,182,256]{2,1,0:T(8,128)(2,1)S(1)}, u32[]{:S(2)}, u32[]{:S(2)}) collective-permute-start(bf16[3,182,256]{2,1,0:T(8,128)(2,1)S(1)} %get-tuple-element.15), channel_id=1, source_target_pairs={{4,0},{8,4},{12,8},{16,12},{20,16},{24,20},{28,24},{5,1},{9,5},{13... | collective-permute-start | bytes 838664 | tf_op jit(solution)/shard_map/ppermute | solution.py:444
  17.5 12.0 %collective-permute-start.3 = (bf16[8,90,128]{2,1,0:T(8,128)(2,1)S(1)}, bf16[8,90,128]{2,1,0:T(8,128)(2,1)S(1)}, u32[]{:S(2)}, u32[]{:S(2)}) collective-permute-start(bf16[8,90,128]{2,1,0:T(8,128)(2,1)S(1)} %encode.3.refs_0_), channel_id=1, source_target_pairs={{0,2},{1,3},{2,0},{3,1},{4,6},{5,7},{6,4},{7,5},{8,10},{9,11},{10,... | collective-permute-start | bytes 552968 | tf_op jit(solution)/shard_map/ppermute | solution.py:458
  18.7 13.0 %collective-permute-start.2 = (bf16[8,90,128]{2,1,0:T(8,128)(2,1)S(1)}, bf16[8,90,128]{2,1,0:T(8,128)(2,1)S(1)}, u32[]{:S(2)}, u32[]{:S(2)}) collective-permute-start(bf16[8,90,128]{2,1,0:T(8,128)(2,1)S(1)} %encode.3.refs_0_), channel_id=1, source_target_pairs={{0,1},{1,0},{2,3},{3,2},{4,5},{5,4},{6,7},{7,6},{8,9},{9,8},{10,11... | collective-permute-start | bytes 552968 | tf_op jit(solution)/shard_map/ppermute | solution.py:459
  22.7 9.7 %copy-start = (bf16[1152,256]{1,0:T(8,128)(2,1)S(1)}, bf16[1152,256]{1,0:T(8,128)(2,1)}, u32[]{:S(2)}) copy-start(bf16[1152,256]{1,0:T(8,128)(2,1)} %get-tuple-element.18.refs_8_.refs_12_) | copy-start | bytes 1769476
  22.7 9.7 %copy-start.1 = (bf16[368,368]{1,0:T(8,128)(2,1)S(1)}, bf16[368,368]{1,0:T(8,128)(2,1)}, u32[]{:S(2)}) copy-start(bf16[368,368]{1,0:T(8,128)(2,1)} %get-tuple-element.20.refs_10_.refs_14_) | copy-start | bytes 812548
  22.7 9.7 %copy-start.2 = (f32[8,256]{1,0:T(8,128)S(1)}, f32[8,256]{1,0:T(8,128)}, u32[]{:S(2)}) copy-start(f32[8,256]{1,0:T(8,128)} %get-tuple-element.19.refs_9_.refs_13_) | copy-start | bytes 24580
  22.7 6.7 %collective-permute-start.8 = (bf16[8,90,128]{2,1,0:T(8,128)(2,1)S(1)}, bf16[8,90,128]{2,1,0:T(8,128)(2,1)S(1)}, u32[]{:S(2)}, u32[]{:S(2)}) collective-permute-start(bf16[8,90,128]{2,1,0:T(8,128)(2,1)S(1)} %encode.5.refs_4_), channel_id=1, source_target_pairs={{0,2},{1,3},{2,0},{3,1},{4,6},{5,7},{6,4},{7,5},{8,10},{9,11},{10,... | collective-permute-start | bytes 552968 | tf_op jit(solution)/shard_map/ppermute | solution.py:458
  23.5 8.6 %collective-permute-start.7 = (bf16[8,90,128]{2,1,0:T(8,128)(2,1)S(1)}, bf16[8,90,128]{2,1,0:T(8,128)(2,1)S(1)}, u32[]{:S(2)}, u32[]{:S(2)}) collective-permute-start(bf16[8,90,128]{2,1,0:T(8,128)(2,1)S(1)} %encode.5.refs_4_), channel_id=1, source_target_pairs={{0,1},{1,0},{2,3},{3,2},{4,5},{5,4},{6,7},{7,6},{8,9},{9,8},{10,11... | collective-permute-start | bytes 552968 | tf_op jit(solution)/shard_map/ppermute | solution.py:459
  29.5 2.9 %collective-permute-start.6 = (bf16[8,90,128]{2,1,0:T(8,128)(2,1)S(1)}, bf16[8,90,128]{2,1,0:T(8,128)(2,1)S(1)}, u32[]{:S(2)}, u32[]{:S(2)}) collective-permute-start(bf16[8,90,128]{2,1,0:T(8,128)(2,1)S(1)} %collective-permute-done.3.refs_2_), channel_id=1, source_target_pairs={{0,1},{1,0},{2,3},{3,2},{4,5},{5,4},{6,7},{7,6},{8,9},{9,8},{10,11... | collective-permute-start | bytes 552968 | tf_op jit(solution)/shard_map/ppermute | solution.py:464
  30.2 2.2 %collective-permute-start.9 = (bf16[8,90,128]{2,1,0:T(8,128)(2,1)S(1)}, bf16[8,90,128]{2,1,0:T(8,128)(2,1)S(1)}, u32[]{:S(2)}, u32[]{:S(2)}) collective-permute-start(bf16[8,90,128]{2,1,0:T(8,128)(2,1)S(1)} %collective-permute-done.8.refs_6_), channel_id=1, source_target_pairs={{0,1},{1,0},{2,3},{3,2},{4,5},{5,4},{6,7},{7,6},{8,9},{9,8},{10,11... | collective-permute-start | bytes 552968 | tf_op jit(solution)/shard_map/ppermute | solution.py:464
  30.2 7.5 %collective-permute-start.12 = (bf16[6,90,128]{2,1,0:T(8,128)(2,1)S(1)}, bf16[6,90,128]{2,1,0:T(8,128)(2,1)S(1)}, u32[]{:S(2)}, u32[]{:S(2)}) collective-permute-start(bf16[6,90,128]{2,1,0:T(8,128)(2,1)S(1)} %encode.4.refs_8_), channel_id=1, source_target_pairs={{0,3},{1,2},{2,1},{3,0},{4,7},{5,6},{6,5},{7,4},{8,11},{9,10},{10,... | collective-permute-start | bytes 414728 | tf_op jit(solution)/shard_map/ppermute | solution.py:461
  31.6 7.7 %collective-permute-start.11 = (bf16[6,90,128]{2,1,0:T(8,128)(2,1)S(1)}, bf16[6,90,128]{2,1,0:T(8,128)(2,1)S(1)}, u32[]{:S(2)}, u32[]{:S(2)}) collective-permute-start(bf16[6,90,128]{2,1,0:T(8,128)(2,1)S(1)} %encode.4.refs_8_), channel_id=1, source_target_pairs={{0,2},{1,3},{2,0},{3,1},{4,6},{5,7},{6,4},{7,5},{8,10},{9,11},{10,... | collective-permute-start | bytes 414728 | tf_op jit(solution)/shard_map/ppermute | solution.py:458
  32.0 7.3 %collective-permute-start.10 = (bf16[6,90,128]{2,1,0:T(8,128)(2,1)S(1)}, bf16[6,90,128]{2,1,0:T(8,128)(2,1)S(1)}, u32[]{:S(2)}, u32[]{:S(2)}) collective-permute-start(bf16[6,90,128]{2,1,0:T(8,128)(2,1)S(1)} %encode.4.refs_8_), channel_id=1, source_target_pairs={{0,1},{1,0},{2,3},{3,2},{4,5},{5,4},{6,7},{7,6},{8,9},{9,8},{10,11... | collective-permute-start | bytes 414728 | tf_op jit(solution)/shard_map/ppermute | solution.py:459

commit v11 on v10

--- a/solution.py
+++ b/solution.py
@@ -312,7 +312,7 @@
     first = (lat == 0).astype(F32) * vec_ref[BIAS : BIAS + 1, :]
     last = (lat == lax.axis_size("lat") - 1).astype(F32) * vec_ref[BIAS + 2 : BIAS + 3, :]
 
-    wanted = [sorted({n * STEP + i for i in range(STEP + 2)}) for n in blocks]
+    wanted = [list(range(a, a + n + 2)) for a, n in blocks]
     slots = {r: k for k, r in enumerate(sorted(set(sum(wanted, []))))}
     staged = set()
 
@@ -329,18 +329,19 @@
             yield
 
     def conv(n):
-        half = STEP // 2
-        for h in range(2):
-            p = [ps[slots[r]] for r in wanted[n][h * half : (h + 1) * half + 2]]
-            lhs = [jnp.concatenate(p[i : i + 3], axis=1) for i in range(half)]
-            at = slice(h * half * wide, (h + 1) * half * wide)
+        count = blocks[n][1]
+        half = -(-count // 2)
+        for lo, hi in ((0, half), (half, count)):
+            p = [ps[slots[r]] for r in wanted[n][lo : hi + 2]]
+            lhs = [jnp.concatenate(p[i : i + 3], axis=1) for i in range(hi - lo)]
+            at = slice(lo * wide, hi * wide)
             cs[n % 2][at] = jnp.dot(jnp.concatenate(lhs, axis=0), ws_ref[...], preferred_element_type=F32)
             yield
             yield
 
     def finish(n):
-        for i in range(STEP):
-            row = blocks[n] * STEP + i
+        for i in range(blocks[n][1]):
+            row = blocks[n][0] + i
             near = bias - first if row == 0 else (bias - last if row == rows - 1 else bias)
             y = cs[n % 2][i * wide : (i + 1) * wide] + near
             mixed = jnp.dot(zs_ref[...], gelu_twice(y), preferred_element_type=F32)
@@ -357,8 +358,8 @@
         for lead in range(leads):
             sends.append(
                 pltpu.make_async_copy(
-                    outs.at[n, lead],
-                    out_ref.at[lead, blocks[n] * STEP : (blocks[n] + 1) * STEP],
+                    outs.at[n, lead, : blocks[n][1]],
+                    out_ref.at[lead, blocks[n][0] : sum(blocks[n])],
                     out_sem.at[n, lead],
                 )
             )
@@ -382,7 +383,8 @@
     shards = cols // arrays[0].shape[-2]
     wide = zs.shape[0]
     vmem = pl.BlockSpec(memory_space=pltpu.VMEM)
-    staged = len({n * STEP + i for n in blocks for i in range(STEP + 2)})
+    staged = len({a + i for a, n in blocks for i in range(n + 2)})
+    tall = max(n for _, n in blocks)
     operands = [*arrays, ws, vec, zs]
     in_specs = [vmem] * len(operands)
     alias = {}
@@ -397,16 +399,16 @@
         out_shape=jax.ShapeDtypeStruct(shape, BF),
         scratch_shapes=[
             pltpu.VMEM((staged, wide, 3 * ch), BF),
-            pltpu.VMEM((STEP * wide, leads * ch), F32),
-            pltpu.VMEM((STEP * wide, leads * ch), F32),
-            pltpu.VMEM((len(blocks), leads, STEP, cols, ch), BF),
+            pltpu.VMEM((tall * wide, leads * ch), F32),
+            pltpu.VMEM((tall * wide, leads * ch), F32),
+            pltpu.VMEM((len(blocks), leads, tall, cols, ch), BF),
             pltpu.SemaphoreType.DMA((len(blocks), leads)),
         ],
         input_output_aliases=alias,
         compiler_params=params(24 * -(-cols // 360)),
         cost_estimate=pl.CostEstimate(
-            flops=len(blocks) * STEP * cols * leads * ch * 2 * (9 * ch + cols),
-            transcendentals=len(blocks) * STEP * cols * leads * ch,
+            flops=sum(n for _, n in blocks) * cols * leads * ch * 2 * (9 * ch + cols),
+            transcendentals=sum(n for _, n in blocks) * cols * leads * ch,
             bytes_accessed=len(blocks) * 8 * 1024 * 1024,
         ),
         name="heads",
@@ -468,7 +470,11 @@
 
     shape = (leads, band_rows, cols // 2 * lon, head)
     upper, lower = middle - EDGE, band_rows - EDGE - middle
-    blocks = band_rows // STEP
+    near = EDGE + 1
+    count = band_rows - 2 * near
+    parts = -(-count // STEP)
+    cuts = [near + -(-count * i // parts) for i in range(parts + 1)]
+    inside = [(a, b - a) for a, b in zip(cuts, cuts[1:])]
     at = [
         {EDGE + 1 + r: r for r in range(upper)},
         {middle + 1 + r: r for r in range(lower)},
@@ -476,10 +482,10 @@
     ]
     chunks = [(len(a), rows_at) for a, rows_at in zip(sent, at)]
     inner = forecast_heads(
-        sent[0] + sent[1], chunks[:2], ws, vec, zs, None, list(range(1, blocks - 1)), shape
+        sent[0] + sent[1], chunks[:2], ws, vec, zs, None, inside, shape
     )
     return forecast_heads(
-        sent[0] + sent[1] + sent[2], chunks, ws, vec, zs, inner, [0, blocks - 1], shape
+        sent[0] + sent[1] + sent[2], chunks, ws, vec, zs, inner, [(0, near), (band_rows - near, near)], shape
     )
 
 

time: 43.8 us -> 43 us (0.982)
  waiting for transfers between devices: 2.81 us -> 2.13 us
    ppermute x3, waiting for transfers between devices: 1.53 us -> 0.85 us  [shards(): across = lax.ppermute(own, 'lon', swap(lon, 2))]
  transfers between devices with their start and end apart: 13 -> 13, of which waited for: 2 -> 2; matrix products, arithmetic and copies ran while one was open for 0% -> 0% of each run, Pallas kernels for 48% -> 50%
where the time goes in v11:
time: 43 us; the launch traced here: 42.7 us
  Pallas kernels  24.8 us (58%)
  starting transfers between devices  13.7 us (32%)
  waiting for transfers between devices  2.13 us (5%)
  local copies, waits for them, and re-layouts  1.82 us (4%)
    pallas_call x3, Pallas kernels, encode(): pl.pallas_call(functools.partial(encoder_kernel, first=first, group=group...  11.9 us
    pallas_call x2, Pallas kernels, forecast_heads(): pl.pallas_call(functools.partial(head_kernel, chunks=chunks, blocks=block...  9.29 us
    pallas_call x1, Pallas kernels, prepare(): pl.pallas_call(weights_kernel, in_specs=[smem] + [hbm] * 5, out_specs=[vm...  3.46 us
    ppermute x1, starting transfers between devices, shards(): above = lax.ppermute(up, 'lat', lat_up)  3.41 us
    ppermute x1, starting transfers between devices, shards(): below = lax.ppermute(dn, 'lat', lat_dn)  3.07 us
    ppermute x3, starting transfers between devices, shards(): across = lax.ppermute(own, 'lon', swap(lon, 2))  2.36 us
    ppermute x1, starting transfers between devices, shards(): both = lax.ppermute(own, 'lon', swap(lon, 3))  1.4 us
    ppermute x1, waiting for transfers between devices, shards(): below = lax.ppermute(dn, 'lat', lat_dn)  1.25 us
  transfers between devices with their start and end apart: 13, of which 2 were waited for; matrix products, arithmetic and copies ran while one was open for 0% of the time, Pallas kernels for 50%

profile of v11, /device:TPU:25, one launch (start us, length us, event | category | flops | bytes accessed | tf_op | source)
XLA Modules:
  0.0 42.7 jit_solution(3698173010930503083)
XLA Ops:
  0.0 0.7 %slice_bitcast_fusion = (bf16[40,256]{1,0:T(8,128)(2,1)S(1)}, bf16[40,256]{1,0:T(8,128)(2,1)S(1)}) fusion(bf16[180,40,256]{2,1,0:T(8,128)(2,1)} %bitcast.5), kind=kLoop, calls=%fused_computation | loop fusion | bytes 81920 | tf_op jit(solution)/shard_map/squeeze | solution.py:441
  0.7 0.7 %collective-permute-start.1 = (bf16[40,256]{1,0:T(8,128)(2,1)S(1)}, bf16[40,256]{1,0:T(8,128)(2,1)S(1)}, u32[]{:S(2)}, u32[]{:S(2)}) collective-permute-start(bf16[40,256]{1,0:T(8,128)(2,1)S(1)} %get-tuple-element.21), channel_id=1, source_target_pairs={{1,0},{2,1},{3,2},{0,3},{5,4},{6,5},{7,6},{4,7},{9,8},{10,9},{11,1... | collective-permute-start | bytes 61448 | tf_op jit(solution)/shard_map/ppermute | solution.py:441
  1.4 1.1 %collective-permute-start = (bf16[40,256]{1,0:T(8,128)(2,1)S(1)}, bf16[40,256]{1,0:T(8,128)(2,1)S(1)}, u32[]{:S(2)}, u32[]{:S(2)}) collective-permute-start(bf16[40,256]{1,0:T(8,128)(2,1)S(1)} %get-tuple-element.22), channel_id=1, source_target_pairs={{0,1},{1,2},{2,3},{3,0},{4,5},{5,6},{6,7},{7,4},{8,9},{9,10},{10,1... | collective-permute-start | bytes 61448 | tf_op jit(solution)/shard_map/ppermute | solution.py:440
  2.5 3.5 %weights.1 = (bf16[1152,256]{1,0:T(8,128)(2,1)}, f32[8,256]{1,0:T(8,128)}, bf16[368,368]{1,0:T(8,128)(2,1)}, bf16[2,3,180,256]{3,2,1,0:T(8,128)(2,1)}) custom-call(s32[8]{0:T(128)} %ids_ref.1, bf16[180,40,256]{2,1,0:T(8,128)(2,1)} %bitcast.6, bf16[3,3,128,128]{3,2,1,0:T(8,128)(2,1)} %wh_hbm.1, f32[720,128]{1,0:T(8,128)} %scale_hbm.1, f32[720,128]{1,0:T(8,128)} %shift_hbm.1, ...), custom_call_target="tpu_custom_call" | custom-call | flops 2147483648 | bytes 12582912 | tf_op jit(solution)/shard_map/weights/pallas_call | solution.py:98
  6.0 0.0 collective-permute-done.west_ref
  6.0 1.0 %copy-done.6 = bf16[2,3,180,256]{3,2,1,0:T(8,128)(2,1)S(1)} copy-done((bf16[2,3,180,256]{3,2,1,0:T(8,128)(2,1)S(1)}, bf16[2,3,180,256]{3,2,1,0:T(8,128)(2,1)}, u32[]{:S(2)}) %copy-start.6) | copy-done | bytes 552984
  7.1 0.1 slabs.1
  7.2 3.4 %collective-permute-start.4 = (bf16[3,182,256]{2,1,0:T(8,128)(2,1)S(1)}, bf16[3,182,256]{2,1,0:T(8,128)(2,1)S(1)}, u32[]{:S(2)}, u32[]{:S(2)}) collective-permute-start(bf16[3,182,256]{2,1,0:T(8,128)(2,1)S(1)} %get-tuple-element.14), channel_id=1, source_target_pairs={{0,4},{4,8},{8,12},{12,16},{16,20},{20,24},{24,28},{1,5},{5,9},{9,... | collective-permute-start | bytes 838664 | tf_op jit(solution)/shard_map/ppermute | solution.py:445
  10.6 3.1 %collective-permute-start.5 = (bf16[3,182,256]{2,1,0:T(8,128)(2,1)S(1)}, bf16[3,182,256]{2,1,0:T(8,128)(2,1)S(1)}, u32[]{:S(2)}, u32[]{:S(2)}) collective-permute-start(bf16[3,182,256]{2,1,0:T(8,128)(2,1)S(1)} %get-tuple-element.15), channel_id=1, source_target_pairs={{4,0},{8,4},{12,8},{16,12},{20,16},{24,20},{28,24},{5,1},{9,5},{13... | collective-permute-start | bytes 838664 | tf_op jit(solution)/shard_map/ppermute | solution.py:446
  13.7 3.7 %encode.3.refs_0_ = bf16[8,90,128]{2,1,0:T(8,128)(2,1)S(1)} custom-call(bf16[180,40,256]{2,1,0:T(8,128)(2,1)S(1)} %bitcast.7, bf16[40,256]{1,0:T(8,128)(2,1)S(1)} %collective-permute-done.west_ref, bf16[40,256]{1,0:T(8,128)(2,1)S(1)} %collective-permute-done.1.east_ref, bf16[3,3,256,256]{3,2,1,0:T(8,128)(2,1)S(1)} %copy-done.4, bf16[256,128]{1,0:T(8,128)(2,1)S(1)} %copy-done.5), custom_call_target="tpu_custom_call" | custom-call | flops 2264924160 | bytes 8388608 | tf_op jit(solution)/shard_map/encode/pallas_call | solution.py:269
  17.5 1.2 %collective-permute-start.3 = (bf16[8,90,128]{2,1,0:T(8,128)(2,1)S(1)}, bf16[8,90,128]{2,1,0:T(8,128)(2,1)S(1)}, u32[]{:S(2)}, u32[]{:S(2)}) collective-permute-start(bf16[8,90,128]{2,1,0:T(8,128)(2,1)S(1)} %encode.3.refs_0_), channel_id=1, source_target_pairs={{0,2},{1,3},{2,0},{3,1},{4,6},{5,7},{6,4},{7,5},{8,10},{9,11},{10,... | collective-permute-start | bytes 552968 | tf_op jit(solution)/shard_map/ppermute | solution.py:460
  18.7 0.3 collective-permute-start.2
  19.0 3.7 %encode.5.refs_4_ = bf16[8,90,128]{2,1,0:T(8,128)(2,1)S(1)} custom-call(bf16[180,40,256]{2,1,0:T(8,128)(2,1)S(1)} %bitcast.8, bf16[40,256]{1,0:T(8,128)(2,1)S(1)} %collective-permute-done.west_ref, bf16[40,256]{1,0:T(8,128)(2,1)S(1)} %collective-permute-done.1.east_ref, bf16[3,3,256,256]{3,2,1,0:T(8,128)(2,1)S(1)} %copy-done.4, bf16[256,128]{1,0:T(8,128)(2,1)S(1)} %copy-done.5), custom_call_target="tpu_custom_call" | custom-call | flops 2264924160 | bytes 8388608 | tf_op jit(solution)/shard_map/encode/pallas_call | solution.py:269
  22.7 0.0 copy-start
  22.7 0.7 %collective-permute-start.8 = (bf16[8,90,128]{2,1,0:T(8,128)(2,1)S(1)}, bf16[8,90,128]{2,1,0:T(8,128)(2,1)S(1)}, u32[]{:S(2)}, u32[]{:S(2)}) collective-permute-start(bf16[8,90,128]{2,1,0:T(8,128)(2,1)S(1)} %encode.5.refs_4_), channel_id=1, source_target_pairs={{0,2},{1,3},{2,0},{3,1},{4,6},{5,7},{6,4},{7,5},{8,10},{9,11},{10,... | collective-permute-start | bytes 552968 | tf_op jit(solution)/shard_map/ppermute | solution.py:460
  23.5 0.3 collective-permute-start.7
  23.8 1.3 %collective-permute-done.5.refs_1_ = bf16[3,182,256]{2,1,0:T(8,128)(2,1)S(1)} collective-permute-done((bf16[3,182,256]{2,1,0:T(8,128)(2,1)S(1)}, bf16[3,182,256]{2,1,0:T(8,128)(2,1)S(1)}, u32[]{:S(2)}, u32[]{:S(2)}) %collective-permute-start.5) | collective-permute-done | bytes 279584 | tf_op jit(solution)/shard_map/ppermute | solution.py:446
  25.0 4.4 %encode.4.refs_8_ = bf16[6,90,128]{2,1,0:T(8,128)(2,1)S(1)} custom-call(bf16[180,40,256]{2,1,0:T(8,128)(2,1)S(1)} %bitcast.9, bf16[40,256]{1,0:T(8,128)(2,1)S(1)} %collective-permute-done.west_ref, bf16[40,256]{1,0:T(8,128)(2,1)S(1)} %collective-permute-done.1.east_ref, bf16[3,182,256]{2,1,0:T(8,128)(2,1)S(1)} %collective-permute-done.4.refs_0_, ...), custom_call_target="tpu_custom_call" | custom-call | flops 2264924160 | bytes 8388608 | tf_op jit(solution)/shard_map/encode/pallas_call | solution.py:269
  29.5 0.0 collective-permute-done.8.refs_6_
  29.5 0.0 collective-permute-done.3.refs_2_
  29.5 0.7 %collective-permute-start.6 = (bf16[8,90,128]{2,1,0:T(8,128)(2,1)S(1)}, bf16[8,90,128]{2,1,0:T(8,128)(2,1)S(1)}, u32[]{:S(2)}, u32[]{:S(2)}) collective-permute-start(bf16[8,90,128]{2,1,0:T(8,128)(2,1)S(1)} %collective-permute-done.3.refs_2_), channel_id=1, source_target_pairs={{0,1},{1,0},{2,3},{3,2},{4,5},{5,4},{6,7},{7,6},{8,9},{9,8},{10,11... | collective-permute-start | bytes 552968 | tf_op jit(solution)/shard_map/ppermute | solution.py:466
  30.2 0.1 collective-permute-start.9
  30.2 1.4 %collective-permute-start.12 = (bf16[6,90,128]{2,1,0:T(8,128)(2,1)S(1)}, bf16[6,90,128]{2,1,0:T(8,128)(2,1)S(1)}, u32[]{:S(2)}, u32[]{:S(2)}) collective-permute-start(bf16[6,90,128]{2,1,0:T(8,128)(2,1)S(1)} %encode.4.refs_8_), channel_id=1, source_target_pairs={{0,3},{1,2},{2,1},{3,0},{4,7},{5,6},{6,5},{7,4},{8,11},{9,10},{10,... | collective-permute-start | bytes 414728 | tf_op jit(solution)/shard_map/ppermute | solution.py:463
  31.6 0.4 collective-permute-start.11
  32.0 0.3 collective-permute-start.10
  32.4 0.0 collective-permute-done.6.refs_3_
  32.4 0.0 collective-permute-done.9.refs_7_
  32.4 6.0 %heads.2.refs_15_ = bf16[2,20,360,128]{3,2,1,0:T(8,128)(2,1)} custom-call(bf16[8,90,128]{2,1,0:T(8,128)(2,1)S(1)} %encode.3.refs_0_, bf16[8,90,128]{2,1,0:T(8,128)(2,1)S(1)} %collective-permute-done.2.refs_1_, bf16[8,90,128]{2,1,0:T(8,128)(2,1)S(1)} %collective-permute-done.3.refs_2_, bf16[8,90,128]{2,1,0:T(8,128)(2,1)S(1)} %collective-permute-done.6.refs_3_, ...), custom_call_target="tpu_custom_call" | custom-call | flops 3901685760 | bytes 33554432 | tf_op jit(solution)/shard_map/heads/pallas_call | solution.py:395
  38.5 0.0 collective-permute-done.12.refs_11_
  38.5 0.8 %collective-permute-done.11.refs_10_ = bf16[6,90,128]{2,1,0:T(8,128)(2,1)S(1)} collective-permute-done((bf16[6,90,128]{2,1,0:T(8,128)(2,1)S(1)}, bf16[6,90,128]{2,1,0:T(8,128)(2,1)S(1)}, u32[]{:S(2)}, u32[]{:S(2)}) %collective-permute-start.11) | collective-permute-done | bytes 138272 | tf_op jit(solution)/shard_map/ppermute | solution.py:460
  39.3 0.0 collective-permute-done.10.refs_9_
  39.3 3.3 %heads.3 = bf16[2,20,360,128]{3,2,1,0:T(8,128)(2,1)} custom-call(bf16[8,90,128]{2,1,0:T(8,128)(2,1)S(1)} %encode.3.refs_0_, bf16[8,90,128]{2,1,0:T(8,128)(2,1)S(1)} %collective-permute-done.2.refs_1_, bf16[8,90,128]{2,1,0:T(8,128)(2,1)S(1)} %collective-permute-done.3.refs_2_, ...), custom_call_target="tpu_custom_call", output_to_operand_aliasing={{}: (15, {})} | custom-call | flops 1672151040 | bytes 16777216 | tf_op jit(solution)/shard_map/heads/pallas_call | solution.py:395
  (16 shorter events, 0.0 us)
Async XLA Ops:
  0.7 5.2 %collective-permute-start.1 = (bf16[40,256]{1,0:T(8,128)(2,1)S(1)}, bf16[40,256]{1,0:T(8,128)(2,1)S(1)}, u32[]{:S(2)}, u32[]{:S(2)}) collective-permute-start(bf16[40,256]{1,0:T(8,128)(2,1)S(1)} %get-tuple-element.21), channel_id=1, source_target_pairs={{1,0},{2,1},{3,2},{0,3},{5,4},{6,5},{7,6},{4,7},{9,8},{10,9},{11,1... | collective-permute-start | bytes 61448 | tf_op jit(solution)/shard_map/ppermute | solution.py:441
  1.4 4.6 %collective-permute-start = (bf16[40,256]{1,0:T(8,128)(2,1)S(1)}, bf16[40,256]{1,0:T(8,128)(2,1)S(1)}, u32[]{:S(2)}, u32[]{:S(2)}) collective-permute-start(bf16[40,256]{1,0:T(8,128)(2,1)S(1)} %get-tuple-element.22), channel_id=1, source_target_pairs={{0,1},{1,2},{2,3},{3,0},{4,5},{5,6},{6,7},{7,4},{8,9},{9,10},{10,1... | collective-permute-start | bytes 61448 | tf_op jit(solution)/shard_map/ppermute | solution.py:440
  6.0 1.1 %copy-start.6 = (bf16[2,3,180,256]{3,2,1,0:T(8,128)(2,1)S(1)}, bf16[2,3,180,256]{3,2,1,0:T(8,128)(2,1)}, u32[]{:S(2)}) copy-start(bf16[2,3,180,256]{3,2,1,0:T(8,128)(2,1)} %get-tuple-element.13.edge_ref) | copy-start | bytes 1658884
  7.1 6.6 %copy-start.3 = (bf16[40,180,256]{2,0,1:T(8,128)(2,1)S(1)}, bf16[40,180,256]{2,0,1:T(8,128)(2,1)}, u32[]{:S(2)}) copy-start(bf16[40,180,256]{2,0,1:T(8,128)(2,1)} %param.8) | copy-start | bytes 11059204
  7.1 6.6 %copy-start.4 = (bf16[3,3,256,256]{3,2,1,0:T(8,128)(2,1)S(1)}, bf16[3,3,256,256]{3,2,1,0:T(8,128)(2,1)}, u32[]{:S(2)}) copy-start(bf16[3,3,256,256]{3,2,1,0:T(8,128)(2,1)} %refs_0_.3) | copy-start | bytes 3538948
  7.1 6.6 %copy-start.5 = (bf16[256,128]{1,0:T(8,128)(2,1)S(1)}, bf16[256,128]{1,0:T(8,128)(2,1)}, u32[]{:S(2)}) copy-start(bf16[256,128]{1,0:T(8,128)(2,1)} %refs_1_.3) | copy-start | bytes 196612
  7.2 16.3 %collective-permute-start.4 = (bf16[3,182,256]{2,1,0:T(8,128)(2,1)S(1)}, bf16[3,182,256]{2,1,0:T(8,128)(2,1)S(1)}, u32[]{:S(2)}, u32[]{:S(2)}) collective-permute-start(bf16[3,182,256]{2,1,0:T(8,128)(2,1)S(1)} %get-tuple-element.14), channel_id=1, source_target_pairs={{0,4},{4,8},{8,12},{12,16},{16,20},{20,24},{24,28},{1,5},{5,9},{9,... | collective-permute-start | bytes 838664 | tf_op jit(solution)/shard_map/ppermute | solution.py:445
  10.6 14.4 %collective-permute-start.5 = (bf16[3,182,256]{2,1,0:T(8,128)(2,1)S(1)}, bf16[3,182,256]{2,1,0:T(8,128)(2,1)S(1)}, u32[]{:S(2)}, u32[]{:S(2)}) collective-permute-start(bf16[3,182,256]{2,1,0:T(8,128)(2,1)S(1)} %get-tuple-element.15), channel_id=1, source_target_pairs={{4,0},{8,4},{12,8},{16,12},{20,16},{24,20},{28,24},{5,1},{9,5},{13... | collective-permute-start | bytes 838664 | tf_op jit(solution)/shard_map/ppermute | solution.py:446
  17.5 12.0 %collective-permute-start.3 = (bf16[8,90,128]{2,1,0:T(8,128)(2,1)S(1)}, bf16[8,90,128]{2,1,0:T(8,128)(2,1)S(1)}, u32[]{:S(2)}, u32[]{:S(2)}) collective-permute-start(bf16[8,90,128]{2,1,0:T(8,128)(2,1)S(1)} %encode.3.refs_0_), channel_id=1, source_target_pairs={{0,2},{1,3},{2,0},{3,1},{4,6},{5,7},{6,4},{7,5},{8,10},{9,11},{10,... | collective-permute-start | bytes 552968 | tf_op jit(solution)/shard_map/ppermute | solution.py:460
  18.7 13.0 %collective-permute-start.2 = (bf16[8,90,128]{2,1,0:T(8,128)(2,1)S(1)}, bf16[8,90,128]{2,1,0:T(8,128)(2,1)S(1)}, u32[]{:S(2)}, u32[]{:S(2)}) collective-permute-start(bf16[8,90,128]{2,1,0:T(8,128)(2,1)S(1)} %encode.3.refs_0_), channel_id=1, source_target_pairs={{0,1},{1,0},{2,3},{3,2},{4,5},{5,4},{6,7},{7,6},{8,9},{9,8},{10,11... | collective-permute-start | bytes 552968 | tf_op jit(solution)/shard_map/ppermute | solution.py:461
  22.7 9.7 %copy-start = (bf16[1152,256]{1,0:T(8,128)(2,1)S(1)}, bf16[1152,256]{1,0:T(8,128)(2,1)}, u32[]{:S(2)}) copy-start(bf16[1152,256]{1,0:T(8,128)(2,1)} %get-tuple-element.18.refs_8_.refs_12_) | copy-start | bytes 1769476
  22.7 9.7 %copy-start.1 = (bf16[368,368]{1,0:T(8,128)(2,1)S(1)}, bf16[368,368]{1,0:T(8,128)(2,1)}, u32[]{:S(2)}) copy-start(bf16[368,368]{1,0:T(8,128)(2,1)} %get-tuple-element.20.refs_10_.refs_14_) | copy-start | bytes 812548
  22.7 9.7 %copy-start.2 = (f32[8,256]{1,0:T(8,128)S(1)}, f32[8,256]{1,0:T(8,128)}, u32[]{:S(2)}) copy-start(f32[8,256]{1,0:T(8,128)} %get-tuple-element.19.refs_9_.refs_13_) | copy-start | bytes 24580
  22.7 6.7 %collective-permute-start.8 = (bf16[8,90,128]{2,1,0:T(8,128)(2,1)S(1)}, bf16[8,90,128]{2,1,0:T(8,128)(2,1)S(1)}, u32[]{:S(2)}, u32[]{:S(2)}) collective-permute-start(bf16[8,90,128]{2,1,0:T(8,128)(2,1)S(1)} %encode.5.refs_4_), channel_id=1, source_target_pairs={{0,2},{1,3},{2,0},{3,1},{4,6},{5,7},{6,4},{7,5},{8,10},{9,11},{10,... | collective-permute-start | bytes 552968 | tf_op jit(solution)/shard_map/ppermute | solution.py:460
  23.5 8.6 %collective-permute-start.7 = (bf16[8,90,128]{2,1,0:T(8,128)(2,1)S(1)}, bf16[8,90,128]{2,1,0:T(8,128)(2,1)S(1)}, u32[]{:S(2)}, u32[]{:S(2)}) collective-permute-start(bf16[8,90,128]{2,1,0:T(8,128)(2,1)S(1)} %encode.5.refs_4_), channel_id=1, source_target_pairs={{0,1},{1,0},{2,3},{3,2},{4,5},{5,4},{6,7},{7,6},{8,9},{9,8},{10,11... | collective-permute-start | bytes 552968 | tf_op jit(solution)/shard_map/ppermute | solution.py:461
  29.5 2.9 %collective-permute-start.6 = (bf16[8,90,128]{2,1,0:T(8,128)(2,1)S(1)}, bf16[8,90,128]{2,1,0:T(8,128)(2,1)S(1)}, u32[]{:S(2)}, u32[]{:S(2)}) collective-permute-start(bf16[8,90,128]{2,1,0:T(8,128)(2,1)S(1)} %collective-permute-done.3.refs_2_), channel_id=1, source_target_pairs={{0,1},{1,0},{2,3},{3,2},{4,5},{5,4},{6,7},{7,6},{8,9},{9,8},{10,11... | collective-permute-start | bytes 552968 | tf_op jit(solution)/shard_map/ppermute | solution.py:466
  30.2 2.2 %collective-permute-start.9 = (bf16[8,90,128]{2,1,0:T(8,128)(2,1)S(1)}, bf16[8,90,128]{2,1,0:T(8,128)(2,1)S(1)}, u32[]{:S(2)}, u32[]{:S(2)}) collective-permute-start(bf16[8,90,128]{2,1,0:T(8,128)(2,1)S(1)} %collective-permute-done.8.refs_6_), channel_id=1, source_target_pairs={{0,1},{1,0},{2,3},{3,2},{4,5},{5,4},{6,7},{7,6},{8,9},{9,8},{10,11... | collective-permute-start | bytes 552968 | tf_op jit(solution)/shard_map/ppermute | solution.py:466
  30.2 8.2 %collective-permute-start.12 = (bf16[6,90,128]{2,1,0:T(8,128)(2,1)S(1)}, bf16[6,90,128]{2,1,0:T(8,128)(2,1)S(1)}, u32[]{:S(2)}, u32[]{:S(2)}) collective-permute-start(bf16[6,90,128]{2,1,0:T(8,128)(2,1)S(1)} %encode.4.refs_8_), channel_id=1, source_target_pairs={{0,3},{1,2},{2,1},{3,0},{4,7},{5,6},{6,5},{7,4},{8,11},{9,10},{10,... | collective-permute-start | bytes 414728 | tf_op jit(solution)/shard_map/ppermute | solution.py:463
  31.6 7.7 %collective-permute-start.11 = (bf16[6,90,128]{2,1,0:T(8,128)(2,1)S(1)}, bf16[6,90,128]{2,1,0:T(8,128)(2,1)S(1)}, u32[]{:S(2)}, u32[]{:S(2)}) collective-permute-start(bf16[6,90,128]{2,1,0:T(8,128)(2,1)S(1)} %encode.4.refs_8_), channel_id=1, source_target_pairs={{0,2},{1,3},{2,0},{3,1},{4,6},{5,7},{6,4},{7,5},{8,10},{9,11},{10,... | collective-permute-start | bytes 414728 | tf_op jit(solution)/shard_map/ppermute | solution.py:460
  32.0 7.3 %collective-permute-start.10 = (bf16[6,90,128]{2,1,0:T(8,128)(2,1)S(1)}, bf16[6,90,128]{2,1,0:T(8,128)(2,1)S(1)}, u32[]{:S(2)}, u32[]{:S(2)}) collective-permute-start(bf16[6,90,128]{2,1,0:T(8,128)(2,1)S(1)} %encode.4.refs_8_), channel_id=1, source_target_pairs={{0,1},{1,0},{2,3},{3,2},{4,5},{5,4},{6,7},{7,6},{8,9},{9,8},{10,11... | collective-permute-start | bytes 414728 | tf_op jit(solution)/shard_map/ppermute | solution.py:461

commit v12 on v11

--- a/solution.py
+++ b/solution.py
@@ -35,28 +35,14 @@
     return pltpu.CompilerParams(vmem_limit_bytes=mib * MIB)
 
 
-def weights_kernel(
-    ids_ref, x_hbm, wh_hbm, scale_hbm, shift_hbm, z_hbm,
-    ws_ref, vec_ref, zs_ref, edge_ref,
-    wh_ref, tab, z_ref, near, flat, sem,
-):
-    ch = x_hbm.shape[-1]
-    head = wh_ref.shape[-1]
-    leads = ws_ref.shape[1] // head
-    cols = z_ref.shape[0]
-    xcols, rows, _ = x_hbm.shape
+def edges_kernel(x_hbm, edge_ref, near, flat, sem):
+    xcols, rows, ch = x_hbm.shape
     reach = edge_ref.shape[1]
-    ids = [ids_ref[lax.axis_index("lon") * leads + lead] for lead in range(leads)]
-    copies = [(x_hbm.at[:, :8], near.at[0]), (x_hbm.at[:, rows - 8 :], near.at[1])]
-    copies += [(z_hbm, z_ref), (wh_hbm, wh_ref)]
-    for lead in range(leads):
-        block = pl.multiple_of((ids[lead] // 8) * 8, 8)
-        copies.append((scale_hbm.at[pl.ds(block, 8)], tab.at[lead, 0]))
-        copies.append((shift_hbm.at[pl.ds(block, 8)], tab.at[lead, 1]))
-    copies = [pltpu.make_async_copy(one, two, sem.at[i]) for i, (one, two) in enumerate(copies)]
+    copies = [
+        pltpu.make_async_copy(x_hbm.at[:, a : a + 8], near.at[k], sem.at[k]) for k, a in enumerate((0, rows - 8))
+    ]
     for c in copies:
         c.start()
-    zs_ref[...] = jnp.zeros(zs_ref.shape, BF)
     for k in range(2):
         copies[k].wait()
         parts = []
@@ -66,14 +52,37 @@
             parts.append([flat[k, j, pl.ds(first + i, xcols, stride=8), :] for i in range(reach)])
         for i in range(reach):
             edge_ref[k, i] = jnp.concatenate([p[i] for p in parts], axis=1).astype(BF)
-    for c in copies[2:]:
-        c.wait()
+
+
+def edge_rows(x, reach):
+    xcols, _, ch = x.shape
+    return pl.pallas_call(
+        edges_kernel,
+        in_specs=[pl.BlockSpec(memory_space=pltpu.HBM)],
+        out_specs=pl.BlockSpec(memory_space=pltpu.VMEM),
+        out_shape=jax.ShapeDtypeStruct((2, reach, xcols, ch), BF),
+        scratch_shapes=[
+            pltpu.VMEM((2, xcols, 8, ch), BF),
+            pltpu.VMEM((2, ch // 128, xcols * 8, 128), F32),
+            pltpu.SemaphoreType.DMA((2,)),
+        ],
+        compiler_params=params(58),
+        cost_estimate=pl.CostEstimate(flops=1 << 31, transcendentals=0, bytes_accessed=12 * MIB),
+        name="edges",
+    )(x)
+
+
+def weights_kernel(ids_ref, wh_ref, scale_ref, shift_ref, z_ref, ws_ref, vec_ref, zs_ref):
+    head = wh_ref.shape[-1]
+    leads = ws_ref.shape[1] // head
+    cols = z_ref.shape[0]
+    zs_ref[...] = jnp.zeros(zs_ref.shape, BF)
     zs_ref[:cols, :cols] = z_ref[...] * jnp.asarray(0.5, BF)
     for lead in range(leads):
         lanes = slice(lead * head, (lead + 1) * head)
-        at = ids[lead] % 8
-        gain = 1.0 + tab[lead, 0, pl.ds(at, 1), :]
-        shift = tab[lead, 1, pl.ds(at, 1), :]
+        at = ids_ref[lax.axis_index("lon") * leads + lead]
+        gain = 1.0 + scale_ref[pl.ds(at, 1), :]
+        shift = shift_ref[pl.ds(at, 1), :]
         vec_ref[GAIN : GAIN + 1, lanes] = gain
         vec_ref[SHIFT : SHIFT + 1, lanes] = shift
         gain_t = jnp.transpose(jnp.broadcast_to(gain, (head, head)))
@@ -88,35 +97,22 @@
             vec_ref[BIAS + dr : BIAS + dr + 1, lanes] = jnp.sum(total, axis=0, keepdims=True)
 
 
-def prepare(ids, x, w_head, scale, shift, z, leads, reach):
+def prepare(ids, w_head, scale, shift, z, leads):
     head, cols = w_head.shape[-1], z.shape[0]
-    xcols, _, ch = x.shape
     wide = up_to(cols, 16)
     vmem = pl.BlockSpec(memory_space=pltpu.VMEM)
-    smem = pl.BlockSpec(memory_space=pltpu.SMEM)
-    hbm = pl.BlockSpec(memory_space=pltpu.HBM)
     return pl.pallas_call(
         weights_kernel,
-        in_specs=[smem] + [hbm] * 5,
-        out_specs=[vmem] * 4,
+        in_specs=[pl.BlockSpec(memory_space=pltpu.SMEM)] + [vmem] * 4,
+        out_specs=[vmem] * 3,
         out_shape=[
             jax.ShapeDtypeStruct((9 * head, leads * head), BF),
             jax.ShapeDtypeStruct((8, leads * head), F32),
             jax.ShapeDtypeStruct((wide, wide), BF),
-            jax.ShapeDtypeStruct((2, reach, xcols, ch), BF),
         ],
-        scratch_shapes=[
-            pltpu.VMEM(w_head.shape, BF),
-            pltpu.VMEM((leads, 2, 8, head), F32),
-            pltpu.VMEM(z.shape, BF),
-            pltpu.VMEM((2, xcols, 8, ch), BF),
-            pltpu.VMEM((2, ch // 128, xcols * 8, 128), F32),
-            pltpu.SemaphoreType.DMA((4 + 2 * leads,)),
-        ],
-        compiler_params=params(58),
-        cost_estimate=pl.CostEstimate(flops=1 << 31, transcendentals=0, bytes_accessed=12 * MIB),
+        compiler_params=params(16),
         name="weights",
-    )(ids, x, w_head, scale, shift, z)
+    )(ids, w_head, scale, shift, z)
 
 
 def slabs_kernel(edge_ref, west_ref, east_ref, up_ref, dn_ref):
@@ -440,19 +436,21 @@
     west = lax.ppermute(tile[-1], "lon", lon_up)
     east = lax.ppermute(tile[0], "lon", lon_dn)
 
-    ws, vec, zs, edge = prepare(lead_ids, tile, w_head, film_scale, film_shift, zonal_mix, leads, reach)
+    edge = edge_rows(tile, reach)
     up, dn = row_slabs(edge, west, east)
+    west, east, up, dn = lax.optimization_barrier((west, east, up, dn))
     above = lax.ppermute(up, "lat", lat_up)
     below = lax.ppermute(dn, "lat", lat_dn)
 
     middle = band_rows // 2
     group = cols // 6
-    plan = [
-        (2 * EDGE, middle - EDGE, None),
-        (2 * middle, band_rows - EDGE - middle, None),
-        (None, 2 * (EDGE + 1), (above, below)),
-    ]
-    proj = [encode(tile, west, east, halos, w_enc, w_proj, first, n, group) for first, n, halos in plan]
+    upper = encode(tile, west, east, None, w_enc, w_proj, 2 * EDGE, middle - EDGE, group)
+    lower = encode(tile, west, east, None, w_enc, w_proj, 2 * middle, band_rows - EDGE - middle, group)
+    ids, _ = lax.optimization_barrier((lead_ids, lower))
+    ws, vec, zs = prepare(ids, w_head, film_scale, film_shift, zonal_mix, leads)
+    wp, ws, vec, zs = lax.optimization_barrier((w_proj, ws, vec, zs))
+    edges = encode(tile, west, east, (above, below), w_enc, wp, None, 2 * (EDGE + 1), group)
+    proj = [upper, lower, edges]
 
     sent = []
     for k, own in enumerate(proj):

time: 43 us -> 42.4 us (0.986)
  waiting for transfers between devices: 2.13 us -> 0.52 us
  starting transfers between devices: 13.7 us -> 14.3 us
    ppermute x1, waiting for transfers between devices: 1.25 us -> 0.01 us  [shards(): below = lax.ppermute(dn, 'lat', lat_dn)]
    ppermute x3, starting transfers between devices: 0.91 us -> 1.64 us  [shards(): beside = lax.ppermute(own, 'lon', swap(lon, 1))]
    ppermute x3, starting transfers between devices: 2.36 us -> 2.81 us  [shards(): across = lax.ppermute(own, 'lon', swap(lon, 2))]
    pallas_call x1 -> x2, Pallas kernels: 3.46 us -> 3.26 us  [the longest x1 2.36 us: edge_rows(): pl.pallas_call(edges_kernel, in_specs=[pl.BlockSpec(memory_space=pltpu.HB...]
    unnamed x14 -> x18, local copies, waits for them, and re-layouts: 1.07 us -> 1.25 us
  transfers between devices with their start and end apart: 13 -> 13, of which waited for: 2 -> 1; matrix products, arithmetic and copies ran while one was open for 0% -> 0% of each run, Pallas kernels for 50% -> 51%
where the time goes in v12:
time: 42.4 us; the launch traced here: 42.1 us
  Pallas kernels  24.9 us (59%)
  starting transfers between devices  14.3 us (34%)
  local copies, waits for them, and re-layouts  2 us (5%)
  waiting for transfers between devices  0.52 us (1%)
    pallas_call x3, Pallas kernels, encode(): pl.pallas_call(functools.partial(encoder_kernel, first=first, group=group...  12.1 us
    pallas_call x2, Pallas kernels, forecast_heads(): pl.pallas_call(functools.partial(head_kernel, chunks=chunks, blocks=block...  9.38 us
    ppermute x1, starting transfers between devices, shards(): above = lax.ppermute(up, 'lat', lat_up)  3.28 us
    ppermute x1, starting transfers between devices, shards(): below = lax.ppermute(dn, 'lat', lat_dn)  3.03 us
    ppermute x3, starting transfers between devices, shards(): across = lax.ppermute(own, 'lon', swap(lon, 2))  2.81 us
    pallas_call x1, Pallas kernels, edge_rows(): pl.pallas_call(edges_kernel, in_specs=[pl.BlockSpec(memory_space=pltpu.HB...  2.36 us
    ppermute x3, starting transfers between devices, shards(): beside = lax.ppermute(own, 'lon', swap(lon, 1))  1.64 us
    unnamed x18, local copies, waits for them, and re-layouts  1.25 us
  transfers between devices with their start and end apart: 13, of which 1 were waited for; matrix products, arithmetic and copies ran while one was open for 0% of the time, Pallas kernels for 51%

profile of v12, /device:TPU:25, one launch (start us, length us, event | category | flops | bytes accessed | tf_op | source)
XLA Modules:
  0.0 42.1 jit_solution(10765717380959518874)
XLA Ops:
  0.0 0.7 %slice_bitcast_fusion = (bf16[40,256]{1,0:T(8,128)(2,1)S(1)}, bf16[40,256]{1,0:T(8,128)(2,1)S(1)}) fusion(bf16[180,40,256]{2,1,0:T(8,128)(2,1)} %bitcast.5), kind=kLoop, calls=%fused_computation | loop fusion | bytes 81920 | tf_op jit(solution)/shard_map/squeeze | solution.py:437
  0.7 0.7 %collective-permute-start.1 = (bf16[40,256]{1,0:T(8,128)(2,1)S(1)}, bf16[40,256]{1,0:T(8,128)(2,1)S(1)}, u32[]{:S(2)}, u32[]{:S(2)}) collective-permute-start(bf16[40,256]{1,0:T(8,128)(2,1)S(1)} %get-tuple-element.37), channel_id=1, source_target_pairs={{1,0},{2,1},{3,2},{0,3},{5,4},{6,5},{7,6},{4,7},{9,8},{10,9},{11,1... | collective-permute-start | bytes 61448 | tf_op jit(solution)/shard_map/ppermute | solution.py:437
  1.4 1.1 %collective-permute-start = (bf16[40,256]{1,0:T(8,128)(2,1)S(1)}, bf16[40,256]{1,0:T(8,128)(2,1)S(1)}, u32[]{:S(2)}, u32[]{:S(2)}) collective-permute-start(bf16[40,256]{1,0:T(8,128)(2,1)S(1)} %get-tuple-element.38), channel_id=1, source_target_pairs={{0,1},{1,2},{2,3},{3,0},{4,5},{5,6},{6,7},{7,4},{8,9},{9,10},{10,1... | collective-permute-start | bytes 61448 | tf_op jit(solution)/shard_map/ppermute | solution.py:436
  2.5 2.4 %edges.1.edge_ref = bf16[2,3,180,256]{3,2,1,0:T(8,128)(2,1)} custom-call(bf16[180,40,256]{2,1,0:T(8,128)(2,1)} %bitcast.6), custom_call_target="tpu_custom_call" | custom-call | flops 2147483648 | bytes 12582912 | tf_op jit(solution)/shard_map/edges/pallas_call | solution.py:59
  4.9 0.0 copy-start.5
  4.9 0.0 copy-start.6
  4.9 0.0 copy-start.7
  5.0 0.0 copy-start.8
  5.0 1.2 %copy-done.8 = bf16[2,3,180,256]{3,2,1,0:T(8,128)(2,1)S(1)} copy-done((bf16[2,3,180,256]{3,2,1,0:T(8,128)(2,1)S(1)}, bf16[2,3,180,256]{3,2,1,0:T(8,128)(2,1)}, u32[]{:S(2)}) %copy-start.8) | copy-done | bytes 552984
  6.2 0.1 slabs.1
  6.3 3.3 %collective-permute-start.4 = (bf16[3,182,256]{2,1,0:T(8,128)(2,1)S(1)}, bf16[3,182,256]{2,1,0:T(8,128)(2,1)S(1)}, u32[]{:S(2)}, u32[]{:S(2)}) collective-permute-start(bf16[3,182,256]{2,1,0:T(8,128)(2,1)S(1)} %get-tuple-element.25), channel_id=1, source_target_pairs={{0,4},{4,8},{8,12},{12,16},{16,20},{20,24},{24,28},{1,5},{5,9},{9,... | collective-permute-start | bytes 838664 | tf_op jit(solution)/shard_map/ppermute | solution.py:442
  9.6 3.0 %collective-permute-start.5 = (bf16[3,182,256]{2,1,0:T(8,128)(2,1)S(1)}, bf16[3,182,256]{2,1,0:T(8,128)(2,1)S(1)}, u32[]{:S(2)}, u32[]{:S(2)}) collective-permute-start(bf16[3,182,256]{2,1,0:T(8,128)(2,1)S(1)} %get-tuple-element.26), channel_id=1, source_target_pairs={{4,0},{8,4},{12,8},{16,12},{20,16},{24,20},{28,24},{5,1},{9,5},{13... | collective-permute-start | bytes 838664 | tf_op jit(solution)/shard_map/ppermute | solution.py:443
  12.7 3.7 %encode.3.refs_0_ = bf16[8,90,128]{2,1,0:T(8,128)(2,1)S(1)} custom-call(bf16[180,40,256]{2,1,0:T(8,128)(2,1)S(1)} %bitcast.7, bf16[40,256]{1,0:T(8,128)(2,1)S(1)} %collective-permute-done.west_ref, bf16[40,256]{1,0:T(8,128)(2,1)S(1)} %collective-permute-done.1.east_ref, bf16[3,3,256,256]{3,2,1,0:T(8,128)(2,1)S(1)} %copy-done.6, bf16[256,128]{1,0:T(8,128)(2,1)S(1)} %copy-done.7), custom_call_target="tpu_custom_call" | custom-call | flops 2264924160 | bytes 8388608 | tf_op jit(solution)/shard_map/encode/pallas_call | solution.py:265
  16.4 0.0 copy-start
  16.4 0.0 copy-start.1
  16.4 0.0 copy-start.3
  16.4 0.0 copy-start.4
  16.5 1.2 %collective-permute-start.3 = (bf16[8,90,128]{2,1,0:T(8,128)(2,1)S(1)}, bf16[8,90,128]{2,1,0:T(8,128)(2,1)S(1)}, u32[]{:S(2)}, u32[]{:S(2)}) collective-permute-start(bf16[8,90,128]{2,1,0:T(8,128)(2,1)S(1)} %encode.3.refs_0_), channel_id=1, source_target_pairs={{0,2},{1,3},{2,0},{3,1},{4,6},{5,7},{6,4},{7,5},{8,10},{9,11},{10,... | collective-permute-start | bytes 552968 | tf_op jit(solution)/shard_map/ppermute | solution.py:458
  17.7 0.7 %collective-permute-start.2 = (bf16[8,90,128]{2,1,0:T(8,128)(2,1)S(1)}, bf16[8,90,128]{2,1,0:T(8,128)(2,1)S(1)}, u32[]{:S(2)}, u32[]{:S(2)}) collective-permute-start(bf16[8,90,128]{2,1,0:T(8,128)(2,1)S(1)} %encode.3.refs_0_), channel_id=1, source_target_pairs={{0,1},{1,0},{2,3},{3,2},{4,5},{5,4},{6,7},{7,6},{8,9},{9,8},{10,11... | collective-permute-start | bytes 552968 | tf_op jit(solution)/shard_map/ppermute | solution.py:459
  18.4 3.7 %encode.4.refs_4_ = bf16[8,90,128]{2,1,0:T(8,128)(2,1)S(1)} custom-call(bf16[180,40,256]{2,1,0:T(8,128)(2,1)S(1)} %bitcast.8, bf16[40,256]{1,0:T(8,128)(2,1)S(1)} %collective-permute-done.west_ref, bf16[40,256]{1,0:T(8,128)(2,1)S(1)} %collective-permute-done.1.east_ref, bf16[3,3,256,256]{3,2,1,0:T(8,128)(2,1)S(1)} %copy-done.6, bf16[256,128]{1,0:T(8,128)(2,1)S(1)} %copy-done.7), custom_call_target="tpu_custom_call" | custom-call | flops 2264924160 | bytes 8388608 | tf_op jit(solution)/shard_map/encode/pallas_call | solution.py:265
  22.2 1.2 %collective-permute-start.8 = (bf16[8,90,128]{2,1,0:T(8,128)(2,1)S(1)}, bf16[8,90,128]{2,1,0:T(8,128)(2,1)S(1)}, u32[]{:S(2)}, u32[]{:S(2)}) collective-permute-start(bf16[8,90,128]{2,1,0:T(8,128)(2,1)S(1)} %encode.4.refs_4_), channel_id=1, source_target_pairs={{0,2},{1,3},{2,0},{3,1},{4,6},{5,7},{6,4},{7,5},{8,10},{9,11},{10,... | collective-permute-start | bytes 552968 | tf_op jit(solution)/shard_map/ppermute | solution.py:458
  23.4 0.9 %weights.1 = (bf16[1152,256]{1,0:T(8,128)(2,1)S(1)}, f32[8,256]{1,0:T(8,128)S(1)}, bf16[368,368]{1,0:T(8,128)(2,1)S(1)}) custom-call(s32[8]{0:T(128)S(1)} %copy-done.4, bf16[3,3,128,128]{3,2,1,0:T(8,128)(2,1)S(1)} %copy-done.2, f32[720,128]{1,0:T(8,128)S(1)} %copy-done, f32[720,128]{1,0:T(8,128)S(1)} %copy-done.1, bf16[360,360]{1,0:T(8,128)(2,1)S(1)} %copy-done.3), custom_call_target="tpu_custom_call" | custom-call | tf_op jit(solution)/shard_map/weights/pallas_call | solution.py:104
  24.3 0.3 collective-permute-start.7
  24.7 4.6 %encode.5.refs_8_ = bf16[6,90,128]{2,1,0:T(8,128)(2,1)S(1)} custom-call(bf16[180,40,256]{2,1,0:T(8,128)(2,1)S(1)} %bitcast.9, bf16[40,256]{1,0:T(8,128)(2,1)S(1)} %collective-permute-done.west_ref, bf16[40,256]{1,0:T(8,128)(2,1)S(1)} %collective-permute-done.1.east_ref, bf16[3,182,256]{2,1,0:T(8,128)(2,1)S(1)} %collective-permute-done.4.refs_0_, ...), custom_call_target="tpu_custom_call" | custom-call | flops 2264924160 | bytes 8388608 | tf_op jit(solution)/shard_map/encode/pallas_call | solution.py:265
  29.3 0.3 collective-permute-start.6
  29.6 0.3 collective-permute-start.9
  29.9 1.2 %collective-permute-start.12 = (bf16[6,90,128]{2,1,0:T(8,128)(2,1)S(1)}, bf16[6,90,128]{2,1,0:T(8,128)(2,1)S(1)}, u32[]{:S(2)}, u32[]{:S(2)}) collective-permute-start(bf16[6,90,128]{2,1,0:T(8,128)(2,1)S(1)} %encode.5.refs_8_), channel_id=1, source_target_pairs={{0,3},{1,2},{2,1},{3,0},{4,7},{5,6},{6,5},{7,4},{8,11},{9,10},{10,... | collective-permute-start | bytes 414728 | tf_op jit(solution)/shard_map/ppermute | solution.py:461
  31.1 0.4 collective-permute-start.11
  31.5 0.6 %collective-permute-start.10 = (bf16[6,90,128]{2,1,0:T(8,128)(2,1)S(1)}, bf16[6,90,128]{2,1,0:T(8,128)(2,1)S(1)}, u32[]{:S(2)}, u32[]{:S(2)}) collective-permute-start(bf16[6,90,128]{2,1,0:T(8,128)(2,1)S(1)} %encode.5.refs_8_), channel_id=1, source_target_pairs={{0,1},{1,0},{2,3},{3,2},{4,5},{5,4},{6,7},{7,6},{8,9},{9,8},{10,11... | collective-permute-start | bytes 414728 | tf_op jit(solution)/shard_map/ppermute | solution.py:459
  32.0 6.1 %heads.2.refs_15_ = bf16[2,20,360,128]{3,2,1,0:T(8,128)(2,1)} custom-call(bf16[8,90,128]{2,1,0:T(8,128)(2,1)S(1)} %encode.3.refs_0_, bf16[8,90,128]{2,1,0:T(8,128)(2,1)S(1)} %collective-permute-done.2.refs_1_, bf16[8,90,128]{2,1,0:T(8,128)(2,1)S(1)} %collective-permute-done.3.refs_2_, bf16[8,90,128]{2,1,0:T(8,128)(2,1)S(1)} %collective-permute-done.6.refs_3_, ...), custom_call_target="tpu_custom_call" | custom-call | flops 3901685760 | bytes 33554432 | tf_op jit(solution)/shard_map/heads/pallas_call | solution.py:391
  38.1 0.5 %collective-permute-done.11.refs_10_ = bf16[6,90,128]{2,1,0:T(8,128)(2,1)S(1)} collective-permute-done((bf16[6,90,128]{2,1,0:T(8,128)(2,1)S(1)}, bf16[6,90,128]{2,1,0:T(8,128)(2,1)S(1)}, u32[]{:S(2)}, u32[]{:S(2)}) %collective-permute-start.11) | collective-permute-done | bytes 138272 | tf_op jit(solution)/shard_map/ppermute | solution.py:458
  38.6 3.3 %heads.3 = bf16[2,20,360,128]{3,2,1,0:T(8,128)(2,1)} custom-call(bf16[8,90,128]{2,1,0:T(8,128)(2,1)S(1)} %encode.3.refs_0_, bf16[8,90,128]{2,1,0:T(8,128)(2,1)S(1)} %collective-permute-done.2.refs_1_, bf16[8,90,128]{2,1,0:T(8,128)(2,1)S(1)} %collective-permute-done.3.refs_2_, ...), custom_call_target="tpu_custom_call", output_to_operand_aliasing={{}: (15, {})} | custom-call | flops 1672151040 | bytes 16777216 | tf_op jit(solution)/shard_map/heads/pallas_call | solution.py:391
  (21 shorter events, 0.1 us)
Async XLA Ops:
  0.7 4.2 %collective-permute-start.1 = (bf16[40,256]{1,0:T(8,128)(2,1)S(1)}, bf16[40,256]{1,0:T(8,128)(2,1)S(1)}, u32[]{:S(2)}, u32[]{:S(2)}) collective-permute-start(bf16[40,256]{1,0:T(8,128)(2,1)S(1)} %get-tuple-element.37), channel_id=1, source_target_pairs={{1,0},{2,1},{3,2},{0,3},{5,4},{6,5},{7,6},{4,7},{9,8},{10,9},{11,1... | collective-permute-start | bytes 61448 | tf_op jit(solution)/shard_map/ppermute | solution.py:437
  1.4 3.5 %collective-permute-start = (bf16[40,256]{1,0:T(8,128)(2,1)S(1)}, bf16[40,256]{1,0:T(8,128)(2,1)S(1)}, u32[]{:S(2)}, u32[]{:S(2)}) collective-permute-start(bf16[40,256]{1,0:T(8,128)(2,1)S(1)} %get-tuple-element.38), channel_id=1, source_target_pairs={{0,1},{1,2},{2,3},{3,0},{4,5},{5,6},{6,7},{7,4},{8,9},{9,10},{10,1... | collective-permute-start | bytes 61448 | tf_op jit(solution)/shard_map/ppermute | solution.py:436
  4.9 7.7 %copy-start.5 = (bf16[40,180,256]{2,0,1:T(8,128)(2,1)S(1)}, bf16[40,180,256]{2,0,1:T(8,128)(2,1)}, u32[]{:S(2)}) copy-start(bf16[40,180,256]{2,0,1:T(8,128)(2,1)} %param.8) | copy-start | bytes 11059204
  4.9 7.7 %copy-start.6 = (bf16[3,3,256,256]{3,2,1,0:T(8,128)(2,1)S(1)}, bf16[3,3,256,256]{3,2,1,0:T(8,128)(2,1)}, u32[]{:S(2)}) copy-start(bf16[3,3,256,256]{3,2,1,0:T(8,128)(2,1)} %refs_2_.1) | copy-start | bytes 3538948
  4.9 7.7 %copy-start.7 = (bf16[256,128]{1,0:T(8,128)(2,1)S(1)}, bf16[256,128]{1,0:T(8,128)(2,1)}, u32[]{:S(2)}) copy-start(bf16[256,128]{1,0:T(8,128)(2,1)} %refs_3_) | copy-start | bytes 196612
  5.0 1.2 %copy-start.8 = (bf16[2,3,180,256]{3,2,1,0:T(8,128)(2,1)S(1)}, bf16[2,3,180,256]{3,2,1,0:T(8,128)(2,1)}, u32[]{:S(2)}) copy-start(bf16[2,3,180,256]{3,2,1,0:T(8,128)(2,1)} %edges.1.edge_ref) | copy-start | bytes 1658884
  6.3 18.0 %collective-permute-start.4 = (bf16[3,182,256]{2,1,0:T(8,128)(2,1)S(1)}, bf16[3,182,256]{2,1,0:T(8,128)(2,1)S(1)}, u32[]{:S(2)}, u32[]{:S(2)}) collective-permute-start(bf16[3,182,256]{2,1,0:T(8,128)(2,1)S(1)} %get-tuple-element.25), channel_id=1, source_target_pairs={{0,4},{4,8},{8,12},{12,16},{16,20},{20,24},{24,28},{1,5},{5,9},{9,... | collective-permute-start | bytes 838664 | tf_op jit(solution)/shard_map/ppermute | solution.py:442
  9.6 15.1 %collective-permute-start.5 = (bf16[3,182,256]{2,1,0:T(8,128)(2,1)S(1)}, bf16[3,182,256]{2,1,0:T(8,128)(2,1)S(1)}, u32[]{:S(2)}, u32[]{:S(2)}) collective-permute-start(bf16[3,182,256]{2,1,0:T(8,128)(2,1)S(1)} %get-tuple-element.26), channel_id=1, source_target_pairs={{4,0},{8,4},{12,8},{16,12},{20,16},{24,20},{28,24},{5,1},{9,5},{13... | collective-permute-start | bytes 838664 | tf_op jit(solution)/shard_map/ppermute | solution.py:443
  16.4 7.0 %copy-start = (f32[720,128]{1,0:T(8,128)S(1)}, f32[720,128]{1,0:T(8,128)}, u32[]{:S(2)}) copy-start(f32[720,128]{1,0:T(8,128)} %scale_ref.1) | copy-start | bytes 1105924
  16.4 7.0 %copy-start.1 = (f32[720,128]{1,0:T(8,128)S(1)}, f32[720,128]{1,0:T(8,128)}, u32[]{:S(2)}) copy-start(f32[720,128]{1,0:T(8,128)} %shift_ref.1) | copy-start | bytes 1105924
  16.4 7.0 %copy-start.2 = (bf16[3,3,128,128]{3,2,1,0:T(8,128)(2,1)S(1)}, bf16[3,3,128,128]{3,2,1,0:T(8,128)(2,1)}, u32[]{:S(2)}) copy-start(bf16[3,3,128,128]{3,2,1,0:T(8,128)(2,1)} %wh_ref.1) | copy-start | bytes 884740
  16.4 6.9 %copy-start.3 = (bf16[360,360]{1,0:T(8,128)(2,1)S(1)}, bf16[360,360]{1,0:T(8,128)(2,1)}, u32[]{:S(2)}) copy-start(bf16[360,360]{1,0:T(8,128)(2,1)} %z_ref.1) | copy-start | bytes 777604
  16.4 6.9 %copy-start.4 = (s32[8]{0:T(128)S(1)}, s32[8]{0:T(128)}, u32[]{:S(2)}) copy-start(s32[8]{0:T(128)} %ids_ref) | copy-start | bytes 100
  16.5 12.8 %collective-permute-start.3 = (bf16[8,90,128]{2,1,0:T(8,128)(2,1)S(1)}, bf16[8,90,128]{2,1,0:T(8,128)(2,1)S(1)}, u32[]{:S(2)}, u32[]{:S(2)}) collective-permute-start(bf16[8,90,128]{2,1,0:T(8,128)(2,1)S(1)} %encode.3.refs_0_), channel_id=1, source_target_pairs={{0,2},{1,3},{2,0},{3,1},{4,6},{5,7},{6,4},{7,5},{8,10},{9,11},{10,... | collective-permute-start | bytes 552968 | tf_op jit(solution)/shard_map/ppermute | solution.py:458
  17.7 13.4 %collective-permute-start.2 = (bf16[8,90,128]{2,1,0:T(8,128)(2,1)S(1)}, bf16[8,90,128]{2,1,0:T(8,128)(2,1)S(1)}, u32[]{:S(2)}, u32[]{:S(2)}) collective-permute-start(bf16[8,90,128]{2,1,0:T(8,128)(2,1)S(1)} %encode.3.refs_0_), channel_id=1, source_target_pairs={{0,1},{1,0},{2,3},{3,2},{4,5},{5,4},{6,7},{7,6},{8,9},{9,8},{10,11... | collective-permute-start | bytes 552968 | tf_op jit(solution)/shard_map/ppermute | solution.py:459
  22.2 7.1 %collective-permute-start.8 = (bf16[8,90,128]{2,1,0:T(8,128)(2,1)S(1)}, bf16[8,90,128]{2,1,0:T(8,128)(2,1)S(1)}, u32[]{:S(2)}, u32[]{:S(2)}) collective-permute-start(bf16[8,90,128]{2,1,0:T(8,128)(2,1)S(1)} %encode.4.refs_4_), channel_id=1, source_target_pairs={{0,2},{1,3},{2,0},{3,1},{4,6},{5,7},{6,4},{7,5},{8,10},{9,11},{10,... | collective-permute-start | bytes 552968 | tf_op jit(solution)/shard_map/ppermute | solution.py:458
  24.3 7.2 %collective-permute-start.7 = (bf16[8,90,128]{2,1,0:T(8,128)(2,1)S(1)}, bf16[8,90,128]{2,1,0:T(8,128)(2,1)S(1)}, u32[]{:S(2)}, u32[]{:S(2)}) collective-permute-start(bf16[8,90,128]{2,1,0:T(8,128)(2,1)S(1)} %encode.4.refs_4_), channel_id=1, source_target_pairs={{0,1},{1,0},{2,3},{3,2},{4,5},{5,4},{6,7},{7,6},{8,9},{9,8},{10,11... | collective-permute-start | bytes 552968 | tf_op jit(solution)/shard_map/ppermute | solution.py:459
  29.3 2.7 %collective-permute-start.6 = (bf16[8,90,128]{2,1,0:T(8,128)(2,1)S(1)}, bf16[8,90,128]{2,1,0:T(8,128)(2,1)S(1)}, u32[]{:S(2)}, u32[]{:S(2)}) collective-permute-start(bf16[8,90,128]{2,1,0:T(8,128)(2,1)S(1)} %collective-permute-done.3.refs_2_), channel_id=1, source_target_pairs={{0,1},{1,0},{2,3},{3,2},{4,5},{5,4},{6,7},{7,6},{8,9},{9,8},{10,11... | collective-permute-start | bytes 552968 | tf_op jit(solution)/shard_map/ppermute | solution.py:464
  29.6 2.4 %collective-permute-start.9 = (bf16[8,90,128]{2,1,0:T(8,128)(2,1)S(1)}, bf16[8,90,128]{2,1,0:T(8,128)(2,1)S(1)}, u32[]{:S(2)}, u32[]{:S(2)}) collective-permute-start(bf16[8,90,128]{2,1,0:T(8,128)(2,1)S(1)} %collective-permute-done.8.refs_6_), channel_id=1, source_target_pairs={{0,1},{1,0},{2,3},{3,2},{4,5},{5,4},{6,7},{7,6},{8,9},{9,8},{10,11... | collective-permute-start | bytes 552968 | tf_op jit(solution)/shard_map/ppermute | solution.py:464
  29.9 8.3 %collective-permute-start.12 = (bf16[6,90,128]{2,1,0:T(8,128)(2,1)S(1)}, bf16[6,90,128]{2,1,0:T(8,128)(2,1)S(1)}, u32[]{:S(2)}, u32[]{:S(2)}) collective-permute-start(bf16[6,90,128]{2,1,0:T(8,128)(2,1)S(1)} %encode.5.refs_8_), channel_id=1, source_target_pairs={{0,3},{1,2},{2,1},{3,0},{4,7},{5,6},{6,5},{7,4},{8,11},{9,10},{10,... | collective-permute-start | bytes 414728 | tf_op jit(solution)/shard_map/ppermute | solution.py:461
  31.1 7.5 %collective-permute-start.11 = (bf16[6,90,128]{2,1,0:T(8,128)(2,1)S(1)}, bf16[6,90,128]{2,1,0:T(8,128)(2,1)S(1)}, u32[]{:S(2)}, u32[]{:S(2)}) collective-permute-start(bf16[6,90,128]{2,1,0:T(8,128)(2,1)S(1)} %encode.5.refs_8_), channel_id=1, source_target_pairs={{0,2},{1,3},{2,0},{3,1},{4,6},{5,7},{6,4},{7,5},{8,10},{9,11},{10,... | collective-permute-start | bytes 414728 | tf_op jit(solution)/shard_map/ppermute | solution.py:458
  31.5 7.2 %collective-permute-start.10 = (bf16[6,90,128]{2,1,0:T(8,128)(2,1)S(1)}, bf16[6,90,128]{2,1,0:T(8,128)(2,1)S(1)}, u32[]{:S(2)}, u32[]{:S(2)}) collective-permute-start(bf16[6,90,128]{2,1,0:T(8,128)(2,1)S(1)} %encode.5.refs_8_), channel_id=1, source_target_pairs={{0,1},{1,0},{2,3},{3,2},{4,5},{5,4},{6,7},{7,6},{8,9},{9,8},{10,11... | collective-permute-start | bytes 414728 | tf_op jit(solution)/shard_map/ppermute | solution.py:459

commit v13 on v12

--- a/solution.py
+++ b/solution.py
@@ -66,7 +66,7 @@
             pltpu.VMEM((2, ch // 128, xcols * 8, 128), F32),
             pltpu.SemaphoreType.DMA((2,)),
         ],
-        compiler_params=params(58),
+        compiler_params=params(51),
         cost_estimate=pl.CostEstimate(flops=1 << 31, transcendentals=0, bytes_accessed=12 * MIB),
         name="edges",
     )(x)

time: 42.4 us -> 41.3 us (0.974)
  local copies, waits for them, and re-layouts: 2 us -> 0.8 us
  Pallas kernels: 24.9 us -> 24.1 us
  starting transfers between devices: 14.3 us -> 14.9 us
    unnamed x18 -> x16, local copies, waits for them, and re-layouts: 1.25 us -> 0.05 us
    pallas_call x1, Pallas kernels: 2.36 us -> 1.56 us  [edge_rows(): pl.pallas_call(edges_kernel, in_specs=[pl.BlockSpec(memory_space=pltpu.HB...]
  transfers between devices with their start and end apart: 13 -> 13, of which waited for: 1 -> 1; matrix products, arithmetic and copies ran while one was open for 0% -> 0% of each run, Pallas kernels for 51% -> 50%
where the time goes in v13:
time: 41.3 us; the launch traced here: 41.1 us
  Pallas kernels  24.1 us (58%)
  starting transfers between devices  14.9 us (36%)
  waiting for transfers between devices  0.94 us (2%)
  local copies, waits for them, and re-layouts  0.8 us (2%)
    pallas_call x3, Pallas kernels, encode(): pl.pallas_call(functools.partial(encoder_kernel, first=first, group=group...  12.1 us
    pallas_call x2, Pallas kernels, forecast_heads(): pl.pallas_call(functools.partial(head_kernel, chunks=chunks, blocks=block...  9.38 us
    ppermute x1, starting transfers between devices, shards(): above = lax.ppermute(up, 'lat', lat_up)  3.41 us
    ppermute x3, starting transfers between devices, shards(): across = lax.ppermute(own, 'lon', swap(lon, 2))  3.1 us
    ppermute x1, starting transfers between devices, shards(): below = lax.ppermute(dn, 'lat', lat_dn)  3.03 us
    ppermute x3, starting transfers between devices, shards(): beside = lax.ppermute(own, 'lon', swap(lon, 1))  1.77 us
    pallas_call x1, Pallas kernels, edge_rows(): pl.pallas_call(edges_kernel, in_specs=[pl.BlockSpec(memory_space=pltpu.HB...  1.56 us
    ppermute x1, starting transfers between devices, shards(): both = lax.ppermute(own, 'lon', swap(lon, 3))  1.2 us
  transfers between devices with their start and end apart: 13, of which 1 were waited for; matrix products, arithmetic and copies ran while one was open for 0% of the time, Pallas kernels for 50%

profile of v13, /device:TPU:25, one launch (start us, length us, event | category | flops | bytes accessed | tf_op | source)
XLA Modules:
  0.0 41.1 jit_solution(3734463190412732948)
XLA Ops:
  0.0 0.7 %slice_bitcast_fusion = (bf16[40,256]{1,0:T(8,128)(2,1)S(1)}, bf16[40,256]{1,0:T(8,128)(2,1)S(1)}) fusion(bf16[180,40,256]{2,1,0:T(8,128)(2,1)} %bitcast.5), kind=kLoop, calls=%fused_computation | loop fusion | bytes 81920 | tf_op jit(solution)/shard_map/squeeze | solution.py:437
  0.7 0.7 %collective-permute-start.1 = (bf16[40,256]{1,0:T(8,128)(2,1)S(1)}, bf16[40,256]{1,0:T(8,128)(2,1)S(1)}, u32[]{:S(2)}, u32[]{:S(2)}) collective-permute-start(bf16[40,256]{1,0:T(8,128)(2,1)S(1)} %get-tuple-element.37), channel_id=1, source_target_pairs={{1,0},{2,1},{3,2},{0,3},{5,4},{6,5},{7,6},{4,7},{9,8},{10,9},{11,1... | collective-permute-start | bytes 61448 | tf_op jit(solution)/shard_map/ppermute | solution.py:437
  1.4 1.1 %collective-permute-start = (bf16[40,256]{1,0:T(8,128)(2,1)S(1)}, bf16[40,256]{1,0:T(8,128)(2,1)S(1)}, u32[]{:S(2)}, u32[]{:S(2)}) collective-permute-start(bf16[40,256]{1,0:T(8,128)(2,1)S(1)} %get-tuple-element.38), channel_id=1, source_target_pairs={{0,1},{1,2},{2,3},{3,0},{4,5},{5,6},{6,7},{7,4},{8,9},{9,10},{10,1... | collective-permute-start | bytes 61448 | tf_op jit(solution)/shard_map/ppermute | solution.py:436
  2.5 1.6 %edges.1.edge_ref = bf16[2,3,180,256]{3,2,1,0:T(8,128)(2,1)S(1)} custom-call(bf16[180,40,256]{2,1,0:T(8,128)(2,1)} %bitcast.6), custom_call_target="tpu_custom_call" | custom-call | flops 2147483648 | bytes 12582912 | tf_op jit(solution)/shard_map/edges/pallas_call | solution.py:59
  4.1 0.0 copy-start.5
  4.1 0.0 copy-start.6
  4.1 0.0 copy-start.7
  4.1 0.0 collective-permute-done.west_ref
  4.1 0.1 slabs.1
  4.3 3.4 %collective-permute-start.4 = (bf16[3,182,256]{2,1,0:T(8,128)(2,1)S(1)}, bf16[3,182,256]{2,1,0:T(8,128)(2,1)S(1)}, u32[]{:S(2)}, u32[]{:S(2)}) collective-permute-start(bf16[3,182,256]{2,1,0:T(8,128)(2,1)S(1)} %get-tuple-element.25), channel_id=1, source_target_pairs={{0,4},{4,8},{8,12},{12,16},{16,20},{20,24},{24,28},{1,5},{5,9},{9,... | collective-permute-start | bytes 838664 | tf_op jit(solution)/shard_map/ppermute | solution.py:442
  7.7 3.0 %collective-permute-start.5 = (bf16[3,182,256]{2,1,0:T(8,128)(2,1)S(1)}, bf16[3,182,256]{2,1,0:T(8,128)(2,1)S(1)}, u32[]{:S(2)}, u32[]{:S(2)}) collective-permute-start(bf16[3,182,256]{2,1,0:T(8,128)(2,1)S(1)} %get-tuple-element.26), channel_id=1, source_target_pairs={{4,0},{8,4},{12,8},{16,12},{20,16},{24,20},{28,24},{5,1},{9,5},{13... | collective-permute-start | bytes 838664 | tf_op jit(solution)/shard_map/ppermute | solution.py:443
  10.8 3.7 %encode.3.refs_0_ = bf16[8,90,128]{2,1,0:T(8,128)(2,1)S(1)} custom-call(bf16[180,40,256]{2,1,0:T(8,128)(2,1)S(1)} %bitcast.7, bf16[40,256]{1,0:T(8,128)(2,1)S(1)} %collective-permute-done.west_ref, bf16[40,256]{1,0:T(8,128)(2,1)S(1)} %collective-permute-done.1.east_ref, bf16[3,3,256,256]{3,2,1,0:T(8,128)(2,1)S(1)} %copy-done.6, bf16[256,128]{1,0:T(8,128)(2,1)S(1)} %copy-done.7), custom_call_target="tpu_custom_call" | custom-call | flops 2264924160 | bytes 8388608 | tf_op jit(solution)/shard_map/encode/pallas_call | solution.py:265
  14.5 0.0 copy-start
  14.5 0.0 copy-start.1
  14.5 0.0 copy-start.2
  14.6 0.0 copy-start.3
  14.6 0.0 copy-start.4
  14.6 1.6 %collective-permute-start.3 = (bf16[8,90,128]{2,1,0:T(8,128)(2,1)S(1)}, bf16[8,90,128]{2,1,0:T(8,128)(2,1)S(1)}, u32[]{:S(2)}, u32[]{:S(2)}) collective-permute-start(bf16[8,90,128]{2,1,0:T(8,128)(2,1)S(1)} %encode.3.refs_0_), channel_id=1, source_target_pairs={{0,2},{1,3},{2,0},{3,1},{4,6},{5,7},{6,4},{7,5},{8,10},{9,11},{10,... | collective-permute-start | bytes 552968 | tf_op jit(solution)/shard_map/ppermute | solution.py:458
  16.2 1.1 %collective-permute-start.2 = (bf16[8,90,128]{2,1,0:T(8,128)(2,1)S(1)}, bf16[8,90,128]{2,1,0:T(8,128)(2,1)S(1)}, u32[]{:S(2)}, u32[]{:S(2)}) collective-permute-start(bf16[8,90,128]{2,1,0:T(8,128)(2,1)S(1)} %encode.3.refs_0_), channel_id=1, source_target_pairs={{0,1},{1,0},{2,3},{3,2},{4,5},{5,4},{6,7},{7,6},{8,9},{9,8},{10,11... | collective-permute-start | bytes 552968 | tf_op jit(solution)/shard_map/ppermute | solution.py:459
  17.3 3.7 %encode.4.refs_4_ = bf16[8,90,128]{2,1,0:T(8,128)(2,1)S(1)} custom-call(bf16[180,40,256]{2,1,0:T(8,128)(2,1)S(1)} %bitcast.8, bf16[40,256]{1,0:T(8,128)(2,1)S(1)} %collective-permute-done.west_ref, bf16[40,256]{1,0:T(8,128)(2,1)S(1)} %collective-permute-done.1.east_ref, bf16[3,3,256,256]{3,2,1,0:T(8,128)(2,1)S(1)} %copy-done.6, bf16[256,128]{1,0:T(8,128)(2,1)S(1)} %copy-done.7), custom_call_target="tpu_custom_call" | custom-call | flops 2264924160 | bytes 8388608 | tf_op jit(solution)/shard_map/encode/pallas_call | solution.py:265
  21.0 0.9 %collective-permute-start.8 = (bf16[8,90,128]{2,1,0:T(8,128)(2,1)S(1)}, bf16[8,90,128]{2,1,0:T(8,128)(2,1)S(1)}, u32[]{:S(2)}, u32[]{:S(2)}) collective-permute-start(bf16[8,90,128]{2,1,0:T(8,128)(2,1)S(1)} %encode.4.refs_4_), channel_id=1, source_target_pairs={{0,2},{1,3},{2,0},{3,1},{4,6},{5,7},{6,4},{7,5},{8,10},{9,11},{10,... | collective-permute-start | bytes 552968 | tf_op jit(solution)/shard_map/ppermute | solution.py:458
  21.9 0.9 %weights.1 = (bf16[1152,256]{1,0:T(8,128)(2,1)S(1)}, f32[8,256]{1,0:T(8,128)S(1)}, bf16[368,368]{1,0:T(8,128)(2,1)S(1)}) custom-call(s32[8]{0:T(128)S(1)} %copy-done.4, bf16[3,3,128,128]{3,2,1,0:T(8,128)(2,1)S(1)} %copy-done.2, f32[720,128]{1,0:T(8,128)S(1)} %copy-done, f32[720,128]{1,0:T(8,128)S(1)} %copy-done.1, bf16[360,360]{1,0:T(8,128)(2,1)S(1)} %copy-done.3), custom_call_target="tpu_custom_call" | custom-call | tf_op jit(solution)/shard_map/weights/pallas_call | solution.py:104
  22.9 0.3 collective-permute-start.7
  23.2 4.6 %encode.5.refs_8_ = bf16[6,90,128]{2,1,0:T(8,128)(2,1)S(1)} custom-call(bf16[180,40,256]{2,1,0:T(8,128)(2,1)S(1)} %bitcast.9, bf16[40,256]{1,0:T(8,128)(2,1)S(1)} %collective-permute-done.west_ref, bf16[40,256]{1,0:T(8,128)(2,1)S(1)} %collective-permute-done.1.east_ref, bf16[3,182,256]{2,1,0:T(8,128)(2,1)S(1)} %collective-permute-done.4.refs_0_, ...), custom_call_target="tpu_custom_call" | custom-call | flops 2264924160 | bytes 8388608 | tf_op jit(solution)/shard_map/encode/pallas_call | solution.py:265
  27.8 0.5 %collective-permute-start.6 = (bf16[8,90,128]{2,1,0:T(8,128)(2,1)S(1)}, bf16[8,90,128]{2,1,0:T(8,128)(2,1)S(1)}, u32[]{:S(2)}, u32[]{:S(2)}) collective-permute-start(bf16[8,90,128]{2,1,0:T(8,128)(2,1)S(1)} %collective-permute-done.3.refs_2_), channel_id=1, source_target_pairs={{0,1},{1,0},{2,3},{3,2},{4,5},{5,4},{6,7},{7,6},{8,9},{9,8},{10,11... | collective-permute-start | bytes 552968 | tf_op jit(solution)/shard_map/ppermute | solution.py:464
  28.4 0.0 collective-permute-start.9
  28.4 1.2 %collective-permute-start.12 = (bf16[6,90,128]{2,1,0:T(8,128)(2,1)S(1)}, bf16[6,90,128]{2,1,0:T(8,128)(2,1)S(1)}, u32[]{:S(2)}, u32[]{:S(2)}) collective-permute-start(bf16[6,90,128]{2,1,0:T(8,128)(2,1)S(1)} %encode.5.refs_8_), channel_id=1, source_target_pairs={{0,3},{1,2},{2,1},{3,0},{4,7},{5,6},{6,5},{7,4},{8,11},{9,10},{10,... | collective-permute-start | bytes 414728 | tf_op jit(solution)/shard_map/ppermute | solution.py:461
  29.6 0.6 %collective-permute-start.11 = (bf16[6,90,128]{2,1,0:T(8,128)(2,1)S(1)}, bf16[6,90,128]{2,1,0:T(8,128)(2,1)S(1)}, u32[]{:S(2)}, u32[]{:S(2)}) collective-permute-start(bf16[6,90,128]{2,1,0:T(8,128)(2,1)S(1)} %encode.5.refs_8_), channel_id=1, source_target_pairs={{0,2},{1,3},{2,0},{3,1},{4,6},{5,7},{6,4},{7,5},{8,10},{9,11},{10,... | collective-permute-start | bytes 414728 | tf_op jit(solution)/shard_map/ppermute | solution.py:458
  30.3 0.3 collective-permute-start.10
  30.6 6.1 %heads.2.refs_15_ = bf16[2,20,360,128]{3,2,1,0:T(8,128)(2,1)} custom-call(bf16[8,90,128]{2,1,0:T(8,128)(2,1)S(1)} %encode.3.refs_0_, bf16[8,90,128]{2,1,0:T(8,128)(2,1)S(1)} %collective-permute-done.2.refs_1_, bf16[8,90,128]{2,1,0:T(8,128)(2,1)S(1)} %collective-permute-done.3.refs_2_, bf16[8,90,128]{2,1,0:T(8,128)(2,1)S(1)} %collective-permute-done.6.refs_3_, ...), custom_call_target="tpu_custom_call" | custom-call | flops 3901685760 | bytes 33554432 | tf_op jit(solution)/shard_map/heads/pallas_call | solution.py:391
  36.7 0.9 %collective-permute-done.11.refs_10_ = bf16[6,90,128]{2,1,0:T(8,128)(2,1)S(1)} collective-permute-done((bf16[6,90,128]{2,1,0:T(8,128)(2,1)S(1)}, bf16[6,90,128]{2,1,0:T(8,128)(2,1)S(1)}, u32[]{:S(2)}, u32[]{:S(2)}) %collective-permute-start.11) | collective-permute-done | bytes 138272 | tf_op jit(solution)/shard_map/ppermute | solution.py:458
  37.6 3.3 %heads.3 = bf16[2,20,360,128]{3,2,1,0:T(8,128)(2,1)} custom-call(bf16[8,90,128]{2,1,0:T(8,128)(2,1)S(1)} %encode.3.refs_0_, bf16[8,90,128]{2,1,0:T(8,128)(2,1)S(1)} %collective-permute-done.2.refs_1_, bf16[8,90,128]{2,1,0:T(8,128)(2,1)S(1)} %collective-permute-done.3.refs_2_, ...), custom_call_target="tpu_custom_call", output_to_operand_aliasing={{}: (15, {})} | custom-call | flops 1672151040 | bytes 16777216 | tf_op jit(solution)/shard_map/heads/pallas_call | solution.py:391
  (19 shorter events, 0.0 us)
Async XLA Ops:
  0.7 3.4 %collective-permute-start.1 = (bf16[40,256]{1,0:T(8,128)(2,1)S(1)}, bf16[40,256]{1,0:T(8,128)(2,1)S(1)}, u32[]{:S(2)}, u32[]{:S(2)}) collective-permute-start(bf16[40,256]{1,0:T(8,128)(2,1)S(1)} %get-tuple-element.37), channel_id=1, source_target_pairs={{1,0},{2,1},{3,2},{0,3},{5,4},{6,5},{7,6},{4,7},{9,8},{10,9},{11,1... | collective-permute-start | bytes 61448 | tf_op jit(solution)/shard_map/ppermute | solution.py:437
  1.4 2.7 %collective-permute-start = (bf16[40,256]{1,0:T(8,128)(2,1)S(1)}, bf16[40,256]{1,0:T(8,128)(2,1)S(1)}, u32[]{:S(2)}, u32[]{:S(2)}) collective-permute-start(bf16[40,256]{1,0:T(8,128)(2,1)S(1)} %get-tuple-element.38), channel_id=1, source_target_pairs={{0,1},{1,2},{2,3},{3,0},{4,5},{5,6},{6,7},{7,4},{8,9},{9,10},{10,1... | collective-permute-start | bytes 61448 | tf_op jit(solution)/shard_map/ppermute | solution.py:436
  4.1 6.7 %copy-start.5 = (bf16[40,180,256]{2,0,1:T(8,128)(2,1)S(1)}, bf16[40,180,256]{2,0,1:T(8,128)(2,1)}, u32[]{:S(2)}) copy-start(bf16[40,180,256]{2,0,1:T(8,128)(2,1)} %param.8) | copy-start | bytes 11059204
  4.1 6.7 %copy-start.6 = (bf16[3,3,256,256]{3,2,1,0:T(8,128)(2,1)S(1)}, bf16[3,3,256,256]{3,2,1,0:T(8,128)(2,1)}, u32[]{:S(2)}) copy-start(bf16[3,3,256,256]{3,2,1,0:T(8,128)(2,1)} %refs_2_.1) | copy-start | bytes 3538948
  4.1 6.7 %copy-start.7 = (bf16[256,128]{1,0:T(8,128)(2,1)S(1)}, bf16[256,128]{1,0:T(8,128)(2,1)}, u32[]{:S(2)}) copy-start(bf16[256,128]{1,0:T(8,128)(2,1)} %refs_3_) | copy-start | bytes 196612
  4.3 18.6 %collective-permute-start.4 = (bf16[3,182,256]{2,1,0:T(8,128)(2,1)S(1)}, bf16[3,182,256]{2,1,0:T(8,128)(2,1)S(1)}, u32[]{:S(2)}, u32[]{:S(2)}) collective-permute-start(bf16[3,182,256]{2,1,0:T(8,128)(2,1)S(1)} %get-tuple-element.25), channel_id=1, source_target_pairs={{0,4},{4,8},{8,12},{12,16},{16,20},{20,24},{24,28},{1,5},{5,9},{9,... | collective-permute-start | bytes 838664 | tf_op jit(solution)/shard_map/ppermute | solution.py:442
  7.7 15.5 %collective-permute-start.5 = (bf16[3,182,256]{2,1,0:T(8,128)(2,1)S(1)}, bf16[3,182,256]{2,1,0:T(8,128)(2,1)S(1)}, u32[]{:S(2)}, u32[]{:S(2)}) collective-permute-start(bf16[3,182,256]{2,1,0:T(8,128)(2,1)S(1)} %get-tuple-element.26), channel_id=1, source_target_pairs={{4,0},{8,4},{12,8},{16,12},{20,16},{24,20},{28,24},{5,1},{9,5},{13... | collective-permute-start | bytes 838664 | tf_op jit(solution)/shard_map/ppermute | solution.py:443
  14.5 7.4 %copy-start = (f32[720,128]{1,0:T(8,128)S(1)}, f32[720,128]{1,0:T(8,128)}, u32[]{:S(2)}) copy-start(f32[720,128]{1,0:T(8,128)} %scale_ref.1) | copy-start | bytes 1105924
  14.5 7.4 %copy-start.1 = (f32[720,128]{1,0:T(8,128)S(1)}, f32[720,128]{1,0:T(8,128)}, u32[]{:S(2)}) copy-start(f32[720,128]{1,0:T(8,128)} %shift_ref.1) | copy-start | bytes 1105924
  14.5 7.4 %copy-start.2 = (bf16[3,3,128,128]{3,2,1,0:T(8,128)(2,1)S(1)}, bf16[3,3,128,128]{3,2,1,0:T(8,128)(2,1)}, u32[]{:S(2)}) copy-start(bf16[3,3,128,128]{3,2,1,0:T(8,128)(2,1)} %wh_ref.1) | copy-start | bytes 884740
  14.6 7.4 %copy-start.3 = (bf16[360,360]{1,0:T(8,128)(2,1)S(1)}, bf16[360,360]{1,0:T(8,128)(2,1)}, u32[]{:S(2)}) copy-start(bf16[360,360]{1,0:T(8,128)(2,1)} %z_ref.1) | copy-start | bytes 777604
  14.6 7.4 %copy-start.4 = (s32[8]{0:T(128)S(1)}, s32[8]{0:T(128)}, u32[]{:S(2)}) copy-start(s32[8]{0:T(128)} %ids_ref) | copy-start | bytes 100
  14.6 13.3 %collective-permute-start.3 = (bf16[8,90,128]{2,1,0:T(8,128)(2,1)S(1)}, bf16[8,90,128]{2,1,0:T(8,128)(2,1)S(1)}, u32[]{:S(2)}, u32[]{:S(2)}) collective-permute-start(bf16[8,90,128]{2,1,0:T(8,128)(2,1)S(1)} %encode.3.refs_0_), channel_id=1, source_target_pairs={{0,2},{1,3},{2,0},{3,1},{4,6},{5,7},{6,4},{7,5},{8,10},{9,11},{10,... | collective-permute-start | bytes 552968 | tf_op jit(solution)/shard_map/ppermute | solution.py:458
  16.2 13.5 %collective-permute-start.2 = (bf16[8,90,128]{2,1,0:T(8,128)(2,1)S(1)}, bf16[8,90,128]{2,1,0:T(8,128)(2,1)S(1)}, u32[]{:S(2)}, u32[]{:S(2)}) collective-permute-start(bf16[8,90,128]{2,1,0:T(8,128)(2,1)S(1)} %encode.3.refs_0_), channel_id=1, source_target_pairs={{0,1},{1,0},{2,3},{3,2},{4,5},{5,4},{6,7},{7,6},{8,9},{9,8},{10,11... | collective-permute-start | bytes 552968 | tf_op jit(solution)/shard_map/ppermute | solution.py:459
  21.0 6.8 %collective-permute-start.8 = (bf16[8,90,128]{2,1,0:T(8,128)(2,1)S(1)}, bf16[8,90,128]{2,1,0:T(8,128)(2,1)S(1)}, u32[]{:S(2)}, u32[]{:S(2)}) collective-permute-start(bf16[8,90,128]{2,1,0:T(8,128)(2,1)S(1)} %encode.4.refs_4_), channel_id=1, source_target_pairs={{0,2},{1,3},{2,0},{3,1},{4,6},{5,7},{6,4},{7,5},{8,10},{9,11},{10,... | collective-permute-start | bytes 552968 | tf_op jit(solution)/shard_map/ppermute | solution.py:458
  22.9 7.4 %collective-permute-start.7 = (bf16[8,90,128]{2,1,0:T(8,128)(2,1)S(1)}, bf16[8,90,128]{2,1,0:T(8,128)(2,1)S(1)}, u32[]{:S(2)}, u32[]{:S(2)}) collective-permute-start(bf16[8,90,128]{2,1,0:T(8,128)(2,1)S(1)} %encode.4.refs_4_), channel_id=1, source_target_pairs={{0,1},{1,0},{2,3},{3,2},{4,5},{5,4},{6,7},{7,6},{8,9},{9,8},{10,11... | collective-permute-start | bytes 552968 | tf_op jit(solution)/shard_map/ppermute | solution.py:459
  27.8 2.7 %collective-permute-start.6 = (bf16[8,90,128]{2,1,0:T(8,128)(2,1)S(1)}, bf16[8,90,128]{2,1,0:T(8,128)(2,1)S(1)}, u32[]{:S(2)}, u32[]{:S(2)}) collective-permute-start(bf16[8,90,128]{2,1,0:T(8,128)(2,1)S(1)} %collective-permute-done.3.refs_2_), channel_id=1, source_target_pairs={{0,1},{1,0},{2,3},{3,2},{4,5},{5,4},{6,7},{7,6},{8,9},{9,8},{10,11... | collective-permute-start | bytes 552968 | tf_op jit(solution)/shard_map/ppermute | solution.py:464
  28.4 2.2 %collective-permute-start.9 = (bf16[8,90,128]{2,1,0:T(8,128)(2,1)S(1)}, bf16[8,90,128]{2,1,0:T(8,128)(2,1)S(1)}, u32[]{:S(2)}, u32[]{:S(2)}) collective-permute-start(bf16[8,90,128]{2,1,0:T(8,128)(2,1)S(1)} %collective-permute-done.8.refs_6_), channel_id=1, source_target_pairs={{0,1},{1,0},{2,3},{3,2},{4,5},{5,4},{6,7},{7,6},{8,9},{9,8},{10,11... | collective-permute-start | bytes 552968 | tf_op jit(solution)/shard_map/ppermute | solution.py:464
  28.4 8.3 %collective-permute-start.12 = (bf16[6,90,128]{2,1,0:T(8,128)(2,1)S(1)}, bf16[6,90,128]{2,1,0:T(8,128)(2,1)S(1)}, u32[]{:S(2)}, u32[]{:S(2)}) collective-permute-start(bf16[6,90,128]{2,1,0:T(8,128)(2,1)S(1)} %encode.5.refs_8_), channel_id=1, source_target_pairs={{0,3},{1,2},{2,1},{3,0},{4,7},{5,6},{6,5},{7,4},{8,11},{9,10},{10,... | collective-permute-start | bytes 414728 | tf_op jit(solution)/shard_map/ppermute | solution.py:461
  29.6 8.0 %collective-permute-start.11 = (bf16[6,90,128]{2,1,0:T(8,128)(2,1)S(1)}, bf16[6,90,128]{2,1,0:T(8,128)(2,1)S(1)}, u32[]{:S(2)}, u32[]{:S(2)}) collective-permute-start(bf16[6,90,128]{2,1,0:T(8,128)(2,1)S(1)} %encode.5.refs_8_), channel_id=1, source_target_pairs={{0,2},{1,3},{2,0},{3,1},{4,6},{5,7},{6,4},{7,5},{8,10},{9,11},{10,... | collective-permute-start | bytes 414728 | tf_op jit(solution)/shard_map/ppermute | solution.py:458
  30.3 7.3 %collective-permute-start.10 = (bf16[6,90,128]{2,1,0:T(8,128)(2,1)S(1)}, bf16[6,90,128]{2,1,0:T(8,128)(2,1)S(1)}, u32[]{:S(2)}, u32[]{:S(2)}) collective-permute-start(bf16[6,90,128]{2,1,0:T(8,128)(2,1)S(1)} %encode.5.refs_8_), channel_id=1, source_target_pairs={{0,1},{1,0},{2,3},{3,2},{4,5},{5,4},{6,7},{7,6},{8,9},{9,8},{10,11... | collective-permute-start | bytes 414728 | tf_op jit(solution)/shard_map/ppermute | solution.py:459

commit v14 on v13

--- a/solution.py
+++ b/solution.py
@@ -11,7 +11,7 @@
 F32 = jnp.float32
 MIB = 1024 * 1024
 EDGE = 2
-STEP = 4
+STEP = 5
 BIAS, GAIN, SHIFT = 0, 3, 4
 
 

time: 41.3 us -> 41.3 us (level)
  no operation moved by 1% of the time
where the time goes in v14:
time: 41.3 us; the launch traced here: 41.1 us
  Pallas kernels  24.1 us (58%)
  starting transfers between devices  14.9 us (36%)
  waiting for transfers between devices  0.9 us (2%)
  local copies, waits for them, and re-layouts  0.8 us (2%)
    pallas_call x3, Pallas kernels, encode(): pl.pallas_call(functools.partial(encoder_kernel, first=first, group=group...  12.1 us
    pallas_call x2, Pallas kernels, forecast_heads(): pl.pallas_call(functools.partial(head_kernel, chunks=chunks, blocks=block...  9.43 us
    ppermute x1, starting transfers between devices, shards(): above = lax.ppermute(up, 'lat', lat_up)  3.41 us
    ppermute x3, starting transfers between devices, shards(): across = lax.ppermute(own, 'lon', swap(lon, 2))  3.1 us
    ppermute x1, starting transfers between devices, shards(): below = lax.ppermute(dn, 'lat', lat_dn)  3.03 us
    ppermute x3, starting transfers between devices, shards(): beside = lax.ppermute(own, 'lon', swap(lon, 1))  1.77 us
    pallas_call x1, Pallas kernels, edge_rows(): pl.pallas_call(edges_kernel, in_specs=[pl.BlockSpec(memory_space=pltpu.HB...  1.56 us
    ppermute x1, starting transfers between devices, shards(): both = lax.ppermute(own, 'lon', swap(lon, 3))  1.2 us
  transfers between devices with their start and end apart: 13, of which 1 were waited for; matrix products, arithmetic and copies ran while one was open for 0% of the time, Pallas kernels for 50%

profile of v14, /device:TPU:25, one launch (start us, length us, event | category | flops | bytes accessed | tf_op | source)
XLA Modules:
  0.0 41.1 jit_solution(6597381487554207803)
XLA Ops:
  0.0 0.7 %slice_bitcast_fusion = (bf16[40,256]{1,0:T(8,128)(2,1)S(1)}, bf16[40,256]{1,0:T(8,128)(2,1)S(1)}) fusion(bf16[180,40,256]{2,1,0:T(8,128)(2,1)} %bitcast.5), kind=kLoop, calls=%fused_computation | loop fusion | bytes 81920 | tf_op jit(solution)/shard_map/squeeze | solution.py:437
  0.7 0.7 %collective-permute-start.1 = (bf16[40,256]{1,0:T(8,128)(2,1)S(1)}, bf16[40,256]{1,0:T(8,128)(2,1)S(1)}, u32[]{:S(2)}, u32[]{:S(2)}) collective-permute-start(bf16[40,256]{1,0:T(8,128)(2,1)S(1)} %get-tuple-element.37), channel_id=1, source_target_pairs={{1,0},{2,1},{3,2},{0,3},{5,4},{6,5},{7,6},{4,7},{9,8},{10,9},{11,1... | collective-permute-start | bytes 61448 | tf_op jit(solution)/shard_map/ppermute | solution.py:437
  1.4 1.1 %collective-permute-start = (bf16[40,256]{1,0:T(8,128)(2,1)S(1)}, bf16[40,256]{1,0:T(8,128)(2,1)S(1)}, u32[]{:S(2)}, u32[]{:S(2)}) collective-permute-start(bf16[40,256]{1,0:T(8,128)(2,1)S(1)} %get-tuple-element.38), channel_id=1, source_target_pairs={{0,1},{1,2},{2,3},{3,0},{4,5},{5,6},{6,7},{7,4},{8,9},{9,10},{10,1... | collective-permute-start | bytes 61448 | tf_op jit(solution)/shard_map/ppermute | solution.py:436
  2.5 1.6 %edges.1.edge_ref = bf16[2,3,180,256]{3,2,1,0:T(8,128)(2,1)S(1)} custom-call(bf16[180,40,256]{2,1,0:T(8,128)(2,1)} %bitcast.6), custom_call_target="tpu_custom_call" | custom-call | flops 2147483648 | bytes 12582912 | tf_op jit(solution)/shard_map/edges/pallas_call | solution.py:59
  4.1 0.0 copy-start.5
  4.1 0.0 copy-start.6
  4.1 0.0 copy-start.7
  4.1 0.0 collective-permute-done.1.east_ref
  4.1 0.1 slabs.1
  4.3 3.4 %collective-permute-start.4 = (bf16[3,182,256]{2,1,0:T(8,128)(2,1)S(1)}, bf16[3,182,256]{2,1,0:T(8,128)(2,1)S(1)}, u32[]{:S(2)}, u32[]{:S(2)}) collective-permute-start(bf16[3,182,256]{2,1,0:T(8,128)(2,1)S(1)} %get-tuple-element.25), channel_id=1, source_target_pairs={{0,4},{4,8},{8,12},{12,16},{16,20},{20,24},{24,28},{1,5},{5,9},{9,... | collective-permute-start | bytes 838664 | tf_op jit(solution)/shard_map/ppermute | solution.py:442
  7.7 3.0 %collective-permute-start.5 = (bf16[3,182,256]{2,1,0:T(8,128)(2,1)S(1)}, bf16[3,182,256]{2,1,0:T(8,128)(2,1)S(1)}, u32[]{:S(2)}, u32[]{:S(2)}) collective-permute-start(bf16[3,182,256]{2,1,0:T(8,128)(2,1)S(1)} %get-tuple-element.26), channel_id=1, source_target_pairs={{4,0},{8,4},{12,8},{16,12},{20,16},{24,20},{28,24},{5,1},{9,5},{13... | collective-permute-start | bytes 838664 | tf_op jit(solution)/shard_map/ppermute | solution.py:443
  10.8 3.7 %encode.3.refs_0_ = bf16[8,90,128]{2,1,0:T(8,128)(2,1)S(1)} custom-call(bf16[180,40,256]{2,1,0:T(8,128)(2,1)S(1)} %bitcast.7, bf16[40,256]{1,0:T(8,128)(2,1)S(1)} %collective-permute-done.west_ref, bf16[40,256]{1,0:T(8,128)(2,1)S(1)} %collective-permute-done.1.east_ref, bf16[3,3,256,256]{3,2,1,0:T(8,128)(2,1)S(1)} %copy-done.6, bf16[256,128]{1,0:T(8,128)(2,1)S(1)} %copy-done.7), custom_call_target="tpu_custom_call" | custom-call | flops 2264924160 | bytes 8388608 | tf_op jit(solution)/shard_map/encode/pallas_call | solution.py:265
  14.5 0.0 copy-start
  14.5 0.0 copy-start.1
  14.5 0.0 copy-start.2
  14.6 0.0 copy-start.3
  14.6 0.0 copy-start.4
  14.6 1.6 %collective-permute-start.3 = (bf16[8,90,128]{2,1,0:T(8,128)(2,1)S(1)}, bf16[8,90,128]{2,1,0:T(8,128)(2,1)S(1)}, u32[]{:S(2)}, u32[]{:S(2)}) collective-permute-start(bf16[8,90,128]{2,1,0:T(8,128)(2,1)S(1)} %encode.3.refs_0_), channel_id=1, source_target_pairs={{0,2},{1,3},{2,0},{3,1},{4,6},{5,7},{6,4},{7,5},{8,10},{9,11},{10,... | collective-permute-start | bytes 552968 | tf_op jit(solution)/shard_map/ppermute | solution.py:458
  16.2 1.1 %collective-permute-start.2 = (bf16[8,90,128]{2,1,0:T(8,128)(2,1)S(1)}, bf16[8,90,128]{2,1,0:T(8,128)(2,1)S(1)}, u32[]{:S(2)}, u32[]{:S(2)}) collective-permute-start(bf16[8,90,128]{2,1,0:T(8,128)(2,1)S(1)} %encode.3.refs_0_), channel_id=1, source_target_pairs={{0,1},{1,0},{2,3},{3,2},{4,5},{5,4},{6,7},{7,6},{8,9},{9,8},{10,11... | collective-permute-start | bytes 552968 | tf_op jit(solution)/shard_map/ppermute | solution.py:459
  17.3 3.7 %encode.4.refs_4_ = bf16[8,90,128]{2,1,0:T(8,128)(2,1)S(1)} custom-call(bf16[180,40,256]{2,1,0:T(8,128)(2,1)S(1)} %bitcast.8, bf16[40,256]{1,0:T(8,128)(2,1)S(1)} %collective-permute-done.west_ref, bf16[40,256]{1,0:T(8,128)(2,1)S(1)} %collective-permute-done.1.east_ref, bf16[3,3,256,256]{3,2,1,0:T(8,128)(2,1)S(1)} %copy-done.6, bf16[256,128]{1,0:T(8,128)(2,1)S(1)} %copy-done.7), custom_call_target="tpu_custom_call" | custom-call | flops 2264924160 | bytes 8388608 | tf_op jit(solution)/shard_map/encode/pallas_call | solution.py:265
  21.0 0.9 %collective-permute-start.8 = (bf16[8,90,128]{2,1,0:T(8,128)(2,1)S(1)}, bf16[8,90,128]{2,1,0:T(8,128)(2,1)S(1)}, u32[]{:S(2)}, u32[]{:S(2)}) collective-permute-start(bf16[8,90,128]{2,1,0:T(8,128)(2,1)S(1)} %encode.4.refs_4_), channel_id=1, source_target_pairs={{0,2},{1,3},{2,0},{3,1},{4,6},{5,7},{6,4},{7,5},{8,10},{9,11},{10,... | collective-permute-start | bytes 552968 | tf_op jit(solution)/shard_map/ppermute | solution.py:458
  21.9 0.9 %weights.1 = (bf16[1152,256]{1,0:T(8,128)(2,1)S(1)}, f32[8,256]{1,0:T(8,128)S(1)}, bf16[368,368]{1,0:T(8,128)(2,1)S(1)}) custom-call(s32[8]{0:T(128)S(1)} %copy-done.4, bf16[3,3,128,128]{3,2,1,0:T(8,128)(2,1)S(1)} %copy-done.2, f32[720,128]{1,0:T(8,128)S(1)} %copy-done, f32[720,128]{1,0:T(8,128)S(1)} %copy-done.1, bf16[360,360]{1,0:T(8,128)(2,1)S(1)} %copy-done.3), custom_call_target="tpu_custom_call" | custom-call | tf_op jit(solution)/shard_map/weights/pallas_call | solution.py:104
  22.9 0.3 collective-permute-start.7
  23.2 4.6 %encode.5.refs_8_ = bf16[6,90,128]{2,1,0:T(8,128)(2,1)S(1)} custom-call(bf16[180,40,256]{2,1,0:T(8,128)(2,1)S(1)} %bitcast.9, bf16[40,256]{1,0:T(8,128)(2,1)S(1)} %collective-permute-done.west_ref, bf16[40,256]{1,0:T(8,128)(2,1)S(1)} %collective-permute-done.1.east_ref, bf16[3,182,256]{2,1,0:T(8,128)(2,1)S(1)} %collective-permute-done.4.refs_0_, ...), custom_call_target="tpu_custom_call" | custom-call | flops 2264924160 | bytes 8388608 | tf_op jit(solution)/shard_map/encode/pallas_call | solution.py:265
  27.8 0.5 %collective-permute-start.6 = (bf16[8,90,128]{2,1,0:T(8,128)(2,1)S(1)}, bf16[8,90,128]{2,1,0:T(8,128)(2,1)S(1)}, u32[]{:S(2)}, u32[]{:S(2)}) collective-permute-start(bf16[8,90,128]{2,1,0:T(8,128)(2,1)S(1)} %collective-permute-done.3.refs_2_), channel_id=1, source_target_pairs={{0,1},{1,0},{2,3},{3,2},{4,5},{5,4},{6,7},{7,6},{8,9},{9,8},{10,11... | collective-permute-start | bytes 552968 | tf_op jit(solution)/shard_map/ppermute | solution.py:464
  28.4 0.0 collective-permute-start.9
  28.4 1.2 %collective-permute-start.12 = (bf16[6,90,128]{2,1,0:T(8,128)(2,1)S(1)}, bf16[6,90,128]{2,1,0:T(8,128)(2,1)S(1)}, u32[]{:S(2)}, u32[]{:S(2)}) collective-permute-start(bf16[6,90,128]{2,1,0:T(8,128)(2,1)S(1)} %encode.5.refs_8_), channel_id=1, source_target_pairs={{0,3},{1,2},{2,1},{3,0},{4,7},{5,6},{6,5},{7,4},{8,11},{9,10},{10,... | collective-permute-start | bytes 414728 | tf_op jit(solution)/shard_map/ppermute | solution.py:461
  29.6 0.6 %collective-permute-start.11 = (bf16[6,90,128]{2,1,0:T(8,128)(2,1)S(1)}, bf16[6,90,128]{2,1,0:T(8,128)(2,1)S(1)}, u32[]{:S(2)}, u32[]{:S(2)}) collective-permute-start(bf16[6,90,128]{2,1,0:T(8,128)(2,1)S(1)} %encode.5.refs_8_), channel_id=1, source_target_pairs={{0,2},{1,3},{2,0},{3,1},{4,6},{5,7},{6,4},{7,5},{8,10},{9,11},{10,... | collective-permute-start | bytes 414728 | tf_op jit(solution)/shard_map/ppermute | solution.py:458
  30.3 0.3 collective-permute-start.10
  30.6 6.1 %heads.2.refs_15_ = bf16[2,20,360,128]{3,2,1,0:T(8,128)(2,1)} custom-call(bf16[8,90,128]{2,1,0:T(8,128)(2,1)S(1)} %encode.3.refs_0_, bf16[8,90,128]{2,1,0:T(8,128)(2,1)S(1)} %collective-permute-done.2.refs_1_, bf16[8,90,128]{2,1,0:T(8,128)(2,1)S(1)} %collective-permute-done.3.refs_2_, bf16[8,90,128]{2,1,0:T(8,128)(2,1)S(1)} %collective-permute-done.6.refs_3_, ...), custom_call_target="tpu_custom_call" | custom-call | flops 3901685760 | bytes 25165824 | tf_op jit(solution)/shard_map/heads/pallas_call | solution.py:391
  36.7 0.9 %collective-permute-done.11.refs_10_ = bf16[6,90,128]{2,1,0:T(8,128)(2,1)S(1)} collective-permute-done((bf16[6,90,128]{2,1,0:T(8,128)(2,1)S(1)}, bf16[6,90,128]{2,1,0:T(8,128)(2,1)S(1)}, u32[]{:S(2)}, u32[]{:S(2)}) %collective-permute-start.11) | collective-permute-done | bytes 138272 | tf_op jit(solution)/shard_map/ppermute | solution.py:458
  37.6 3.3 %heads.3 = bf16[2,20,360,128]{3,2,1,0:T(8,128)(2,1)} custom-call(bf16[8,90,128]{2,1,0:T(8,128)(2,1)S(1)} %encode.3.refs_0_, bf16[8,90,128]{2,1,0:T(8,128)(2,1)S(1)} %collective-permute-done.2.refs_1_, bf16[8,90,128]{2,1,0:T(8,128)(2,1)S(1)} %collective-permute-done.3.refs_2_, ...), custom_call_target="tpu_custom_call", output_to_operand_aliasing={{}: (15, {})} | custom-call | flops 1672151040 | bytes 16777216 | tf_op jit(solution)/shard_map/heads/pallas_call | solution.py:391
  (19 shorter events, 0.0 us)
Async XLA Ops:
  0.7 3.4 %collective-permute-start.1 = (bf16[40,256]{1,0:T(8,128)(2,1)S(1)}, bf16[40,256]{1,0:T(8,128)(2,1)S(1)}, u32[]{:S(2)}, u32[]{:S(2)}) collective-permute-start(bf16[40,256]{1,0:T(8,128)(2,1)S(1)} %get-tuple-element.37), channel_id=1, source_target_pairs={{1,0},{2,1},{3,2},{0,3},{5,4},{6,5},{7,6},{4,7},{9,8},{10,9},{11,1... | collective-permute-start | bytes 61448 | tf_op jit(solution)/shard_map/ppermute | solution.py:437
  1.4 2.7 %collective-permute-start = (bf16[40,256]{1,0:T(8,128)(2,1)S(1)}, bf16[40,256]{1,0:T(8,128)(2,1)S(1)}, u32[]{:S(2)}, u32[]{:S(2)}) collective-permute-start(bf16[40,256]{1,0:T(8,128)(2,1)S(1)} %get-tuple-element.38), channel_id=1, source_target_pairs={{0,1},{1,2},{2,3},{3,0},{4,5},{5,6},{6,7},{7,4},{8,9},{9,10},{10,1... | collective-permute-start | bytes 61448 | tf_op jit(solution)/shard_map/ppermute | solution.py:436
  4.1 6.7 %copy-start.5 = (bf16[40,180,256]{2,0,1:T(8,128)(2,1)S(1)}, bf16[40,180,256]{2,0,1:T(8,128)(2,1)}, u32[]{:S(2)}) copy-start(bf16[40,180,256]{2,0,1:T(8,128)(2,1)} %param.8) | copy-start | bytes 11059204
  4.1 6.7 %copy-start.6 = (bf16[3,3,256,256]{3,2,1,0:T(8,128)(2,1)S(1)}, bf16[3,3,256,256]{3,2,1,0:T(8,128)(2,1)}, u32[]{:S(2)}) copy-start(bf16[3,3,256,256]{3,2,1,0:T(8,128)(2,1)} %refs_2_.1) | copy-start | bytes 3538948
  4.1 6.7 %copy-start.7 = (bf16[256,128]{1,0:T(8,128)(2,1)S(1)}, bf16[256,128]{1,0:T(8,128)(2,1)}, u32[]{:S(2)}) copy-start(bf16[256,128]{1,0:T(8,128)(2,1)} %refs_3_) | copy-start | bytes 196612
  4.3 18.6 %collective-permute-start.4 = (bf16[3,182,256]{2,1,0:T(8,128)(2,1)S(1)}, bf16[3,182,256]{2,1,0:T(8,128)(2,1)S(1)}, u32[]{:S(2)}, u32[]{:S(2)}) collective-permute-start(bf16[3,182,256]{2,1,0:T(8,128)(2,1)S(1)} %get-tuple-element.25), channel_id=1, source_target_pairs={{0,4},{4,8},{8,12},{12,16},{16,20},{20,24},{24,28},{1,5},{5,9},{9,... | collective-permute-start | bytes 838664 | tf_op jit(solution)/shard_map/ppermute | solution.py:442
  7.7 15.5 %collective-permute-start.5 = (bf16[3,182,256]{2,1,0:T(8,128)(2,1)S(1)}, bf16[3,182,256]{2,1,0:T(8,128)(2,1)S(1)}, u32[]{:S(2)}, u32[]{:S(2)}) collective-permute-start(bf16[3,182,256]{2,1,0:T(8,128)(2,1)S(1)} %get-tuple-element.26), channel_id=1, source_target_pairs={{4,0},{8,4},{12,8},{16,12},{20,16},{24,20},{28,24},{5,1},{9,5},{13... | collective-permute-start | bytes 838664 | tf_op jit(solution)/shard_map/ppermute | solution.py:443
  14.5 7.4 %copy-start = (f32[720,128]{1,0:T(8,128)S(1)}, f32[720,128]{1,0:T(8,128)}, u32[]{:S(2)}) copy-start(f32[720,128]{1,0:T(8,128)} %scale_ref.1) | copy-start | bytes 1105924
  14.5 7.4 %copy-start.1 = (f32[720,128]{1,0:T(8,128)S(1)}, f32[720,128]{1,0:T(8,128)}, u32[]{:S(2)}) copy-start(f32[720,128]{1,0:T(8,128)} %shift_ref.1) | copy-start | bytes 1105924
  14.5 7.4 %copy-start.2 = (bf16[3,3,128,128]{3,2,1,0:T(8,128)(2,1)S(1)}, bf16[3,3,128,128]{3,2,1,0:T(8,128)(2,1)}, u32[]{:S(2)}) copy-start(bf16[3,3,128,128]{3,2,1,0:T(8,128)(2,1)} %wh_ref.1) | copy-start | bytes 884740
  14.6 7.4 %copy-start.3 = (bf16[360,360]{1,0:T(8,128)(2,1)S(1)}, bf16[360,360]{1,0:T(8,128)(2,1)}, u32[]{:S(2)}) copy-start(bf16[360,360]{1,0:T(8,128)(2,1)} %z_ref.1) | copy-start | bytes 777604
  14.6 7.4 %copy-start.4 = (s32[8]{0:T(128)S(1)}, s32[8]{0:T(128)}, u32[]{:S(2)}) copy-start(s32[8]{0:T(128)} %ids_ref) | copy-start | bytes 100
  14.6 13.3 %collective-permute-start.3 = (bf16[8,90,128]{2,1,0:T(8,128)(2,1)S(1)}, bf16[8,90,128]{2,1,0:T(8,128)(2,1)S(1)}, u32[]{:S(2)}, u32[]{:S(2)}) collective-permute-start(bf16[8,90,128]{2,1,0:T(8,128)(2,1)S(1)} %encode.3.refs_0_), channel_id=1, source_target_pairs={{0,2},{1,3},{2,0},{3,1},{4,6},{5,7},{6,4},{7,5},{8,10},{9,11},{10,... | collective-permute-start | bytes 552968 | tf_op jit(solution)/shard_map/ppermute | solution.py:458
  16.2 13.5 %collective-permute-start.2 = (bf16[8,90,128]{2,1,0:T(8,128)(2,1)S(1)}, bf16[8,90,128]{2,1,0:T(8,128)(2,1)S(1)}, u32[]{:S(2)}, u32[]{:S(2)}) collective-permute-start(bf16[8,90,128]{2,1,0:T(8,128)(2,1)S(1)} %encode.3.refs_0_), channel_id=1, source_target_pairs={{0,1},{1,0},{2,3},{3,2},{4,5},{5,4},{6,7},{7,6},{8,9},{9,8},{10,11... | collective-permute-start | bytes 552968 | tf_op jit(solution)/shard_map/ppermute | solution.py:459
  21.0 6.8 %collective-permute-start.8 = (bf16[8,90,128]{2,1,0:T(8,128)(2,1)S(1)}, bf16[8,90,128]{2,1,0:T(8,128)(2,1)S(1)}, u32[]{:S(2)}, u32[]{:S(2)}) collective-permute-start(bf16[8,90,128]{2,1,0:T(8,128)(2,1)S(1)} %encode.4.refs_4_), channel_id=1, source_target_pairs={{0,2},{1,3},{2,0},{3,1},{4,6},{5,7},{6,4},{7,5},{8,10},{9,11},{10,... | collective-permute-start | bytes 552968 | tf_op jit(solution)/shard_map/ppermute | solution.py:458
  22.9 7.4 %collective-permute-start.7 = (bf16[8,90,128]{2,1,0:T(8,128)(2,1)S(1)}, bf16[8,90,128]{2,1,0:T(8,128)(2,1)S(1)}, u32[]{:S(2)}, u32[]{:S(2)}) collective-permute-start(bf16[8,90,128]{2,1,0:T(8,128)(2,1)S(1)} %encode.4.refs_4_), channel_id=1, source_target_pairs={{0,1},{1,0},{2,3},{3,2},{4,5},{5,4},{6,7},{7,6},{8,9},{9,8},{10,11... | collective-permute-start | bytes 552968 | tf_op jit(solution)/shard_map/ppermute | solution.py:459
  27.8 2.7 %collective-permute-start.6 = (bf16[8,90,128]{2,1,0:T(8,128)(2,1)S(1)}, bf16[8,90,128]{2,1,0:T(8,128)(2,1)S(1)}, u32[]{:S(2)}, u32[]{:S(2)}) collective-permute-start(bf16[8,90,128]{2,1,0:T(8,128)(2,1)S(1)} %collective-permute-done.3.refs_2_), channel_id=1, source_target_pairs={{0,1},{1,0},{2,3},{3,2},{4,5},{5,4},{6,7},{7,6},{8,9},{9,8},{10,11... | collective-permute-start | bytes 552968 | tf_op jit(solution)/shard_map/ppermute | solution.py:464
  28.4 2.2 %collective-permute-start.9 = (bf16[8,90,128]{2,1,0:T(8,128)(2,1)S(1)}, bf16[8,90,128]{2,1,0:T(8,128)(2,1)S(1)}, u32[]{:S(2)}, u32[]{:S(2)}) collective-permute-start(bf16[8,90,128]{2,1,0:T(8,128)(2,1)S(1)} %collective-permute-done.8.refs_6_), channel_id=1, source_target_pairs={{0,1},{1,0},{2,3},{3,2},{4,5},{5,4},{6,7},{7,6},{8,9},{9,8},{10,11... | collective-permute-start | bytes 552968 | tf_op jit(solution)/shard_map/ppermute | solution.py:464
  28.4 8.3 %collective-permute-start.12 = (bf16[6,90,128]{2,1,0:T(8,128)(2,1)S(1)}, bf16[6,90,128]{2,1,0:T(8,128)(2,1)S(1)}, u32[]{:S(2)}, u32[]{:S(2)}) collective-permute-start(bf16[6,90,128]{2,1,0:T(8,128)(2,1)S(1)} %encode.5.refs_8_), channel_id=1, source_target_pairs={{0,3},{1,2},{2,1},{3,0},{4,7},{5,6},{6,5},{7,4},{8,11},{9,10},{10,... | collective-permute-start | bytes 414728 | tf_op jit(solution)/shard_map/ppermute | solution.py:461
  29.6 8.0 %collective-permute-start.11 = (bf16[6,90,128]{2,1,0:T(8,128)(2,1)S(1)}, bf16[6,90,128]{2,1,0:T(8,128)(2,1)S(1)}, u32[]{:S(2)}, u32[]{:S(2)}) collective-permute-start(bf16[6,90,128]{2,1,0:T(8,128)(2,1)S(1)} %encode.5.refs_8_), channel_id=1, source_target_pairs={{0,2},{1,3},{2,0},{3,1},{4,6},{5,7},{6,4},{7,5},{8,10},{9,11},{10,... | collective-permute-start | bytes 414728 | tf_op jit(solution)/shard_map/ppermute | solution.py:458
  30.3 7.3 %collective-permute-start.10 = (bf16[6,90,128]{2,1,0:T(8,128)(2,1)S(1)}, bf16[6,90,128]{2,1,0:T(8,128)(2,1)S(1)}, u32[]{:S(2)}, u32[]{:S(2)}) collective-permute-start(bf16[6,90,128]{2,1,0:T(8,128)(2,1)S(1)} %encode.5.refs_8_), channel_id=1, source_target_pairs={{0,1},{1,0},{2,3},{3,2},{4,5},{5,4},{6,7},{7,6},{8,9},{9,8},{10,11... | collective-permute-start | bytes 414728 | tf_op jit(solution)/shard_map/ppermute | solution.py:459
